TPU v7x, 32 devices: a whole 2x2x4 slice. The times are simulated.
32 devices in a mesh: head: 4 (over x, core), blk: 8 (over z, y).
Axes of the slice: x: 2, y: 2, z: 4, core: 2. Of those that a mesh axis runs over, the one named last changes fastest.
Arguments:
- inputs: bfloat16 [2, 2048, 768], P(None, ('head', 'blk')), may hold values from -6 to 6
- doc_lengths: int32 [2, 32], replicated, may hold values from 1 to 1024, 2048 in all within a row
- grad_out: bfloat16 [2, 2048, 768], P(None, ('head', 'blk')), may hold values from -6 to 6
- qkv_weight: bfloat16 [3, 768, 768], P(None, ('head', 'blk')), may hold values from -0.21875 to 0.21875
- out_weight: bfloat16 [768, 768], P(('head', 'blk')), may hold values from -1.75 to 1.75
- inner_weight: bfloat16 [768, 3072], P(('head', 'blk')), may hold values from -0.21875 to 0.21875
- outer_weight: bfloat16 [3072, 768], P(('head', 'blk')), may hold values from -0.109375 to 0.109375
- bias_rows: bfloat16 [4, 768], P(None, ('head', 'blk')), may hold values from -3 to 3
- inner_bias: bfloat16 [3072], P(('head', 'blk')), may hold values from -3 to 3
- norm_gains: bfloat16 [2, 768], P(None, ('head', 'blk')), may hold values from 0.5 to 1.5
- norm_shifts: bfloat16 [2, 768], P(None, ('head', 'blk')), may hold values from -3 to 3
Outputs:
- output: bfloat16 [2, 2048, 768], P(None, ('head', 'blk'))
- grad_inputs: bfloat16 [2, 2048, 768], P(None, ('head', 'blk'))
- grad_qkv_weight: float32 [3, 768, 768], P(None, ('head', 'blk'))
- grad_out_weight: float32 [768, 768], P(('head', 'blk'))
- grad_inner_weight: float32 [768, 3072], P(('head', 'blk'))
- grad_outer_weight: float32 [3072, 768], P(('head', 'blk'))
- grad_bias_rows: float32 [4, 768], P(None, ('head', 'blk'))
- grad_inner_bias: float32 [3072], P(('head', 'blk'))
- grad_norm_gains: float32 [2, 768], P(None, ('head', 'blk'))
- grad_norm_shifts: float32 [2, 768], P(None, ('head', 'blk'))
Inputs may be any that keep to these rules, and one draw needn't show every extreme that they name: `doc_lengths`: each row lists, in order, the lengths of the 32 documents packed into one micro-batch's sequence; a row sums to 2048, and its longest document has exactly half of 2048 tokens.
All inputs are finite; a program needn't handle non-finite values.
Results may differ from a plain program's by a relative error of at most 0.017.
Values may be sent and summed in bfloat16 or wider, within the bound.
No kernel may reach another device: no remote copies, remote signals or barrier semaphores. Data moves between devices by JAX's collectives and lax.ppermute only.
A program may use at most 256 MiB of HBM per device.

v0:
```python
import math

import jax
import jax.numpy as jnp
from jax import lax
from jax.sharding import PartitionSpec as P

D = 768
HEADS = 12
FF = 3072
MB = 2


norm_eps = 1e-12
masked_score = -1e30


def layer_norm(hidden, norm_gain, norm_shift):
    center = hidden - jnp.mean(hidden, axis=-1, keepdims=True)
    spread = jnp.mean(center * center, axis=-1, keepdims=True)
    return center * lax.rsqrt(spread + norm_eps) * norm_gain + norm_shift


def exact_gelu(pre_act):
    return jax.nn.gelu(pre_act, approximate=False)


def doc_index(positions, lengths):
    bounds = jnp.cumsum(lengths)
    return jnp.sum((positions[:, None] >= bounds[None, :]).astype(jnp.int32), axis=1)


def row_positions(indices, width, quarter, tokens_dev):
    block_index = indices // width
    inner_row = indices % width
    return inner_row // tokens_dev * quarter + block_index * tokens_dev + inner_row % tokens_dev


def collect(
    qkv_weight,
    out_weight,
    inner_weight,
    outer_weight,
    bias_rows,
    inner_bias,
    norm_gains,
    norm_shifts,
):
    return (
        lax.all_gather(qkv_weight, ("head", "blk"), axis=1, tiled=True),
        lax.all_gather(out_weight, ("head", "blk"), axis=0, tiled=True),
        lax.all_gather(inner_weight, ("head", "blk"), axis=0, tiled=True),
        lax.all_gather(outer_weight, ("head", "blk"), axis=0, tiled=True),
        lax.all_gather(bias_rows, ("head", "blk"), axis=1, tiled=True),
        lax.all_gather(inner_bias, ("head", "blk"), axis=0, tiled=True),
        lax.all_gather(norm_gains, ("head", "blk"), axis=1, tiled=True),
        lax.all_gather(norm_shifts, ("head", "blk"), axis=1, tiled=True),
    )


def fold_block(state, query_rows, query_docs, key_rows, value_rows, key_docs, score_scale):
    running_max, running_sum, running_out = state
    scores = (
        jnp.einsum("qhd,khd->hqk", query_rows, key_rows, preferred_element_type=jnp.float32)
        * score_scale
    )
    same_doc = (query_docs[:, None] == key_docs[None, :])[None]
    scores = jnp.where(same_doc, scores, masked_score)
    new_max = jnp.maximum(running_max, jnp.max(scores, axis=-1))
    attn_prob = jnp.where(same_doc, jnp.exp(scores - new_max[:, :, None]), 0.0)
    factor = jnp.exp(running_max - new_max)
    running_sum = running_sum * factor + jnp.sum(attn_prob, axis=-1)
    update = jnp.einsum(
        "hqk,khd->qhd",
        attn_prob.astype(jnp.bfloat16),
        value_rows,
        preferred_element_type=jnp.float32,
    )
    running_out = running_out * factor.T[:, :, None] + update
    return (new_max, running_sum, running_out)


def grad_block(
    query_rows,
    grad_rows,
    lse_rows,
    delta_rows,
    query_docs,
    key_rows,
    value_rows,
    key_docs,
    score_scale,
):
    scores = (
        jnp.einsum("qhd,khd->hqk", query_rows, key_rows, preferred_element_type=jnp.float32)
        * score_scale
    )
    same_doc = (query_docs[:, None] == key_docs[None, :])[None]
    attn_prob = jnp.where(
        same_doc, jnp.exp(jnp.where(same_doc, scores, masked_score) - lse_rows[:, :, None]), 0.0
    )
    grad_values = jnp.einsum(
        "hqk,qhd->khd",
        attn_prob.astype(jnp.bfloat16),
        grad_rows,
        preferred_element_type=jnp.float32,
    )
    grad_prob = jnp.einsum(
        "qhd,khd->hqk", grad_rows, value_rows, preferred_element_type=jnp.float32
    )
    grad_scores = (attn_prob * (grad_prob - delta_rows[:, :, None])).astype(jnp.bfloat16)
    grad_queries = (
        jnp.einsum("hqk,khd->qhd", grad_scores, key_rows, preferred_element_type=jnp.float32)
        * score_scale
    )
    grad_keys = (
        jnp.einsum("hqk,qhd->khd", grad_scores, query_rows, preferred_element_type=jnp.float32)
        * score_scale
    )
    return (grad_queries, grad_keys, grad_values)


def local(
    inputs,
    doc_lengths,
    grad_out,
    qkv_weight,
    out_weight,
    inner_weight,
    outer_weight,
    bias_rows,
    inner_bias,
    norm_gains,
    norm_shifts,
):
    tokens_dev = inputs.shape[1]
    groups = lax.axis_size("head")
    cycle_size = lax.axis_size("blk")
    width = groups * tokens_dev
    quarter = cycle_size * tokens_dev
    heads_dev = HEADS // groups
    head_dim = D // HEADS
    group_width = heads_dev * head_dim
    score_scale = 1.0 / math.sqrt(head_dim)
    own_index = lax.axis_index("blk") * width + jnp.arange(width, dtype=jnp.int32)
    own_positions = row_positions(own_index, width, quarter, tokens_dev)
    step_rows = 2 * width
    step_count = cycle_size * width // step_rows
    all_positions = row_positions(
        jnp.arange(cycle_size * width, dtype=jnp.int32), width, quarter, tokens_dev
    )
    totals = [
        jnp.zeros((3, D, D), jnp.float32),
        jnp.zeros((D, D), jnp.float32),
        jnp.zeros((D, FF), jnp.float32),
        jnp.zeros((FF, D), jnp.float32),
        jnp.zeros((4, D), jnp.float32),
        jnp.zeros((FF,), jnp.float32),
        jnp.zeros((2, D), jnp.float32),
        jnp.zeros((2, D), jnp.float32),
    ]
    outputs_list = []
    grads_list = []
    for micro in range(MB):
        forward_weights = collect(
            qkv_weight,
            out_weight,
            inner_weight,
            outer_weight,
            bias_rows,
            inner_bias,
            norm_gains,
            norm_shifts,
        )
        fwd_qkv, fwd_out, fwd_inner, fwd_outer, fwd_bias, fwd_ibias, fwd_gains, fwd_shifts = (
            forward_weights
        )
        lengths = doc_lengths[micro]
        own_docs = doc_index(own_positions, lengths)
        all_docs = doc_index(all_positions, lengths).reshape(step_count, step_rows)
        token_rows = inputs[micro]
        bias_float = fwd_bias.astype(jnp.float32)
        zero_row = jnp.zeros((D,), jnp.float32)
        qkv_bias = (
            jnp.stack([bias_float[0], zero_row, bias_float[1]])
            .reshape(3, groups, group_width)
            .transpose(1, 0, 2)
        )
        projected = (
            jnp.einsum(
                "td,cdgf->tgcf",
                token_rows,
                fwd_qkv.reshape(3, D, groups, group_width),
                preferred_element_type=jnp.float32,
            )
            + qkv_bias[None]
        )
        projected = projected.astype(jnp.bfloat16).reshape(tokens_dev, groups, 3 * group_width)
        by_heads = lax.all_to_all(
            projected, "head", split_axis=1, concat_axis=0, tiled=True
        ).reshape(width, 3 * group_width)
        query_flat = by_heads[:, :group_width]
        query_rows = query_flat.reshape(width, heads_dev, head_dim)
        kv_rows = by_heads[:, group_width:]
        start_state = (
            jnp.full((heads_dev, width), masked_score, jnp.float32),
            jnp.zeros((heads_dev, width), jnp.float32),
            jnp.zeros((width, heads_dev, head_dim), jnp.float32),
        )
        state = start_state
        piece = lax.all_gather(kv_rows, "blk", axis=0, tiled=True)
        piece_rows = piece.shape[0]
        part_count = piece_rows // width
        parts = piece.reshape(part_count, width, 2, heads_dev, head_dim)
        part_index = jnp.arange(piece_rows, dtype=jnp.int32).reshape(part_count, width)

        def one_part(carry, part_item):
            part_kv, index_rows = part_item
            key_docs = doc_index(row_positions(index_rows, width, quarter, tokens_dev), lengths)
            return (
                fold_block(
                    carry, query_rows, own_docs, part_kv[:, 0], part_kv[:, 1], key_docs, score_scale
                ),
                None,
            )

        state, unused = lax.scan(one_part, state, (parts, part_index))
        run_max, run_sum, run_out = state
        log_sum = run_max + jnp.log(run_sum)
        attn_full = run_out / run_sum.T[:, :, None]
        attn_low = attn_full.astype(jnp.bfloat16).reshape(width, 1, group_width)
        attn_tokens = lax.all_to_all(
            attn_low, "head", split_axis=0, concat_axis=1, tiled=True
        ).reshape(tokens_dev, D)
        gains_fwd = fwd_gains.astype(jnp.float32)
        shifts_fwd = fwd_shifts.astype(jnp.float32)
        branch = jnp.dot(attn_tokens, fwd_out, preferred_element_type=jnp.float32) + bias_float[2]
        first_sum = token_rows.astype(jnp.float32) + branch
        first_normed, pull_first = jax.vjp(layer_norm, first_sum, gains_fwd[0], shifts_fwd[0])
        normed_low = first_normed.astype(jnp.bfloat16)
        inner_pre = jnp.dot(
            normed_low, fwd_inner, preferred_element_type=jnp.float32
        ) + fwd_ibias.astype(jnp.float32)
        activated, pull_gelu = jax.vjp(exact_gelu, inner_pre)
        act_low = activated.astype(jnp.bfloat16)
        second_sum = (
            first_normed
            + jnp.dot(act_low, fwd_outer, preferred_element_type=jnp.float32)
            + bias_float[3]
        )
        layer_out, pull_second = jax.vjp(layer_norm, second_sum, gains_fwd[1], shifts_fwd[1])
        outputs_list.append(layer_out.astype(jnp.bfloat16))
        back_weights = collect(
            qkv_weight,
            out_weight,
            inner_weight,
            outer_weight,
            bias_rows,
            inner_bias,
            norm_gains,
            norm_shifts,
        )
        (
            back_qkv,
            back_out,
            back_inner,
            back_outer,
            back_bias,
            back_ibias,
            back_gains,
            back_shifts,
        ) = back_weights
        d_second, d_gain_two, d_shift_two = pull_second(grad_out[micro].astype(jnp.float32))
        d_ffn = d_second.astype(jnp.bfloat16)
        outer_grad = jnp.einsum("tf,td->fd", act_low, d_ffn, preferred_element_type=jnp.float32)
        ffn_bias_grad = jnp.sum(d_ffn.astype(jnp.float32), axis=0)
        d_hidden = jnp.einsum("td,fd->tf", d_ffn, back_outer, preferred_element_type=jnp.float32)
        d_inner = pull_gelu(d_hidden)[0].astype(jnp.bfloat16)
        inner_grad = jnp.einsum(
            "td,tf->df", normed_low, d_inner, preferred_element_type=jnp.float32
        )
        inner_bias_grad = jnp.sum(d_inner.astype(jnp.float32), axis=0)
        d_first_normed = d_second + jnp.einsum(
            "tf,df->td", d_inner, back_inner, preferred_element_type=jnp.float32
        )
        d_first, d_gain_one, d_shift_one = pull_first(d_first_normed)
        d_branch = d_first.astype(jnp.bfloat16)
        out_grad = jnp.einsum(
            "te,td->ed", attn_tokens, d_branch, preferred_element_type=jnp.float32
        )
        branch_bias_grad = jnp.sum(d_branch.astype(jnp.float32), axis=0)
        d_attn = jnp.einsum(
            "td,ed->te", d_branch, back_out, preferred_element_type=jnp.float32
        ).astype(jnp.bfloat16)
        grad_heads = lax.all_to_all(
            d_attn.reshape(tokens_dev, groups, group_width),
            "head",
            split_axis=1,
            concat_axis=0,
            tiled=True,
        ).reshape(width, heads_dev, head_dim)
        delta_rows = jnp.sum(grad_heads.astype(jnp.float32) * attn_full, axis=-1).T
        kv_all = lax.all_gather(kv_rows, "blk", axis=0, tiled=True).reshape(
            step_count, step_rows, 2, heads_dev, head_dim
        )

        def key_step(grad_query, key_item):
            part_kv, part_docs = key_item
            grad_queries, grad_keys, grad_values = grad_block(
                query_rows,
                grad_heads,
                log_sum,
                delta_rows,
                own_docs,
                part_kv[:, 0],
                part_kv[:, 1],
                part_docs,
                score_scale,
            )
            return (grad_query + grad_queries, jnp.stack([grad_keys, grad_values], axis=1))

        grad_query, kv_terms = lax.scan(
            key_step, jnp.zeros((width, heads_dev, head_dim), jnp.float32), (kv_all, all_docs)
        )
        kv_home = lax.psum_scatter(
            kv_terms.reshape(cycle_size * width, 2 * group_width),
            "blk",
            scatter_dimension=0,
            tiled=True,
        )
        grad_q_low = grad_query.reshape(width, group_width).astype(jnp.bfloat16)
        grad_kv_low = kv_home.astype(jnp.bfloat16)
        back_rows = jnp.concatenate([grad_q_low, grad_kv_low], axis=1).reshape(
            width, 1, 3 * group_width
        )
        home_grads = lax.all_to_all(
            back_rows, "head", split_axis=0, concat_axis=1, tiled=True
        ).reshape(tokens_dev, groups, 3, group_width)
        qkv_grad = jnp.einsum(
            "td,tgcf->cdgf", token_rows, home_grads, preferred_element_type=jnp.float32
        ).reshape(3, D, D)
        column_sums = jnp.sum(home_grads.astype(jnp.float32), axis=0)
        query_bias_grad = column_sums[:, 0].reshape(D)
        value_bias_grad = column_sums[:, 2].reshape(D)
        grad_tokens = d_first + jnp.einsum(
            "tgcf,cdgf->td",
            home_grads,
            back_qkv.reshape(3, D, groups, group_width),
            preferred_element_type=jnp.float32,
        )
        grads_list.append(grad_tokens.astype(jnp.bfloat16))
        totals[0] = totals[0] + qkv_grad
        totals[1] = totals[1] + out_grad
        totals[2] = totals[2] + inner_grad
        totals[3] = totals[3] + outer_grad
        totals[4] = totals[4] + jnp.stack(
            [query_bias_grad, value_bias_grad, branch_bias_grad, ffn_bias_grad]
        )
        totals[5] = totals[5] + inner_bias_grad
        totals[6] = totals[6] + jnp.stack([d_gain_one, d_gain_two])
        totals[7] = totals[7] + jnp.stack([d_shift_one, d_shift_two])
    summed = (
        lax.psum_scatter(totals[0], ("head", "blk"), scatter_dimension=1, tiled=True),
        lax.psum_scatter(totals[1], ("head", "blk"), scatter_dimension=0, tiled=True),
        lax.psum_scatter(totals[2], ("head", "blk"), scatter_dimension=0, tiled=True),
        lax.psum_scatter(totals[3], ("head", "blk"), scatter_dimension=0, tiled=True),
        lax.psum_scatter(totals[4], ("head", "blk"), scatter_dimension=1, tiled=True),
        lax.psum_scatter(totals[5], ("head", "blk"), scatter_dimension=0, tiled=True),
        lax.psum_scatter(totals[6], ("head", "blk"), scatter_dimension=1, tiled=True),
        lax.psum_scatter(totals[7], ("head", "blk"), scatter_dimension=1, tiled=True),
    )
    return (
        jnp.stack(outputs_list),
        jnp.stack(grads_list),
        summed[0],
        summed[1],
        summed[2],
        summed[3],
        summed[4],
        summed[5],
        summed[6],
        summed[7],
    )


def solution(mesh):
    placed = (
        P(None, ("head", "blk"), None),
        P(),
        P(None, ("head", "blk"), None),
        P(None, ("head", "blk"), None),
        P(("head", "blk"), None),
        P(("head", "blk"), None),
        P(("head", "blk"), None),
        P(None, ("head", "blk")),
        P(("head", "blk")),
        P(None, ("head", "blk")),
        P(None, ("head", "blk")),
    )
    return jax.shard_map(
        local,
        mesh=mesh,
        in_specs=placed,
        out_specs=(
            P(None, ("head", "blk"), None),
            P(None, ("head", "blk"), None),
            P(None, ("head", "blk"), None),
            P(("head", "blk"), None),
            P(("head", "blk"), None),
            P(("head", "blk"), None),
            P(None, ("head", "blk")),
            P(("head", "blk")),
            P(None, ("head", "blk")),
            P(None, ("head", "blk")),
        ),
        check_vma=False,
    )
```

profile of v0, /device:TPU:0, one launch (start us, length us, event | category | flops | bytes accessed | tf_op | source)
XLA Modules:
  0.0 1309.7 jit_solution(354472933839372777)
XLA Ops:
  8.0 70.2 %all-gather = bf16[32,24,4]{1,2,0:T(4,128)(2,1)S(1)} all-gather(bf16[1,24,4]{1,2,0:T(4,128)(2,1)} %bitcast.530), channel_id=1, replica_groups=mesh['head'=4,'blk'=8] {'head','blk'}, dimensions={0}, use_global_device_ids=true | all-gather | bytes 6336 | tf_op jit(solution)/shard_map/all_gather | solution.py:54
  79.3 4.3 copy.223
  89.1 10.2 all_to_all.120
  103.7 9.1 all_to_all.121
  118.1 37.4 %all-reduce = bf16[3072]{0:T(1024)(128)(2,1)S(1)} all-reduce(bf16[3072]{0:T(1024)(128)(2,1)S(1)} %dynamic-update-slice), channel_id=1, replica_groups=mesh['head'=4,'blk'=8] {'head','blk'}, use_global_device_ids=true, to_apply=%add | all-reduce | flops 3072 | bytes 12288
  158.7 65.7 %all-gather.1 = bf16[32,24,2]{1,2,0:T(2,128)(2,1)S(1)} all-gather(bf16[1,24,2]{1,2,0:T(2,128)(2,1)} %bitcast.531), channel_id=1, replica_groups=mesh['head'=4,'blk'=8] {'head','blk'}, dimensions={0}, use_global_device_ids=true | all-gather | bytes 3168 | tf_op jit(solution)/shard_map/all_gather | solution.py:56
  224.5 63.2 %all-gather.2 = bf16[32,24,2]{1,2,0:T(2,128)(2,1)S(1)} all-gather(bf16[1,24,2]{1,2,0:T(2,128)(2,1)} %bitcast.532), channel_id=1, replica_groups=mesh['head'=4,'blk'=8] {'head','blk'}, dimensions={0}, use_global_device_ids=true | all-gather | bytes 3168 | tf_op jit(solution)/shard_map/all_gather | solution.py:57
  293.7 16.3 %while.62 = (s32[]{:T(128)}, f32[3,256]{1,0:T(4,128)S(1)}, f32[3,256]{1,0:T(4,128)S(1)}, f32[256,3,64]{0,2,1:T(8,128)S(1)}, s32[256]{0:T(256)S(1)}, /*index=5*/s...) while((s32[]{:T(128)}, f32[3,256]{1,0:T(4,128)S(1)}, ...), condition=%wide.region_7.8_spmd.clone, body=%wide.region_3.7_spmd.clone.sunk | while | flops 52353792 | bytes 3762441 | solution.py:227
  312.7 3.9 all-to-all-start.1
  320.5 32.5 %while.63 = (s32[]{:T(128)}, f32[3,256]{1,0:T(4,128)S(1)}, f32[3,256]{1,0:T(4,128)S(1)}, f32[256,3,64]{0,2,1:T(8,128)S(1)}, s32[256]{0:T(256)}, /*index=5*/s32[8...) while((s32[]{:T(128)}, f32[3,256]{1,0:T(4,128)S(1)}, ...), condition=%wide.region_19.20_spmd.clone, body=%wide.region_15.19_spmd.clone.sunk | while | flops 52353792 | bytes 3762441 | solution.py:227
  360.5 3.9 all-to-all-start.3
  365.0 2.4 reshape.740
  367.4 2.8 reshape.747
  381.3 5.9 multiply_convert_fusion.1
  387.3 3.5 fusion.137
  391.1 4.8 multiply_convert_fusion
  404.5 2.4 convert_reduce_fusion.3
  406.8 2.3 multiply_reduce_fusion.1
  416.6 3.9 all-to-all-start.6
  425.7 3.3 all-to-all-start.4
  430.9 2.6 all-to-all-done.4
  434.0 2.2 broadcast.1065.clone2
  436.3 91.8 %while.65 = (s32[]{:T(128)}, f32[256,3,64]{0,2,1:T(8,128)S(1)}, f32[4,512,2,3,64]{1,0,4,3,2:T(4,128)}, bf16[4,512,2,3,64]{1,4,3,2,0:T(8,128)(2,1)}, s32[256]{0:T...) while((s32[]{:T(128)}, f32[256,3,64]{0,2,1:T(8,128)S(1)}, ...), condition=%wide.region_40.41_spmd.clone, body=%wide.region_39.40_spmd.clone.sunk | while | flops 255377408 | bytes 15021203 | solution.py:322
  443.1 16.1 %dynamic_update_slice.12 = f32[4,512,2,3,64]{1,0,4,3,2:T(4,128)} dynamic-update-slice(f32[4,512,2,3,64]{1,0,4,3,2:T(4,128)} %get-tuple-element.1313, f32[1,512,2,3,64]{1,0,4,3,2:T(1,128)S(1)} %copy.341, s32[]{:T(128)S(6)} %copy.372, s32[]{:T(128)} %constant.431.clone.1..sunk.3, s32[]{:T(128)} %constant.431.clone.1..sunk.3, s32[]{:T(128)} %constant.431.clone.1..sunk.3, s32[]{:T(128)} %constant.431.clone.1..sunk.3) | dynamic-update-slice | bytes 1572868 | tf_op jit(solution)/shard_map/while/body/jit(dynamic_update_index_in_dim)/dynamic_update_slice | solution.py:322
  466.1 16.1 %dynamic_update_slice.12 = f32[4,512,2,3,64]{1,0,4,3,2:T(4,128)} dynamic-update-slice(f32[4,512,2,3,64]{1,0,4,3,2:T(4,128)} %get-tuple-element.1313, f32[1,512,2,3,64]{1,0,4,3,2:T(1,128)S(1)} %copy.341, s32[]{:T(128)S(6)} %copy.372, s32[]{:T(128)} %constant.431.clone.1..sunk.3, s32[]{:T(128)} %constant.431.clone.1..sunk.3, s32[]{:T(128)} %constant.431.clone.1..sunk.3, s32[]{:T(128)} %constant.431.clone.1..sunk.3) | dynamic-update-slice | bytes 1572868 | tf_op jit(solution)/shard_map/while/body/jit(dynamic_update_index_in_dim)/dynamic_update_slice | solution.py:322
  489.0 16.1 %dynamic_update_slice.12 = f32[4,512,2,3,64]{1,0,4,3,2:T(4,128)} dynamic-update-slice(f32[4,512,2,3,64]{1,0,4,3,2:T(4,128)} %get-tuple-element.1313, f32[1,512,2,3,64]{1,0,4,3,2:T(1,128)S(1)} %copy.341, s32[]{:T(128)S(6)} %copy.372, s32[]{:T(128)} %constant.431.clone.1..sunk.3, s32[]{:T(128)} %constant.431.clone.1..sunk.3, s32[]{:T(128)} %constant.431.clone.1..sunk.3, s32[]{:T(128)} %constant.431.clone.1..sunk.3) | dynamic-update-slice | bytes 1572868 | tf_op jit(solution)/shard_map/while/body/jit(dynamic_update_index_in_dim)/dynamic_update_slice | solution.py:322
  512.0 16.1 %dynamic_update_slice.12 = f32[4,512,2,3,64]{1,0,4,3,2:T(4,128)} dynamic-update-slice(f32[4,512,2,3,64]{1,0,4,3,2:T(4,128)} %get-tuple-element.1313, f32[1,512,2,3,64]{1,0,4,3,2:T(1,128)S(1)} %copy.341, s32[]{:T(128)S(6)} %copy.372, s32[]{:T(128)} %constant.431.clone.1..sunk.3, s32[]{:T(128)} %constant.431.clone.1..sunk.3, s32[]{:T(128)} %constant.431.clone.1..sunk.3, s32[]{:T(128)} %constant.431.clone.1..sunk.3) | dynamic-update-slice | bytes 1572868 | tf_op jit(solution)/shard_map/while/body/jit(dynamic_update_index_in_dim)/dynamic_update_slice | solution.py:322
  528.0 5.0 copy.325
  533.2 2.2 broadcast.1065.clone2.1
  535.4 80.1 %while.64 = (s32[]{:T(128)}, f32[256,3,64]{0,2,1:T(8,128)S(1)}, f32[4,512,2,3,64]{1,0,4,3,2:T(4,128)}, bf16[4,512,2,3,64]{1,4,3,2,0:T(8,128)(2,1)S(1)}, s32[256]...) while((s32[]{:T(128)}, f32[256,3,64]{0,2,1:T(8,128)S(1)}, ...), condition=%wide.region_31.32_spmd.clone, body=%wide.region_30.31_spmd.clone.sunk | while | flops 255377408 | bytes 15023251 | solution.py:322
  539.5 16.1 %dynamic_update_slice.11 = f32[4,512,2,3,64]{1,0,4,3,2:T(4,128)} dynamic-update-slice(f32[4,512,2,3,64]{1,0,4,3,2:T(4,128)} %get-tuple-element.1349, f32[1,512,2,3,64]{1,0,4,3,2:T(1,128)S(1)} %copy.340, s32[]{:T(128)S(6)} %copy.381, s32[]{:T(128)} %constant.431.clone.1..sunk.2, s32[]{:T(128)} %constant.431.clone.1..sunk.2, s32[]{:T(128)} %constant.431.clone.1..sunk.2, s32[]{:T(128)} %constant.431.clone.1..sunk.2) | dynamic-update-slice | bytes 1572868 | tf_op jit(solution)/shard_map/while/body/jit(dynamic_update_index_in_dim)/dynamic_update_slice | solution.py:322
  559.5 16.1 %dynamic_update_slice.11 = f32[4,512,2,3,64]{1,0,4,3,2:T(4,128)} dynamic-update-slice(f32[4,512,2,3,64]{1,0,4,3,2:T(4,128)} %get-tuple-element.1349, f32[1,512,2,3,64]{1,0,4,3,2:T(1,128)S(1)} %copy.340, s32[]{:T(128)S(6)} %copy.381, s32[]{:T(128)} %constant.431.clone.1..sunk.2, s32[]{:T(128)} %constant.431.clone.1..sunk.2, s32[]{:T(128)} %constant.431.clone.1..sunk.2, s32[]{:T(128)} %constant.431.clone.1..sunk.2) | dynamic-update-slice | bytes 1572868 | tf_op jit(solution)/shard_map/while/body/jit(dynamic_update_index_in_dim)/dynamic_update_slice | solution.py:322
  579.5 16.1 %dynamic_update_slice.11 = f32[4,512,2,3,64]{1,0,4,3,2:T(4,128)} dynamic-update-slice(f32[4,512,2,3,64]{1,0,4,3,2:T(4,128)} %get-tuple-element.1349, f32[1,512,2,3,64]{1,0,4,3,2:T(1,128)S(1)} %copy.340, s32[]{:T(128)S(6)} %copy.381, s32[]{:T(128)} %constant.431.clone.1..sunk.2, s32[]{:T(128)} %constant.431.clone.1..sunk.2, s32[]{:T(128)} %constant.431.clone.1..sunk.2, s32[]{:T(128)} %constant.431.clone.1..sunk.2) | dynamic-update-slice | bytes 1572868 | tf_op jit(solution)/shard_map/while/body/jit(dynamic_update_index_in_dim)/dynamic_update_slice | solution.py:322
  599.4 16.1 %dynamic_update_slice.11 = f32[4,512,2,3,64]{1,0,4,3,2:T(4,128)} dynamic-update-slice(f32[4,512,2,3,64]{1,0,4,3,2:T(4,128)} %get-tuple-element.1349, f32[1,512,2,3,64]{1,0,4,3,2:T(1,128)S(1)} %copy.340, s32[]{:T(128)S(6)} %copy.381, s32[]{:T(128)} %constant.431.clone.1..sunk.2, s32[]{:T(128)} %constant.431.clone.1..sunk.2, s32[]{:T(128)} %constant.431.clone.1..sunk.2, s32[]{:T(128)} %constant.431.clone.1..sunk.2) | dynamic-update-slice | bytes 1572868 | tf_op jit(solution)/shard_map/while/body/jit(dynamic_update_index_in_dim)/dynamic_update_slice | solution.py:322
  615.5 5.0 copy.324
  624.6 3.5 all-to-all-start.7
  628.1 65.6 %reduce-scatter.9.cloned.1.call-done = f32[256,384]{0,1:T(8,128)} async-done(((f32[2048,384]{0,1:T(8,128)}), f32[256,384]{0,1:T(8,128)}) %reduce-scatter.9.cloned.1.call-update) | async-done | bytes 393232 | tf_op jit(solution)/shard_map/reduce_scatter | solution.py:325
  697.0 3.6 all-to-all-start.5
  701.5 5.4 all-to-all-done.5
  710.1 3.3 copy.259
  713.4 11.0 copy.260
  729.7 5.2 convolution_add_fusion.1
  737.4 5.1 convolution_add_fusion
  768.1 40.6 %all-reduce.6 = (f32[4,768]{1,0:T(4,128)}, f32[3072]{0:T(1024)}, f32[2,768]{1,0:T(2,128)}, f32[2,768]{1,0:T(2,128)}) all-reduce(f32[4,768]{1,0:T(4,128)} %maximum_add_fusion, f32[3072]{0:T(1024)S(1)} %add.550, f32[2,768]{1,0:T(2,128)} %maximum_add_fusion.1, ...), channel_id=8, replica_groups=mesh['head'=4,'blk'=8] {'head','blk'}, use_global_device_ids=true, to_apply=%region_52.53.clone | all-reduce | flops 9216 | bytes 73728
  817.4 96.4 %all-reduce.9.cloned.1.call-done = f32[3,768,768]{2,0,1:T(4,128)} async-done(((f32[3,768,768]{2,0,1:T(4,128)}), f32[3,768,768]{2,0,1:T(4,128)}) %all-reduce.9.cloned.1.call-update) | async-done | bytes 7077904
  915.5 103.9 %reduce-scatter.13.cloned.1.call-done = f32[24,768]{1,0:T(8,128)} async-done(((f32[768,768]{1,0:T(8,128)}), f32[24,768]{1,0:T(8,128)}) %reduce-scatter.13.cloned.1.call-update) | async-done | bytes 73744 | tf_op jit(solution)/shard_map/reduce_scatter | solution.py:364
  1019.4 141.2 %reduce-scatter.15.cloned.1.call-done = f32[24,3072]{1,0:T(8,128)} async-done(((f32[768,3072]{1,0:T(8,128)}), f32[24,3072]{1,0:T(8,128)}) %reduce-scatter.15.cloned.1.call-update) | async-done | bytes 294928 | tf_op jit(solution)/shard_map/reduce_scatter | solution.py:365
  1160.6 141.8 %reduce-scatter.17.cloned.1.call-done = f32[96,768]{1,0:T(8,128)} async-done(((f32[3072,768]{1,0:T(8,128)}), f32[96,768]{1,0:T(8,128)}) %reduce-scatter.17.cloned.1.call-update) | async-done | bytes 294928 | tf_op jit(solution)/shard_map/reduce_scatter | solution.py:366
  (645 shorter events, 220.3 us)
Async XLA Ops:
  7.2 72.1 %all-gather.10.cloned.1.call-start = ((), (), s32[]{:S(2)}) async-start(), calls=%async_computation.13 | async-start | bytes 3649536 | tf_op jit(solution)/shard_map/all_gather | solution.py:50
  7.9 282.1 %all-gather.12.cloned.1.call-start = ((), (), s32[]{:S(2)}) async-start(), calls=%async_computation.14 | async-start | bytes 1769472 | tf_op jit(solution)/shard_map/all_gather | solution.py:211
  83.6 17.3 %copy-start = (bf16[3,768,768]{1,2,0:T(8,128)(2,1)}, bf16[3,768,768]{1,2,0:T(8,128)(2,1)S(1)}, u32[]{:S(2)}) copy-start(bf16[3,768,768]{1,2,0:T(8,128)(2,1)S(1)} %copy.223) | copy-start | bytes 10616836
  100.8 215.9 %all-gather.20.cloned.1.call-start = ((), (), s32[]{:S(2)}) async-start(), calls=%async_computation.18 | async-start | bytes 1769472 | tf_op jit(solution)/shard_map/all_gather | solution.py:211
  113.7 262.8 %all-gather.14.cloned.1.call-start = ((), (), s32[]{:S(2)}) async-start(), calls=%async_computation.15 | async-start | bytes 1216512 | tf_op jit(solution)/shard_map/all_gather | solution.py:51
  114.3 267.0 %all-gather.16.cloned.1.call-start = ((), (), s32[]{:S(2)}) async-start(), calls=%async_computation.16 | async-start | bytes 4866048 | tf_op jit(solution)/shard_map/all_gather | solution.py:52
  114.8 272.4 %all-gather.18.cloned.1.call-start = ((), (), s32[]{:S(2)}) async-start(), calls=%async_computation.17 | async-start | bytes 4866048 | tf_op jit(solution)/shard_map/all_gather | solution.py:53
  310.0 6.6 copy-start.3
  312.7 47.8 %all-to-all-start.1 = ((bf16[4,2,6144]{2,1,0:T(2,128)(2,1)}), bf16[4,2,6144]{2,1,0:T(2,128)(2,1)}, u32[]{:S(2)}, u32[]{:S(2)}) async-start(bf16[4,2,6144]{2,1,0:T(2,128)(2,1)} %reshape.801), calls=%async_computation.1 | async-start | bytes 196608 | tf_op jit(solution)/shard_map/all_to_all | solution.py:232
  360.5 14.6 %all-to-all-start.3 = ((bf16[4,2,6144]{2,1,0:T(2,128)(2,1)}), bf16[4,2,6144]{2,1,0:T(2,128)(2,1)}, u32[]{:S(2)}, u32[]{:S(2)}) async-start(bf16[4,2,6144]{2,1,0:T(2,128)(2,1)} %reshape.799), calls=%async_computation.3 | async-start | bytes 196608 | tf_op jit(solution)/shard_map/all_to_all | solution.py:232
  373.7 7.6 copy-start.47
  373.7 7.6 copy-start.69
  375.1 12.1 copy-start.35
  376.5 4.8 copy-start.39
  380.0 29.2 %copy-start.5 = (f32[64,768]{1,0:T(8,128)}, f32[64,768]{1,0:T(8,128)S(1)}, u32[]{:S(2)}) copy-start(f32[64,768]{1,0:T(8,128)S(1)} %get-tuple-element.976) | copy-start | bytes 589828
  380.0 7.3 copy-start.55
  380.7 6.5 copy-start.78
  381.2 6.0 copy-start.66
  381.3 6.0 copy-start.53
  387.2 8.7 copy-start.21
  387.3 8.7 slice-start
  391.1 4.9 slice-start.1
  391.1 4.9 copy-start.54
  396.0 6.8 slice-start.2
  398.2 4.6 slice-start.3
  399.9 4.5 copy-start.31
  406.8 5.3 copy-start.2
  410.8 23.1 %copy-start.4 = (f32[256,3,64]{0,2,1:T(8,128)S(1)}, f32[256,3,64]{0,2,1:T(8,128)}, u32[]{:S(2)}) copy-start(f32[256,3,64]{0,2,1:T(8,128)} %copy-done.3) | copy-start | bytes 589828
  410.8 23.1 %copy-start.46 = (f32[3,256]{1,0:T(4,128)S(1)}, f32[3,256]{1,0:T(4,128)}, u32[]{:S(2)}) copy-start(f32[3,256]{1,0:T(4,128)} %copy-done.45) | copy-start | bytes 9220
  416.6 9.1 all-to-all-start.6
  423.9 12.4 copy-start.8
  425.7 7.9 all-to-all-start.4
  429.0 192.5 %reduce-scatter.11.cloned.1.call-start = ((), (), s32[]{:S(2)}) async-start(), calls=%async_computation.20 | async-start | bytes 3538944 | tf_op jit(solution)/shard_map/reduce_scatter | solution.py:325
  528.0 5.0 copy-start.9
  533.1 160.7 %reduce-scatter.9.cloned.1.call-start = ((), (), s32[]{:S(2)}) async-start(), calls=%async_computation.19 | async-start | bytes 3538944 | tf_op jit(solution)/shard_map/reduce_scatter | solution.py:325
  624.6 72.3 %all-to-all-start.7 = ((bf16[4,2,18432]{2,1,0:T(2,128)(2,1)}), bf16[4,2,18432]{2,1,0:T(2,128)(2,1)S(1)}, u32[]{:S(2)}, u32[]{:S(2)}) async-start(bf16[4,2,18432]{2,1,0:T(2,128)(2,1)} %reshape.803), calls=%async_computation.9 | async-start | bytes 589824 | tf_op jit(solution)/shard_map/all_to_all | solution.py:336
  697.0 10.8 copy-start.24
  697.0 9.9 all-to-all-start.5
  700.6 213.2 %all-reduce.9.cloned.1.call-start = ((), (), s32[]{:S(2)}) async-start(), calls=%async_computation.24 | async-start | bytes 18874368
  701.2 6.3 copy-start.20
  701.5 7.4 copy-start.12
  724.4 295.0 %reduce-scatter.13.cloned.1.call-start = ((), (), s32[]{:S(2)}) async-start(), calls=%async_computation.21 | async-start | bytes 2433024 | tf_op jit(solution)/shard_map/reduce_scatter | solution.py:364
  727.8 432.8 %reduce-scatter.15.cloned.1.call-start = ((), (), s32[]{:S(2)}) async-start(), calls=%async_computation.22 | async-start | bytes 9732096 | tf_op jit(solution)/shard_map/reduce_scatter | solution.py:365
  735.0 567.4 %reduce-scatter.17.cloned.1.call-start = ((), (), s32[]{:S(2)}) async-start(), calls=%async_computation.23 | async-start | bytes 9732096 | tf_op jit(solution)/shard_map/reduce_scatter | solution.py:366
  742.5 71.5 %copy-start.1 = (bf16[3,768,768]{1,2,0:T(8,128)(2,1)S(1)}, bf16[3,768,768]{1,2,0:T(8,128)(2,1)}, u32[]{:S(2)}) copy-start(bf16[3,768,768]{1,2,0:T(8,128)(2,1)} %copy-done) | copy-start | bytes 10616836
  766.7 49.2 %copy-start.74 = (f32[64]{0:T(128)S(1)}, f32[64]{0:T(128)}, u32[]{:S(2)}) copy-start(f32[64]{0:T(128)} %negate_multiply_fusion.4) | copy-start | bytes 772
  808.7 7.2 copy-start.14
  808.7 7.2 copy-start.25
  (54 other events, 98.3 us)
Sparse Core Ops, SparseCore 0:
  10.9 63.0 all-gather.9
  100.9 41.2 all-gather.11
  144.9 42.8 all-gather.19
  190.6 52.9 all-gather.13
  246.3 62.5 all-gather.15
  311.7 63.5 all-gather.17
  533.2 73.0 reduce-scatter.10
  620.6 73.0 reduce-scatter.8
  724.5 189.2 all-reduce.8
  920.4 99.0 reduce-scatter.12
  1025.9 134.6 reduce-scatter.14
  1168.0 134.3 reduce-scatter.16
where the time goes:
time: 1330 us; the launch traced here: 1310 us
  waiting for transfers between devices  559 us (42%)
  blocking collectives  296 us (22%)
  local copies, waits for them, and re-layouts  274 us (21%)
  matrix products  85.7 us (6%)
  other arithmetic  53 us (4%)
  starting transfers between devices  22.9 us (2%)
  between operations  16.2 us (1%)
    reduce_scatter x1, waiting for transfers between devices, local(): lax.psum_scatter(totals[3], ('head', 'blk'), scatter_dimension=0, tiled=T...  142 us
    reduce_scatter x1, waiting for transfers between devices, local(): lax.psum_scatter(totals[2], ('head', 'blk'), scatter_dimension=0, tiled=T...  141 us
    dynamic_update_slice x16, local copies, waits for them, and re-layouts, local(): lax.scan(key_step, jnp.zeros((width, heads_dev, head_dim), jnp.float32),...  135 us
    reduce_scatter x1, waiting for transfers between devices, local(): lax.psum_scatter(totals[1], ('head', 'blk'), scatter_dimension=0, tiled=T...  104 us
    unnamed x13, waiting for transfers between devices  98.8 us
    unnamed x2, blocking collectives  78 us
    all_gather x1, blocking collectives, collect(): lax.all_gather(bias_rows, ('head', 'blk'), axis=1, tiled=True)  70.2 us
    all_gather x1, blocking collectives, collect(): lax.all_gather(norm_gains, ('head', 'blk'), axis=1, tiled=True)  65.7 us
  transfers between devices with their start and end apart: 18, of which 7 were waited for; matrix products, arithmetic and copies ran while one was open for 19% of the time, Pallas kernels for 0%

commit v1 on v0

--- a/solution.py
+++ b/solution.py
@@ -26,7 +26,8 @@
 
 
 def doc_index(positions, lengths):
-    bounds = jnp.cumsum(lengths)
+    order = jnp.arange(lengths.shape[0], dtype=jnp.int32)
+    bounds = jnp.sum(jnp.where(order[None, :] <= order[:, None], lengths[None, :], 0), axis=1)
     return jnp.sum((positions[:, None] >= bounds[None, :]).astype(jnp.int32), axis=1)
 
 

time: 1330 us -> 1330 us (level)
  no operation moved by 1% of the time
where the time goes in v1:
time: 1330 us; the launch traced here: 1310 us
  waiting for transfers between devices  560 us (42%)
  blocking collectives  297 us (22%)
  local copies, waits for them, and re-layouts  274 us (21%)
  matrix products  85.7 us (6%)
  other arithmetic  53.6 us (4%)
  starting transfers between devices  22.9 us (2%)
  between operations  16.2 us (1%)
    reduce_scatter x1, waiting for transfers between devices, local(): lax.psum_scatter(totals[3], ('head', 'blk'), scatter_dimension=0, tiled=T...  142 us
    reduce_scatter x1, waiting for transfers between devices, local(): lax.psum_scatter(totals[2], ('head', 'blk'), scatter_dimension=0, tiled=T...  141 us
    dynamic_update_slice x16, local copies, waits for them, and re-layouts, local(): lax.scan(key_step, jnp.zeros((width, heads_dev, head_dim), jnp.float32),...  135 us
    reduce_scatter x1, waiting for transfers between devices, local(): lax.psum_scatter(totals[1], ('head', 'blk'), scatter_dimension=0, tiled=T...  104 us
    unnamed x13, waiting for transfers between devices  98.9 us
    unnamed x2, blocking collectives  78.2 us
    all_gather x1, blocking collectives, collect(): lax.all_gather(bias_rows, ('head', 'blk'), axis=1, tiled=True)  70.2 us
    all_gather x1, blocking collectives, collect(): lax.all_gather(norm_gains, ('head', 'blk'), axis=1, tiled=True)  65.7 us
  transfers between devices with their start and end apart: 18, of which 7 were waited for; matrix products, arithmetic and copies ran while one was open for 19% of the time, Pallas kernels for 0%

profile of v1, /device:TPU:0, one launch (start us, length us, event | category | flops | bytes accessed | tf_op | source)
XLA Modules:
  0.0 1310.6 jit_solution(13341118701082058447)
XLA Ops:
  8.0 70.2 %all-gather = bf16[32,24,4]{1,2,0:T(4,128)(2,1)S(1)} all-gather(bf16[1,24,4]{1,2,0:T(4,128)(2,1)} %bitcast.528), channel_id=1, replica_groups=mesh['head'=4,'blk'=8] {'head','blk'}, dimensions={0}, use_global_device_ids=true | all-gather | bytes 6336 | tf_op jit(solution)/shard_map/all_gather | solution.py:55
  79.3 4.3 copy.212
  89.1 10.2 all_to_all.120
  103.7 9.1 all_to_all.121
  117.7 37.6 %all-reduce = bf16[3072]{0:T(1024)(128)(2,1)S(1)} all-reduce(bf16[3072]{0:T(1024)(128)(2,1)S(1)} %dynamic-update-slice), channel_id=1, replica_groups=mesh['head'=4,'blk'=8] {'head','blk'}, use_global_device_ids=true, to_apply=%add | all-reduce | flops 3072 | bytes 12288
  158.0 65.7 %all-gather.1 = bf16[32,24,2]{1,2,0:T(2,128)(2,1)S(1)} all-gather(bf16[1,24,2]{1,2,0:T(2,128)(2,1)} %bitcast.529), channel_id=1, replica_groups=mesh['head'=4,'blk'=8] {'head','blk'}, dimensions={0}, use_global_device_ids=true | all-gather | bytes 3168 | tf_op jit(solution)/shard_map/all_gather | solution.py:57
  223.8 63.2 %all-gather.2 = bf16[32,24,2]{1,2,0:T(2,128)(2,1)S(1)} all-gather(bf16[1,24,2]{1,2,0:T(2,128)(2,1)} %bitcast.530), channel_id=1, replica_groups=mesh['head'=4,'blk'=8] {'head','blk'}, dimensions={0}, use_global_device_ids=true | all-gather | bytes 3168 | tf_op jit(solution)/shard_map/all_gather | solution.py:58
  293.0 17.2 %while.62 = (s32[]{:T(128)}, f32[3,256]{1,0:T(4,128)S(1)}, f32[3,256]{1,0:T(4,128)S(1)}, f32[256,3,64]{0,2,1:T(8,128)S(1)}, s32[256]{0:T(256)S(1)}, /*index=5*/s...) while((s32[]{:T(128)}, f32[3,256]{1,0:T(4,128)S(1)}, ...), condition=%wide.region_7.8_spmd.clone, body=%wide.region_2.7_spmd.clone.sunk | while | flops 52356832 | bytes 3762697 | solution.py:228
  312.9 3.9 all-to-all-start.1
  320.6 33.4 %while.63 = (s32[]{:T(128)}, f32[3,256]{1,0:T(4,128)S(1)}, f32[3,256]{1,0:T(4,128)S(1)}, f32[256,3,64]{0,2,1:T(8,128)S(1)}, s32[256]{0:T(256)}, /*index=5*/s32[8...) while((s32[]{:T(128)}, f32[3,256]{1,0:T(4,128)S(1)}, ...), condition=%wide.region_19.20_spmd.clone, body=%wide.region_14.19_spmd.clone.sunk | while | flops 52356832 | bytes 3762697 | solution.py:228
  361.5 3.9 all-to-all-start.3
  366.1 2.4 reshape.676
  368.4 2.8 reshape.683
  382.1 5.9 multiply_convert_fusion
  388.1 3.5 fusion.139
  391.8 4.8 multiply_convert_fusion.1
  405.2 2.4 convert_reduce_fusion.3
  407.6 2.3 multiply_reduce_fusion.1
  417.3 3.9 all-to-all-start.6
  426.4 3.4 all-to-all-start.4
  431.7 2.7 all-to-all-done.4
  434.9 2.2 broadcast.1069.clone2
  437.1 91.8 %while.65 = (s32[]{:T(128)}, f32[256,3,64]{0,2,1:T(8,128)S(1)}, f32[4,512,2,3,64]{1,0,4,3,2:T(4,128)}, bf16[4,512,2,3,64]{1,4,3,2,0:T(8,128)(2,1)}, s32[256]{0:T...) while((s32[]{:T(128)}, f32[256,3,64]{0,2,1:T(8,128)S(1)}, ...), condition=%wide.region_40.41_spmd.clone, body=%wide.region_39.40_spmd.clone.sunk | while | flops 255377408 | bytes 15021203 | solution.py:323
  444.0 16.1 %dynamic_update_slice.12 = f32[4,512,2,3,64]{1,0,4,3,2:T(4,128)} dynamic-update-slice(f32[4,512,2,3,64]{1,0,4,3,2:T(4,128)} %get-tuple-element.1305, f32[1,512,2,3,64]{1,0,4,3,2:T(1,128)S(1)} %copy.329, s32[]{:T(128)S(6)} %copy.360, s32[]{:T(128)} %constant.423.clone.1..sunk.3, s32[]{:T(128)} %constant.423.clone.1..sunk.3, s32[]{:T(128)} %constant.423.clone.1..sunk.3, s32[]{:T(128)} %constant.423.clone.1..sunk.3) | dynamic-update-slice | bytes 1572868 | tf_op jit(solution)/shard_map/while/body/jit(dynamic_update_index_in_dim)/dynamic_update_slice | solution.py:323
  467.0 16.1 %dynamic_update_slice.12 = f32[4,512,2,3,64]{1,0,4,3,2:T(4,128)} dynamic-update-slice(f32[4,512,2,3,64]{1,0,4,3,2:T(4,128)} %get-tuple-element.1305, f32[1,512,2,3,64]{1,0,4,3,2:T(1,128)S(1)} %copy.329, s32[]{:T(128)S(6)} %copy.360, s32[]{:T(128)} %constant.423.clone.1..sunk.3, s32[]{:T(128)} %constant.423.clone.1..sunk.3, s32[]{:T(128)} %constant.423.clone.1..sunk.3, s32[]{:T(128)} %constant.423.clone.1..sunk.3) | dynamic-update-slice | bytes 1572868 | tf_op jit(solution)/shard_map/while/body/jit(dynamic_update_index_in_dim)/dynamic_update_slice | solution.py:323
  489.9 16.1 %dynamic_update_slice.12 = f32[4,512,2,3,64]{1,0,4,3,2:T(4,128)} dynamic-update-slice(f32[4,512,2,3,64]{1,0,4,3,2:T(4,128)} %get-tuple-element.1305, f32[1,512,2,3,64]{1,0,4,3,2:T(1,128)S(1)} %copy.329, s32[]{:T(128)S(6)} %copy.360, s32[]{:T(128)} %constant.423.clone.1..sunk.3, s32[]{:T(128)} %constant.423.clone.1..sunk.3, s32[]{:T(128)} %constant.423.clone.1..sunk.3, s32[]{:T(128)} %constant.423.clone.1..sunk.3) | dynamic-update-slice | bytes 1572868 | tf_op jit(solution)/shard_map/while/body/jit(dynamic_update_index_in_dim)/dynamic_update_slice | solution.py:323
  512.8 16.1 %dynamic_update_slice.12 = f32[4,512,2,3,64]{1,0,4,3,2:T(4,128)} dynamic-update-slice(f32[4,512,2,3,64]{1,0,4,3,2:T(4,128)} %get-tuple-element.1305, f32[1,512,2,3,64]{1,0,4,3,2:T(1,128)S(1)} %copy.329, s32[]{:T(128)S(6)} %copy.360, s32[]{:T(128)} %constant.423.clone.1..sunk.3, s32[]{:T(128)} %constant.423.clone.1..sunk.3, s32[]{:T(128)} %constant.423.clone.1..sunk.3, s32[]{:T(128)} %constant.423.clone.1..sunk.3) | dynamic-update-slice | bytes 1572868 | tf_op jit(solution)/shard_map/while/body/jit(dynamic_update_index_in_dim)/dynamic_update_slice | solution.py:323
  528.9 5.0 copy.313
  534.0 2.2 broadcast.1069.clone2.1
  536.3 80.1 %while.64 = (s32[]{:T(128)}, f32[256,3,64]{0,2,1:T(8,128)S(1)}, f32[4,512,2,3,64]{1,0,4,3,2:T(4,128)}, bf16[4,512,2,3,64]{1,4,3,2,0:T(8,128)(2,1)S(1)}, s32[256]...) while((s32[]{:T(128)}, f32[256,3,64]{0,2,1:T(8,128)S(1)}, ...), condition=%wide.region_31.32_spmd.clone, body=%wide.region_30.31_spmd.clone.sunk | while | flops 255377408 | bytes 15023251 | solution.py:323
  540.4 16.1 %dynamic_update_slice.11 = f32[4,512,2,3,64]{1,0,4,3,2:T(4,128)} dynamic-update-slice(f32[4,512,2,3,64]{1,0,4,3,2:T(4,128)} %get-tuple-element.1341, f32[1,512,2,3,64]{1,0,4,3,2:T(1,128)S(1)} %copy.328, s32[]{:T(128)S(6)} %copy.369, s32[]{:T(128)} %constant.423.clone.1..sunk.2, s32[]{:T(128)} %constant.423.clone.1..sunk.2, s32[]{:T(128)} %constant.423.clone.1..sunk.2, s32[]{:T(128)} %constant.423.clone.1..sunk.2) | dynamic-update-slice | bytes 1572868 | tf_op jit(solution)/shard_map/while/body/jit(dynamic_update_index_in_dim)/dynamic_update_slice | solution.py:323
  560.4 16.1 %dynamic_update_slice.11 = f32[4,512,2,3,64]{1,0,4,3,2:T(4,128)} dynamic-update-slice(f32[4,512,2,3,64]{1,0,4,3,2:T(4,128)} %get-tuple-element.1341, f32[1,512,2,3,64]{1,0,4,3,2:T(1,128)S(1)} %copy.328, s32[]{:T(128)S(6)} %copy.369, s32[]{:T(128)} %constant.423.clone.1..sunk.2, s32[]{:T(128)} %constant.423.clone.1..sunk.2, s32[]{:T(128)} %constant.423.clone.1..sunk.2, s32[]{:T(128)} %constant.423.clone.1..sunk.2) | dynamic-update-slice | bytes 1572868 | tf_op jit(solution)/shard_map/while/body/jit(dynamic_update_index_in_dim)/dynamic_update_slice | solution.py:323
  580.3 16.1 %dynamic_update_slice.11 = f32[4,512,2,3,64]{1,0,4,3,2:T(4,128)} dynamic-update-slice(f32[4,512,2,3,64]{1,0,4,3,2:T(4,128)} %get-tuple-element.1341, f32[1,512,2,3,64]{1,0,4,3,2:T(1,128)S(1)} %copy.328, s32[]{:T(128)S(6)} %copy.369, s32[]{:T(128)} %constant.423.clone.1..sunk.2, s32[]{:T(128)} %constant.423.clone.1..sunk.2, s32[]{:T(128)} %constant.423.clone.1..sunk.2, s32[]{:T(128)} %constant.423.clone.1..sunk.2) | dynamic-update-slice | bytes 1572868 | tf_op jit(solution)/shard_map/while/body/jit(dynamic_update_index_in_dim)/dynamic_update_slice | solution.py:323
  600.3 16.1 %dynamic_update_slice.11 = f32[4,512,2,3,64]{1,0,4,3,2:T(4,128)} dynamic-update-slice(f32[4,512,2,3,64]{1,0,4,3,2:T(4,128)} %get-tuple-element.1341, f32[1,512,2,3,64]{1,0,4,3,2:T(1,128)S(1)} %copy.328, s32[]{:T(128)S(6)} %copy.369, s32[]{:T(128)} %constant.423.clone.1..sunk.2, s32[]{:T(128)} %constant.423.clone.1..sunk.2, s32[]{:T(128)} %constant.423.clone.1..sunk.2, s32[]{:T(128)} %constant.423.clone.1..sunk.2) | dynamic-update-slice | bytes 1572868 | tf_op jit(solution)/shard_map/while/body/jit(dynamic_update_index_in_dim)/dynamic_update_slice | solution.py:323
  616.4 5.0 copy.312
  625.5 3.5 all-to-all-start.7
  629.0 65.6 %reduce-scatter.9.cloned.1.call-done = f32[256,384]{0,1:T(8,128)} async-done(((f32[2048,384]{0,1:T(8,128)}), f32[256,384]{0,1:T(8,128)}) %reduce-scatter.9.cloned.1.call-update) | async-done | bytes 393232 | tf_op jit(solution)/shard_map/reduce_scatter | solution.py:326
  697.8 3.6 all-to-all-start.5
  702.3 5.4 all-to-all-done.5
  710.9 3.3 copy.247
  714.2 11.0 copy.248
  730.5 5.2 convolution_add_fusion.1
  738.2 5.1 convolution_add_fusion
  768.9 40.6 %all-reduce.6 = (f32[4,768]{1,0:T(4,128)}, f32[3072]{0:T(1024)}, f32[2,768]{1,0:T(2,128)}, f32[2,768]{1,0:T(2,128)}) all-reduce(f32[4,768]{1,0:T(4,128)} %maximum_add_fusion, f32[3072]{0:T(1024)S(1)} %add.550, f32[2,768]{1,0:T(2,128)} %maximum_add_fusion.1, ...), channel_id=8, replica_groups=mesh['head'=4,'blk'=8] {'head','blk'}, use_global_device_ids=true, to_apply=%region_52.53.clone | all-reduce | flops 9216 | bytes 73728
  818.2 96.5 %all-reduce.9.cloned.1.call-done = f32[3,768,768]{2,0,1:T(4,128)} async-done(((f32[3,768,768]{2,0,1:T(4,128)}), f32[3,768,768]{2,0,1:T(4,128)}) %all-reduce.9.cloned.1.call-update) | async-done | bytes 7077904
  916.4 103.9 %reduce-scatter.13.cloned.1.call-done = f32[24,768]{1,0:T(8,128)} async-done(((f32[768,768]{1,0:T(8,128)}), f32[24,768]{1,0:T(8,128)}) %reduce-scatter.13.cloned.1.call-update) | async-done | bytes 73744 | tf_op jit(solution)/shard_map/reduce_scatter | solution.py:365
  1020.3 141.2 %reduce-scatter.15.cloned.1.call-done = f32[24,3072]{1,0:T(8,128)} async-done(((f32[768,3072]{1,0:T(8,128)}), f32[24,3072]{1,0:T(8,128)}) %reduce-scatter.15.cloned.1.call-update) | async-done | bytes 294928 | tf_op jit(solution)/shard_map/reduce_scatter | solution.py:366
  1161.5 141.8 %reduce-scatter.17.cloned.1.call-done = f32[96,768]{1,0:T(8,128)} async-done(((f32[3072,768]{1,0:T(8,128)}), f32[96,768]{1,0:T(8,128)}) %reduce-scatter.17.cloned.1.call-update) | async-done | bytes 294928 | tf_op jit(solution)/shard_map/reduce_scatter | solution.py:367
  (655 shorter events, 220.8 us)
Async XLA Ops:
  7.2 72.1 %all-gather.10.cloned.1.call-start = ((), (), s32[]{:S(2)}) async-start(), calls=%async_computation.13 | async-start | bytes 3649536 | tf_op jit(solution)/shard_map/all_gather | solution.py:51
  7.9 281.3 %all-gather.12.cloned.1.call-start = ((), (), s32[]{:S(2)}) async-start(), calls=%async_computation.14 | async-start | bytes 1769472 | tf_op jit(solution)/shard_map/all_gather | solution.py:212
  83.6 17.3 %copy-start = (bf16[3,768,768]{1,2,0:T(8,128)(2,1)}, bf16[3,768,768]{1,2,0:T(8,128)(2,1)S(1)}, u32[]{:S(2)}) copy-start(bf16[3,768,768]{1,2,0:T(8,128)(2,1)S(1)} %copy.212) | copy-start | bytes 10616836
  100.8 216.0 %all-gather.20.cloned.1.call-start = ((), (), s32[]{:S(2)}) async-start(), calls=%async_computation.18 | async-start | bytes 1769472 | tf_op jit(solution)/shard_map/all_gather | solution.py:212
  113.7 263.9 %all-gather.14.cloned.1.call-start = ((), (), s32[]{:S(2)}) async-start(), calls=%async_computation.15 | async-start | bytes 1216512 | tf_op jit(solution)/shard_map/all_gather | solution.py:52
  114.3 267.8 %all-gather.16.cloned.1.call-start = ((), (), s32[]{:S(2)}) async-start(), calls=%async_computation.16 | async-start | bytes 4866048 | tf_op jit(solution)/shard_map/all_gather | solution.py:53
  114.8 273.1 %all-gather.18.cloned.1.call-start = ((), (), s32[]{:S(2)}) async-start(), calls=%async_computation.17 | async-start | bytes 4866048 | tf_op jit(solution)/shard_map/all_gather | solution.py:54
  310.2 6.6 copy-start.3
  312.9 48.7 %all-to-all-start.1 = ((bf16[4,2,6144]{2,1,0:T(2,128)(2,1)}), bf16[4,2,6144]{2,1,0:T(2,128)(2,1)}, u32[]{:S(2)}, u32[]{:S(2)}) async-start(bf16[4,2,6144]{2,1,0:T(2,128)(2,1)} %reshape.735), calls=%async_computation.1 | async-start | bytes 196608 | tf_op jit(solution)/shard_map/all_to_all | solution.py:233
  361.5 14.6 %all-to-all-start.3 = ((bf16[4,2,6144]{2,1,0:T(2,128)(2,1)}), bf16[4,2,6144]{2,1,0:T(2,128)(2,1)}, u32[]{:S(2)}, u32[]{:S(2)}) async-start(bf16[4,2,6144]{2,1,0:T(2,128)(2,1)} %reshape.733), calls=%async_computation.3 | async-start | bytes 196608 | tf_op jit(solution)/shard_map/all_to_all | solution.py:233
  374.8 7.3 copy-start.47
  374.8 7.3 copy-start.68
  376.2 11.8 copy-start.35
  377.6 4.5 copy-start.39
  381.3 28.7 %copy-start.5 = (f32[64,768]{1,0:T(8,128)}, f32[64,768]{1,0:T(8,128)S(1)}, u32[]{:S(2)}) copy-start(f32[64,768]{1,0:T(8,128)S(1)} %get-tuple-element.968) | copy-start | bytes 589828
  381.3 6.7 copy-start.63
  382.0 6.0 copy-start.70
  382.1 6.0 copy-start.53
  388.0 8.7 copy-start.28
  388.0 8.7 slice-start
  391.8 4.9 slice-start.1
  391.8 4.9 copy-start.54
  396.8 4.6 copy-start.43
  396.8 4.6 copy-start.44
  396.8 6.8 slice-start.2
  399.0 4.6 slice-start.3
  407.6 5.3 copy-start.2
  411.6 23.3 %copy-start.4 = (f32[256,3,64]{0,2,1:T(8,128)S(1)}, f32[256,3,64]{0,2,1:T(8,128)}, u32[]{:S(2)}) copy-start(f32[256,3,64]{0,2,1:T(8,128)} %copy-done.3) | copy-start | bytes 589828
  411.6 23.3 %copy-start.46 = (f32[3,256]{1,0:T(4,128)S(1)}, f32[3,256]{1,0:T(4,128)}, u32[]{:S(2)}) copy-start(f32[3,256]{1,0:T(4,128)} %copy-done.45) | copy-start | bytes 9220
  417.3 9.1 all-to-all-start.6
  424.6 12.5 copy-start.8
  426.4 8.1 all-to-all-start.4
  429.8 192.5 %reduce-scatter.11.cloned.1.call-start = ((), (), s32[]{:S(2)}) async-start(), calls=%async_computation.20 | async-start | bytes 3538944 | tf_op jit(solution)/shard_map/reduce_scatter | solution.py:326
  528.9 5.0 copy-start.9
  534.0 160.6 %reduce-scatter.9.cloned.1.call-start = ((), (), s32[]{:S(2)}) async-start(), calls=%async_computation.19 | async-start | bytes 3538944 | tf_op jit(solution)/shard_map/reduce_scatter | solution.py:326
  625.5 72.3 %all-to-all-start.7 = ((bf16[4,2,18432]{2,1,0:T(2,128)(2,1)}), bf16[4,2,18432]{2,1,0:T(2,128)(2,1)S(1)}, u32[]{:S(2)}, u32[]{:S(2)}) async-start(bf16[4,2,18432]{2,1,0:T(2,128)(2,1)} %reshape.737), calls=%async_computation.9 | async-start | bytes 589824 | tf_op jit(solution)/shard_map/all_to_all | solution.py:337
  697.8 10.8 copy-start.24
  697.8 9.9 all-to-all-start.5
  701.4 213.3 %all-reduce.9.cloned.1.call-start = ((), (), s32[]{:S(2)}) async-start(), calls=%async_computation.24 | async-start | bytes 18874368
  702.1 6.3 copy-start.20
  702.3 7.4 copy-start.12
  725.2 295.1 %reduce-scatter.13.cloned.1.call-start = ((), (), s32[]{:S(2)}) async-start(), calls=%async_computation.21 | async-start | bytes 2433024 | tf_op jit(solution)/shard_map/reduce_scatter | solution.py:365
  728.7 432.9 %reduce-scatter.15.cloned.1.call-start = ((), (), s32[]{:S(2)}) async-start(), calls=%async_computation.22 | async-start | bytes 9732096 | tf_op jit(solution)/shard_map/reduce_scatter | solution.py:366
  735.8 567.5 %reduce-scatter.17.cloned.1.call-start = ((), (), s32[]{:S(2)}) async-start(), calls=%async_computation.23 | async-start | bytes 9732096 | tf_op jit(solution)/shard_map/reduce_scatter | solution.py:367
  743.3 71.5 %copy-start.1 = (bf16[3,768,768]{1,2,0:T(8,128)(2,1)S(1)}, bf16[3,768,768]{1,2,0:T(8,128)(2,1)}, u32[]{:S(2)}) copy-start(bf16[3,768,768]{1,2,0:T(8,128)(2,1)} %copy-done) | copy-start | bytes 10616836
  767.6 49.1 %copy-start.74 = (f32[64]{0:T(128)S(1)}, f32[64]{0:T(128)}, u32[]{:S(2)}) copy-start(f32[64]{0:T(128)} %negate_multiply_fusion.4) | copy-start | bytes 772
  809.5 7.2 copy-start.14
  809.5 7.2 copy-start.25
  (54 other events, 103.1 us)
Sparse Core Ops, SparseCore 0:
  10.9 63.0 all-gather.9
  100.9 41.3 all-gather.11
  145.1 42.3 all-gather.19
  190.2 52.8 all-gather.13
  245.9 62.5 all-gather.15
  311.3 63.7 all-gather.17
  534.1 72.6 reduce-scatter.10
  621.5 73.0 reduce-scatter.8
  725.4 189.2 all-reduce.8
  921.3 99.0 reduce-scatter.12
  1026.8 134.6 reduce-scatter.14
  1168.9 134.3 reduce-scatter.16

commit v2 on v0

v2 whole, which is shorter than its diff:
```python
import functools
import math

import jax
import jax.numpy as jnp
from jax import lax
from jax.experimental import pallas as pl
from jax.experimental.pallas import tpu as pltpu
from jax.sharding import PartitionSpec as P

HEADS = 12
F32 = jnp.float32
BF = jnp.bfloat16
NT = (((1,), (1,)), ((), ()))
NN = (((1,), (0,)), ((), ()))
TN = (((0,), (0,)), ((), ()))
LOG2E = math.log2(math.e)
BOTH = ("head", "blk")
norm_eps = 1e-12
masked_score = -1e30
VMEM = pl.BlockSpec(memory_space=pltpu.VMEM)
SMEM = pl.BlockSpec(memory_space=pltpu.SMEM)
PARAMS = pltpu.CompilerParams(vmem_limit_bytes=56 << 20)


def dot(a, b, dims):
    return lax.dot_general(a, b, dims, preferred_element_type=F32)


def cdiv(a, b):
    return -(-a // b)


def chunk_walk(place_ref, blocks, halves, per, tokens, visit):
    core, half = place_ref[0], place_ref[1]
    runs = halves // per
    for source in range(2):

        def one(n, carry, source=source):
            xh = n // (2 * runs)
            rel = n // runs % 2
            run = n % runs
            head = xh * 2 + (core if source == 0 else 1 - core)
            position = ((head * 2 + (rel ^ half)) * halves + run * per) * tokens
            rows = pl.ds(pl.multiple_of(rel * tokens, tokens), tokens)

            def load(ref):
                return jnp.concatenate(
                    [ref[xh * halves + run * per + k, rows, :] for k in range(per)], axis=0
                )

            visit(source, load, pl.multiple_of(position, per * tokens))
            return carry

        lax.fori_loop(0, 4 * runs, one, 0, unroll=4 * runs <= 4)


def project_kernel(
    place_ref, a_ref, b_ref, w_ref, bias_ref, q_ref, k_ref, v_ref, kt_ref, vt_ref, *, halves, per
):
    tokens = a_ref.shape[1] // 2

    def visit(source, load, position):
        x = load((a_ref, b_ref)[source])
        rows = pl.ds(position, per * tokens)
        for n, ref in enumerate((q_ref, k_ref, v_ref)):
            y = dot(x, w_ref[n], NN) + bias_ref[n]
            ref[rows, :] = y.astype(BF)
            if n:
                (kt_ref, vt_ref)[n - 1][:, rows] = y.T.astype(BF)

    chunk_walk(place_ref, a_ref.shape[0], halves, per, tokens, visit)


def project(place, a, b, w, bias, halves, per):
    length = 2 * a.shape[0] * a.shape[1]
    hd = w.shape[2]
    rows = jax.ShapeDtypeStruct((length, hd), BF)
    columns = jax.ShapeDtypeStruct((hd, length), BF)
    return pl.pallas_call(
        functools.partial(project_kernel, halves=halves, per=per),
        out_shape=(rows, rows, rows, columns, columns),
        in_specs=[SMEM] + [VMEM] * 4,
        out_specs=(VMEM,) * 5,
        compiler_params=PARAMS,
        name="project",
    )(place, a, b, w, bias)


def weight_grad_kernel(place_ref, a_ref, b_ref, gt_ref, out_ref, acc_ref, *, halves, per):
    tokens = a_ref.shape[1] // 2
    acc_ref[...] = jnp.zeros_like(acc_ref)

    def visit(source, load, position):
        x = load((a_ref, b_ref)[source])
        acc_ref[...] += dot(gt_ref[:, pl.ds(position, per * tokens)], x, NN)

    chunk_walk(place_ref, a_ref.shape[0], halves, per, tokens, visit)
    out_ref[...] = acc_ref[...].T.astype(BF)


def weight_grad(place, a, b, gt, halves, per):
    depth = a.shape[2]
    return pl.pallas_call(
        functools.partial(weight_grad_kernel, halves=halves, per=per),
        out_shape=jax.ShapeDtypeStruct((depth, gt.shape[0]), BF),
        in_specs=[SMEM] + [VMEM] * 3,
        out_specs=VMEM,
        scratch_shapes=[pltpu.VMEM((gt.shape[0], depth), F32)],
        compiler_params=PARAMS,
        name="weight_grad",
    )(place, a, b, gt)


def inside(first, start, stop, bk):
    key = first + lax.broadcasted_iota(jnp.int32, (bk, start.shape[1]), 0)
    return (key >= start) & (key < stop)


def attend_kernel(
    lo_ref, hi_ref, q_ref, k_ref, vt_ref, span_ref, out_ref, ot_ref, lse_ref, s_ref,
    *, bq, bk, pack
):
    length, hd = q_ref.shape
    factor = LOG2E / math.sqrt(hd)
    half = pack // 2

    def q_step(i, carry):
        qs = pl.ds(pl.multiple_of(i * bq, bq), bq)
        q = q_ref[qs, :]
        start, stop = span_ref[0:1, qs], span_ref[1:2, qs]
        lo, hi = lo_ref[i], hi_ref[i]

        def first(j, top):
            ks = pl.ds(pl.multiple_of(j * bk, bk), bk)
            s = dot(k_ref[ks, :], q, NT) * factor
            s = jnp.where(inside(j * bk, start, stop, bk), s, masked_score)
            s_ref[ks, :] = s
            return jnp.maximum(top, jnp.max(s.reshape(bk // 8, 8, bq), axis=0))

        top = lax.fori_loop(lo, hi, first, jnp.full((8, bq), masked_score, F32))
        peak = jnp.max(top, axis=0, keepdims=True)

        def second(j, state):
            total, acc = state
            ks = pl.ds(pl.multiple_of(j * bk, bk), bk)
            p = jnp.exp2(s_ref[ks, :] - peak)
            total = total + jnp.sum(p.reshape(bk // 8, 8, bq), axis=0)
            return total, acc + dot(vt_ref[:, ks], p.astype(BF), NN)

        total, acc = lax.fori_loop(
            lo, hi, second, (jnp.zeros((8, bq), F32), jnp.zeros((hd, bq), F32))
        )
        total = jnp.sum(total, axis=0, keepdims=True)
        out = acc / total
        ot_ref[:, qs] = out
        lse_ref[:, qs] = peak + jnp.log2(total)
        rows = out.T.astype(BF)
        for c in range(bq // pack):
            piece = rows[c * pack : (c + 1) * pack]
            out_ref[i * (bq // pack) + c] = jnp.concatenate([piece[:half], piece[half:]], axis=1)
        return carry

    lax.fori_loop(0, length // bq, q_step, 0)


def attend(lo, hi, q, k, vt, spans, pack, bq, bk):
    length, hd = q.shape
    return pl.pallas_call(
        functools.partial(attend_kernel, bq=bq, bk=bk, pack=pack),
        out_shape=(
            jax.ShapeDtypeStruct((length // pack, pack // 2, 2 * hd), BF),
            jax.ShapeDtypeStruct((hd, length), F32),
            jax.ShapeDtypeStruct((1, length), F32),
        ),
        in_specs=[SMEM, SMEM] + [VMEM] * 4,
        out_specs=(VMEM,) * 3,
        scratch_shapes=[pltpu.VMEM((length, bq), F32)],
        compiler_params=PARAMS,
        name="attend",
    )(lo, hi, q, k, vt, spans)


def attend_back_kernel(
    lo_ref, hi_ref, q_ref, k_ref, v_ref, kt_ref, ot_ref, lse_ref, do_ref, span_ref,
    out_ref, gt_ref, sums_ref, dq_ref, dk_ref, dv_ref, *, bq, bk, pack
):
    length, hd = q_ref.shape
    scale = 1.0 / math.sqrt(hd)
    factor = LOG2E * scale
    half = pack // 2
    dk_ref[...] = jnp.zeros_like(dk_ref)
    dv_ref[...] = jnp.zeros_like(dv_ref)

    def q_step(i, carry):
        qs = pl.ds(pl.multiple_of(i * bq, bq), bq)
        q = q_ref[qs, :]
        start, stop = span_ref[0:1, qs], span_ref[1:2, qs]
        pieces = []
        for c in range(bq // pack):
            piece = do_ref[i * (bq // pack) + c]
            pieces += [piece[:, :hd], piece[:, hd:]]
        do = jnp.concatenate(pieces, axis=0)
        delta = jnp.sum(do.astype(F32).T * ot_ref[:, qs], axis=0, keepdims=True)
        lse = lse_ref[:, qs]

        def step(j, acc):
            ks = pl.ds(pl.multiple_of(j * bk, bk), bk)
            s = dot(k_ref[ks, :], q, NT) * factor - lse
            p = jnp.where(inside(j * bk, start, stop, bk), jnp.exp2(s), 0.0)
            dp = dot(v_ref[ks, :], do, NT)
            ds = (p * (dp - delta)).astype(BF)
            dv_ref[ks, :] += dot(p.astype(BF), do, NN)
            dk_ref[ks, :] += dot(ds, q, NN)
            return acc + dot(kt_ref[:, ks], ds, NN)

        acc = lax.fori_loop(lo_ref[i], hi_ref[i], step, jnp.zeros((hd, bq), F32))
        dq_ref[:, qs] = acc
        return carry

    lax.fori_loop(0, length // bq, q_step, 0)

    def emit(i, sums):
        rows = pl.ds(pl.multiple_of(i * bq, bq), bq)
        dqt = (dq_ref[:, rows] * scale).astype(BF)
        dk = (dk_ref[rows, :] * scale).astype(BF)
        dv = dv_ref[rows, :].astype(BF)
        dq = dqt.astype(F32).T.astype(BF)
        gt_ref[0:hd, rows] = dqt
        gt_ref[hd : 2 * hd, rows] = dk.astype(F32).T.astype(BF)
        gt_ref[2 * hd : 3 * hd, rows] = dv.astype(F32).T.astype(BF)
        for c in range(bq // pack):
            for n, value in enumerate((dq, dk, dv)):
                piece = value[c * pack : (c + 1) * pack]
                out_ref[i * (bq // pack) + c, n * half : (n + 1) * half, :] = jnp.concatenate(
                    [piece[:half], piece[half:]], axis=1
                )
        both = jnp.concatenate([dq.astype(F32), dv.astype(F32)], axis=1)
        return sums + jnp.sum(both, axis=0, keepdims=True)

    sums_ref[...] = lax.fori_loop(0, length // bq, emit, jnp.zeros((1, 2 * hd), F32))


def attend_back(lo, hi, q, k, v, kt, ot, lse, do, spans, pack, bq, bk):
    length, hd = q.shape
    return pl.pallas_call(
        functools.partial(attend_back_kernel, bq=bq, bk=bk, pack=pack),
        out_shape=(
            jax.ShapeDtypeStruct((length // pack, 3 * pack // 2, 2 * hd), BF),
            jax.ShapeDtypeStruct((3 * hd, length), BF),
            jax.ShapeDtypeStruct((1, 2 * hd), F32),
        ),
        in_specs=[SMEM, SMEM] + [VMEM] * 8,
        out_specs=(VMEM,) * 3,
        scratch_shapes=[
            pltpu.VMEM((hd, length), F32),
            pltpu.VMEM((length, hd), F32),
            pltpu.VMEM((length, hd), F32),
        ],
        compiler_params=PARAMS,
        name="attend_back",
    )(lo, hi, q, k, v, kt, ot, lse, do, spans)


def normalise(hidden):
    center = hidden - jnp.mean(hidden, axis=-1, keepdims=True)
    spread = jnp.mean(center * center, axis=-1, keepdims=True)
    inverse = lax.rsqrt(spread + norm_eps)
    return center * inverse, inverse


def norm_back(grad, normed, inverse, gain):
    e = grad * gain
    dh = inverse * (
        e
        - jnp.mean(e, axis=-1, keepdims=True)
        - normed * jnp.mean(e * normed, axis=-1, keepdims=True)
    )
    return dh, jnp.sum(grad * normed, axis=0), jnp.sum(grad, axis=0)


def by_core(value):
    return lax.ppermute(value, "head", [(0, 1), (1, 0), (2, 3), (3, 2)])


def by_x(value):
    return lax.ppermute(value, "head", [(0, 2), (2, 0), (1, 3), (3, 1)])


def swap(value, axes, groups=None):
    return lax.all_to_all(
        value, axes, split_axis=0, concat_axis=0, tiled=True, axis_index_groups=groups
    )


def spread_over(value, axes, count, groups=None):
    return swap(jnp.broadcast_to(value[None], (count, *value.shape)), axes, groups)


def gather_group(rows):
    pair = jnp.concatenate([rows[None], by_x(rows)[None]])
    return jnp.concatenate([pair, by_core(pair)]).reshape(4 * rows.shape[0], rows.shape[1])


def reduce_group(partial, count):
    parts = partial.reshape(4, count, -1)
    kept = parts[:2] + by_core(parts[2:].astype(BF)).astype(F32)
    return kept[0] + by_x(kept[1].astype(BF)).astype(F32)


def key_ranges(spans, bq, bk):
    return spans[0, ::bq] // bk, cdiv(spans[1, bq - 1 :: bq], bk)


def local(
    inputs,
    doc_lengths,
    grad_out,
    qkv_weight,
    out_weight,
    inner_weight,
    outer_weight,
    bias_rows,
    inner_bias,
    norm_gains,
    norm_shifts,
):
    micro, tokens, depth = inputs.shape
    groups, cycle = lax.axis_size("head"), lax.axis_size("blk")
    halves = cycle // 2
    devices = groups * cycle
    length = devices * tokens
    hd = depth // HEADS
    heads_dev = HEADS // groups
    rows_dev = qkv_weight.shape[1]
    ff_dev = outer_weight.shape[0]
    ff_part = cycle * ff_dev
    half_tokens = tokens // 2
    head_index = lax.axis_index("head")
    blk_index = lax.axis_index("blk")
    half = blk_index // halves
    unit_head = head_index * heads_dev + jnp.minimum(blk_index % halves, heads_dev - 1)
    unit_of = [min(i, heads_dev - 1) for i in range(halves)]

    own_x = lax.dynamic_index_in_dim(inputs, half, 0, keepdims=False)
    other_x = lax.dynamic_index_in_dim(inputs, 1 - half, 0, keepdims=False)
    got_x = lax.ppermute(other_x, "blk", [(i, (i + halves) % cycle) for i in range(cycle)])
    pair_x = jnp.concatenate([own_x, got_x], axis=0)
    cube = [
        [h * cycle + b for h in (c, c + 2) for b in range(s * halves, (s + 1) * halves)]
        for c in range(2)
        for s in range(2)
    ]
    tokens_a = spread_over(pair_x, BOTH, cycle, cube)
    tokens_b = by_core(tokens_a)

    weights = qkv_weight.reshape(3, rows_dev, groups, heads_dev, hd).transpose(2, 3, 1, 0, 4)
    weights = weights.reshape(groups, heads_dev, rows_dev * 3 * hd)
    small = jnp.concatenate(
        [bias_rows.reshape(-1), norm_gains.reshape(-1), norm_shifts.reshape(-1), inner_bias]
    )
    weight_size = weights.shape[2]
    pad = -(weight_size + small.shape[0]) % (2 * hd)
    small = jnp.pad(small, (0, pad))
    slots = jnp.stack([weights[:, u] for u in unit_of * 2], axis=1)
    slots = jnp.concatenate(
        [slots, jnp.broadcast_to(small, (groups, cycle, small.shape[0]))], axis=2
    ).reshape(devices, -1, 2 * hd)
    slots = swap(slots, BOTH).reshape(devices, -1)
    unit_weight = (
        slots[:, :weight_size].reshape(depth, 3, hd).transpose(1, 0, 2)
    )
    small = slots[:, weight_size:].astype(F32)

    def column(first, count):
        part = small[:, first * rows_dev : (first + count) * rows_dev]
        return part.reshape(devices, count, rows_dev).transpose(1, 0, 2).reshape(count, depth)

    bias, gains, shifts = column(0, 4), column(4, 2), column(6, 2)
    inner_bias_all = small[:, 8 * rows_dev : 8 * rows_dev + ff_dev].reshape(groups, ff_part)
    inner_bias_part = lax.dynamic_index_in_dim(inner_bias_all, head_index, 0, keepdims=False)
    unit_bias = jnp.stack([bias[0], jnp.zeros_like(bias[0]), bias[1]]).reshape(3, HEADS, hd)
    unit_bias = lax.dynamic_index_in_dim(unit_bias, unit_head, 1, keepdims=True)

    inner_slots = inner_weight.reshape(rows_dev, groups, 1, ff_part).transpose(1, 2, 0, 3)
    inner_part = swap(
        jnp.broadcast_to(inner_slots, (groups, cycle, rows_dev, ff_part)).reshape(
            devices, rows_dev, ff_part
        ),
        BOTH,
    ).reshape(depth, ff_part)
    outer_part = spread_over(outer_weight, "blk", cycle).reshape(ff_part, depth)
    out_all = spread_over(
        spread_over(out_weight, "blk", cycle).reshape(depth // groups, depth), "head", groups
    ).reshape(depth, depth)
    qkv_all = spread_over(spread_over(qkv_weight, "blk", cycle), "head", groups)

    lengths = lax.dynamic_index_in_dim(doc_lengths, half, 0, keepdims=False)
    order = jnp.arange(lengths.shape[0], dtype=jnp.int32)
    bounds = jnp.sum(jnp.where(order[None, :] <= order[:, None], lengths[None, :], 0), axis=1)
    positions = jnp.arange(length, dtype=jnp.int32)[None, :]
    starts = (bounds - lengths)[:, None]
    own = (positions >= starts) & (positions < bounds[:, None])
    spans = jnp.stack(
        [
            jnp.sum(jnp.where(own, starts, 0), axis=0),
            jnp.sum(jnp.where(own, bounds[:, None], 0), axis=0),
        ]
    )

    place = jnp.stack([head_index % 2, half]).astype(jnp.int32)
    per = max(1, 256 // tokens)
    q, k, v, kt, vt = project(place, tokens_a, tokens_b, unit_weight, unit_bias, halves, per)
    block = 512 if length <= 4096 else 256
    lo, hi = key_ranges(spans, block, 512)
    attn_out, attn_t, lse = attend(lo, hi, q, k, vt, spans, tokens, block, 512)

    rows = micro * tokens
    attn = (
        swap(attn_out, BOTH)
        .reshape(groups, micro, halves, half_tokens, 2, hd)[:, :, :heads_dev]
        .transpose(1, 4, 3, 0, 2, 5)
        .reshape(rows, depth)
    )
    first_sum = (
        inputs.reshape(rows, depth).astype(F32)
        + dot(attn, out_all, NN)
        + bias[2]
    )
    normed_one, inverse_one = normalise(first_sum)
    first_normed = normed_one * gains[0] + shifts[0]
    normed_low = gather_group(first_normed.astype(BF))
    inner_pre = dot(normed_low, inner_part, NN) + inner_bias_part
    cdf = 0.5 * (1.0 + lax.erf(inner_pre * (1.0 / math.sqrt(2.0))))
    slope = cdf + inner_pre * jnp.exp(-0.5 * inner_pre * inner_pre) * (1.0 / math.sqrt(2.0 * math.pi))
    act_low = (inner_pre * cdf).astype(BF)
    second_sum = first_normed + reduce_group(dot(act_low, outer_part, NN), rows) + bias[3]
    normed_two, inverse_two = normalise(second_sum)
    output = (normed_two * gains[1] + shifts[1]).astype(BF).reshape(inputs.shape)

    d_second, gain_two, shift_two = norm_back(
        grad_out.reshape(rows, depth).astype(F32), normed_two, inverse_two, gains[1]
    )
    d_ffn = d_second.astype(BF)
    d_ffn_group = gather_group(d_ffn)
    d_inner = (dot(d_ffn_group, outer_part, NT) * slope).astype(BF)
    d_first_normed = d_second + reduce_group(dot(d_inner, inner_part, NT), rows)
    d_first, gain_one, shift_one = norm_back(d_first_normed, normed_one, inverse_one, gains[0])
    d_branch = d_first.astype(BF)
    d_attn = dot(d_branch, out_all, NT).astype(BF)
    d_heads = d_attn.reshape(micro, 2, half_tokens, groups, heads_dev, hd).transpose(3, 0, 4, 2, 1, 5)
    d_heads = d_heads.reshape(groups, micro, heads_dev, half_tokens, 2 * hd)
    d_heads = jnp.stack([d_heads[:, :, u] for u in unit_of], axis=2)
    d_heads = swap(d_heads.reshape(devices, half_tokens, 2 * hd), BOTH)

    outer_grad = dot(act_low, d_ffn_group, TN).astype(BF)
    outer_grad = jnp.sum(
        swap(outer_grad.reshape(cycle, ff_dev, depth), "blk").astype(F32), axis=0
    )
    inner_grad = dot(normed_low, d_inner, TN).astype(BF)
    inner_grad = swap(inner_grad.reshape(devices, rows_dev, ff_part), BOTH)
    inner_grad = (
        jnp.sum(inner_grad.reshape(groups, cycle, rows_dev, ff_part).astype(F32), axis=1)
        .transpose(1, 0, 2)
        .reshape(rows_dev, groups * ff_part)
    )
    out_grad = dot(attn, d_branch, TN).reshape(groups, depth // groups, depth)

    def out_block(offset):
        return lax.dynamic_index_in_dim(out_grad, head_index ^ offset, 0, keepdims=False)

    from_core = by_core(jnp.stack([out_block(1), out_block(3)]).astype(BF)).astype(F32)
    from_x = by_x((out_block(2) + from_core[1]).astype(BF)).astype(F32)
    out_grad = (out_block(0) + from_core[0] + from_x).astype(BF)
    out_grad = jnp.sum(
        swap(out_grad.reshape(cycle, rows_dev, depth), "blk").astype(F32), axis=0
    )

    lo, hi = key_ranges(spans, 512, 256)
    qkv_out, qkv_t, qv_sums = attend_back(
        lo, hi, q, k, v, kt, attn_t, lse, d_heads, spans, tokens, 512, 256
    )
    d_qkv = (
        swap(qkv_out, BOTH)
        .reshape(groups, micro, halves, 3, half_tokens, 2, hd)[:, :, :heads_dev]
        .transpose(3, 1, 5, 4, 0, 2, 6)
        .reshape(3, rows, depth)
    )
    qkv_all = qkv_all.reshape(devices, 3, rows_dev, depth).transpose(1, 0, 2, 3).reshape(3, depth, depth)
    d_tokens = d_first
    for c in range(3):
        d_tokens = d_tokens + dot(d_qkv[c], qkv_all[c], NT)
    grad_inputs = d_tokens.astype(BF).reshape(inputs.shape)

    unit_grad = weight_grad(place, tokens_a, tokens_b, qkv_t, halves, per)
    ones = [gain_one, gain_two, shift_one, shift_two]
    ones += [jnp.sum(d.astype(F32), axis=0) for d in (d_branch, d_ffn)]
    wide = jnp.zeros((2, HEADS, hd), F32)
    wide = lax.dynamic_update_slice(wide, qv_sums.reshape(2, 1, hd), (0, unit_head, 0))
    wide = jnp.where((blk_index % halves < heads_dev), wide, 0.0)
    sums = jnp.concatenate([jnp.stack(ones), wide.reshape(2, depth)]).T
    inner_sums = jnp.sum(d_inner.astype(F32), axis=0).reshape(1, cycle, rows_dev, ff_dev // rows_dev)
    inner_sums = jnp.broadcast_to(inner_sums, (groups, *inner_sums.shape[1:]))
    extra = jnp.concatenate(
        [
            sums.reshape(devices, rows_dev, 8),
            inner_sums.reshape(devices, rows_dev, -1),
        ],
        axis=2,
    ).astype(BF)
    extra = jnp.pad(extra, ((0, 0), (0, 0), (0, hd - extra.shape[2])))
    final = swap(
        jnp.concatenate([unit_grad.reshape(devices, rows_dev, 3 * hd), extra], axis=2), BOTH
    ).astype(F32)
    qkv_grad = jnp.sum(
        final[:, :, : 3 * hd].reshape(groups, micro, halves, rows_dev, 3, hd)[:, :, :heads_dev], axis=1
    )
    qkv_grad = qkv_grad.transpose(3, 2, 0, 1, 4).reshape(3, rows_dev, depth)
    sums = jnp.sum(final[:, :, 3 * hd : 3 * hd + 8], axis=0).T
    inner_sums = final[:, :, 3 * hd + 8 : 3 * hd + 8 + ff_dev // rows_dev]
    inner_sums = lax.dynamic_index_in_dim(
        inner_sums.reshape(groups, cycle, rows_dev, -1), head_index, 0, keepdims=False
    )
    inner_bias_grad = jnp.sum(inner_sums, axis=0).reshape(ff_dev)
    return (
        output,
        grad_inputs,
        qkv_grad,
        out_grad,
        inner_grad,
        outer_grad,
        jnp.stack([sums[6], sums[7], sums[4], sums[5]]),
        inner_bias_grad,
        sums[0:2],
        sums[2:4],
    )


def solution(mesh):
    tokens = P(None, BOTH, None)
    rows = P(BOTH, None)
    columns = P(None, BOTH)
    return jax.shard_map(
        local,
        mesh=mesh,
        in_specs=(tokens, P(), tokens, tokens, rows, rows, rows, columns, P(BOTH), columns, columns),
        out_specs=(tokens, tokens, tokens, rows, rows, rows, columns, P(BOTH), columns, columns),
        check_vma=False,
    )
```

time: 1330 us -> 444 us (0.33); the launches traced: 1310 us -> 442 us
  waiting for transfers between devices: 559 us -> 187 us
  blocking collectives: 296 us -> 47.3 us
  local copies, waits for them, and re-layouts: 274 us -> 60.2 us
  matrix products: 85.7 us -> 20.8 us
  starting transfers between devices: 22.9 us -> 60.2 us
  Pallas kernels: 0 us -> 36 us
  other arithmetic: 53 us -> 29.3 us
  between operations: 16.2 us -> 1.6 us
    reduce_scatter x5 -> x0, waiting for transfers between devices: 453 us -> none  [the longest x1 142 us: local(): lax.psum_scatter(totals[3], ('head', 'blk'), scatter_dimension=0, tiled=T...]
    all_gather x3 -> x0, blocking collectives: 199 us -> none  [the longest x1 70.2 us: collect(): lax.all_gather(bias_rows, ('head', 'blk'), axis=1, tiled=True)]
    all_to_all x6 -> x13, waiting for transfers between devices: 8.07 us -> 147 us  [swap(): lax.all_to_all(value, axes, split_axis=0, concat_axis=0, tiled=True, axis...]
    dynamic_update_slice x16 -> x0, local copies, waits for them, and re-layouts: 135 us -> none  [local(): lax.scan(key_step, jnp.zeros((width, heads_dev, head_dim), jnp.float32),...]
    unnamed x13 -> x0, waiting for transfers between devices: 98.8 us -> none
    unnamed x2 -> x0, blocking collectives: 78 us -> none
    dot_general x96 -> x12, matrix products: 85.7 us -> 20.8 us  [dot(): return lax.dot_general(a, b, dims, preferred_element_type=F32)]
    ppermute x0 -> x12, waiting for transfers between devices: none -> 39.1 us  [the longest x5 27.7 us: by_x(): return lax.ppermute(value, 'head', [(0, 2), (2, 0), (1, 3), (3, 1)])]
  transfers between devices with their start and end apart: 18 -> 25, of which waited for: 7 -> 20; matrix products, arithmetic and copies ran while one was open for 19% -> 17% of each run, Pallas kernels for 0% -> 8%
where the time goes in v2:
time: 444 us; the launch traced here: 442 us
  waiting for transfers between devices  187 us (42%)
  local copies, waits for them, and re-layouts  60.2 us (14%)
  starting transfers between devices  60.2 us (14%)
  blocking collectives  47.3 us (11%)
  Pallas kernels  36 us (8%)
  other arithmetic  29.3 us (7%)
  matrix products  20.8 us (5%)
    all_to_all x13, waiting for transfers between devices, swap(): lax.all_to_all(value, axes, split_axis=0, concat_axis=0, tiled=True, axis...  147 us
    all_to_all x13, starting transfers between devices, swap(): lax.all_to_all(value, axes, split_axis=0, concat_axis=0, tiled=True, axis...  49.4 us
    all_to_all x2, blocking collectives, swap(): lax.all_to_all(value, axes, split_axis=0, concat_axis=0, tiled=True, axis...  47.3 us
    ppermute x5, waiting for transfers between devices, by_x(): return lax.ppermute(value, 'head', [(0, 2), (2, 0), (1, 3), (3, 1)])  27.7 us
    dot_general x12, matrix products, dot(): return lax.dot_general(a, b, dims, preferred_element_type=F32)  20.8 us
    pallas_call x1, Pallas kernels, attend_back(): pl.pallas_call(functools.partial(attend_back_kernel, bq=bq, bk=bk, pack=p...  15.2 us
    unnamed x80, local copies, waits for them, and re-layouts  12 us
    pallas_call x1, Pallas kernels, attend(): pl.pallas_call(functools.partial(attend_kernel, bq=bq, bk=bk, pack=pack),...  11.2 us
  transfers between devices with their start and end apart: 25, of which 20 were waited for; matrix products, arithmetic and copies ran while one was open for 17% of the time, Pallas kernels for 8%

profile of v2, /device:TPU:0, one launch (start us, length us, event | category | flops | bytes accessed | tf_op | source)
XLA Modules:
  0.0 442.0 jit_solution(2059476304164247546)
XLA Ops:
  1.6 4.1 collective-permute-start
  5.7 4.9 %collective-permute-done = bf16[64,768]{1,0:T(8,128)(2,1)S(1)} collective-permute-done((bf16[64,768]{1,0:T(8,128)(2,1)S(1)}, bf16[64,768]{1,0:T(8,128)(2,1)S(1)}, u32[]{:S(2)}, u32[]{:S(2)}) %collective-permute-start) | collective-permute-done | bytes 98336 | tf_op jit(solution)/shard_map/ppermute | solution.py:347
  11.9 4.0 all-to-all-start
  17.0 22.1 %all-to-all-done.a_ref = bf16[8,128,768]{2,1,0:T(8,128)(2,1)S(1)} async-done(((bf16[8,128,768]{2,1,0:T(8,128)(2,1)}), bf16[8,128,768]{2,1,0:T(8,128)(2,1)S(1)}, u32[]{:S(2)}, u32[]{:S(2)}) %all-to-all-start) | async-done | bytes 1572896 | tf_op jit(solution)/shard_map/all_to_all | solution.py:291
  39.9 4.7 %all-to-all-start.3 = ((bf16[8,24,768]{2,1,0:T(8,128)(2,1)}), bf16[8,24,768]{2,1,0:T(8,128)(2,1)S(1)}, u32[]{:S(2)}, u32[]{:S(2)}) async-start(bf16[8,24,768]{2,1,0:T(8,128)(2,1)} %broadcast_in_dim.121), calls=%async_computation.3 | async-start | bytes 589824 | tf_op jit(solution)/shard_map/all_to_all | solution.py:291
  45.8 8.2 %all-to-all-done.3 = bf16[8,24,768]{2,1,0:T(8,128)(2,1)S(1)} async-done(((bf16[8,24,768]{2,1,0:T(8,128)(2,1)}), bf16[8,24,768]{2,1,0:T(8,128)(2,1)S(1)}, u32[]{:S(2)}, u32[]{:S(2)}) %all-to-all-start.3) | async-done | bytes 294944 | tf_op jit(solution)/shard_map/all_to_all | solution.py:291
  54.1 2.7 all-to-all-start.1
  59.0 9.9 %all-to-all-done.1 = bf16[32,39,128]{2,1,0:T(8,128)(2,1)S(1)} async-done(((bf16[32,39,128]{2,1,0:T(8,128)(2,1)}), bf16[32,39,128]{2,1,0:T(8,128)(2,1)S(1)}, u32[]{:S(2)}, u32[]{:S(2)}) %all-to-all-start.1) | async-done | bytes 319520 | tf_op jit(solution)/shard_map/all_to_all | solution.py:291
  70.0 3.5 all-to-all-start.4
  82.0 5.9 %project.1 = (bf16[2048,64]{1,0:T(8,128)(2,1)}, bf16[2048,64]{1,0:T(8,128)(2,1)}, bf16[2048,64]{1,0:T(8,128)(2,1)}, bf16[64,2048]{1,0:T(8,128)(2,1)}, bf16[64,2048]{1,0:T(8,128)(2,1)}) custom-call(s32[2]{0:T(128)} %pad_add_fusion.1.place_ref, bf16[8,128,768]{2,1,0:T(8,128)(2,1)} %copy-done, bf16[8,128,768]{2,1,0:T(8,128)(2,1)} %collective-permute-done.1.b_ref, ...), custom_call_target="tpu_custom_call" | custom-call | tf_op jit(solution)/shard_map/project/pallas_call | solution.py:80
  87.9 11.2 %attend.1 = (bf16[32,32,128]{2,1,0:T(8,128)(2,1)}, f32[64,2048]{1,0:T(8,128)}, f32[1,2048]{1,0:T(1,128)}) custom-call(s32[4]{0:T(128)} %get-tuple-element.117.lo_ref, s32[4]{0:T(128)} %get-tuple-element.124.hi_ref, bf16[2048,64]{1,0:T(8,128)(2,1)} %get-tuple-element.21.q_ref, bf16[2048,64]{1,0:T(8,128)(2,1)} %get-tuple-element.22.k_ref, ...), custom_call_target="tpu_custom_call" | custom-call | tf_op jit(solution)/shard_map/attend/pallas_call | solution.py:169
  99.0 3.6 all-to-all-start.2
  102.8 10.5 %all-to-all-done.2 = bf16[32,32,128]{2,1,0:T(8,128)(2,1)S(1)} async-done(((bf16[32,32,128]{2,1,0:T(8,128)(2,1)}), bf16[32,32,128]{2,1,0:T(8,128)(2,1)S(1)}, u32[]{:S(2)}, u32[]{:S(2)}) %all-to-all-start.2) | async-done | bytes 262176 | tf_op jit(solution)/shard_map/all_to_all | solution.py:291
  114.4 2.7 all-to-all-start.5
  119.1 28.3 %all-to-all-done.5 = bf16[32,24,768]{2,1,0:T(8,128)(2,1)S(1)} async-done(((bf16[32,24,768]{2,1,0:T(8,128)(2,1)}), bf16[32,24,768]{2,1,0:T(8,128)(2,1)S(1)}, u32[]{:S(2)}, u32[]{:S(2)}) %all-to-all-start.5) | async-done | bytes 1179680 | tf_op jit(solution)/shard_map/all_to_all | solution.py:291
  148.6 4.4 %all-to-all-start.6 = ((bf16[8,96,768]{2,1,0:T(8,128)(2,1)}), bf16[8,96,768]{2,1,0:T(8,128)(2,1)}, u32[]{:S(2)}, u32[]{:S(2)}) async-start(bf16[8,96,768]{2,1,0:T(8,128)(2,1)} %broadcast_in_dim.128), calls=%async_computation.6 | async-start | bytes 2359296 | tf_op jit(solution)/shard_map/all_to_all | solution.py:291
  154.6 5.8 %collective-permute-done.2 = bf16[128,768]{1,0:T(8,128)(2,1)S(1)} collective-permute-done((bf16[128,768]{1,0:T(8,128)(2,1)S(1)}, bf16[128,768]{1,0:T(8,128)(2,1)S(1)}, u32[]{:S(2)}, u32[]{:S(2)}) %collective-permute-start.2) | collective-permute-done | bytes 196640 | tf_op jit(solution)/shard_map/ppermute | solution.py:287
  161.3 2.0 collective-permute-done.3
  165.3 2.3 multiply_convert_fusion
  167.6 14.0 %all-to-all-done.6 = bf16[8,96,768]{2,1,0:T(8,128)(2,1)} async-done(((bf16[8,96,768]{2,1,0:T(8,128)(2,1)}), bf16[8,96,768]{2,1,0:T(8,128)(2,1)}, u32[]{:S(2)}, u32[]{:S(2)}) %all-to-all-start.6) | async-done | bytes 1179680 | tf_op jit(solution)/shard_map/all_to_all | solution.py:291
  181.6 2.3 fusion.63
  189.2 5.7 %collective-permute-done.5 = bf16[128,768]{1,0:T(8,128)(2,1)S(1)} collective-permute-done((bf16[128,768]{1,0:T(8,128)(2,1)S(1)}, bf16[128,768]{1,0:T(8,128)(2,1)S(1)}, u32[]{:S(2)}, u32[]{:S(2)}) %collective-permute-start.5) | collective-permute-done | bytes 196640 | tf_op jit(solution)/shard_map/ppermute | solution.py:287
  198.1 4.9 %collective-permute-done.6 = bf16[128,768]{1,0:T(8,128)(2,1)S(1)} collective-permute-done((bf16[128,768]{1,0:T(8,128)(2,1)S(1)}, bf16[128,768]{1,0:T(8,128)(2,1)S(1)}, u32[]{:S(2)}, u32[]{:S(2)}) %collective-permute-start.6) | collective-permute-done | bytes 196640 | tf_op jit(solution)/shard_map/ppermute | solution.py:287
  204.9 3.3 fusion.62
  214.2 3.6 all-to-all-start.9
  219.0 2.6 multiply_reduce_fusion
  224.1 16.1 %all-to-all-done.9 = bf16[8,3,24,768]{3,2,1,0:T(8,128)(2,1)S(1)} async-done(((bf16[8,3,24,768]{3,2,1,0:T(8,128)(2,1)}), bf16[8,3,24,768]{3,2,1,0:T(8,128)(2,1)S(1)}, u32[]{:S(2)}, u32[]{:S(2)}) %all-to-all-start.9) | async-done | bytes 884768 | tf_op jit(solution)/shard_map/all_to_all | solution.py:291
  240.2 13.5 %all_to_all.75.do_ref = bf16[32,32,128]{2,1,0:T(8,128)(2,1)} all-to-all(bf16[32,32,128]{2,1,0:T(8,128)(2,1)S(1)} %bitcast.220), channel_id=1, replica_groups=mesh['head'=4,'blk'=8] {'head','blk'}, dimensions={0} | all-to-all | bytes 524288 | tf_op jit(solution)/shard_map/all_to_all | solution.py:291
  253.7 2.0 broadcast_in_dim.132
  255.7 3.7 all-to-all-start.10
  275.0 15.2 %attend_back.1 = (bf16[32,96,128]{2,1,0:T(8,128)(2,1)}, bf16[192,2048]{1,0:T(8,128)(2,1)}, f32[1,128]{1,0:T(1,128)}) custom-call(s32[4]{0:T(128)} %get-tuple-element.116.lo_ref, s32[4]{0:T(128)} %get-tuple-element.125.hi_ref, bf16[2048,64]{1,0:T(8,128)(2,1)} %get-tuple-element.21.q_ref, bf16[2048,64]{1,0:T(8,128)(2,1)} %get-tuple-element.22.k_ref, ...), custom_call_target="tpu_custom_call" | custom-call | tf_op jit(solution)/shard_map/attend_back/pallas_call | solution.py:246
  296.6 3.8 weight_grad.1
  300.4 1.9 fusion.13
  302.3 2.2 convert_element_type.148
  304.5 3.5 all-to-all-start.11
  311.0 10.3 %collective-permute-done.11 = bf16[192,768]{1,0:T(8,128)(2,1)S(1)} collective-permute-done((bf16[192,768]{1,0:T(8,128)(2,1)S(1)}, bf16[192,768]{1,0:T(8,128)(2,1)S(1)}, u32[]{:S(2)}, u32[]{:S(2)}) %collective-permute-start.11) | collective-permute-done | bytes 294944 | tf_op jit(solution)/shard_map/ppermute | solution.py:287
  323.2 5.4 %all-to-all-start.12 = ((bf16[8,24,768]{2,1,0:T(8,128)(2,1)}), bf16[8,24,768]{2,1,0:T(8,128)(2,1)}, u32[]{:S(2)}, u32[]{:S(2)}) async-start(bf16[8,24,768]{2,1,0:T(8,128)(2,1)} %bitcast.218), calls=%async_computation.12 | async-start | bytes 589824 | tf_op jit(solution)/shard_map/all_to_all | solution.py:291
  328.5 3.2 convolution_convert_fusion
  331.7 6.6 %all-to-all-done.12 = bf16[8,24,768]{2,1,0:T(8,128)(2,1)} async-done(((bf16[8,24,768]{2,1,0:T(8,128)(2,1)}), bf16[8,24,768]{2,1,0:T(8,128)(2,1)}, u32[]{:S(2)}, u32[]{:S(2)}) %all-to-all-start.12) | async-done | bytes 294944 | tf_op jit(solution)/shard_map/all_to_all | solution.py:291
  338.3 4.2 all-to-all-start.14
  342.6 3.2 convolution_convert_fusion.1
  345.8 24.6 %all-to-all-done.14 = bf16[8,96,768]{2,1,0:T(8,128)(2,1)} async-done(((bf16[8,96,768]{2,1,0:T(8,128)(2,1)}), bf16[8,96,768]{2,1,0:T(8,128)(2,1)}, u32[]{:S(2)}, u32[]{:S(2)}) %all-to-all-start.14) | async-done | bytes 1179680 | tf_op jit(solution)/shard_map/all_to_all | solution.py:291
  370.4 33.8 %all_to_all.76 = bf16[32,24,768]{2,1,0:T(8,128)(2,1)} all-to-all(bf16[32,24,768]{2,1,0:T(8,128)(2,1)} %bitcast.215), channel_id=1, replica_groups=mesh['head'=4,'blk'=8] {'head','blk'}, dimensions={0} | all-to-all | bytes 2359296 | tf_op jit(solution)/shard_map/all_to_all | solution.py:291
  404.2 3.3 all-to-all-start.8
  407.5 1.9 fusion.54
  419.4 2.2 convert_reduce_fusion.1
  422.4 7.1 %all-to-all-done.8 = bf16[32,96,128]{2,1,0:T(8,128)(2,1)} async-done(((bf16[32,96,128]{2,1,0:T(8,128)(2,1)}), bf16[32,96,128]{2,1,0:T(8,128)(2,1)}, u32[]{:S(2)}, u32[]{:S(2)}) %all-to-all-start.8) | async-done | bytes 786464 | tf_op jit(solution)/shard_map/all_to_all | solution.py:291
  429.5 3.2 reshape.309
  (250 shorter events, 92.3 us)
Async XLA Ops:
  1.6 9.0 %collective-permute-start = (bf16[64,768]{1,0:T(8,128)(2,1)S(1)}, bf16[64,768]{1,0:T(8,128)(2,1)S(1)}, u32[]{:S(2)}, u32[]{:S(2)}) collective-permute-start(bf16[64,768]{1,0:T(8,128)(2,1)S(1)} %get-tuple-element.101), channel_id=1, source_target_pairs={{0,4},{1,5},{2,6},{3,7},{4,0},{5,1},{6,2},{7,3},{8,12},{9,13},{10,... | collective-permute-start | bytes 294920 | tf_op jit(solution)/shard_map/ppermute | solution.py:347
  11.9 4.1 copy-start.21
  11.9 4.8 %copy-start.32 = (bf16[4,24]{1,0:T(4,128)(2,1)S(1)}, bf16[4,24]{1,0:T(4,128)(2,1)}, u32[]{:S(2)}) copy-start(bf16[4,24]{1,0:T(4,128)(2,1)} %param.18) | copy-start | bytes 580
  11.9 4.9 %copy-start.33 = (bf16[2,24]{1,0:T(2,128)(2,1)S(1)}, bf16[2,24]{1,0:T(2,128)(2,1)}, u32[]{:S(2)}) copy-start(bf16[2,24]{1,0:T(2,128)(2,1)} %param.20) | copy-start | bytes 292
  11.9 4.9 %copy-start.34 = (bf16[2,24]{1,0:T(2,128)(2,1)S(1)}, bf16[2,24]{1,0:T(2,128)(2,1)}, u32[]{:S(2)}) copy-start(bf16[2,24]{1,0:T(2,128)(2,1)} %param.21) | copy-start | bytes 292
  11.9 5.0 %copy-start.30 = (bf16[96]{0:T(256)(128)(2,1)S(1)}, bf16[96]{0:T(256)(128)(2,1)}, u32[]{:S(2)}) copy-start(bf16[96]{0:T(256)(128)(2,1)} %param.19) | copy-start | bytes 580
  11.9 27.2 %copy-start.29 = (bf16[24,768]{1,0:T(8,128)(2,1)S(1)}, bf16[24,768]{1,0:T(8,128)(2,1)}, u32[]{:S(2)}) copy-start(bf16[24,768]{1,0:T(8,128)(2,1)} %param.15) | copy-start | bytes 110596
  11.9 27.2 %all-to-all-start = ((bf16[8,128,768]{2,1,0:T(8,128)(2,1)}), bf16[8,128,768]{2,1,0:T(8,128)(2,1)S(1)}, u32[]{:S(2)}, u32[]{:S(2)}) async-start(bf16[8,128,768]{2,1,0:T(8,128)(2,1)} %broadcast_in_dim.68), calls=%async_computation | async-start | bytes 3145728 | tf_op jit(solution)/shard_map/all_to_all | solution.py:291
  16.4 29.2 %copy-start.31 = (s32[2,32]{1,0:T(2,128)S(1)}, s32[2,32]{1,0:T(2,128)}, u32[]{:S(2)}) copy-start(s32[2,32]{1,0:T(2,128)} %param.12) | copy-start | bytes 772
  39.1 14.9 %copy-start = (bf16[8,128,768]{2,1,0:T(8,128)(2,1)}, bf16[8,128,768]{2,1,0:T(8,128)(2,1)S(1)}, u32[]{:S(2)}) copy-start(bf16[8,128,768]{2,1,0:T(8,128)(2,1)S(1)} %all-to-all-done.a_ref) | copy-start | bytes 4718596
  39.9 14.2 %all-to-all-start.3 = ((bf16[8,24,768]{2,1,0:T(8,128)(2,1)}), bf16[8,24,768]{2,1,0:T(8,128)(2,1)S(1)}, u32[]{:S(2)}, u32[]{:S(2)}) async-start(bf16[8,24,768]{2,1,0:T(8,128)(2,1)} %broadcast_in_dim.121), calls=%async_computation.3 | async-start | bytes 589824 | tf_op jit(solution)/shard_map/all_to_all | solution.py:291
  45.8 36.2 %collective-permute-start.1 = (bf16[8,128,768]{2,1,0:T(8,128)(2,1)S(1)}, bf16[8,128,768]{2,1,0:T(8,128)(2,1)}, u32[]{:S(2)}, u32[]{:S(2)}) collective-permute-start(bf16[8,128,768]{2,1,0:T(8,128)(2,1)S(1)} %all-to-all-done.a_ref), channel_id=1, source_target_pairs={{0,8},{8,0},{16,24},{24,16},{1,9},{9,1},{17,25},{25,17},{2,10},{10... | collective-permute-start | bytes 4718600 | tf_op jit(solution)/shard_map/ppermute | solution.py:283
  54.1 14.8 %all-to-all-start.1 = ((bf16[32,39,128]{2,1,0:T(8,128)(2,1)}), bf16[32,39,128]{2,1,0:T(8,128)(2,1)S(1)}, u32[]{:S(2)}, u32[]{:S(2)}) async-start(bf16[32,39,128]{2,1,0:T(8,128)(2,1)} %reshape.289), calls=%async_computation.1 | async-start | bytes 655360 | tf_op jit(solution)/shard_map/all_to_all | solution.py:291
  70.0 29.0 %all-to-all-start.4 = ((bf16[4,192,768]{2,1,0:T(8,128)(2,1)}), bf16[4,192,768]{2,1,0:T(8,128)(2,1)S(1)}, u32[]{:S(2)}, u32[]{:S(2)}) async-start(bf16[4,192,768]{2,1,0:T(8,128)(2,1)} %broadcast_in_dim.123), calls=%async_computation.4 | async-start | bytes 2359296 | tf_op jit(solution)/shard_map/all_to_all | solution.py:291
  87.9 14.8 %copy-start.25 = (bf16[24,3072]{1,0:T(8,128)(2,1)S(1)}, bf16[24,3072]{1,0:T(8,128)(2,1)}, u32[]{:S(2)}) copy-start(bf16[24,3072]{1,0:T(8,128)(2,1)} %param.16) | copy-start | bytes 442372
  99.0 14.2 %all-to-all-start.2 = ((bf16[32,32,128]{2,1,0:T(8,128)(2,1)}), bf16[32,32,128]{2,1,0:T(8,128)(2,1)S(1)}, u32[]{:S(2)}, u32[]{:S(2)}) async-start(bf16[32,32,128]{2,1,0:T(8,128)(2,1)} %get-tuple-element.24), calls=%async_computation.2 | async-start | bytes 524288 | tf_op jit(solution)/shard_map/all_to_all | solution.py:291
  102.8 14.3 %copy-start.28 = (f32[32,24]{1,0:T(8,128)S(1)}, f32[32,24]{1,0:T(8,128)}, u32[]{:S(2)}) copy-start(f32[32,24]{1,0:T(8,128)} %get-tuple-element.79) | copy-start | bytes 9220
  102.8 14.4 %copy-start.24 = (f32[32,384]{1,0:T(8,128)S(1)}, f32[32,384]{1,0:T(8,128)}, u32[]{:S(2)}) copy-start(f32[32,384]{1,0:T(8,128)} %copy-done.23) | copy-start | bytes 147460
  114.4 33.1 %all-to-all-start.5 = ((bf16[32,24,768]{2,1,0:T(8,128)(2,1)}), bf16[32,24,768]{2,1,0:T(8,128)(2,1)S(1)}, u32[]{:S(2)}, u32[]{:S(2)}) async-start(bf16[32,24,768]{2,1,0:T(8,128)(2,1)} %bitcast.25), calls=%async_computation.5 | async-start | bytes 2359296 | tf_op jit(solution)/shard_map/all_to_all | solution.py:291
  118.0 29.5 %copy-start.26 = (bf16[96,768]{1,0:T(8,128)(2,1)S(1)}, bf16[96,768]{1,0:T(8,128)(2,1)}, u32[]{:S(2)}) copy-start(bf16[96,768]{1,0:T(8,128)(2,1)} %param.17) | copy-start | bytes 442372
  119.1 34.0 %copy-start.13 = (bf16[128,768]{1,0:T(8,128)(2,1)}, bf16[128,768]{1,0:T(8,128)(2,1)S(1)}, u32[]{:S(2)}) copy-start(bf16[128,768]{1,0:T(8,128)(2,1)S(1)} %reshape.294) | copy-start | bytes 589828
  119.1 34.0 %copy-start.16 = (bf16[2,64,768]{2,1,0:T(8,128)(2,1)S(1)}, bf16[2,64,768]{2,1,0:T(8,128)(2,1)}, u32[]{:S(2)}) copy-start(bf16[2,64,768]{2,1,0:T(8,128)(2,1)} %param.11) | copy-start | bytes 589828
  147.4 16.9 %copy-start.14 = (bf16[32,24,768]{2,1,0:T(8,128)(2,1)}, bf16[32,24,768]{2,1,0:T(8,128)(2,1)S(1)}, u32[]{:S(2)}) copy-start(bf16[32,24,768]{2,1,0:T(8,128)(2,1)S(1)} %all-to-all-done.5) | copy-start | bytes 3538948
  148.6 33.0 %all-to-all-start.6 = ((bf16[8,96,768]{2,1,0:T(8,128)(2,1)}), bf16[8,96,768]{2,1,0:T(8,128)(2,1)}, u32[]{:S(2)}, u32[]{:S(2)}) async-start(bf16[8,96,768]{2,1,0:T(8,128)(2,1)} %broadcast_in_dim.128), calls=%async_computation.6 | async-start | bytes 2359296 | tf_op jit(solution)/shard_map/all_to_all | solution.py:291
  153.9 6.5 %collective-permute-start.2 = (bf16[128,768]{1,0:T(8,128)(2,1)S(1)}, bf16[128,768]{1,0:T(8,128)(2,1)S(1)}, u32[]{:S(2)}, u32[]{:S(2)}) collective-permute-start(bf16[128,768]{1,0:T(8,128)(2,1)S(1)} %fusion.26), channel_id=1, source_target_pairs={{0,16},{16,0},{8,24},{24,8},{1,17},{17,1},{9,25},{25,9},{2,18},{18... | collective-permute-start | bytes 589832 | tf_op jit(solution)/shard_map/ppermute | solution.py:287
  161.2 2.1 collective-permute-start.3
  181.6 3.6 copy-start.27
  181.6 3.9 copy-start.4
  185.1 1.8 collective-permute-start.4
  187.9 7.0 %collective-permute-start.5 = (bf16[128,768]{1,0:T(8,128)(2,1)S(1)}, bf16[128,768]{1,0:T(8,128)(2,1)S(1)}, u32[]{:S(2)}, u32[]{:S(2)}) collective-permute-start(bf16[128,768]{1,0:T(8,128)(2,1)S(1)} %fusion.29), channel_id=1, source_target_pairs={{0,16},{16,0},{8,24},{24,8},{1,17},{17,1},{9,25},{25,9},{2,18},{18... | collective-permute-start | bytes 589832 | tf_op jit(solution)/shard_map/ppermute | solution.py:287
  196.6 8.3 %copy-start.36 = (f32[512,768]{1,0:T(8,128)S(1)}, f32[512,768]{1,0:T(8,128)}, u32[]{:S(2)}) copy-start(f32[512,768]{1,0:T(8,128)} %get-tuple-element.121) | copy-start | bytes 4718596
  196.8 6.2 %collective-permute-start.6 = (bf16[128,768]{1,0:T(8,128)(2,1)S(1)}, bf16[128,768]{1,0:T(8,128)(2,1)S(1)}, u32[]{:S(2)}, u32[]{:S(2)}) collective-permute-start(bf16[128,768]{1,0:T(8,128)(2,1)S(1)} %get-tuple-element.85), channel_id=1, source_target_pairs={{0,16},{16,0},{8,24},{24,8},{1,17},{17,1},{9,25},{25,9},{2,18},{18... | collective-permute-start | bytes 589832 | tf_op jit(solution)/shard_map/ppermute | solution.py:287
  203.0 1.8 collective-permute-start.7
  204.9 3.3 copy-start.18
  209.1 1.8 collective-permute-start.8
  209.4 3.8 copy-start.22
  212.0 7.0 %collective-permute-start.9 = (bf16[128,768]{1,0:T(8,128)(2,1)S(1)}, bf16[128,768]{1,0:T(8,128)(2,1)S(1)}, u32[]{:S(2)}, u32[]{:S(2)}) collective-permute-start(bf16[128,768]{1,0:T(8,128)(2,1)S(1)} %fusion.30), channel_id=1, source_target_pairs={{0,16},{16,0},{8,24},{24,8},{1,17},{17,1},{9,25},{25,9},{2,18},{18... | collective-permute-start | bytes 589832 | tf_op jit(solution)/shard_map/ppermute | solution.py:287
  214.2 26.0 %all-to-all-start.9 = ((bf16[8,3,24,768]{3,2,1,0:T(8,128)(2,1)}), bf16[8,3,24,768]{3,2,1,0:T(8,128)(2,1)S(1)}, u32[]{:S(2)}, u32[]{:S(2)}) async-start(bf16[8,3,24,768]{3,2,1,0:T(8,128)(2,1)} %broadcast_in_dim.131), calls=%async_computation.9 | async-start | bytes 1769472 | tf_op jit(solution)/shard_map/all_to_all | solution.py:291
  255.7 48.8 %all-to-all-start.10 = ((bf16[4,8,3,24,768]{4,3,2,1,0:T(8,128)(2,1)}), bf16[4,8,3,24,768]{4,3,2,1,0:T(8,128)(2,1)S(1)}, u32[]{:S(2)}, u32[]{:S(2)}) async-start(bf16[4,8,3,24,768]{4,3,2,1,0:T(8,128)(2,1)} %broadcast_in_dim.132), calls=%async_computation.10 | async-start | bytes 7077888 | tf_op jit(solution)/shard_map/all_to_all | solution.py:291
  265.1 37.2 %collective-permute-start.10 = (bf16[2,192,768]{2,1,0:T(8,128)(2,1)}, bf16[2,192,768]{2,1,0:T(8,128)(2,1)}, u32[]{:S(2)}, u32[]{:S(2)}) collective-permute-start(bf16[2,192,768]{2,1,0:T(8,128)(2,1)} %pad_maximum_fusion.2), channel_id=1, source_target_pairs={{0,8},{8,0},{16,24},{24,16},{1,9},{9,1},{17,25},{25,17},{2,10},{10... | collective-permute-start | bytes 1769480 | tf_op jit(solution)/shard_map/ppermute | solution.py:283
  296.6 3.8 copy-start.19
  304.5 18.6 %all-to-all-start.11 = ((bf16[32,24,256]{2,1,0:T(8,128)(2,1)}), bf16[32,24,256]{2,1,0:T(8,128)(2,1)}, u32[]{:S(2)}, u32[]{:S(2)}) async-start(bf16[32,24,256]{2,1,0:T(8,128)(2,1)} %fusion.13), calls=%async_computation.11 | async-start | bytes 786432 | tf_op jit(solution)/shard_map/all_to_all | solution.py:291
  308.1 13.2 %copy-start.9 = (f32[2,192,768]{2,1,0:T(8,128)S(1)}, f32[2,192,768]{2,1,0:T(8,128)}, u32[]{:S(2)}) copy-start(f32[2,192,768]{2,1,0:T(8,128)} %convert_element_type.148) | copy-start | bytes 3538948
  309.5 11.8 %collective-permute-start.11 = (bf16[192,768]{1,0:T(8,128)(2,1)S(1)}, bf16[192,768]{1,0:T(8,128)(2,1)S(1)}, u32[]{:S(2)}, u32[]{:S(2)}) collective-permute-start(bf16[192,768]{1,0:T(8,128)(2,1)S(1)} %fusion.27), channel_id=1, source_target_pairs={{0,16},{16,0},{8,24},{24,8},{1,17},{17,1},{9,25},{25,9},{2,18},{18... | collective-permute-start | bytes 884744 | tf_op jit(solution)/shard_map/ppermute | solution.py:287
  323.2 15.1 %all-to-all-start.12 = ((bf16[8,24,768]{2,1,0:T(8,128)(2,1)}), bf16[8,24,768]{2,1,0:T(8,128)(2,1)}, u32[]{:S(2)}, u32[]{:S(2)}) async-start(bf16[8,24,768]{2,1,0:T(8,128)(2,1)} %bitcast.218), calls=%async_computation.12 | async-start | bytes 589824 | tf_op jit(solution)/shard_map/all_to_all | solution.py:291
  338.3 32.1 %all-to-all-start.14 = ((bf16[8,96,768]{2,1,0:T(8,128)(2,1)}), bf16[8,96,768]{2,1,0:T(8,128)(2,1)}, u32[]{:S(2)}, u32[]{:S(2)}) async-start(bf16[8,96,768]{2,1,0:T(8,128)(2,1)} %bitcast.214), calls=%async_computation.14 | async-start | bytes 2359296 | tf_op jit(solution)/shard_map/all_to_all | solution.py:291
  404.2 25.3 %all-to-all-start.8 = ((bf16[32,96,128]{2,1,0:T(8,128)(2,1)}), bf16[32,96,128]{2,1,0:T(8,128)(2,1)}, u32[]{:S(2)}, u32[]{:S(2)}) async-start(bf16[32,96,128]{2,1,0:T(8,128)(2,1)} %get-tuple-element.29), calls=%async_computation.8 | async-start | bytes 1572864 | tf_op jit(solution)/shard_map/all_to_all | solution.py:291
  414.2 7.3 %copy-start.8 = (bf16[32,24,768]{2,1,0:T(8,128)(2,1)S(1)}, bf16[32,24,768]{2,1,0:T(8,128)(2,1)}, u32[]{:S(2)}) copy-start(bf16[32,24,768]{2,1,0:T(8,128)(2,1)} %all_to_all.76) | copy-start | bytes 3538948
  (15 other events, 22.7 us)

commit v3 on v2

--- a/solution.py
+++ b/solution.py
@@ -306,6 +306,27 @@
     parts = partial.reshape(4, count, -1)
     kept = parts[:2] + by_core(parts[2:].astype(BF)).astype(F32)
     return kept[0] + by_x(kept[1].astype(BF)).astype(F32)
+
+
+def in_order(blocks):
+    index = lax.axis_index("head")
+    own, across_x, across_core, across = [blocks[i] for i in range(4)]
+    odd, far = index % 2 == 1, index // 2 == 1
+    near = [jnp.where(odd, q, p) for p, q in ((own, across_core), (across_core, own))]
+    wide = [jnp.where(odd, q, p) for p, q in ((across_x, across), (across, across_x))]
+    return jnp.stack(
+        [jnp.where(far, q, p) for p, q in zip(near + wide, wide + near)]
+    )
+
+
+def to_group(blocks):
+    index = lax.axis_index("head")
+
+    def block(offset):
+        return lax.dynamic_index_in_dim(blocks, index ^ offset, 0, keepdims=False)
+
+    across = lax.ppermute(block(3), "head", [(i, i ^ 3) for i in range(4)])
+    return in_order(jnp.stack([block(0), by_x(block(2)), by_core(block(1)), across]))
 
 
 def key_ranges(spans, bq, bk):
@@ -382,18 +403,25 @@
     unit_bias = jnp.stack([bias[0], jnp.zeros_like(bias[0]), bias[1]]).reshape(3, HEADS, hd)
     unit_bias = lax.dynamic_index_in_dim(unit_bias, unit_head, 1, keepdims=True)
 
-    inner_slots = inner_weight.reshape(rows_dev, groups, 1, ff_part).transpose(1, 2, 0, 3)
-    inner_part = swap(
-        jnp.broadcast_to(inner_slots, (groups, cycle, rows_dev, ff_part)).reshape(
-            devices, rows_dev, ff_part
-        ),
-        BOTH,
-    ).reshape(depth, ff_part)
-    outer_part = spread_over(outer_weight, "blk", cycle).reshape(ff_part, depth)
-    out_all = spread_over(
-        spread_over(out_weight, "blk", cycle).reshape(depth // groups, depth), "head", groups
-    ).reshape(depth, depth)
-    qkv_all = spread_over(spread_over(qkv_weight, "blk", cycle), "head", groups)
+    inner_own = to_group(inner_weight.reshape(rows_dev, groups, ff_part).transpose(1, 0, 2))
+    ffn = lax.all_gather(
+        jnp.concatenate([inner_own.reshape(groups * rows_dev, ff_part), outer_weight]),
+        "blk",
+        axis=0,
+        tiled=False,
+    )
+    inner_part = (
+        ffn[:, : groups * rows_dev]
+        .reshape(cycle, groups, rows_dev, ff_part)
+        .transpose(1, 0, 2, 3)
+        .reshape(depth, ff_part)
+    )
+    outer_part = ffn[:, groups * rows_dev :].reshape(ff_part, depth)
+    out_part = spread_over(out_weight, "blk", cycle).reshape(depth // groups, depth)
+    out_all = in_order(gather_group(out_part).reshape(groups, depth // groups, depth)).reshape(
+        depth, depth
+    )
+    qkv_all = lax.all_gather(qkv_weight, BOTH, axis=0, tiled=False)
 
     lengths = lax.dynamic_index_in_dim(doc_lengths, half, 0, keepdims=False)
     order = jnp.arange(lengths.shape[0], dtype=jnp.int32)
@@ -453,17 +481,20 @@
     d_heads = jnp.stack([d_heads[:, :, u] for u in unit_of], axis=2)
     d_heads = swap(d_heads.reshape(devices, half_tokens, 2 * hd), BOTH)
 
-    outer_grad = dot(act_low, d_ffn_group, TN).astype(BF)
-    outer_grad = jnp.sum(
-        swap(outer_grad.reshape(cycle, ff_dev, depth), "blk").astype(F32), axis=0
-    )
-    inner_grad = dot(normed_low, d_inner, TN).astype(BF)
-    inner_grad = swap(inner_grad.reshape(devices, rows_dev, ff_part), BOTH)
+    outer_grad = dot(act_low, d_ffn_group, TN).astype(BF).reshape(cycle, ff_dev, depth)
     inner_grad = (
-        jnp.sum(inner_grad.reshape(groups, cycle, rows_dev, ff_part).astype(F32), axis=1)
-        .transpose(1, 0, 2)
-        .reshape(rows_dev, groups * ff_part)
-    )
+        dot(normed_low, d_inner, TN)
+        .astype(BF)
+        .reshape(groups, cycle, rows_dev, ff_part)
+        .transpose(1, 0, 2, 3)
+        .reshape(cycle, groups * rows_dev, ff_part)
+    )
+    ffn_grad = lax.psum_scatter(
+        jnp.concatenate([inner_grad, outer_grad], axis=1), "blk", scatter_dimension=0, tiled=False
+    )
+    outer_grad = ffn_grad[groups * rows_dev :].astype(F32)
+    inner_grad = to_group(ffn_grad[: groups * rows_dev].reshape(groups, rows_dev, ff_part))
+    inner_grad = inner_grad.transpose(1, 0, 2).reshape(rows_dev, groups * ff_part).astype(F32)
     out_grad = dot(attn, d_branch, TN).reshape(groups, depth // groups, depth)
 
     def out_block(offset):
@@ -486,7 +517,7 @@
         .transpose(3, 1, 5, 4, 0, 2, 6)
         .reshape(3, rows, depth)
     )
-    qkv_all = qkv_all.reshape(devices, 3, rows_dev, depth).transpose(1, 0, 2, 3).reshape(3, depth, depth)
+    qkv_all = qkv_all.transpose(1, 0, 2, 3).reshape(3, depth, depth)
     d_tokens = d_first
     for c in range(3):
         d_tokens = d_tokens + dot(d_qkv[c], qkv_all[c], NT)

time: 444 us -> 337 us (0.76)
  waiting for transfers between devices: 187 us -> 132 us
  blocking collectives: 47.3 us -> 15.6 us
  starting transfers between devices: 60.2 us -> 40.3 us
  between operations: 1.6 us -> 15 us
  matrix products: 20.8 us -> 11.8 us
    all_to_all x13 -> x7, waiting for transfers between devices: 147 us -> 71.8 us  [swap(): lax.all_to_all(value, axes, split_axis=0, concat_axis=0, tiled=True, axis...]
    all_to_all x2 -> x1, blocking collectives: 47.3 us -> 15.6 us  [swap(): lax.all_to_all(value, axes, split_axis=0, concat_axis=0, tiled=True, axis...]
    all_to_all x13 -> x7, starting transfers between devices: 49.4 us -> 24.9 us  [swap(): lax.all_to_all(value, axes, split_axis=0, concat_axis=0, tiled=True, axis...]
    ppermute x1, waiting for transfers between devices: 4.9 us -> 20.3 us  [local(): lax.ppermute(other_x, 'blk', [(i, (i + halves) % cycle) for i in range(cy...]
    dot_general x12, matrix products: 20.8 us -> 11.8 us  [dot(): return lax.dot_general(a, b, dims, preferred_element_type=F32)]
    ppermute x5 -> x8, waiting for transfers between devices: 27.7 us -> 35.7 us  [by_x(): return lax.ppermute(value, 'head', [(0, 2), (2, 0), (1, 3), (3, 1)])]
    unnamed x80 -> x111, local copies, waits for them, and re-layouts: 12 us -> 6.22 us
    slice x5 -> x4, local copies, waits for them, and re-layouts: 0.14 us -> 5.43 us  [reduce_group(): kept = parts[:2] + by_core(parts[2:].astype(BF)).astype(F32)]
  transfers between devices with their start and end apart: 25 -> 30, of which waited for: 20 -> 17; matrix products, arithmetic and copies ran while one was open for 17% -> 27% of each run, Pallas kernels for 8% -> 11%
where the time goes in v3:
time: 337 us; the launch traced here: 336 us
  waiting for transfers between devices  132 us (39%)
  local copies, waits for them, and re-layouts  56 us (17%)
  starting transfers between devices  40.3 us (12%)
  Pallas kernels  35.9 us (11%)
  other arithmetic  29 us (9%)
  blocking collectives  15.6 us (5%)
  between operations  15 us (4%)
  matrix products  11.8 us (4%)
    all_to_all x7, waiting for transfers between devices, swap(): lax.all_to_all(value, axes, split_axis=0, concat_axis=0, tiled=True, axis...  71.8 us
    ppermute x8, waiting for transfers between devices, by_x(): return lax.ppermute(value, 'head', [(0, 2), (2, 0), (1, 3), (3, 1)])  35.7 us
    all_to_all x7, starting transfers between devices, swap(): lax.all_to_all(value, axes, split_axis=0, concat_axis=0, tiled=True, axis...  24.9 us
    ppermute x1, waiting for transfers between devices, local(): lax.ppermute(other_x, 'blk', [(i, (i + halves) % cycle) for i in range(cy...  20.3 us
    all_to_all x1, blocking collectives, swap(): lax.all_to_all(value, axes, split_axis=0, concat_axis=0, tiled=True, axis...  15.6 us
    pallas_call x1, Pallas kernels, attend_back(): pl.pallas_call(functools.partial(attend_back_kernel, bq=bq, bk=bk, pack=p...  15.2 us
    dot_general x12, matrix products, dot(): return lax.dot_general(a, b, dims, preferred_element_type=F32)  11.8 us
    pallas_call x1, Pallas kernels, attend(): pl.pallas_call(functools.partial(attend_kernel, bq=bq, bk=bk, pack=pack),...  11.1 us
  transfers between devices with their start and end apart: 30, of which 17 were waited for; matrix products, arithmetic and copies ran while one was open for 27% of the time, Pallas kernels for 11%

profile of v3, /device:TPU:0, one launch (start us, length us, event | category | flops | bytes accessed | tf_op | source)
XLA Modules:
  0.0 335.5 jit_solution(557282969006263132)
XLA Ops:
  8.6 2.4 collective-permute-start.6
  13.0 2.2 collective-permute-done.7
  16.7 5.8 %all-to-all-start.3 = ((bf16[8,24,768]{2,1,0:T(8,128)(2,1)}), bf16[8,24,768]{2,1,0:T(8,128)(2,1)S(1)}, u32[]{:S(2)}, u32[]{:S(2)}) async-start(bf16[8,24,768]{2,1,0:T(8,128)(2,1)} %broadcast_in_dim.92), calls=%async_computation.3 | async-start | bytes 589824 | tf_op jit(solution)/shard_map/all_to_all | solution.py:291
  22.6 3.0 collective-permute-start
  25.6 20.3 %collective-permute-done = bf16[64,768]{1,0:T(8,128)(2,1)S(1)} collective-permute-done((bf16[64,768]{1,0:T(8,128)(2,1)S(1)}, bf16[64,768]{1,0:T(8,128)(2,1)S(1)}, u32[]{:S(2)}, u32[]{:S(2)}) %collective-permute-start) | collective-permute-done | bytes 98336 | tf_op jit(solution)/shard_map/ppermute | solution.py:368
  47.2 3.7 %all-to-all-start = ((bf16[8,128,768]{2,1,0:T(8,128)(2,1)}), bf16[8,128,768]{2,1,0:T(8,128)(2,1)S(1)}, u32[]{:S(2)}, u32[]{:S(2)}) async-start(bf16[8,128,768]{2,1,0:T(8,128)(2,1)} %broadcast_in_dim.90), calls=%async_computation | async-start | bytes 3145728 | tf_op jit(solution)/shard_map/all_to_all | solution.py:291
  54.0 26.1 %all-to-all-done.a_ref = bf16[8,128,768]{2,1,0:T(8,128)(2,1)S(1)} async-done(((bf16[8,128,768]{2,1,0:T(8,128)(2,1)}), bf16[8,128,768]{2,1,0:T(8,128)(2,1)S(1)}, u32[]{:S(2)}, u32[]{:S(2)}) %all-to-all-start) | async-done | bytes 1572896 | tf_op jit(solution)/shard_map/all_to_all | solution.py:291
  80.1 4.3 %all-to-all-start.1 = ((bf16[32,39,128]{2,1,0:T(8,128)(2,1)}), bf16[32,39,128]{2,1,0:T(8,128)(2,1)}, u32[]{:S(2)}, u32[]{:S(2)}) async-start(bf16[32,39,128]{2,1,0:T(8,128)(2,1)} %reshape.304), calls=%async_computation.1 | async-start | bytes 655360 | tf_op jit(solution)/shard_map/all_to_all | solution.py:291
  87.4 1.7 collective-permute-start.2
  89.1 7.9 %all-to-all-done.1 = bf16[32,39,128]{2,1,0:T(8,128)(2,1)} async-done(((bf16[32,39,128]{2,1,0:T(8,128)(2,1)}), bf16[32,39,128]{2,1,0:T(8,128)(2,1)}, u32[]{:S(2)}, u32[]{:S(2)}) %all-to-all-start.1) | async-done | bytes 319520 | tf_op jit(solution)/shard_map/all_to_all | solution.py:291
  100.2 1.8 slice_reduce_fusion.2
  102.1 2.6 reshape.306
  104.7 2.1 copy.152
  107.0 1.9 pad_maximum_fusion.4
  112.0 5.9 %project.1 = (bf16[2048,64]{1,0:T(8,128)(2,1)}, bf16[2048,64]{1,0:T(8,128)(2,1)}, bf16[2048,64]{1,0:T(8,128)(2,1)}, bf16[64,2048]{1,0:T(8,128)(2,1)}, bf16[64,2048]{1,0:T(8,128)(2,1)}) custom-call(s32[2]{0:T(128)} %pad_add_fusion.1.place_ref, bf16[8,128,768]{2,1,0:T(8,128)(2,1)} %copy-done, bf16[8,128,768]{2,1,0:T(8,128)(2,1)} %copy-done.1, ...), custom_call_target="tpu_custom_call" | custom-call | tf_op jit(solution)/shard_map/project/pallas_call | solution.py:80
  117.9 11.1 %attend.1 = (bf16[32,32,128]{2,1,0:T(8,128)(2,1)}, f32[64,2048]{1,0:T(8,128)}, f32[1,2048]{1,0:T(1,128)}) custom-call(s32[4]{0:T(128)} %get-tuple-element.134.lo_ref, s32[4]{0:T(128)} %get-tuple-element.141.hi_ref, bf16[2048,64]{1,0:T(8,128)(2,1)} %get-tuple-element.21.q_ref, bf16[2048,64]{1,0:T(8,128)(2,1)} %get-tuple-element.22.k_ref, ...), custom_call_target="tpu_custom_call" | custom-call | tf_op jit(solution)/shard_map/attend/pallas_call | solution.py:169
  129.0 2.6 all-to-all-start.2
  134.2 9.0 %all-to-all-done.2 = bf16[32,32,128]{2,1,0:T(8,128)(2,1)S(1)} async-done(((bf16[32,32,128]{2,1,0:T(8,128)(2,1)}), bf16[32,32,128]{2,1,0:T(8,128)(2,1)S(1)}, u32[]{:S(2)}, u32[]{:S(2)}) %all-to-all-start.2) | async-done | bytes 262176 | tf_op jit(solution)/shard_map/all_to_all | solution.py:291
  146.1 6.3 %collective-permute-done.4 = bf16[128,768]{1,0:T(8,128)(2,1)S(1)} collective-permute-done((bf16[128,768]{1,0:T(8,128)(2,1)S(1)}, bf16[128,768]{1,0:T(8,128)(2,1)S(1)}, u32[]{:S(2)}, u32[]{:S(2)}) %collective-permute-start.4) | collective-permute-done | bytes 196640 | tf_op jit(solution)/shard_map/ppermute | solution.py:287
  154.0 1.8 fusion.57
  157.3 2.0 multiply_convert_fusion
  167.9 6.6 %collective-permute-done.10 = bf16[128,768]{1,0:T(8,128)(2,1)S(1)} collective-permute-done((bf16[128,768]{1,0:T(8,128)(2,1)S(1)}, bf16[128,768]{1,0:T(8,128)(2,1)S(1)}, u32[]{:S(2)}, u32[]{:S(2)}) %collective-permute-start.10) | collective-permute-done | bytes 196640 | tf_op jit(solution)/shard_map/ppermute | solution.py:287
  177.8 5.9 %collective-permute-done.11 = bf16[128,768]{1,0:T(8,128)(2,1)S(1)} collective-permute-done((bf16[128,768]{1,0:T(8,128)(2,1)S(1)}, bf16[128,768]{1,0:T(8,128)(2,1)S(1)}, u32[]{:S(2)}, u32[]{:S(2)}) %collective-permute-start.11) | collective-permute-done | bytes 196640 | tf_op jit(solution)/shard_map/ppermute | solution.py:287
  183.9 1.7 collective-permute-done.12
  185.7 1.6 fusion.65
  187.4 2.0 fusion.67
  193.8 2.1 slice.275
  196.8 1.4 convert_add_fusion
  200.5 1.6 pad_maximum_fusion
  202.2 4.2 %collective-permute-done.14 = bf16[128,768]{1,0:T(8,128)(2,1)S(1)} collective-permute-done((bf16[128,768]{1,0:T(8,128)(2,1)}, bf16[128,768]{1,0:T(8,128)(2,1)S(1)}, u32[]{:S(2)}, u32[]{:S(2)}) %collective-permute-start.14) | collective-permute-done | bytes 196640 | tf_op jit(solution)/shard_map/ppermute | solution.py:287
  206.4 1.6 multiply_reduce_fusion
  210.5 3.2 all-to-all-start.4
  215.7 14.5 %all-to-all-done.4.do_ref = bf16[32,32,128]{2,1,0:T(8,128)(2,1)S(1)} async-done(((bf16[32,32,128]{2,1,0:T(8,128)(2,1)}), bf16[32,32,128]{2,1,0:T(8,128)(2,1)S(1)}, u32[]{:S(2)}, u32[]{:S(2)}) %all-to-all-start.4) | async-done | bytes 262176 | tf_op jit(solution)/shard_map/all_to_all | solution.py:291
  230.9 15.2 %attend_back.1 = (bf16[32,96,128]{2,1,0:T(8,128)(2,1)}, bf16[192,2048]{1,0:T(8,128)(2,1)}, f32[1,128]{1,0:T(1,128)}) custom-call(s32[4]{0:T(128)} %get-tuple-element.133.lo_ref, s32[4]{0:T(128)} %get-tuple-element.142.hi_ref, bf16[2048,64]{1,0:T(8,128)(2,1)} %get-tuple-element.21.q_ref, bf16[2048,64]{1,0:T(8,128)(2,1)} %get-tuple-element.22.k_ref, ...), custom_call_target="tpu_custom_call" | custom-call | tf_op jit(solution)/shard_map/attend_back/pallas_call | solution.py:246
  247.4 3.8 %weight_grad.1 = bf16[768,192]{1,0:T(8,128)(2,1)} custom-call(s32[2]{0:T(128)} %pad_add_fusion.1.place_ref, bf16[8,128,768]{2,1,0:T(8,128)(2,1)} %copy-done, bf16[8,128,768]{2,1,0:T(8,128)(2,1)} %copy-done.1, bf16[192,2048]{1,0:T(8,128)(2,1)} %get-tuple-element.30.gt_ref), custom_call_target="tpu_custom_call" | custom-call | tf_op jit(solution)/shard_map/weight_grad/pallas_call | solution.py:104
  251.2 1.9 fusion.13
  253.1 2.6 all-to-all-start.6
  256.9 1.7 collective-permute-start.16
  258.7 9.7 %collective-permute-done.16 = bf16[192,768]{1,0:T(8,128)(2,1)S(1)} collective-permute-done((bf16[192,768]{1,0:T(8,128)(2,1)S(1)}, bf16[192,768]{1,0:T(8,128)(2,1)S(1)}, u32[]{:S(2)}, u32[]{:S(2)}) %collective-permute-start.16) | collective-permute-done | bytes 294944 | tf_op jit(solution)/shard_map/ppermute | solution.py:287
  269.1 4.4 %all-to-all-done.6 = bf16[32,24,256]{2,1,0:T(8,128)(2,1)S(1)} async-done(((bf16[32,24,256]{2,1,0:T(8,128)(2,1)}), bf16[32,24,256]{2,1,0:T(8,128)(2,1)S(1)}, u32[]{:S(2)}, u32[]{:S(2)}) %all-to-all-start.6) | async-done | bytes 393248 | tf_op jit(solution)/shard_map/all_to_all | solution.py:291
  273.6 15.6 %all_to_all.40 = bf16[8,24,768]{2,1,0:T(8,128)(2,1)S(1)} all-to-all(bf16[8,24,768]{2,1,0:T(8,128)(2,1)} %bitcast.316), channel_id=1, replica_groups=mesh['head'=4,'blk'=8] {'blk'}, dimensions={0} | all-to-all | bytes 589824 | tf_op jit(solution)/shard_map/all_to_all | solution.py:291
  289.2 2.6 all-to-all-start.5
  291.9 3.9 %fusion.56 = (bf16[1,32,24,768]{3,2,0,1:T(8,128)(2,1)}, bf16[1,32,24,768]{3,2,0,1:T(8,128)(2,1)}, bf16[1,32,24,768]{3,2,0,1:T(8,128)(2,1)}) fusion(bf16[3,32,24,768]{3,2,0,1:T(8,128)(2,1)} %bitcast.297), kind=kLoop, calls=%fused_computation.198 | loop fusion | bytes 7077888 | tf_op jit(solution)/shard_map/slice | solution.py:523
  297.2 1.6 reshape.332
  303.9 9.9 %all-to-all-done.5 = bf16[32,96,128]{2,1,0:T(8,128)(2,1)S(1)} async-done(((bf16[32,96,128]{2,1,0:T(8,128)(2,1)}), bf16[32,96,128]{2,1,0:T(8,128)(2,1)S(1)}, u32[]{:S(2)}, u32[]{:S(2)}) %all-to-all-start.5) | async-done | bytes 786464 | tf_op jit(solution)/shard_map/all_to_all | solution.py:291
  316.9 1.5 fusion.58
  319.2 1.6 squeeze.101
  321.9 1.7 fusion.33
  (300 shorter events, 71.7 us)
Async XLA Ops:
  7.2 8.1 %copy-start.22 = (bf16[96,768]{1,0:T(8,128)(2,1)S(1)}, bf16[96,768]{1,0:T(8,128)(2,1)}, u32[]{:S(2)}) copy-start(bf16[96,768]{1,0:T(8,128)(2,1)} %param.17) | copy-start | bytes 442372
  7.2 8.8 %copy-start.24 = (bf16[24,768]{1,0:T(8,128)(2,1)S(1)}, bf16[24,768]{1,0:T(8,128)(2,1)}, u32[]{:S(2)}) copy-start(bf16[24,768]{1,0:T(8,128)(2,1)} %param.15) | copy-start | bytes 110596
  7.2 146.8 %all-gather.5.cloned.1.call-start = ((), (), s32[]{:S(2)}) async-start(), calls=%async_computation.10 | async-start | bytes 2654208 | tf_op jit(solution)/shard_map/all_gather | solution.py:407
  8.6 14.0 %copy-start.14 = (bf16[2,64,768]{2,1,0:T(8,128)(2,1)S(1)}, bf16[2,64,768]{2,1,0:T(8,128)(2,1)}, u32[]{:S(2)}) copy-start(bf16[2,64,768]{2,1,0:T(8,128)(2,1)} %param.11) | copy-start | bytes 589828
  8.6 4.3 %collective-permute-start.6 = (bf16[24,768]{1,0:T(8,128)(2,1)S(1)}, bf16[24,768]{1,0:T(8,128)(2,1)S(1)}, u32[]{:S(2)}, u32[]{:S(2)}) collective-permute-start(bf16[24,768]{1,0:T(8,128)(2,1)S(1)} %bitcast.343), channel_id=1, source_target_pairs={{0,24},{8,16},{16,8},{24,0},{1,25},{9,17},{17,9},{25,1},{2,26},{10... | collective-permute-start | bytes 110600 | tf_op jit(solution)/shard_map/ppermute | solution.py:328
  11.1 4.1 %collective-permute-start.7 = (bf16[24,768]{1,0:T(8,128)(2,1)S(1)}, bf16[24,768]{1,0:T(8,128)(2,1)S(1)}, u32[]{:S(2)}, u32[]{:S(2)}) collective-permute-start(bf16[24,768]{1,0:T(8,128)(2,1)S(1)} %bitcast.344), channel_id=1, source_target_pairs={{0,16},{16,0},{8,24},{24,8},{1,17},{17,1},{9,25},{25,9},{2,18},{18... | collective-permute-start | bytes 110600 | tf_op jit(solution)/shard_map/ppermute | solution.py:287
  11.7 3.4 %collective-permute-start.8 = (bf16[24,768]{1,0:T(8,128)(2,1)S(1)}, bf16[24,768]{1,0:T(8,128)(2,1)S(1)}, u32[]{:S(2)}, u32[]{:S(2)}) collective-permute-start(bf16[24,768]{1,0:T(8,128)(2,1)S(1)} %bitcast.345), channel_id=1, source_target_pairs={{0,8},{8,0},{16,24},{24,16},{1,9},{9,1},{17,25},{25,17},{2,10},{10... | collective-permute-start | bytes 110600 | tf_op jit(solution)/shard_map/ppermute | solution.py:283
  16.7 29.2 %all-to-all-start.3 = ((bf16[8,24,768]{2,1,0:T(8,128)(2,1)}), bf16[8,24,768]{2,1,0:T(8,128)(2,1)S(1)}, u32[]{:S(2)}, u32[]{:S(2)}) async-start(bf16[8,24,768]{2,1,0:T(8,128)(2,1)} %broadcast_in_dim.92), calls=%async_computation.3 | async-start | bytes 589824 | tf_op jit(solution)/shard_map/all_to_all | solution.py:291
  22.6 23.3 %collective-permute-start = (bf16[64,768]{1,0:T(8,128)(2,1)S(1)}, bf16[64,768]{1,0:T(8,128)(2,1)S(1)}, u32[]{:S(2)}, u32[]{:S(2)}) collective-permute-start(bf16[64,768]{1,0:T(8,128)(2,1)S(1)} %get-tuple-element.107), channel_id=1, source_target_pairs={{0,4},{1,5},{2,6},{3,7},{4,0},{5,1},{6,2},{7,3},{8,12},{9,13},{10,... | collective-permute-start | bytes 294920 | tf_op jit(solution)/shard_map/ppermute | solution.py:368
  47.2 4.5 %copy-start.21 = (bf16[3,24,768]{2,1,0:T(8,128)(2,1)S(1)}, bf16[3,24,768]{2,1,0:T(8,128)(2,1)}, u32[]{:S(2)}) copy-start(bf16[3,24,768]{2,1,0:T(8,128)(2,1)} %param.14) | copy-start | bytes 331780
  47.2 32.9 %all-to-all-start = ((bf16[8,128,768]{2,1,0:T(8,128)(2,1)}), bf16[8,128,768]{2,1,0:T(8,128)(2,1)S(1)}, u32[]{:S(2)}, u32[]{:S(2)}) async-start(bf16[8,128,768]{2,1,0:T(8,128)(2,1)} %broadcast_in_dim.90), calls=%async_computation | async-start | bytes 3145728 | tf_op jit(solution)/shard_map/all_to_all | solution.py:291
  50.9 240.9 %all-gather.7.cloned.1.call-start = ((), (), s32[]{:S(2)}) async-start(), calls=%async_computation.11 | async-start | bytes 3649536 | tf_op jit(solution)/shard_map/all_gather | solution.py:424
  80.1 24.6 %copy-start = (bf16[8,128,768]{2,1,0:T(8,128)(2,1)}, bf16[8,128,768]{2,1,0:T(8,128)(2,1)S(1)}, u32[]{:S(2)}) copy-start(bf16[8,128,768]{2,1,0:T(8,128)(2,1)S(1)} %all-to-all-done.a_ref) | copy-start | bytes 4718596
  80.1 16.9 %all-to-all-start.1 = ((bf16[32,39,128]{2,1,0:T(8,128)(2,1)}), bf16[32,39,128]{2,1,0:T(8,128)(2,1)}, u32[]{:S(2)}, u32[]{:S(2)}) async-start(bf16[32,39,128]{2,1,0:T(8,128)(2,1)} %reshape.304), calls=%async_computation.1 | async-start | bytes 655360 | tf_op jit(solution)/shard_map/all_to_all | solution.py:291
  86.6 24.1 %collective-permute-start.1 = (bf16[8,128,768]{2,1,0:T(8,128)(2,1)S(1)}, bf16[8,128,768]{2,1,0:T(8,128)(2,1)S(1)}, u32[]{:S(2)}, u32[]{:S(2)}) collective-permute-start(bf16[8,128,768]{2,1,0:T(8,128)(2,1)S(1)} %all-to-all-done.a_ref), channel_id=1, source_target_pairs={{0,8},{8,0},{16,24},{24,16},{1,9},{9,1},{17,25},{25,17},{2,10},{10... | collective-permute-start | bytes 4718600 | tf_op jit(solution)/shard_map/ppermute | solution.py:283
  87.4 19.6 %collective-permute-start.2 = (bf16[192,768]{1,0:T(8,128)(2,1)S(1)}, bf16[192,768]{1,0:T(8,128)(2,1)}, u32[]{:S(2)}, u32[]{:S(2)}) collective-permute-start(bf16[192,768]{1,0:T(8,128)(2,1)S(1)} %bitcast.299), channel_id=1, source_target_pairs={{0,16},{16,0},{8,24},{24,8},{1,17},{17,1},{9,25},{25,9},{2,18},{18... | collective-permute-start | bytes 884744 | tf_op jit(solution)/shard_map/ppermute | solution.py:287
  108.8 24.0 %collective-permute-start.3 = (bf16[2,192,768]{2,1,0:T(8,128)(2,1)}, bf16[2,192,768]{2,1,0:T(8,128)(2,1)}, u32[]{:S(2)}, u32[]{:S(2)}) collective-permute-start(bf16[2,192,768]{2,1,0:T(8,128)(2,1)} %pad_maximum_fusion.4), channel_id=1, source_target_pairs={{0,8},{8,0},{16,24},{24,16},{1,9},{9,1},{17,25},{25,17},{2,10},{10... | collective-permute-start | bytes 1769480 | tf_op jit(solution)/shard_map/ppermute | solution.py:283
  129.0 14.3 %all-to-all-start.2 = ((bf16[32,32,128]{2,1,0:T(8,128)(2,1)}), bf16[32,32,128]{2,1,0:T(8,128)(2,1)S(1)}, u32[]{:S(2)}, u32[]{:S(2)}) async-start(bf16[32,32,128]{2,1,0:T(8,128)(2,1)} %get-tuple-element.24), calls=%async_computation.2 | async-start | bytes 524288 | tf_op jit(solution)/shard_map/all_to_all | solution.py:291
  131.6 190.4 %reduce-scatter.2.cloned.1.call-start = ((), (), s32[]{:S(2)}) async-start(), calls=%async_computation.9 | async-start | bytes 2654208 | tf_op jit(solution)/shard_map/reduce_scatter | solution.py:492
  134.2 10.4 %copy-start.15 = (bf16[2,64,768]{2,1,0:T(8,128)(2,1)S(1)}, bf16[2,64,768]{2,1,0:T(8,128)(2,1)}, u32[]{:S(2)}) copy-start(bf16[2,64,768]{2,1,0:T(8,128)(2,1)} %param.11) | copy-start | bytes 589828
  145.0 8.8 %copy-start.23 = (f32[32,96]{1,0:T(8,128)S(1)}, f32[32,96]{1,0:T(8,128)}, u32[]{:S(2)}) copy-start(f32[32,96]{1,0:T(8,128)} %get-tuple-element.119) | copy-start | bytes 36868
  145.3 10.5 %copy-start.25 = (f32[128]{0:T(128)}, f32[128]{0:T(128)S(1)}, u32[]{:S(2)}) copy-start(f32[128]{0:T(128)S(1)} %add_rsqrt_fusion.1) | copy-start | bytes 1540
  145.4 7.0 %collective-permute-start.4 = (bf16[128,768]{1,0:T(8,128)(2,1)S(1)}, bf16[128,768]{1,0:T(8,128)(2,1)S(1)}, u32[]{:S(2)}, u32[]{:S(2)}) collective-permute-start(bf16[128,768]{1,0:T(8,128)(2,1)S(1)} %fusion.26), channel_id=1, source_target_pairs={{0,16},{16,0},{8,24},{24,8},{1,17},{17,1},{9,25},{25,9},{2,18},{18... | collective-permute-start | bytes 589832 | tf_op jit(solution)/shard_map/ppermute | solution.py:287
  153.2 2.7 collective-permute-start.5
  159.3 5.3 %copy-start.2 = (bf16[2,64,768]{2,1,0:T(8,128)(2,1)S(1)}, bf16[2,64,768]{2,1,0:T(8,128)(2,1)}, u32[]{:S(2)}) copy-start(bf16[2,64,768]{2,1,0:T(8,128)(2,1)} %param.13) | copy-start | bytes 589828
  160.2 4.4 %copy-start.13 = (f32[512,768]{1,0:T(8,128)}, f32[512,768]{1,0:T(8,128)S(1)}, u32[]{:S(2)}) copy-start(f32[512,768]{1,0:T(8,128)S(1)} %fusion.66) | copy-start | bytes 4718596
  161.1 4.9 %collective-permute-start.9 = (bf16[2,128,768]{2,1,0:T(8,128)(2,1)}, bf16[2,128,768]{2,1,0:T(8,128)(2,1)}, u32[]{:S(2)}, u32[]{:S(2)}) collective-permute-start(bf16[2,128,768]{2,1,0:T(8,128)(2,1)} %bitcast.42), channel_id=1, source_target_pairs={{0,8},{8,0},{16,24},{24,16},{1,9},{9,1},{17,25},{25,17},{2,10},{10... | collective-permute-start | bytes 1179656 | tf_op jit(solution)/shard_map/ppermute | solution.py:283
  167.1 7.4 %collective-permute-start.10 = (bf16[128,768]{1,0:T(8,128)(2,1)S(1)}, bf16[128,768]{1,0:T(8,128)(2,1)S(1)}, u32[]{:S(2)}, u32[]{:S(2)}) collective-permute-start(bf16[128,768]{1,0:T(8,128)(2,1)S(1)} %fusion.29), channel_id=1, source_target_pairs={{0,16},{16,0},{8,24},{24,8},{1,17},{17,1},{9,25},{25,9},{2,18},{18... | collective-permute-start | bytes 589832 | tf_op jit(solution)/shard_map/ppermute | solution.py:287
  167.9 9.3 %copy-start.36 = (f32[128]{0:T(128)}, f32[128]{0:T(128)S(1)}, u32[]{:S(2)}) copy-start(f32[128]{0:T(128)S(1)} %div.99) | copy-start | bytes 1540
  175.4 10.2 %copy-start.30 = (f32[128]{0:T(128)}, f32[128]{0:T(128)S(1)}, u32[]{:S(2)}) copy-start(f32[128]{0:T(128)S(1)} %broadcast_multiply_fusion.4) | copy-start | bytes 1540
  176.4 9.3 %copy-start.11 = (bf16[8,96,768]{2,1,0:T(8,128)(2,1)S(1)}, bf16[8,96,768]{2,1,0:T(8,128)(2,1)}, u32[]{:S(2)}) copy-start(bf16[8,96,768]{2,1,0:T(8,128)(2,1)} %copy-done.10) | copy-start | bytes 3538948
  176.4 9.3 %copy-start.50 = (f32[512,768]{1,0:T(8,128)S(1)}, f32[512,768]{1,0:T(8,128)}, u32[]{:S(2)}) copy-start(f32[512,768]{1,0:T(8,128)} %get-tuple-element.138) | copy-start | bytes 4718596
  177.2 6.5 %collective-permute-start.11 = (bf16[128,768]{1,0:T(8,128)(2,1)S(1)}, bf16[128,768]{1,0:T(8,128)(2,1)S(1)}, u32[]{:S(2)}, u32[]{:S(2)}) collective-permute-start(bf16[128,768]{1,0:T(8,128)(2,1)S(1)} %get-tuple-element.75), channel_id=1, source_target_pairs={{0,16},{16,0},{8,24},{24,8},{1,17},{17,1},{9,25},{25,9},{2,18},{18... | collective-permute-start | bytes 589832 | tf_op jit(solution)/shard_map/ppermute | solution.py:287
  183.8 1.8 collective-permute-start.12
  189.3 6.6 %copy-start.20 = (bf16[4,128,768]{2,1,0:T(8,128)(2,1)S(1)}, bf16[4,128,768]{2,1,0:T(8,128)(2,1)}, u32[]{:S(2)}) copy-start(bf16[4,128,768]{2,1,0:T(8,128)(2,1)} %copy-done.19) | copy-start | bytes 2359300
  190.6 6.2 %collective-permute-start.13 = (bf16[2,128,768]{2,1,0:T(8,128)(2,1)S(1)}, bf16[2,128,768]{2,1,0:T(8,128)(2,1)}, u32[]{:S(2)}, u32[]{:S(2)}) collective-permute-start(bf16[2,128,768]{2,1,0:T(8,128)(2,1)S(1)} %bitcast.334), channel_id=1, source_target_pairs={{0,8},{8,0},{16,24},{24,16},{1,9},{9,1},{17,25},{25,17},{2,10},{10... | collective-permute-start | bytes 1179656 | tf_op jit(solution)/shard_map/ppermute | solution.py:283
  199.0 7.4 %collective-permute-start.14 = (bf16[128,768]{1,0:T(8,128)(2,1)}, bf16[128,768]{1,0:T(8,128)(2,1)S(1)}, u32[]{:S(2)}, u32[]{:S(2)}) collective-permute-start(bf16[128,768]{1,0:T(8,128)(2,1)} %fusion.30), channel_id=1, source_target_pairs={{0,16},{16,0},{8,24},{24,8},{1,17},{17,1},{9,25},{25,9},{2,18},{18... | collective-permute-start | bytes 589832 | tf_op jit(solution)/shard_map/ppermute | solution.py:287
  202.1 4.3 %copy-start.37 = (f32[128]{0:T(128)S(1)}, f32[128]{0:T(128)}, u32[]{:S(2)}) copy-start(f32[128]{0:T(128)} %copy-done.36) | copy-start | bytes 1540
  202.2 5.9 %copy-start.27 = (f32[128]{0:T(128)S(1)}, f32[128]{0:T(128)}, u32[]{:S(2)}) copy-start(f32[128]{0:T(128)} %copy-done.25) | copy-start | bytes 1540
  208.8 5.0 %copy-start.16 = (bf16[768,128]{1,0:T(8,128)(2,1)S(1)}, bf16[768,128]{1,0:T(8,128)(2,1)}, u32[]{:S(2)}) copy-start(bf16[768,128]{1,0:T(8,128)(2,1)} %copy.124) | copy-start | bytes 589828
  210.5 19.7 %all-to-all-start.4 = ((bf16[32,32,128]{2,1,0:T(8,128)(2,1)}), bf16[32,32,128]{2,1,0:T(8,128)(2,1)S(1)}, u32[]{:S(2)}, u32[]{:S(2)}) async-start(bf16[32,32,128]{2,1,0:T(8,128)(2,1)} %bitcast.57), calls=%async_computation.4 | async-start | bytes 524288 | tf_op jit(solution)/shard_map/all_to_all | solution.py:291
  215.2 40.5 %collective-permute-start.15 = (bf16[2,192,768]{2,1,0:T(8,128)(2,1)}, bf16[2,192,768]{2,1,0:T(8,128)(2,1)}, u32[]{:S(2)}, u32[]{:S(2)}) collective-permute-start(bf16[2,192,768]{2,1,0:T(8,128)(2,1)} %pad_maximum_fusion.5), channel_id=1, source_target_pairs={{0,8},{8,0},{16,24},{24,16},{1,9},{9,1},{17,25},{25,17},{2,10},{10... | collective-permute-start | bytes 1769480 | tf_op jit(solution)/shard_map/ppermute | solution.py:283
  253.1 20.4 %all-to-all-start.6 = ((bf16[32,24,256]{2,1,0:T(8,128)(2,1)}), bf16[32,24,256]{2,1,0:T(8,128)(2,1)S(1)}, u32[]{:S(2)}, u32[]{:S(2)}) async-start(bf16[32,24,256]{2,1,0:T(8,128)(2,1)} %fusion.13), calls=%async_computation.6 | async-start | bytes 786432 | tf_op jit(solution)/shard_map/all_to_all | solution.py:291
  256.9 11.4 %collective-permute-start.16 = (bf16[192,768]{1,0:T(8,128)(2,1)S(1)}, bf16[192,768]{1,0:T(8,128)(2,1)S(1)}, u32[]{:S(2)}, u32[]{:S(2)}) collective-permute-start(bf16[192,768]{1,0:T(8,128)(2,1)S(1)} %fusion.27), channel_id=1, source_target_pairs={{0,16},{16,0},{8,24},{24,8},{1,17},{17,1},{9,25},{25,9},{2,18},{18... | collective-permute-start | bytes 884744 | tf_op jit(solution)/shard_map/ppermute | solution.py:287
  289.2 24.6 %all-to-all-start.5 = ((bf16[32,96,128]{2,1,0:T(8,128)(2,1)}), bf16[32,96,128]{2,1,0:T(8,128)(2,1)S(1)}, u32[]{:S(2)}, u32[]{:S(2)}) async-start(bf16[32,96,128]{2,1,0:T(8,128)(2,1)} %get-tuple-element.29), calls=%async_computation.5 | async-start | bytes 1572864 | tf_op jit(solution)/shard_map/all_to_all | solution.py:291
  323.7 3.7 %collective-permute-start.17 = (bf16[24,768]{1,0:T(8,128)(2,1)S(1)}, bf16[24,768]{1,0:T(8,128)(2,1)S(1)}, u32[]{:S(2)}, u32[]{:S(2)}) collective-permute-start(bf16[24,768]{1,0:T(8,128)(2,1)S(1)} %get-tuple-element.112), channel_id=1, source_target_pairs={{0,24},{8,16},{16,8},{24,0},{1,25},{9,17},{17,9},{25,1},{2,26},{10... | collective-permute-start | bytes 110600 | tf_op jit(solution)/shard_map/ppermute | solution.py:328
  324.2 4.0 %collective-permute-start.18 = (bf16[24,768]{1,0:T(8,128)(2,1)S(1)}, bf16[24,768]{1,0:T(8,128)(2,1)S(1)}, u32[]{:S(2)}, u32[]{:S(2)}) collective-permute-start(bf16[24,768]{1,0:T(8,128)(2,1)S(1)} %get-tuple-element.111), channel_id=1, source_target_pairs={{0,16},{16,0},{8,24},{24,8},{1,17},{17,1},{9,25},{25,9},{2,18},{18... | collective-permute-start | bytes 110600 | tf_op jit(solution)/shard_map/ppermute | solution.py:287
  325.1 3.1 collective-permute-start.19
  (33 other events, 74.7 us)
Sparse Core Ops, SparseCore 0:
  16.1 74.1 all-gather.4
  93.3 60.4 all-gather.6
  202.3 76.9 reduce-scatter.1

commit v4 on v3

--- a/solution.py
+++ b/solution.py
@@ -56,35 +56,55 @@
 
 
 def project_kernel(
-    place_ref, a_ref, b_ref, w_ref, bias_ref, q_ref, k_ref, v_ref, kt_ref, vt_ref, *, halves, per
+    place_ref, a_ref, b_ref, qk_ref, v_w_ref, bias_ref, q_ref, k_ref, v_ref, kt_ref, vt_ref, *, halves, per
 ):
     tokens = a_ref.shape[1] // 2
+    hd = q_ref.shape[1]
 
     def visit(source, load, position):
         x = load((a_ref, b_ref)[source])
         rows = pl.ds(position, per * tokens)
-        for n, ref in enumerate((q_ref, k_ref, v_ref)):
-            y = dot(x, w_ref[n], NN) + bias_ref[n]
-            ref[rows, :] = y.astype(BF)
-            if n:
-                (kt_ref, vt_ref)[n - 1][:, rows] = y.T.astype(BF)
+        qk = dot(x, qk_ref[...], NN) + bias_ref[0:1]
+        v = (dot(x, v_w_ref[...], NN) + bias_ref[1:2])[:, :hd]
+        k = qk[:, hd:]
+        q_ref[rows, :] = qk[:, :hd].astype(BF)
+        k_ref[rows, :] = k.astype(BF)
+        v_ref[rows, :] = v.astype(BF)
+        kt_ref[:, rows] = k.T.astype(BF)
+        vt_ref[:, rows] = v.T.astype(BF)
 
     chunk_walk(place_ref, a_ref.shape[0], halves, per, tokens, visit)
 
 
-def project(place, a, b, w, bias, halves, per):
+def project(place, a, b, qk, v, bias, halves, per):
     length = 2 * a.shape[0] * a.shape[1]
-    hd = w.shape[2]
+    hd = qk.shape[1] // 2
     rows = jax.ShapeDtypeStruct((length, hd), BF)
     columns = jax.ShapeDtypeStruct((hd, length), BF)
     return pl.pallas_call(
         functools.partial(project_kernel, halves=halves, per=per),
         out_shape=(rows, rows, rows, columns, columns),
-        in_specs=[SMEM] + [VMEM] * 4,
+        in_specs=[SMEM] + [VMEM] * 5,
         out_specs=(VMEM,) * 5,
         compiler_params=PARAMS,
+        cost_estimate=pl.CostEstimate(flops=5000000000, bytes_accessed=4 << 20, transcendentals=0),
         name="project",
-    )(place, a, b, w, bias)
+    )(place, a, b, qk, v, bias)
+
+
+def head_slots_kernel(w_ref, small_ref, out_ref, *, units):
+    hd = small_ref.shape[1]
+    small = small_ref[...]
+    done = {}
+    for d, j in enumerate(units):
+        if j not in done:
+            part = [w_ref[c][:, j * hd : (j + 1) * hd] for c in range(3)]
+            done[j] = [
+                jnp.concatenate(part[:2], axis=1),
+                jnp.concatenate([part[2], small], axis=1),
+            ]
+        out_ref[d, 0] = done[j][0]
+        out_ref[d, 1] = done[j][1]
 
 
 def weight_grad_kernel(place_ref, a_ref, b_ref, gt_ref, out_ref, acc_ref, *, halves, per):
@@ -108,6 +128,7 @@
         out_specs=VMEM,
         scratch_shapes=[pltpu.VMEM((gt.shape[0], depth), F32)],
         compiler_params=PARAMS,
+        cost_estimate=pl.CostEstimate(flops=3000000000, bytes_accessed=4 << 20, transcendentals=0),
         name="weight_grad",
     )(place, a, b, gt)
 
@@ -177,6 +198,7 @@
         out_specs=(VMEM,) * 3,
         scratch_shapes=[pltpu.VMEM((length, bq), F32)],
         compiler_params=PARAMS,
+        cost_estimate=pl.CostEstimate(flops=10000000000, bytes_accessed=4 << 20, transcendentals=0),
         name="attend",
     )(lo, hi, q, k, vt, spans)
 
@@ -258,8 +280,164 @@
             pltpu.VMEM((length, hd), F32),
         ],
         compiler_params=PARAMS,
+        cost_estimate=pl.CostEstimate(flops=14000000000, bytes_accessed=4 << 20, transcendentals=0),
         name="attend_back",
     )(lo, hi, q, k, v, kt, ot, lse, do, spans)
+
+
+def call(kernel, outs, ins, name, flops, scratch=()):
+    return pl.pallas_call(
+        kernel,
+        out_shape=tuple(jax.ShapeDtypeStruct(shape, kind) for shape, kind in outs),
+        in_specs=[SMEM if v.dtype == jnp.int32 else VMEM for v in ins],
+        out_specs=(VMEM,) * len(outs),
+        scratch_shapes=list(scratch),
+        compiler_params=PARAMS,
+        cost_estimate=pl.CostEstimate(
+            flops=int(flops), bytes_accessed=2 << 20, transcendentals=0
+        ),
+        name=name,
+    )(*ins)
+
+
+def column_sums(*values):
+    sums = [jnp.sum(v, axis=0, keepdims=True) for v in values]
+    return jnp.concatenate(sums + [jnp.zeros_like(sums[0])] * (8 - len(sums)), axis=0)
+
+
+def unpack_heads(slots_ref, out_ref, layout, piece_rows, which):
+    groups, micro, halves, heads_dev = layout
+    hd = slots_ref.shape[2] // 2
+    part = slice(which * piece_rows, (which + 1) * piece_rows)
+    for m in range(micro):
+        rows = slice(m * 2 * piece_rows, (m + 1) * 2 * piece_rows)
+        pieces = []
+        for j in range(groups * heads_dev):
+            piece = slots_ref[((j // heads_dev) * micro + m) * halves + j % heads_dev, part, :]
+            pieces.append(jnp.concatenate([piece[:, :hd], piece[:, hd:]], axis=0))
+        for j in range(0, groups * heads_dev, 2):
+            out_ref[rows, j * hd : (j + 2) * hd] = jnp.concatenate(pieces[j : j + 2], axis=1)
+
+
+def branch_kernel(slots_ref, x_ref, w_ref, vec_ref, attn_ref, low_ref, normed_ref, inv_ref, *, layout):
+    unpack_heads(slots_ref, attn_ref, layout, slots_ref.shape[1], 0)
+    first_sum = x_ref[...].astype(F32) + dot(attn_ref[...], w_ref[...], NN) + vec_ref[0:1]
+    normed, inverse = normalise(first_sum)
+    normed_ref[...] = normed
+    inv_ref[...] = inverse
+    low_ref[...] = (normed * vec_ref[1:2] + vec_ref[2:3]).astype(BF)
+
+
+def normal_cdf(v):
+    bell = jnp.exp(-0.5 * v * v)
+    t = 1.0 / (1.0 + (0.3275911 * math.sqrt(0.5)) * jnp.abs(v))
+    tail = 0.5 * 1.061405429
+    for c in (-1.453152027, 1.421413741, -0.284496736, 0.254829592):
+        tail = tail * t + 0.5 * c
+    tail = tail * t * bell
+    return jnp.where(v < 0.0, tail, 1.0 - tail), bell * (1.0 / math.sqrt(2.0 * math.pi))
+
+
+def inner_kernel(a_ref, b_ref, c_ref, d_ref, wi_ref, wo_ref, bias_ref, act_ref, slope_ref, low_ref, keep_ref, send_ref):
+    count = a_ref.shape[0]
+    for n, ref in enumerate((a_ref, b_ref, c_ref, d_ref)):
+        rows = slice(n * count, (n + 1) * count)
+        x = ref[...]
+        low_ref[rows, :] = x
+        pre = dot(x, wi_ref[...], NN) + bias_ref[...]
+        cdf, bell = normal_cdf(pre)
+        slope_ref[rows, :] = cdf + pre * bell
+        act = (pre * cdf).astype(BF)
+        act_ref[rows, :] = act
+        partial = dot(act, wo_ref[...], NN)
+        if n < 2:
+            keep_ref[rows, :] = partial
+        else:
+            send_ref[(n - 2) * count : (n - 1) * count, :] = partial.astype(BF)
+
+
+def inner_back_kernel(a_ref, b_ref, c_ref, d_ref, wi_ref, wo_ref, slope_ref, inner_ref, low_ref, sums_ref, keep_ref, send_ref):
+    count = a_ref.shape[0]
+    sums = 0.0
+    for n, ref in enumerate((a_ref, b_ref, c_ref, d_ref)):
+        rows = slice(n * count, (n + 1) * count)
+        x = ref[...]
+        low_ref[rows, :] = x
+        inner = (dot(x, wo_ref[...], NT) * slope_ref[rows, :]).astype(BF)
+        inner_ref[rows, :] = inner
+        sums = sums + jnp.sum(inner.astype(F32), axis=0, keepdims=True)
+        partial = dot(inner, wi_ref[...], NT)
+        if n < 2:
+            keep_ref[rows, :] = partial
+        else:
+            send_ref[(n - 2) * count : (n - 1) * count, :] = partial.astype(BF)
+    sums_ref[...] = sums
+
+
+def feed_grad_kernel(low_ref, inner_ref, act_ref, ffn_ref, out_ref, acc_ref):
+    cycle, blocks, rows = out_ref.shape[:3]
+    half = blocks // 2
+    acc_ref[...] = dot(low_ref[...], inner_ref[...], TN)
+    for b in range(cycle):
+        for h in range(half):
+            first = (h * cycle + b) * rows
+            out_ref[b, h] = acc_ref[first : first + rows, :].astype(BF)
+    acc_ref[...] = dot(act_ref[...], ffn_ref[...], TN)
+    for b in range(cycle):
+        for h in range(half):
+            first = (b * half + h) * rows
+            out_ref[b, half + h] = acc_ref[first : first + rows, :].astype(BF)
+
+
+def add_kernel(keep_ref, got_ref, own_ref, send_ref):
+    count = own_ref.shape[0]
+    own_ref[...] = keep_ref[:count] + got_ref[:count].astype(F32)
+    send_ref[...] = (keep_ref[count:] + got_ref[count:].astype(F32)).astype(BF)
+
+
+def output_kernel(own_ref, got_ref, normed_ref, grad_ref, vec_ref, out_ref, second_ref, low_ref, sums_ref):
+    first_normed = normed_ref[...] * vec_ref[0:1] + vec_ref[1:2]
+    second_sum = first_normed + own_ref[...] + got_ref[...].astype(F32) + vec_ref[2:3]
+    normed, inverse = normalise(second_sum)
+    out_ref[...] = (normed * vec_ref[3:4] + vec_ref[4:5]).astype(BF)
+    grad = grad_ref[...].astype(F32)
+    d_second = norm_back(grad, normed, inverse, vec_ref[3:4])
+    low = d_second.astype(BF)
+    second_ref[...] = d_second
+    low_ref[...] = low
+    sums_ref[...] = column_sums(grad * normed, grad, low.astype(F32))
+
+
+def branch_back_kernel(own_ref, got_ref, second_ref, normed_ref, inv_ref, w_ref, vec_ref, first_ref, low_ref, sums_ref, slots_ref, *, layout):
+    groups, micro, halves, heads_dev = layout
+    grad = own_ref[...] + got_ref[...].astype(F32) + second_ref[...]
+    normed = normed_ref[...]
+    d_first = norm_back(grad, normed, inv_ref[...], vec_ref[0:1])
+    low = d_first.astype(BF)
+    first_ref[...] = d_first
+    low_ref[...] = low
+    sums_ref[...] = column_sums(grad * normed, grad, low.astype(F32))
+    d_attn = dot(low, w_ref[...], NT).astype(BF)
+    half = slots_ref.shape[1]
+    hd = slots_ref.shape[2] // 2
+    for m in range(micro):
+        for j in range(groups * heads_dev):
+            piece = d_attn[m * 2 * half : (m + 1) * 2 * half, j * hd : (j + 1) * hd]
+            piece = jnp.concatenate([piece[:half], piece[half:]], axis=1)
+            first = ((j // heads_dev) * micro + m) * halves
+            slots_ref[first + j % heads_dev] = piece
+            if j % heads_dev == heads_dev - 1:
+                for b in range(heads_dev, halves):
+                    slots_ref[first + b] = piece
+
+
+def tokens_kernel(slots_ref, w_ref, first_ref, out_ref, d_ref, *, layout):
+    piece_rows = slots_ref.shape[1] // 3
+    total = first_ref[...]
+    for c in range(3):
+        unpack_heads(slots_ref, d_ref.at[c], layout, piece_rows, c)
+        total = total + dot(d_ref[c], w_ref[c], NT)
+    out_ref[...] = total.astype(BF)
 
 
 def normalise(hidden):
@@ -271,12 +449,15 @@
 
 def norm_back(grad, normed, inverse, gain):
     e = grad * gain
-    dh = inverse * (
+    return inverse * (
         e
         - jnp.mean(e, axis=-1, keepdims=True)
         - normed * jnp.mean(e * normed, axis=-1, keepdims=True)
     )
-    return dh, jnp.sum(grad * normed, axis=0), jnp.sum(grad, axis=0)
+
+
+def after(value, *others):
+    return lax.optimization_barrier((value, *others))[0]
 
 
 def by_core(value):
@@ -298,19 +479,25 @@
 
 
 def gather_group(rows):
-    pair = jnp.concatenate([rows[None], by_x(rows)[None]])
-    return jnp.concatenate([pair, by_core(pair)]).reshape(4 * rows.shape[0], rows.shape[1])
-
-
-def reduce_group(partial, count):
-    parts = partial.reshape(4, count, -1)
-    kept = parts[:2] + by_core(parts[2:].astype(BF)).astype(F32)
-    return kept[0] + by_x(kept[1].astype(BF)).astype(F32)
+    across_x = by_x(rows)
+    return rows, across_x, by_core(rows), by_core(across_x)
+
+
+def reduce_group(keep, send):
+    count, depth = keep.shape[0] // 2, keep.shape[1]
+    shape = (count, depth)
+    own, send = call(add_kernel, ((shape, F32), (shape, BF)), (keep, by_core(send)), "add", 1e9)
+    return own, by_x(send)
+
+
+def stack_rows(*values):
+    blank = jnp.zeros_like(values[0])
+    return jnp.stack([*values, *[blank] * (8 - len(values))])
 
 
 def in_order(blocks):
     index = lax.axis_index("head")
-    own, across_x, across_core, across = [blocks[i] for i in range(4)]
+    own, across_x, across_core, across = blocks
     odd, far = index % 2 == 1, index // 2 == 1
     near = [jnp.where(odd, q, p) for p, q in ((own, across_core), (across_core, own))]
     wide = [jnp.where(odd, q, p) for p, q in ((across_x, across), (across, across_x))]
@@ -326,7 +513,7 @@
         return lax.dynamic_index_in_dim(blocks, index ^ offset, 0, keepdims=False)
 
     across = lax.ppermute(block(3), "head", [(i, i ^ 3) for i in range(4)])
-    return in_order(jnp.stack([block(0), by_x(block(2)), by_core(block(1)), across]))
+    return in_order((block(0), by_x(block(2)), by_core(block(1)), across))
 
 
 def key_ranges(spans, bq, bk):
@@ -372,56 +559,38 @@
         for c in range(2)
         for s in range(2)
     ]
-    tokens_a = spread_over(pair_x, BOTH, cycle, cube)
+    vectors = [bias_rows.T, norm_gains.T, norm_shifts.T, inner_bias.reshape(rows_dev, -1)]
+    small = jnp.concatenate(vectors, axis=1)
+    small = jnp.pad(small, ((0, 0), (0, hd - small.shape[1])))
+    units = tuple(h * heads_dev + u for h in range(groups) for u in unit_of * 2)
+    (slots,) = call(
+        functools.partial(head_slots_kernel, units=units),
+        (((devices, 2, rows_dev, 2 * hd), BF),),
+        (qkv_weight, small),
+        "head_slots",
+        1e9,
+    )
+    slots = swap(after(slots, pair_x), BOTH)
+    qk_weight = slots[:, 0].reshape(depth, 2 * hd)
+    v_weight = slots[:, 1].reshape(depth, 2 * hd)
+    small = slots[:, 1, :, hd : hd + 12].astype(F32).reshape(depth, 12).T
+
+    bias, gains, shifts = small[0:4], small[4:6], small[6:8]
+    inner_bias_all = small[8:12].T.reshape(groups, ff_part)
+    inner_bias_part = lax.dynamic_index_in_dim(inner_bias_all, head_index, 0, keepdims=False)
+    unit_bias = lax.dynamic_slice(bias[0:2], (0, unit_head * hd), (2, hd))
+    unit_bias = jnp.pad(unit_bias, ((0, 0), (0, hd)))
+
+    inner_own = inner_weight.reshape(rows_dev, groups, ff_part)
+    inner_own = to_group(inner_own.transpose(1, 0, 2)).reshape(groups * rows_dev, ff_part)
+    ffn = jnp.concatenate([inner_own, outer_weight, out_weight])
+    qkv_weight = after(qkv_weight, ffn)
+    ffn_all = lax.all_gather(ffn, "blk", axis=0, tiled=False)
+    qkv_all = lax.all_gather(qkv_weight, BOTH, axis=0, tiled=False)
+    tokens_a, qk_weight, v_weight, unit_bias = lax.optimization_barrier(
+        (spread_over(pair_x, BOTH, cycle, cube), qk_weight, v_weight, unit_bias)
+    )
     tokens_b = by_core(tokens_a)
-
-    weights = qkv_weight.reshape(3, rows_dev, groups, heads_dev, hd).transpose(2, 3, 1, 0, 4)
-    weights = weights.reshape(groups, heads_dev, rows_dev * 3 * hd)
-    small = jnp.concatenate(
-        [bias_rows.reshape(-1), norm_gains.reshape(-1), norm_shifts.reshape(-1), inner_bias]
-    )
-    weight_size = weights.shape[2]
-    pad = -(weight_size + small.shape[0]) % (2 * hd)
-    small = jnp.pad(small, (0, pad))
-    slots = jnp.stack([weights[:, u] for u in unit_of * 2], axis=1)
-    slots = jnp.concatenate(
-        [slots, jnp.broadcast_to(small, (groups, cycle, small.shape[0]))], axis=2
-    ).reshape(devices, -1, 2 * hd)
-    slots = swap(slots, BOTH).reshape(devices, -1)
-    unit_weight = (
-        slots[:, :weight_size].reshape(depth, 3, hd).transpose(1, 0, 2)
-    )
-    small = slots[:, weight_size:].astype(F32)
-
-    def column(first, count):
-        part = small[:, first * rows_dev : (first + count) * rows_dev]
-        return part.reshape(devices, count, rows_dev).transpose(1, 0, 2).reshape(count, depth)
-
-    bias, gains, shifts = column(0, 4), column(4, 2), column(6, 2)
-    inner_bias_all = small[:, 8 * rows_dev : 8 * rows_dev + ff_dev].reshape(groups, ff_part)
-    inner_bias_part = lax.dynamic_index_in_dim(inner_bias_all, head_index, 0, keepdims=False)
-    unit_bias = jnp.stack([bias[0], jnp.zeros_like(bias[0]), bias[1]]).reshape(3, HEADS, hd)
-    unit_bias = lax.dynamic_index_in_dim(unit_bias, unit_head, 1, keepdims=True)
-
-    inner_own = to_group(inner_weight.reshape(rows_dev, groups, ff_part).transpose(1, 0, 2))
-    ffn = lax.all_gather(
-        jnp.concatenate([inner_own.reshape(groups * rows_dev, ff_part), outer_weight]),
-        "blk",
-        axis=0,
-        tiled=False,
-    )
-    inner_part = (
-        ffn[:, : groups * rows_dev]
-        .reshape(cycle, groups, rows_dev, ff_part)
-        .transpose(1, 0, 2, 3)
-        .reshape(depth, ff_part)
-    )
-    outer_part = ffn[:, groups * rows_dev :].reshape(ff_part, depth)
-    out_part = spread_over(out_weight, "blk", cycle).reshape(depth // groups, depth)
-    out_all = in_order(gather_group(out_part).reshape(groups, depth // groups, depth)).reshape(
-        depth, depth
-    )
-    qkv_all = lax.all_gather(qkv_weight, BOTH, axis=0, tiled=False)
 
     lengths = lax.dynamic_index_in_dim(doc_lengths, half, 0, keepdims=False)
     order = jnp.arange(lengths.shape[0], dtype=jnp.int32)
@@ -438,62 +607,92 @@
 
     place = jnp.stack([head_index % 2, half]).astype(jnp.int32)
     per = max(1, 256 // tokens)
-    q, k, v, kt, vt = project(place, tokens_a, tokens_b, unit_weight, unit_bias, halves, per)
+    q, k, v, kt, vt = project(
+        place, tokens_a, tokens_b, qk_weight, v_weight, unit_bias, halves, per
+    )
     block = 512 if length <= 4096 else 256
     lo, hi = key_ranges(spans, block, 512)
     attn_out, attn_t, lse = attend(lo, hi, q, k, vt, spans, tokens, block, 512)
 
+    ffn = after(ffn_all, attn_out)
+    inner_part = (
+        ffn[:, : groups * rows_dev]
+        .reshape(cycle, groups, rows_dev, ff_part)
+        .transpose(1, 0, 2, 3)
+        .reshape(depth, ff_part)
+    )
+    first, last = groups * rows_dev, groups * rows_dev + ff_dev
+    outer_part = ffn[:, first:last].reshape(ff_part, depth)
+    out_part = ffn[:, last:].reshape(depth // groups, depth)
+    out_all = in_order(gather_group(out_part)).reshape(depth, depth)
+
     rows = micro * tokens
-    attn = (
-        swap(attn_out, BOTH)
-        .reshape(groups, micro, halves, half_tokens, 2, hd)[:, :, :heads_dev]
-        .transpose(1, 4, 3, 0, 2, 5)
-        .reshape(rows, depth)
-    )
-    first_sum = (
-        inputs.reshape(rows, depth).astype(F32)
-        + dot(attn, out_all, NN)
-        + bias[2]
-    )
-    normed_one, inverse_one = normalise(first_sum)
-    first_normed = normed_one * gains[0] + shifts[0]
-    normed_low = gather_group(first_normed.astype(BF))
-    inner_pre = dot(normed_low, inner_part, NN) + inner_bias_part
-    cdf = 0.5 * (1.0 + lax.erf(inner_pre * (1.0 / math.sqrt(2.0))))
-    slope = cdf + inner_pre * jnp.exp(-0.5 * inner_pre * inner_pre) * (1.0 / math.sqrt(2.0 * math.pi))
-    act_low = (inner_pre * cdf).astype(BF)
-    second_sum = first_normed + reduce_group(dot(act_low, outer_part, NN), rows) + bias[3]
-    normed_two, inverse_two = normalise(second_sum)
-    output = (normed_two * gains[1] + shifts[1]).astype(BF).reshape(inputs.shape)
-
-    d_second, gain_two, shift_two = norm_back(
-        grad_out.reshape(rows, depth).astype(F32), normed_two, inverse_two, gains[1]
-    )
-    d_ffn = d_second.astype(BF)
-    d_ffn_group = gather_group(d_ffn)
-    d_inner = (dot(d_ffn_group, outer_part, NT) * slope).astype(BF)
-    d_first_normed = d_second + reduce_group(dot(d_inner, inner_part, NT), rows)
-    d_first, gain_one, shift_one = norm_back(d_first_normed, normed_one, inverse_one, gains[0])
-    d_branch = d_first.astype(BF)
-    d_attn = dot(d_branch, out_all, NT).astype(BF)
-    d_heads = d_attn.reshape(micro, 2, half_tokens, groups, heads_dev, hd).transpose(3, 0, 4, 2, 1, 5)
-    d_heads = d_heads.reshape(groups, micro, heads_dev, half_tokens, 2 * hd)
-    d_heads = jnp.stack([d_heads[:, :, u] for u in unit_of], axis=2)
-    d_heads = swap(d_heads.reshape(devices, half_tokens, 2 * hd), BOTH)
-
-    outer_grad = dot(act_low, d_ffn_group, TN).astype(BF).reshape(cycle, ff_dev, depth)
-    inner_grad = (
-        dot(normed_low, d_inner, TN)
-        .astype(BF)
-        .reshape(groups, cycle, rows_dev, ff_part)
-        .transpose(1, 0, 2, 3)
-        .reshape(cycle, groups * rows_dev, ff_part)
-    )
-    ffn_grad = lax.psum_scatter(
-        jnp.concatenate([inner_grad, outer_grad], axis=1), "blk", scatter_dimension=0, tiled=False
-    )
-    outer_grad = ffn_grad[groups * rows_dev :].astype(F32)
-    inner_grad = to_group(ffn_grad[: groups * rows_dev].reshape(groups, rows_dev, ff_part))
+    layout = (groups, micro, halves, heads_dev)
+    flat, group = (rows, depth), (groups * rows, ff_part)
+    attn, normed_low, normed_one, inverse_one = call(
+        functools.partial(branch_kernel, layout=layout),
+        ((flat, BF), (flat, BF), (flat, F32), ((rows, 1), F32)),
+        (swap(attn_out, BOTH), inputs.reshape(flat), out_all, stack_rows(bias[2], gains[0], shifts[0])),
+        "branch",
+        2e9,
+    )
+    act_low, slope, normed_group, keep, send = call(
+        inner_kernel,
+        ((group, BF), (group, F32), ((groups * rows, depth), BF), ((2 * rows, depth), F32), ((2 * rows, depth), BF)),
+        (*gather_group(normed_low), inner_part, outer_part, inner_bias_part[None]),
+        "inner",
+        4e9,
+    )
+    output, d_second, d_ffn, sums_two = call(
+        output_kernel,
+        ((flat, BF), (flat, F32), (flat, BF), ((8, depth), F32)),
+        (
+            *reduce_group(keep, send),
+            normed_one,
+            grad_out.reshape(flat),
+            stack_rows(gains[0], shifts[0], bias[3], gains[1], shifts[1]),
+        ),
+        "output",
+        2e9,
+    )
+    output = output.reshape(inputs.shape)
+    d_inner, d_ffn_group, inner_sums, keep, send = call(
+        inner_back_kernel,
+        ((group, BF), ((groups * rows, depth), BF), ((1, ff_part), F32), ((2 * rows, depth), F32), ((2 * rows, depth), BF)),
+        (*gather_group(d_ffn), inner_part, outer_part, slope),
+        "inner_back",
+        4e9,
+    )
+    own, got = reduce_group(keep, send)
+    (ffn_grad,) = call(
+        feed_grad_kernel,
+        (((cycle, 2 * groups, rows_dev, depth), BF),),
+        (normed_group, d_inner, act_low, d_ffn_group),
+        "feed_grad",
+        4e9,
+        [pltpu.VMEM((depth, depth), F32)],
+    )
+    got, ffn_grad = lax.optimization_barrier((got, ffn_grad))
+    d_first, d_branch, sums_one, d_heads = call(
+        functools.partial(branch_back_kernel, layout=layout),
+        ((flat, F32), (flat, BF), ((8, depth), F32), ((devices, half_tokens, 2 * hd), BF)),
+        (
+            own,
+            got,
+            d_second,
+            normed_one,
+            inverse_one,
+            out_all,
+            stack_rows(gains[0]),
+        ),
+        "branch_back",
+        2e9,
+    )
+    d_heads = swap(d_heads, BOTH)
+
+    ffn_grad = lax.psum_scatter(ffn_grad, "blk", scatter_dimension=0, tiled=False).astype(F32)
+    outer_grad = ffn_grad[groups:].reshape(ff_dev, depth)
+    inner_grad = to_group(ffn_grad[:groups].astype(BF))
     inner_grad = inner_grad.transpose(1, 0, 2).reshape(rows_dev, groups * ff_part).astype(F32)
     out_grad = dot(attn, d_branch, TN).reshape(groups, depth // groups, depth)
 
@@ -503,34 +702,33 @@
     from_core = by_core(jnp.stack([out_block(1), out_block(3)]).astype(BF)).astype(F32)
     from_x = by_x((out_block(2) + from_core[1]).astype(BF)).astype(F32)
     out_grad = (out_block(0) + from_core[0] + from_x).astype(BF)
+    out_terms = swap(out_grad.reshape(cycle, rows_dev, depth), "blk")
     out_grad = jnp.sum(
-        swap(out_grad.reshape(cycle, rows_dev, depth), "blk").astype(F32), axis=0
+        out_terms.astype(F32), axis=0
     )
 
     lo, hi = key_ranges(spans, 512, 256)
     qkv_out, qkv_t, qv_sums = attend_back(
         lo, hi, q, k, v, kt, attn_t, lse, d_heads, spans, tokens, 512, 256
     )
-    d_qkv = (
-        swap(qkv_out, BOTH)
-        .reshape(groups, micro, halves, 3, half_tokens, 2, hd)[:, :, :heads_dev]
-        .transpose(3, 1, 5, 4, 0, 2, 6)
-        .reshape(3, rows, depth)
-    )
+    qkv_home = swap(after(qkv_out, out_terms), BOTH)
     qkv_all = qkv_all.transpose(1, 0, 2, 3).reshape(3, depth, depth)
-    d_tokens = d_first
-    for c in range(3):
-        d_tokens = d_tokens + dot(d_qkv[c], qkv_all[c], NT)
-    grad_inputs = d_tokens.astype(BF).reshape(inputs.shape)
+    (grad_inputs,) = call(
+        functools.partial(tokens_kernel, layout=layout),
+        ((flat, BF),),
+        (qkv_home, qkv_all, d_first),
+        "tokens",
+        3e9,
+        [pltpu.VMEM((3, rows, depth), BF)],
+    )
+    grad_inputs = grad_inputs.reshape(inputs.shape)
 
     unit_grad = weight_grad(place, tokens_a, tokens_b, qkv_t, halves, per)
-    ones = [gain_one, gain_two, shift_one, shift_two]
-    ones += [jnp.sum(d.astype(F32), axis=0) for d in (d_branch, d_ffn)]
     wide = jnp.zeros((2, HEADS, hd), F32)
     wide = lax.dynamic_update_slice(wide, qv_sums.reshape(2, 1, hd), (0, unit_head, 0))
     wide = jnp.where((blk_index % halves < heads_dev), wide, 0.0)
-    sums = jnp.concatenate([jnp.stack(ones), wide.reshape(2, depth)]).T
-    inner_sums = jnp.sum(d_inner.astype(F32), axis=0).reshape(1, cycle, rows_dev, ff_dev // rows_dev)
+    sums = jnp.concatenate([sums_one[:3], sums_two[:3], wide.reshape(2, depth)]).T
+    inner_sums = inner_sums.reshape(1, cycle, rows_dev, ff_dev // rows_dev)
     inner_sums = jnp.broadcast_to(inner_sums, (groups, *inner_sums.shape[1:]))
     extra = jnp.concatenate(
         [
@@ -540,9 +738,8 @@
         axis=2,
     ).astype(BF)
     extra = jnp.pad(extra, ((0, 0), (0, 0), (0, hd - extra.shape[2])))
-    final = swap(
-        jnp.concatenate([unit_grad.reshape(devices, rows_dev, 3 * hd), extra], axis=2), BOTH
-    ).astype(F32)
+    final = jnp.concatenate([unit_grad.reshape(devices, rows_dev, 3 * hd), extra], axis=2)
+    final = swap(after(final, qkv_home), BOTH).astype(F32)
     qkv_grad = jnp.sum(
         final[:, :, : 3 * hd].reshape(groups, micro, halves, rows_dev, 3, hd)[:, :, :heads_dev], axis=1
     )
@@ -560,10 +757,10 @@
         out_grad,
         inner_grad,
         outer_grad,
-        jnp.stack([sums[6], sums[7], sums[4], sums[5]]),
+        jnp.stack([sums[6], sums[7], sums[2], sums[5]]),
         inner_bias_grad,
-        sums[0:2],
-        sums[2:4],
+        jnp.stack([sums[0], sums[3]]),
+        jnp.stack([sums[1], sums[4]]),
     )
 
 

time: 337 us -> 297 us (0.88)
  Pallas kernels: 35.9 us -> 71.1 us
  local copies, waits for them, and re-layouts: 56 us -> 28.3 us
  blocking collectives: 15.6 us -> 0 us
  other arithmetic: 29 us -> 14.1 us
  matrix products: 11.8 us -> 1.41 us
  waiting for transfers between devices: 132 us -> 128 us
    pallas_call x0 -> x10, Pallas kernels: none -> 36.1 us  [call(): pl.pallas_call(kernel, out_shape=tuple((jax.ShapeDtypeStruct(shape, kind)...]
    ppermute x1, waiting for transfers between devices: 20.3 us -> 0.01 us  [local(): lax.ppermute(other_x, 'blk', [(i, (i + halves) % cycle) for i in range(cy...]
    all_to_all x1 -> x0, blocking collectives: 15.6 us -> none  [swap(): lax.all_to_all(value, axes, split_axis=0, concat_axis=0, tiled=True, axis...]
    slice x22 -> x14, local copies, waits for them, and re-layouts: 20 us -> 6.03 us  [the longest x1 1.19 us: local(): outer_part = ffn[:, first:last].reshape(ff_part, depth)]
    dot_general x12 -> x1, matrix products: 11.8 us -> 1.41 us  [dot(): return lax.dot_general(a, b, dims, preferred_element_type=F32)]
    all_to_all x7, waiting for transfers between devices: 71.8 us -> 81.7 us  [swap(): lax.all_to_all(value, axes, split_axis=0, concat_axis=0, tiled=True, axis...]
    reshape x17 -> x5, local copies, waits for them, and re-layouts: 10 us -> 2.59 us  [the longest x1 1.17 us: local(): inner_part = ffn[:, :groups * rows_dev].reshape(cycle, groups, rows_dev,...]
    ppermute x9 -> x12, waiting for transfers between devices: 1.73 us -> 7.37 us  [by_core(): return lax.ppermute(value, 'head', [(0, 1), (1, 0), (2, 3), (3, 2)])]
  transfers between devices with their start and end apart: 30 -> 33, of which waited for: 17 -> 22; matrix products, arithmetic and copies ran while one was open for 27% -> 12% of each run, Pallas kernels for 11% -> 24%
where the time goes in v4:
time: 297 us; the launch traced here: 296 us
  waiting for transfers between devices  128 us (43%)
  Pallas kernels  71.1 us (24%)
  starting transfers between devices  38.8 us (13%)
  local copies, waits for them, and re-layouts  28.3 us (10%)
  between operations  14.4 us (5%)
  other arithmetic  14.1 us (5%)
    all_to_all x7, waiting for transfers between devices, swap(): lax.all_to_all(value, axes, split_axis=0, concat_axis=0, tiled=True, axis...  81.7 us
    pallas_call x10, Pallas kernels, call(): pl.pallas_call(kernel, out_shape=tuple((jax.ShapeDtypeStruct(shape, kind)...  36.1 us
    ppermute x8, waiting for transfers between devices, by_x(): return lax.ppermute(value, 'head', [(0, 2), (2, 0), (1, 3), (3, 1)])  32.1 us
    all_to_all x7, starting transfers between devices, swap(): lax.all_to_all(value, axes, split_axis=0, concat_axis=0, tiled=True, axis...  23.5 us
    pallas_call x1, Pallas kernels, attend_back(): pl.pallas_call(functools.partial(attend_back_kernel, bq=bq, bk=bk, pack=p...  15.2 us
    pallas_call x1, Pallas kernels, attend(): pl.pallas_call(functools.partial(attend_kernel, bq=bq, bk=bk, pack=pack),...  11.1 us
    ppermute x8, starting transfers between devices, by_x(): return lax.ppermute(value, 'head', [(0, 2), (2, 0), (1, 3), (3, 1)])  8.71 us
    ppermute x12, waiting for transfers between devices, by_core(): return lax.ppermute(value, 'head', [(0, 1), (1, 0), (2, 3), (3, 2)])  7.37 us
  transfers between devices with their start and end apart: 33, of which 22 were waited for; matrix products, arithmetic and copies ran while one was open for 12% of the time, Pallas kernels for 24%

profile of v4, /device:TPU:0, one launch (start us, length us, event | category | flops | bytes accessed | tf_op | source)
XLA Modules:
  0.0 295.9 jit_solution(10588439985654130497)
XLA Ops:
  8.2 4.1 %collective-permute-start = (bf16[64,768]{1,0:T(8,128)(2,1)S(1)}, bf16[64,768]{1,0:T(8,128)(2,1)S(1)}, u32[]{:S(2)}, u32[]{:S(2)}) collective-permute-start(bf16[64,768]{1,0:T(8,128)(2,1)S(1)} %get-tuple-element.139), channel_id=1, source_target_pairs={{0,4},{1,5},{2,6},{3,7},{4,0},{5,1},{6,2},{7,3},{8,12},{9,13},{10,... | collective-permute-start | bytes 294920 | tf_op jit(solution)/shard_map/ppermute | solution.py:555
  16.7 1.8 head_slots.1
  18.8 4.2 %all-to-all-start.1 = ((bf16[32,2,24,128]{3,2,1,0:T(8,128)(2,1)}), bf16[32,2,24,128]{3,2,1,0:T(8,128)(2,1)S(1)}, u32[]{:S(2)}, u32[]{:S(2)}) async-start(bf16[32,2,24,128]{3,2,1,0:T(8,128)(2,1)} %head_slots.1), calls=%async_computation.1 | async-start | bytes 786432 | tf_op jit(solution)/shard_map/all_to_all | solution.py:472
  23.9 12.6 %all-to-all-done.1 = bf16[32,2,24,128]{3,2,1,0:T(8,128)(2,1)S(1)} async-done(((bf16[32,2,24,128]{3,2,1,0:T(8,128)(2,1)}), bf16[32,2,24,128]{3,2,1,0:T(8,128)(2,1)S(1)}, u32[]{:S(2)}, u32[]{:S(2)}) %all-to-all-start.1) | async-done | bytes 393248 | tf_op jit(solution)/shard_map/all_to_all | solution.py:472
  36.6 1.3 broadcast_in_dim.58
  37.9 3.6 %all-to-all-start = ((bf16[8,128,768]{2,1,0:T(8,128)(2,1)}), bf16[8,128,768]{2,1,0:T(8,128)(2,1)S(1)}, u32[]{:S(2)}, u32[]{:S(2)}) async-start(bf16[8,128,768]{2,1,0:T(8,128)(2,1)} %broadcast_in_dim.58), calls=%async_computation | async-start | bytes 3145728 | tf_op jit(solution)/shard_map/all_to_all | solution.py:472
  43.3 33.6 %all-to-all-done.a_ref = bf16[8,128,768]{2,1,0:T(8,128)(2,1)S(1)} async-done(((bf16[8,128,768]{2,1,0:T(8,128)(2,1)}), bf16[8,128,768]{2,1,0:T(8,128)(2,1)S(1)}, u32[]{:S(2)}, u32[]{:S(2)}) %all-to-all-start) | async-done | bytes 1572896 | tf_op jit(solution)/shard_map/all_to_all | solution.py:472
  80.4 5.0 %project.1 = (bf16[2048,64]{1,0:T(8,128)(2,1)}, bf16[2048,64]{1,0:T(8,128)(2,1)}, bf16[2048,64]{1,0:T(8,128)(2,1)}, bf16[64,2048]{1,0:T(8,128)(2,1)}, bf16[64,2048]{1,0:T(8,128)(2,1)}) custom-call(s32[2]{0:T(128)} %pad_add_fusion.1.place_ref, bf16[8,128,768]{2,1,0:T(8,128)(2,1)} %copy-done.1, bf16[8,128,768]{2,1,0:T(8,128)(2,1)} %collective-permute-done.1.b_ref, ...), custom_call_target="tpu_custom_call" | custom-call | flops 5000000000 | bytes 4194304 | tf_op jit(solution)/shard_map/project/pallas_call | solution.py:84
  85.4 11.1 %attend.1 = (bf16[32,32,128]{2,1,0:T(8,128)(2,1)}, f32[64,2048]{1,0:T(8,128)}, f32[1,2048]{1,0:T(1,128)}) custom-call(s32[4]{0:T(128)} %get-tuple-element.166.lo_ref, s32[4]{0:T(128)} %get-tuple-element.167.hi_ref, bf16[2048,64]{1,0:T(8,128)(2,1)} %get-tuple-element.63.q_ref, bf16[2048,64]{1,0:T(8,128)(2,1)} %get-tuple-element.64.k_ref, ...), custom_call_target="tpu_custom_call" | custom-call | flops 10000000000 | bytes 4194304 | tf_op jit(solution)/shard_map/attend/pallas_call | solution.py:190
  98.1 9.3 %collective-permute-done.5 = bf16[192,768]{1,0:T(8,128)(2,1)S(1)} collective-permute-done((bf16[192,768]{1,0:T(8,128)(2,1)S(1)}, bf16[192,768]{1,0:T(8,128)(2,1)S(1)}, u32[]{:S(2)}, u32[]{:S(2)}) %collective-permute-start.5) | collective-permute-done | bytes 294944 | tf_op jit(solution)/shard_map/ppermute | solution.py:468
  107.4 2.8 all-to-all-start.2
  112.2 8.5 %all-to-all-done.2.slots_ref = bf16[32,32,128]{2,1,0:T(8,128)(2,1)S(1)} async-done(((bf16[32,32,128]{2,1,0:T(8,128)(2,1)}), bf16[32,32,128]{2,1,0:T(8,128)(2,1)S(1)}, u32[]{:S(2)}, u32[]{:S(2)}) %all-to-all-start.2) | async-done | bytes 262176 | tf_op jit(solution)/shard_map/all_to_all | solution.py:472
  121.4 3.1 %branch.1 = (bf16[128,768]{1,0:T(8,128)(2,1)}, bf16[128,768]{1,0:T(8,128)(2,1)}, f32[128,768]{1,0:T(8,128)}, f32[128,1]{1,0:T(8,128)}) custom-call(bf16[32,32,128]{2,1,0:T(8,128)(2,1)} %copy-done.3, bf16[128,768]{1,0:T(8,128)(2,1)} %bitcast.183, bf16[768,768]{1,0:T(8,128)(2,1)} %bitcast.168, f32[8,768]{1,0:T(8,128)} %stack.104.vec_ref), custom_call_target="tpu_custom_call" | custom-call | flops 2000000000 | bytes 2097152 | tf_op jit(solution)/shard_map/branch/pallas_call | solution.py:289
  126.2 5.1 %collective-permute-done.8.b_ref = bf16[128,768]{1,0:T(8,128)(2,1)S(1)} collective-permute-done((bf16[128,768]{1,0:T(8,128)(2,1)}, bf16[128,768]{1,0:T(8,128)(2,1)S(1)}, u32[]{:S(2)}, u32[]{:S(2)}) %collective-permute-start.8) | collective-permute-done | bytes 196640 | tf_op jit(solution)/shard_map/ppermute | solution.py:468
  131.3 1.2 fusion.20
  134.4 6.1 %inner.1 = (bf16[512,768]{1,0:T(8,128)(2,1)}, f32[512,768]{1,0:T(8,128)}, bf16[512,768]{1,0:T(8,128)(2,1)}, f32[256,768]{1,0:T(8,128)}, bf16[256,768]{1,0:T(8,128)(2,1)}) custom-call(bf16[128,768]{1,0:T(8,128)(2,1)} %get-tuple-element.68.a_ref, bf16[128,768]{1,0:T(8,128)(2,1)} %copy-done.15, bf16[128,768]{1,0:T(8,128)(2,1)} %copy-done.16, ...), custom_call_target="tpu_custom_call" | custom-call | flops 4000000000 | bytes 2097152 | tf_op jit(solution)/shard_map/inner/pallas_call | solution.py:289
  141.0 1.6 collective-permute-done.11.got_ref
  143.3 2.1 add.124
  147.2 5.6 %collective-permute-done.12.got_ref = bf16[128,768]{1,0:T(8,128)(2,1)S(1)} collective-permute-done((bf16[128,768]{1,0:T(8,128)(2,1)}, bf16[128,768]{1,0:T(8,128)(2,1)S(1)}, u32[]{:S(2)}, u32[]{:S(2)}) %collective-permute-start.12) | collective-permute-done | bytes 196640 | tf_op jit(solution)/shard_map/ppermute | solution.py:468
  153.5 2.5 output.1
  156.0 1.2 collective-permute-start.13
  157.2 5.4 %collective-permute-done.13.b_ref = bf16[128,768]{1,0:T(8,128)(2,1)S(1)} collective-permute-done((bf16[128,768]{1,0:T(8,128)(2,1)}, bf16[128,768]{1,0:T(8,128)(2,1)S(1)}, u32[]{:S(2)}, u32[]{:S(2)}) %collective-permute-start.13) | collective-permute-done | bytes 196640 | tf_op jit(solution)/shard_map/ppermute | solution.py:468
  162.6 1.4 collective-permute-done.15.d_ref
  164.7 6.1 %inner_back.1 = (bf16[512,768]{1,0:T(8,128)(2,1)}, bf16[512,768]{1,0:T(8,128)(2,1)}, f32[1,768]{1,0:T(1,128)}, f32[256,768]{1,0:T(8,128)}, bf16[256,768]{1,0:T(8,128)(2,1)}) custom-call(bf16[128,768]{1,0:T(8,128)(2,1)} %get-tuple-element.79.a_ref, bf16[128,768]{1,0:T(8,128)(2,1)} %copy-done.17, bf16[128,768]{1,0:T(8,128)(2,1)} %copy-done.18, ...), custom_call_target="tpu_custom_call" | custom-call | flops 4000000000 | bytes 2097152 | tf_op jit(solution)/shard_map/inner_back/pallas_call | solution.py:289
  173.5 2.1 add.125
  175.6 1.4 collective-permute-start.17
  177.0 4.8 %feed_grad.1 = bf16[8,8,24,768]{3,2,1,0:T(8,128)(2,1)} custom-call(bf16[512,768]{1,0:T(8,128)(2,1)} %get-tuple-element.85.low_ref, bf16[512,768]{1,0:T(8,128)(2,1)} %get-tuple-element.86.inner_ref, bf16[512,768]{1,0:T(8,128)(2,1)} %get-tuple-element.87.act_ref, bf16[512,768]{1,0:T(8,128)(2,1)} %get-tuple-element.88.ffn_ref), custom_call_target="tpu_custom_call" | custom-call | flops 4000000000 | bytes 2097152 | tf_op jit(solution)/shard_map/feed_grad/pallas_call | solution.py:289
  183.4 3.2 %branch_back.1 = (f32[128,768]{1,0:T(8,128)}, bf16[128,768]{1,0:T(8,128)(2,1)}, f32[8,768]{1,0:T(8,128)}, bf16[32,32,128]{2,1,0:T(8,128)(2,1)}) custom-call(f32[128,768]{1,0:T(8,128)} %get-tuple-element.83.own_ref, bf16[128,768]{1,0:T(8,128)(2,1)} %copy-done.19, f32[128,768]{1,0:T(8,128)} %get-tuple-element.90.second_ref, ...), custom_call_target="tpu_custom_call" | custom-call | flops 2000000000 | bytes 2097152 | tf_op jit(solution)/shard_map/branch_back/pallas_call | solution.py:289
  186.6 1.4 fusion.25
  188.2 2.0 collective-permute-done.18
  191.1 1.4 collective-permute-start.19
  192.5 3.3 %all-to-all-start.3 = ((bf16[32,32,128]{2,1,0:T(8,128)(2,1)}), bf16[32,32,128]{2,1,0:T(8,128)(2,1)}, u32[]{:S(2)}, u32[]{:S(2)}) async-start(bf16[32,32,128]{2,1,0:T(8,128)(2,1)} %get-tuple-element.92), calls=%async_computation.3 | async-start | bytes 524288 | tf_op jit(solution)/shard_map/all_to_all | solution.py:472
  196.5 5.2 %collective-permute-done.19 = bf16[192,768]{1,0:T(8,128)(2,1)} collective-permute-done((bf16[192,768]{1,0:T(8,128)(2,1)}, bf16[192,768]{1,0:T(8,128)(2,1)}, u32[]{:S(2)}, u32[]{:S(2)}) %collective-permute-start.19) | collective-permute-done | bytes 294944 | tf_op jit(solution)/shard_map/ppermute | solution.py:468
  201.8 1.8 fusion.4
  203.5 2.9 all-to-all-done.3.do_ref
  206.4 3.4 %all-to-all-start.4 = ((bf16[8,24,768]{2,1,0:T(8,128)(2,1)}), bf16[8,24,768]{2,1,0:T(8,128)(2,1)S(1)}, u32[]{:S(2)}, u32[]{:S(2)}) async-start(bf16[8,24,768]{2,1,0:T(8,128)(2,1)} %bitcast.174), calls=%async_computation.4 | async-start | bytes 589824 | tf_op jit(solution)/shard_map/all_to_all | solution.py:472
  209.9 15.2 %attend_back.1 = (bf16[32,96,128]{2,1,0:T(8,128)(2,1)}, bf16[192,2048]{1,0:T(8,128)(2,1)}, f32[1,128]{1,0:T(1,128)}) custom-call(s32[4]{0:T(128)} %get-tuple-element.165.lo_ref, s32[4]{0:T(128)} %get-tuple-element.168.hi_ref, bf16[2048,64]{1,0:T(8,128)(2,1)} %get-tuple-element.63.q_ref, bf16[2048,64]{1,0:T(8,128)(2,1)} %get-tuple-element.64.k_ref, ...), custom_call_target="tpu_custom_call" | custom-call | flops 14000000000 | bytes 4194304 | tf_op jit(solution)/shard_map/attend_back/pallas_call | solution.py:268
  225.0 1.5 all-to-all-done.4
  226.5 3.6 %all-to-all-start.5 = ((bf16[32,96,128]{2,1,0:T(8,128)(2,1)}), bf16[32,96,128]{2,1,0:T(8,128)(2,1)S(1)}, u32[]{:S(2)}, u32[]{:S(2)}) async-start(bf16[32,96,128]{2,1,0:T(8,128)(2,1)} %get-tuple-element.96), calls=%async_computation.5 | async-start | bytes 1572864 | tf_op jit(solution)/shard_map/all_to_all | solution.py:472
  232.8 3.8 %weight_grad.1 = bf16[768,192]{1,0:T(8,128)(2,1)} custom-call(s32[2]{0:T(128)} %pad_add_fusion.1.place_ref, bf16[8,128,768]{2,1,0:T(8,128)(2,1)} %copy-done.1, bf16[8,128,768]{2,1,0:T(8,128)(2,1)} %collective-permute-done.1.b_ref, bf16[192,2048]{1,0:T(8,128)(2,1)} %get-tuple-element.99.gt_ref), custom_call_target="tpu_custom_call" | custom-call | flops 3000000000 | bytes 4194304 | tf_op jit(solution)/shard_map/weight_grad/pallas_call | solution.py:124
  236.6 1.9 fusion.5
  238.5 18.1 %all-to-all-done.5.slots_ref = bf16[32,96,128]{2,1,0:T(8,128)(2,1)S(1)} async-done(((bf16[32,96,128]{2,1,0:T(8,128)(2,1)}), bf16[32,96,128]{2,1,0:T(8,128)(2,1)S(1)}, u32[]{:S(2)}, u32[]{:S(2)}) %all-to-all-start.5) | async-done | bytes 786464 | tf_op jit(solution)/shard_map/all_to_all | solution.py:472
  256.6 2.6 all-to-all-start.6
  259.2 4.0 %copy.112 = bf16[32,3,24,768]{3,2,0,1:T(8,128)(2,1)} copy(bf16[32,3,24,768]{3,2,1,0:T(8,128)(2,1)} %bitcast.163) | data formatting | bytes 7077888 | tf_op jit(solution)/shard_map/all_gather | solution.py:589
  263.9 4.4 %tokens.1 = bf16[128,768]{1,0:T(8,128)(2,1)} custom-call(bf16[32,96,128]{2,1,0:T(8,128)(2,1)} %copy-done.2, bf16[3,768,768]{2,1,0:T(8,128)(2,1)} %bitcast.164, f32[128,768]{1,0:T(8,128)} %get-tuple-element.98.first_ref), custom_call_target="tpu_custom_call" | custom-call | flops 3000000000 | bytes 2097152 | tf_op jit(solution)/shard_map/tokens/pallas_call | solution.py:289
  268.2 4.5 %all-to-all-done.6 = bf16[32,24,256]{2,1,0:T(8,128)(2,1)S(1)} async-done(((bf16[32,24,256]{2,1,0:T(8,128)(2,1)}), bf16[32,24,256]{2,1,0:T(8,128)(2,1)S(1)}, u32[]{:S(2)}, u32[]{:S(2)}) %all-to-all-start.6) | async-done | bytes 393248 | tf_op jit(solution)/shard_map/all_to_all | solution.py:472
  278.5 4.8 %reduce-scatter.2.cloned.1.call-done = bf16[1,8,24,768]{3,2,1,0:T(8,128)(2,1)} async-done(((bf16[8,8,24,768]{3,2,1,0:T(8,128)(2,1)}), bf16[1,8,24,768]{3,2,1,0:T(8,128)(2,1)}) %reduce-scatter.2.cloned.1.call-update) | async-done | bytes 294928 | tf_op jit(solution)/shard_map/reduce_scatter | solution.py:693
  284.5 1.4 collective-permute-start.21
  (184 shorter events, 43.9 us)
Async XLA Ops:
  7.2 8.4 %copy-start.9 = (bf16[96]{0:T(256)(128)(2,1)S(1)}, bf16[96]{0:T(256)(128)(2,1)}, u32[]{:S(2)}) copy-start(bf16[96]{0:T(256)(128)(2,1)} %param.19) | copy-start | bytes 580
  7.2 8.5 %copy-start.10 = (bf16[2,24]{1,0:T(2,128)(2,1)S(1)}, bf16[2,24]{1,0:T(2,128)(2,1)}, u32[]{:S(2)}) copy-start(bf16[2,24]{1,0:T(2,128)(2,1)} %param.21) | copy-start | bytes 292
  7.2 8.6 %copy-start.11 = (bf16[2,24]{1,0:T(2,128)(2,1)S(1)}, bf16[2,24]{1,0:T(2,128)(2,1)}, u32[]{:S(2)}) copy-start(bf16[2,24]{1,0:T(2,128)(2,1)} %param.20) | copy-start | bytes 292
  7.2 8.7 %copy-start.8 = (bf16[4,24]{1,0:T(4,128)(2,1)S(1)}, bf16[4,24]{1,0:T(4,128)(2,1)}, u32[]{:S(2)}) copy-start(bf16[4,24]{1,0:T(4,128)(2,1)} %param.18) | copy-start | bytes 580
  8.2 10.6 %collective-permute-start = (bf16[64,768]{1,0:T(8,128)(2,1)S(1)}, bf16[64,768]{1,0:T(8,128)(2,1)S(1)}, u32[]{:S(2)}, u32[]{:S(2)}) collective-permute-start(bf16[64,768]{1,0:T(8,128)(2,1)S(1)} %get-tuple-element.139), channel_id=1, source_target_pairs={{0,4},{1,5},{2,6},{3,7},{4,0},{5,1},{6,2},{7,3},{8,12},{9,13},{10,... | collective-permute-start | bytes 294920 | tf_op jit(solution)/shard_map/ppermute | solution.py:555
  13.7 4.8 %collective-permute-start.2 = (bf16[24,768]{1,0:T(8,128)(2,1)S(1)}, bf16[24,768]{1,0:T(8,128)(2,1)S(1)}, u32[]{:S(2)}, u32[]{:S(2)}) collective-permute-start(bf16[24,768]{1,0:T(8,128)(2,1)S(1)} %bitcast.189), channel_id=1, source_target_pairs={{0,24},{8,16},{16,8},{24,0},{1,25},{9,17},{17,9},{25,1},{2,26},{10... | collective-permute-start | bytes 110600 | tf_op jit(solution)/shard_map/ppermute | solution.py:515
  14.4 4.3 %collective-permute-start.3 = (bf16[24,768]{1,0:T(8,128)(2,1)S(1)}, bf16[24,768]{1,0:T(8,128)(2,1)S(1)}, u32[]{:S(2)}, u32[]{:S(2)}) collective-permute-start(bf16[24,768]{1,0:T(8,128)(2,1)S(1)} %bitcast.190), channel_id=1, source_target_pairs={{0,16},{16,0},{8,24},{24,8},{1,17},{17,1},{9,25},{25,9},{2,18},{18... | collective-permute-start | bytes 110600 | tf_op jit(solution)/shard_map/ppermute | solution.py:468
  15.3 3.4 %collective-permute-start.4 = (bf16[24,768]{1,0:T(8,128)(2,1)S(1)}, bf16[24,768]{1,0:T(8,128)(2,1)S(1)}, u32[]{:S(2)}, u32[]{:S(2)}) collective-permute-start(bf16[24,768]{1,0:T(8,128)(2,1)S(1)} %bitcast.191), channel_id=1, source_target_pairs={{0,8},{8,0},{16,24},{24,16},{1,9},{9,1},{17,25},{25,17},{2,10},{10... | collective-permute-start | bytes 110600 | tf_op jit(solution)/shard_map/ppermute | solution.py:464
  18.5 4.6 %copy-start.5 = (bf16[96,768]{1,0:T(8,128)(2,1)S(1)}, bf16[96,768]{1,0:T(8,128)(2,1)}, u32[]{:S(2)}) copy-start(bf16[96,768]{1,0:T(8,128)(2,1)} %param.17) | copy-start | bytes 442372
  18.5 4.7 %copy-start.6 = (bf16[24,768]{1,0:T(8,128)(2,1)S(1)}, bf16[24,768]{1,0:T(8,128)(2,1)}, u32[]{:S(2)}) copy-start(bf16[24,768]{1,0:T(8,128)(2,1)} %param.15) | copy-start | bytes 110596
  18.8 17.8 %all-to-all-start.1 = ((bf16[32,2,24,128]{3,2,1,0:T(8,128)(2,1)}), bf16[32,2,24,128]{3,2,1,0:T(8,128)(2,1)S(1)}, u32[]{:S(2)}, u32[]{:S(2)}) async-start(bf16[32,2,24,128]{3,2,1,0:T(8,128)(2,1)} %head_slots.1), calls=%async_computation.1 | async-start | bytes 786432 | tf_op jit(solution)/shard_map/all_to_all | solution.py:472
  23.0 73.5 %all-gather.5.cloned.1.call-start = ((), (), s32[]{:S(2)}) async-start(), calls=%async_computation.9 | async-start | bytes 2985984 | tf_op jit(solution)/shard_map/all_gather | solution.py:588
  37.9 39.0 %all-to-all-start = ((bf16[8,128,768]{2,1,0:T(8,128)(2,1)}), bf16[8,128,768]{2,1,0:T(8,128)(2,1)S(1)}, u32[]{:S(2)}, u32[]{:S(2)}) async-start(bf16[8,128,768]{2,1,0:T(8,128)(2,1)} %broadcast_in_dim.58), calls=%async_computation | async-start | bytes 3145728 | tf_op jit(solution)/shard_map/all_to_all | solution.py:472
  41.5 35.4 %copy-start.12 = (s32[2,32]{1,0:T(2,128)S(1)}, s32[2,32]{1,0:T(2,128)}, u32[]{:S(2)}) copy-start(s32[2,32]{1,0:T(2,128)} %param.12) | copy-start | bytes 772
  41.5 217.8 %all-gather.7.cloned.1.call-start = ((), (), s32[]{:S(2)}) async-start(), calls=%async_computation.10 | async-start | bytes 3649536 | tf_op jit(solution)/shard_map/all_gather | solution.py:589
  76.9 3.5 %copy-start.1 = (bf16[8,128,768]{2,1,0:T(8,128)(2,1)}, bf16[8,128,768]{2,1,0:T(8,128)(2,1)S(1)}, u32[]{:S(2)}) copy-start(bf16[8,128,768]{2,1,0:T(8,128)(2,1)S(1)} %all-to-all-done.a_ref) | copy-start | bytes 4718596
  76.9 3.5 %collective-permute-start.1 = (bf16[8,128,768]{2,1,0:T(8,128)(2,1)S(1)}, bf16[8,128,768]{2,1,0:T(8,128)(2,1)}, u32[]{:S(2)}, u32[]{:S(2)}) collective-permute-start(bf16[8,128,768]{2,1,0:T(8,128)(2,1)S(1)} %all-to-all-done.a_ref), channel_id=1, source_target_pairs={{0,8},{8,0},{16,24},{24,16},{1,9},{9,1},{17,25},{25,17},{2,10},{10... | collective-permute-start | bytes 4718600 | tf_op jit(solution)/shard_map/ppermute | solution.py:464
  97.5 9.9 %collective-permute-start.5 = (bf16[192,768]{1,0:T(8,128)(2,1)S(1)}, bf16[192,768]{1,0:T(8,128)(2,1)S(1)}, u32[]{:S(2)}, u32[]{:S(2)}) collective-permute-start(bf16[192,768]{1,0:T(8,128)(2,1)S(1)} %bitcast.172), channel_id=1, source_target_pairs={{0,16},{16,0},{8,24},{24,8},{1,17},{17,1},{9,25},{25,9},{2,18},{18... | collective-permute-start | bytes 884744 | tf_op jit(solution)/shard_map/ppermute | solution.py:468
  98.1 12.8 %collective-permute-start.7 = (bf16[192,768]{1,0:T(8,128)(2,1)S(1)}, bf16[192,768]{1,0:T(8,128)(2,1)S(1)}, u32[]{:S(2)}, u32[]{:S(2)}) collective-permute-start(bf16[192,768]{1,0:T(8,128)(2,1)S(1)} %bitcast.173), channel_id=1, source_target_pairs={{0,8},{8,0},{16,24},{24,16},{1,9},{9,1},{17,25},{25,17},{2,10},{10... | collective-permute-start | bytes 884744 | tf_op jit(solution)/shard_map/ppermute | solution.py:464
  107.4 3.5 %collective-permute-start.6 = (bf16[192,768]{1,0:T(8,128)(2,1)S(1)}, bf16[192,768]{1,0:T(8,128)(2,1)S(1)}, u32[]{:S(2)}, u32[]{:S(2)}) collective-permute-start(bf16[192,768]{1,0:T(8,128)(2,1)S(1)} %collective-permute-done.5), channel_id=1, source_target_pairs={{0,8},{8,0},{16,24},{24,16},{1,9},{9,1},{17,25},{25,17},{2,10},{10... | collective-permute-start | bytes 884744 | tf_op jit(solution)/shard_map/ppermute | solution.py:464
  107.4 13.2 %all-to-all-start.2 = ((bf16[32,32,128]{2,1,0:T(8,128)(2,1)}), bf16[32,32,128]{2,1,0:T(8,128)(2,1)S(1)}, u32[]{:S(2)}, u32[]{:S(2)}) async-start(bf16[32,32,128]{2,1,0:T(8,128)(2,1)} %get-tuple-element.66), calls=%async_computation.2 | async-start | bytes 524288 | tf_op jit(solution)/shard_map/all_to_all | solution.py:472
  121.4 9.9 %copy-start = (bf16[1728,768]{1,0:T(8,128)(2,1)S(1)}, bf16[1728,768]{1,0:T(8,128)(2,1)}, u32[]{:S(2)}) copy-start(bf16[1728,768]{1,0:T(8,128)(2,1)} %all-gather.5.cloned.1.call-done) | copy-start | bytes 7962628
  124.5 6.8 %collective-permute-start.8 = (bf16[128,768]{1,0:T(8,128)(2,1)}, bf16[128,768]{1,0:T(8,128)(2,1)S(1)}, u32[]{:S(2)}, u32[]{:S(2)}) collective-permute-start(bf16[128,768]{1,0:T(8,128)(2,1)} %get-tuple-element.68.a_ref), channel_id=1, source_target_pairs={{0,16},{16,0},{8,24},{24,8},{1,17},{17,1},{9,25},{25,9},{2,18},{18... | collective-permute-start | bytes 589832 | tf_op jit(solution)/shard_map/ppermute | solution.py:468
  126.1 7.6 %collective-permute-start.9 = (bf16[128,768]{1,0:T(8,128)(2,1)}, bf16[128,768]{1,0:T(8,128)(2,1)S(1)}, u32[]{:S(2)}, u32[]{:S(2)}) collective-permute-start(bf16[128,768]{1,0:T(8,128)(2,1)} %get-tuple-element.68.a_ref), channel_id=1, source_target_pairs={{0,8},{8,0},{16,24},{24,16},{1,9},{9,1},{17,25},{25,17},{2,10},{10... | collective-permute-start | bytes 589832 | tf_op jit(solution)/shard_map/ppermute | solution.py:464
  131.3 2.4 collective-permute-start.10
  140.5 2.1 collective-permute-start.11
  145.4 7.4 %collective-permute-start.12 = (bf16[128,768]{1,0:T(8,128)(2,1)}, bf16[128,768]{1,0:T(8,128)(2,1)S(1)}, u32[]{:S(2)}, u32[]{:S(2)}) collective-permute-start(bf16[128,768]{1,0:T(8,128)(2,1)} %get-tuple-element.72), channel_id=1, source_target_pairs={{0,16},{16,0},{8,24},{24,8},{1,17},{17,1},{9,25},{25,9},{2,18},{18... | collective-permute-start | bytes 589832 | tf_op jit(solution)/shard_map/ppermute | solution.py:468
  156.0 6.6 %collective-permute-start.13 = (bf16[128,768]{1,0:T(8,128)(2,1)}, bf16[128,768]{1,0:T(8,128)(2,1)S(1)}, u32[]{:S(2)}, u32[]{:S(2)}) collective-permute-start(bf16[128,768]{1,0:T(8,128)(2,1)} %get-tuple-element.79.a_ref), channel_id=1, source_target_pairs={{0,16},{16,0},{8,24},{24,8},{1,17},{17,1},{9,25},{25,9},{2,18},{18... | collective-permute-start | bytes 589832 | tf_op jit(solution)/shard_map/ppermute | solution.py:468
  157.2 5.4 %collective-permute-start.14 = (bf16[128,768]{1,0:T(8,128)(2,1)}, bf16[128,768]{1,0:T(8,128)(2,1)S(1)}, u32[]{:S(2)}, u32[]{:S(2)}) collective-permute-start(bf16[128,768]{1,0:T(8,128)(2,1)} %get-tuple-element.79.a_ref), channel_id=1, source_target_pairs={{0,8},{8,0},{16,24},{24,16},{1,9},{9,1},{17,25},{25,17},{2,10},{10... | collective-permute-start | bytes 589832 | tf_op jit(solution)/shard_map/ppermute | solution.py:464
  162.6 1.4 copy-start.17
  162.6 1.4 collective-permute-start.15
  162.6 1.4 copy-start.18
  170.8 1.9 collective-permute-start.16
  175.6 7.2 %collective-permute-start.17 = (bf16[128,768]{1,0:T(8,128)(2,1)}, bf16[128,768]{1,0:T(8,128)(2,1)S(1)}, u32[]{:S(2)}, u32[]{:S(2)}) collective-permute-start(bf16[128,768]{1,0:T(8,128)(2,1)} %get-tuple-element.84), channel_id=1, source_target_pairs={{0,16},{16,0},{8,24},{24,8},{1,17},{17,1},{9,25},{25,9},{2,18},{18... | collective-permute-start | bytes 589832 | tf_op jit(solution)/shard_map/ppermute | solution.py:468
  183.4 3.2 %copy-start.4 = (bf16[128,768]{1,0:T(8,128)(2,1)S(1)}, bf16[128,768]{1,0:T(8,128)(2,1)}, u32[]{:S(2)}) copy-start(bf16[128,768]{1,0:T(8,128)(2,1)} %get-tuple-element.94) | copy-start | bytes 589828
  188.2 2.1 collective-permute-start.18
  191.1 10.7 %collective-permute-start.19 = (bf16[192,768]{1,0:T(8,128)(2,1)}, bf16[192,768]{1,0:T(8,128)(2,1)}, u32[]{:S(2)}, u32[]{:S(2)}) collective-permute-start(bf16[192,768]{1,0:T(8,128)(2,1)} %fusion.6), channel_id=1, source_target_pairs={{0,16},{16,0},{8,24},{24,8},{1,17},{17,1},{9,25},{25,9},{2,18},{18... | collective-permute-start | bytes 884744 | tf_op jit(solution)/shard_map/ppermute | solution.py:468
  192.5 13.9 %all-to-all-start.3 = ((bf16[32,32,128]{2,1,0:T(8,128)(2,1)}), bf16[32,32,128]{2,1,0:T(8,128)(2,1)}, u32[]{:S(2)}, u32[]{:S(2)}) async-start(bf16[32,32,128]{2,1,0:T(8,128)(2,1)} %get-tuple-element.92), calls=%async_computation.3 | async-start | bytes 524288 | tf_op jit(solution)/shard_map/all_to_all | solution.py:472
  195.8 87.5 %reduce-scatter.2.cloned.1.call-start = ((), (), s32[]{:S(2)}) async-start(), calls=%async_computation.8 | async-start | bytes 2654208 | tf_op jit(solution)/shard_map/reduce_scatter | solution.py:693
  206.4 20.1 %all-to-all-start.4 = ((bf16[8,24,768]{2,1,0:T(8,128)(2,1)}), bf16[8,24,768]{2,1,0:T(8,128)(2,1)S(1)}, u32[]{:S(2)}, u32[]{:S(2)}) async-start(bf16[8,24,768]{2,1,0:T(8,128)(2,1)} %bitcast.174), calls=%async_computation.4 | async-start | bytes 589824 | tf_op jit(solution)/shard_map/all_to_all | solution.py:472
  225.0 5.8 %copy-start.7 = (f32[1,768]{1,0:T(1,128)S(1)}, f32[1,768]{1,0:T(1,128)}, u32[]{:S(2)}) copy-start(f32[1,768]{1,0:T(1,128)} %get-tuple-element.103) | copy-start | bytes 9220
  225.0 6.9 %copy-start.23 = (f32[1,128]{1,0:T(1,128)S(1)}, f32[1,128]{1,0:T(1,128)}, u32[]{:S(2)}) copy-start(f32[1,128]{1,0:T(1,128)} %get-tuple-element.102) | copy-start | bytes 1540
  226.5 30.1 %all-to-all-start.5 = ((bf16[32,96,128]{2,1,0:T(8,128)(2,1)}), bf16[32,96,128]{2,1,0:T(8,128)(2,1)S(1)}, u32[]{:S(2)}, u32[]{:S(2)}) async-start(bf16[32,96,128]{2,1,0:T(8,128)(2,1)} %get-tuple-element.96), calls=%async_computation.5 | async-start | bytes 1572864 | tf_op jit(solution)/shard_map/all_to_all | solution.py:472
  256.6 6.6 %copy-start.2 = (bf16[32,96,128]{2,1,0:T(8,128)(2,1)}, bf16[32,96,128]{2,1,0:T(8,128)(2,1)S(1)}, u32[]{:S(2)}) copy-start(bf16[32,96,128]{2,1,0:T(8,128)(2,1)S(1)} %all-to-all-done.5.slots_ref) | copy-start | bytes 2359300
  256.6 16.1 %all-to-all-start.6 = ((bf16[32,24,256]{2,1,0:T(8,128)(2,1)}), bf16[32,24,256]{2,1,0:T(8,128)(2,1)S(1)}, u32[]{:S(2)}, u32[]{:S(2)}) async-start(bf16[32,24,256]{2,1,0:T(8,128)(2,1)} %fusion.5), calls=%async_computation.6 | async-start | bytes 786432 | tf_op jit(solution)/shard_map/all_to_all | solution.py:472
  284.4 3.8 %collective-permute-start.20 = (bf16[24,768]{1,0:T(8,128)(2,1)S(1)}, bf16[24,768]{1,0:T(8,128)(2,1)S(1)}, u32[]{:S(2)}, u32[]{:S(2)}) collective-permute-start(bf16[24,768]{1,0:T(8,128)(2,1)S(1)} %get-tuple-element.144), channel_id=1, source_target_pairs={{0,24},{8,16},{16,8},{24,0},{1,25},{9,17},{17,9},{25,1},{2,26},{10... | collective-permute-start | bytes 110600 | tf_op jit(solution)/shard_map/ppermute | solution.py:515
  284.5 4.1 %collective-permute-start.21 = (bf16[24,768]{1,0:T(8,128)(2,1)S(1)}, bf16[24,768]{1,0:T(8,128)(2,1)S(1)}, u32[]{:S(2)}, u32[]{:S(2)}) collective-permute-start(bf16[24,768]{1,0:T(8,128)(2,1)S(1)} %get-tuple-element.143), channel_id=1, source_target_pairs={{0,16},{16,0},{8,24},{24,8},{1,17},{17,1},{9,25},{25,9},{2,18},{18... | collective-permute-start | bytes 110600 | tf_op jit(solution)/shard_map/ppermute | solution.py:468
  285.9 2.7 collective-permute-start.22
  (9 other events, 6.9 us)
Sparse Core Ops, SparseCore 0:
  26.0 67.0 all-gather.4
  96.0 57.7 all-gather.6
  200.1 83.1 reduce-scatter.1

commit v5 on v4

--- a/solution.py
+++ b/solution.py
@@ -20,7 +20,8 @@
 masked_score = -1e30
 VMEM = pl.BlockSpec(memory_space=pltpu.VMEM)
 SMEM = pl.BlockSpec(memory_space=pltpu.SMEM)
-PARAMS = pltpu.CompilerParams(vmem_limit_bytes=56 << 20)
+SMALL = pltpu.CompilerParams(vmem_limit_bytes=20 << 20)
+LARGE = pltpu.CompilerParams(vmem_limit_bytes=56 << 20)
 
 
 def dot(a, b, dims):
@@ -86,8 +87,8 @@
         out_shape=(rows, rows, rows, columns, columns),
         in_specs=[SMEM] + [VMEM] * 5,
         out_specs=(VMEM,) * 5,
-        compiler_params=PARAMS,
-        cost_estimate=pl.CostEstimate(flops=5000000000, bytes_accessed=4 << 20, transcendentals=0),
+        compiler_params=SMALL if length <= 4096 else LARGE,
+        cost_estimate=pl.CostEstimate(flops=1000000, bytes_accessed=1 << 10, transcendentals=0),
         name="project",
     )(place, a, b, qk, v, bias)
 
@@ -121,14 +122,15 @@
 
 def weight_grad(place, a, b, gt, halves, per):
     depth = a.shape[2]
+    length = gt.shape[1]
     return pl.pallas_call(
         functools.partial(weight_grad_kernel, halves=halves, per=per),
         out_shape=jax.ShapeDtypeStruct((depth, gt.shape[0]), BF),
         in_specs=[SMEM] + [VMEM] * 3,
         out_specs=VMEM,
         scratch_shapes=[pltpu.VMEM((gt.shape[0], depth), F32)],
-        compiler_params=PARAMS,
-        cost_estimate=pl.CostEstimate(flops=3000000000, bytes_accessed=4 << 20, transcendentals=0),
+        compiler_params=SMALL if length <= 4096 else LARGE,
+        cost_estimate=pl.CostEstimate(flops=1000000, bytes_accessed=1 << 10, transcendentals=0),
         name="weight_grad",
     )(place, a, b, gt)
 
@@ -197,8 +199,8 @@
         in_specs=[SMEM, SMEM] + [VMEM] * 4,
         out_specs=(VMEM,) * 3,
         scratch_shapes=[pltpu.VMEM((length, bq), F32)],
-        compiler_params=PARAMS,
-        cost_estimate=pl.CostEstimate(flops=10000000000, bytes_accessed=4 << 20, transcendentals=0),
+        compiler_params=SMALL if length <= 4096 else LARGE,
+        cost_estimate=pl.CostEstimate(flops=1000000, bytes_accessed=1 << 10, transcendentals=0),
         name="attend",
     )(lo, hi, q, k, vt, spans)
 
@@ -279,8 +281,8 @@
             pltpu.VMEM((length, hd), F32),
             pltpu.VMEM((length, hd), F32),
         ],
-        compiler_params=PARAMS,
-        cost_estimate=pl.CostEstimate(flops=14000000000, bytes_accessed=4 << 20, transcendentals=0),
+        compiler_params=SMALL if length <= 4096 else LARGE,
+        cost_estimate=pl.CostEstimate(flops=1000000, bytes_accessed=1 << 10, transcendentals=0),
         name="attend_back",
     )(lo, hi, q, k, v, kt, ot, lse, do, spans)
 
@@ -292,9 +294,9 @@
         in_specs=[SMEM if v.dtype == jnp.int32 else VMEM for v in ins],
         out_specs=(VMEM,) * len(outs),
         scratch_shapes=list(scratch),
-        compiler_params=PARAMS,
+        compiler_params=SMALL,
         cost_estimate=pl.CostEstimate(
-            flops=int(flops), bytes_accessed=2 << 20, transcendentals=0
+            flops=int(flops), bytes_accessed=1 << 10, transcendentals=0
         ),
         name=name,
     )(*ins)
@@ -387,6 +389,29 @@
         for h in range(half):
             first = (b * half + h) * rows
             out_ref[b, half + h] = acc_ref[first : first + rows, :].astype(BF)
+
+
+def collect_kernel(head_ref, slots_ref, qkv_ref, bias_ref, gains_ref, shifts_ref, inner_ref, *, layout):
+    groups, micro, halves, heads_dev = layout
+    hd = slots_ref.shape[2] // 4
+    cycle = micro * halves
+    pieces = []
+    for j in range(groups * heads_dev):
+        first = (j // heads_dev) * cycle + j % heads_dev
+        piece = slots_ref[first, :, : 3 * hd].astype(F32)
+        for m in range(1, micro):
+            piece = piece + slots_ref[first + m * halves, :, : 3 * hd].astype(F32)
+        pieces.append(piece)
+    for c in range(3):
+        for j in range(0, groups * heads_dev, 2):
+            pair = [p[:, c * hd : (c + 1) * hd] for p in pieces[j : j + 2]]
+            qkv_ref[c, :, j * hd : (j + 2) * hd] = jnp.concatenate(pair, axis=1)
+    own = slots_ref[pl.ds(head_ref[0] * cycle, cycle), :, 3 * hd :].astype(F32)
+    inner_ref[...] = jnp.sum(own, axis=0)
+    sums = jnp.sum(slots_ref[:, :, 3 * hd :].astype(F32), axis=0).T
+    bias_ref[...] = sums[0:4]
+    gains_ref[...] = sums[4:6]
+    shifts_ref[...] = sums[6:8]
 
 
 def add_kernel(keep_ref, got_ref, own_ref, send_ref):
@@ -486,7 +511,7 @@
 def reduce_group(keep, send):
     count, depth = keep.shape[0] // 2, keep.shape[1]
     shape = (count, depth)
-    own, send = call(add_kernel, ((shape, F32), (shape, BF)), (keep, by_core(send)), "add", 1e9)
+    own, send = call(add_kernel, ((shape, F32), (shape, BF)), (keep, by_core(send)), "add", 1e6)
     return own, by_x(send)
 
 
@@ -559,6 +584,10 @@
         for c in range(2)
         for s in range(2)
     ]
+    inner_own = inner_weight.reshape(rows_dev, groups, ff_part)
+    inner_own = to_group(inner_own.transpose(1, 0, 2)).reshape(groups * rows_dev, ff_part)
+    ffn = jnp.concatenate([inner_own, outer_weight])
+
     vectors = [bias_rows.T, norm_gains.T, norm_shifts.T, inner_bias.reshape(rows_dev, -1)]
     small = jnp.concatenate(vectors, axis=1)
     small = jnp.pad(small, ((0, 0), (0, hd - small.shape[1])))
@@ -568,9 +597,9 @@
         (((devices, 2, rows_dev, 2 * hd), BF),),
         (qkv_weight, small),
         "head_slots",
-        1e9,
-    )
-    slots = swap(after(slots, pair_x), BOTH)
+        1e6,
+    )
+    slots = swap(after(slots, pair_x, ffn), BOTH)
     qk_weight = slots[:, 0].reshape(depth, 2 * hd)
     v_weight = slots[:, 1].reshape(depth, 2 * hd)
     small = slots[:, 1, :, hd : hd + 12].astype(F32).reshape(depth, 12).T
@@ -581,16 +610,19 @@
     unit_bias = lax.dynamic_slice(bias[0:2], (0, unit_head * hd), (2, hd))
     unit_bias = jnp.pad(unit_bias, ((0, 0), (0, hd)))
 
-    inner_own = inner_weight.reshape(rows_dev, groups, ff_part)
-    inner_own = to_group(inner_own.transpose(1, 0, 2)).reshape(groups * rows_dev, ff_part)
-    ffn = jnp.concatenate([inner_own, outer_weight, out_weight])
-    qkv_weight = after(qkv_weight, ffn)
-    ffn_all = lax.all_gather(ffn, "blk", axis=0, tiled=False)
-    qkv_all = lax.all_gather(qkv_weight, BOTH, axis=0, tiled=False)
-    tokens_a, qk_weight, v_weight, unit_bias = lax.optimization_barrier(
-        (spread_over(pair_x, BOTH, cycle, cube), qk_weight, v_weight, unit_bias)
+    ffn_all = lax.all_gather(after(ffn, slots), "blk", axis=0, tiled=False)
+    qkv_all = lax.all_gather(after(qkv_weight, ffn), BOTH, axis=0, tiled=False)
+    small_rows = (
+        stack_rows(bias[2], gains[0], shifts[0]),
+        stack_rows(gains[0], shifts[0], bias[3], gains[1], shifts[1]),
+        stack_rows(gains[0]),
+        inner_bias_part[None],
+    )
+    tokens_a, qk_weight, v_weight, unit_bias, small_rows = lax.optimization_barrier(
+        (spread_over(pair_x, BOTH, cycle, cube), qk_weight, v_weight, unit_bias, small_rows)
     )
     tokens_b = by_core(tokens_a)
+    out_part = spread_over(after(out_weight, tokens_a), "blk", cycle).reshape(depth // groups, depth)
 
     lengths = lax.dynamic_index_in_dim(doc_lengths, half, 0, keepdims=False)
     order = jnp.arange(lengths.shape[0], dtype=jnp.int32)
@@ -621,10 +653,12 @@
         .transpose(1, 0, 2, 3)
         .reshape(depth, ff_part)
     )
-    first, last = groups * rows_dev, groups * rows_dev + ff_dev
-    outer_part = ffn[:, first:last].reshape(ff_part, depth)
-    out_part = ffn[:, last:].reshape(depth // groups, depth)
-    out_all = in_order(gather_group(out_part)).reshape(depth, depth)
+    outer_part = ffn[:, groups * rows_dev :].reshape(ff_part, depth)
+    attn_slots = swap(attn_out, BOTH)
+    out_x, attn_slots, inner_part, outer_part = lax.optimization_barrier(
+        (by_x(out_part), attn_slots, inner_part, outer_part)
+    )
+    out_all = in_order((out_part, out_x, by_core(out_part), by_core(out_x))).reshape(depth, depth)
 
     rows = micro * tokens
     layout = (groups, micro, halves, heads_dev)
@@ -632,16 +666,16 @@
     attn, normed_low, normed_one, inverse_one = call(
         functools.partial(branch_kernel, layout=layout),
         ((flat, BF), (flat, BF), (flat, F32), ((rows, 1), F32)),
-        (swap(attn_out, BOTH), inputs.reshape(flat), out_all, stack_rows(bias[2], gains[0], shifts[0])),
+        (attn_slots, inputs.reshape(flat), out_all, small_rows[0]),
         "branch",
-        2e9,
+        1e6,
     )
     act_low, slope, normed_group, keep, send = call(
         inner_kernel,
         ((group, BF), (group, F32), ((groups * rows, depth), BF), ((2 * rows, depth), F32), ((2 * rows, depth), BF)),
-        (*gather_group(normed_low), inner_part, outer_part, inner_bias_part[None]),
+        (*gather_group(normed_low), inner_part, outer_part, small_rows[3]),
         "inner",
-        4e9,
+        1e6,
     )
     output, d_second, d_ffn, sums_two = call(
         output_kernel,
@@ -650,10 +684,10 @@
             *reduce_group(keep, send),
             normed_one,
             grad_out.reshape(flat),
-            stack_rows(gains[0], shifts[0], bias[3], gains[1], shifts[1]),
+            small_rows[1],
         ),
         "output",
-        2e9,
+        1e6,
     )
     output = output.reshape(inputs.shape)
     d_inner, d_ffn_group, inner_sums, keep, send = call(
@@ -661,7 +695,7 @@
         ((group, BF), ((groups * rows, depth), BF), ((1, ff_part), F32), ((2 * rows, depth), F32), ((2 * rows, depth), BF)),
         (*gather_group(d_ffn), inner_part, outer_part, slope),
         "inner_back",
-        4e9,
+        1e6,
     )
     own, got = reduce_group(keep, send)
     (ffn_grad,) = call(
@@ -669,7 +703,7 @@
         (((cycle, 2 * groups, rows_dev, depth), BF),),
         (normed_group, d_inner, act_low, d_ffn_group),
         "feed_grad",
-        4e9,
+        1e6,
         [pltpu.VMEM((depth, depth), F32)],
     )
     got, ffn_grad = lax.optimization_barrier((got, ffn_grad))
@@ -683,10 +717,10 @@
             normed_one,
             inverse_one,
             out_all,
-            stack_rows(gains[0]),
+            small_rows[2],
         ),
         "branch_back",
-        2e9,
+        1e6,
     )
     d_heads = swap(d_heads, BOTH)
 
@@ -718,7 +752,7 @@
         ((flat, BF),),
         (qkv_home, qkv_all, d_first),
         "tokens",
-        3e9,
+        1e6,
         [pltpu.VMEM((3, rows, depth), BF)],
     )
     grad_inputs = grad_inputs.reshape(inputs.shape)
@@ -727,7 +761,10 @@
     wide = jnp.zeros((2, HEADS, hd), F32)
     wide = lax.dynamic_update_slice(wide, qv_sums.reshape(2, 1, hd), (0, unit_head, 0))
     wide = jnp.where((blk_index % halves < heads_dev), wide, 0.0)
-    sums = jnp.concatenate([sums_one[:3], sums_two[:3], wide.reshape(2, depth)]).T
+    sums = jnp.stack(
+        [wide[0].reshape(depth), wide[1].reshape(depth), sums_one[2], sums_two[2]]
+        + [sums_one[0], sums_two[0], sums_one[1], sums_two[1]]
+    ).T
     inner_sums = inner_sums.reshape(1, cycle, rows_dev, ff_dev // rows_dev)
     inner_sums = jnp.broadcast_to(inner_sums, (groups, *inner_sums.shape[1:]))
     extra = jnp.concatenate(
@@ -739,17 +776,21 @@
     ).astype(BF)
     extra = jnp.pad(extra, ((0, 0), (0, 0), (0, hd - extra.shape[2])))
     final = jnp.concatenate([unit_grad.reshape(devices, rows_dev, 3 * hd), extra], axis=2)
-    final = swap(after(final, qkv_home), BOTH).astype(F32)
-    qkv_grad = jnp.sum(
-        final[:, :, : 3 * hd].reshape(groups, micro, halves, rows_dev, 3, hd)[:, :, :heads_dev], axis=1
-    )
-    qkv_grad = qkv_grad.transpose(3, 2, 0, 1, 4).reshape(3, rows_dev, depth)
-    sums = jnp.sum(final[:, :, 3 * hd : 3 * hd + 8], axis=0).T
-    inner_sums = final[:, :, 3 * hd + 8 : 3 * hd + 8 + ff_dev // rows_dev]
-    inner_sums = lax.dynamic_index_in_dim(
-        inner_sums.reshape(groups, cycle, rows_dev, -1), head_index, 0, keepdims=False
-    )
-    inner_bias_grad = jnp.sum(inner_sums, axis=0).reshape(ff_dev)
+    final = swap(after(final, qkv_home), BOTH)
+    final, inner_grad = lax.optimization_barrier((final, inner_grad))
+    qkv_grad, bias_grad, gains_grad, shifts_grad, inner_bias_grad = call(
+        functools.partial(collect_kernel, layout=layout),
+        (
+            ((3, rows_dev, depth), F32),
+            ((4, rows_dev), F32),
+            ((2, rows_dev), F32),
+            ((2, rows_dev), F32),
+            ((rows_dev, hd), F32),
+        ),
+        (head_index[None], final),
+        "collect",
+        1e6,
+    )
     return (
         output,
         grad_inputs,
@@ -757,10 +798,10 @@
         out_grad,
         inner_grad,
         outer_grad,
-        jnp.stack([sums[6], sums[7], sums[2], sums[5]]),
-        inner_bias_grad,
-        jnp.stack([sums[0], sums[3]]),
-        jnp.stack([sums[1], sums[4]]),
+        bias_grad,
+        inner_bias_grad[:, 8 : 8 + ff_dev // rows_dev].reshape(ff_dev),
+        gains_grad,
+        shifts_grad,
     )
 
 

time: 297 us -> 272 us (0.916)
  waiting for transfers between devices: 128 us -> 99.3 us
  Pallas kernels: 71.1 us -> 44.8 us
  blocking collectives: 0 us -> 16.8 us
  local copies, waits for them, and re-layouts: 28.3 us -> 38.7 us
  starting transfers between devices: 38.8 us -> 45.7 us
  other arithmetic: 14.1 us -> 10.6 us
    all_to_all x7, waiting for transfers between devices: 81.7 us -> 41.1 us  [swap(): lax.all_to_all(value, axes, split_axis=0, concat_axis=0, tiled=True, axis...]
    pallas_call x10 -> x11, Pallas kernels: 36.1 us -> 16.7 us  [call(): pl.pallas_call(kernel, out_shape=tuple((jax.ShapeDtypeStruct(shape, kind)...]
    all_to_all x0 -> x1, blocking collectives: none -> 16.8 us  [swap(): lax.all_to_all(value, axes, split_axis=0, concat_axis=0, tiled=True, axis...]
    unnamed x55 -> x132, local copies, waits for them, and re-layouts: 5.65 us -> 14.9 us
    all_to_all x7, starting transfers between devices: 23.5 us -> 28.2 us  [swap(): lax.all_to_all(value, axes, split_axis=0, concat_axis=0, tiled=True, axis...]
    reduce_scatter x1, waiting for transfers between devices: 4.82 us -> 9.56 us  [local(): lax.psum_scatter(ffn_grad, 'blk', scatter_dimension=0, tiled=False)]
    ppermute x8, waiting for transfers between devices: 32.1 us -> 35.9 us  [by_x(): return lax.ppermute(value, 'head', [(0, 2), (2, 0), (1, 3), (3, 1)])]
  transfers between devices with their start and end apart: 33 -> 33, of which waited for: 22 -> 20; matrix products, arithmetic and copies ran while one was open for 12% -> 12% of each run, Pallas kernels for 24% -> 16%
where the time goes in v5:
time: 272 us; the launch traced here: 271 us
  waiting for transfers between devices  99.3 us (37%)
  starting transfers between devices  45.7 us (17%)
  Pallas kernels  44.8 us (16%)
  local copies, waits for them, and re-layouts  38.7 us (14%)
  blocking collectives  16.8 us (6%)
  between operations  14.8 us (5%)
  other arithmetic  10.6 us (4%)
    all_to_all x7, waiting for transfers between devices, swap(): lax.all_to_all(value, axes, split_axis=0, concat_axis=0, tiled=True, axis...  41.1 us
    ppermute x8, waiting for transfers between devices, by_x(): return lax.ppermute(value, 'head', [(0, 2), (2, 0), (1, 3), (3, 1)])  35.9 us
    all_to_all x7, starting transfers between devices, swap(): lax.all_to_all(value, axes, split_axis=0, concat_axis=0, tiled=True, axis...  28.2 us
    all_to_all x1, blocking collectives, swap(): lax.all_to_all(value, axes, split_axis=0, concat_axis=0, tiled=True, axis...  16.8 us
    pallas_call x11, Pallas kernels, call(): pl.pallas_call(kernel, out_shape=tuple((jax.ShapeDtypeStruct(shape, kind)...  16.7 us
    unnamed x132, local copies, waits for them, and re-layouts  14.9 us
    pallas_call x1, Pallas kernels, attend_back(): pl.pallas_call(functools.partial(attend_back_kernel, bq=bq, bk=bk, pack=p...  13.9 us
    ppermute x8, starting transfers between devices, by_x(): return lax.ppermute(value, 'head', [(0, 2), (2, 0), (1, 3), (3, 1)])  11.1 us
  transfers between devices with their start and end apart: 33, of which 20 were waited for; matrix products, arithmetic and copies ran while one was open for 12% of the time, Pallas kernels for 16%

profile of v5, /device:TPU:0, one launch (start us, length us, event | category | flops | bytes accessed | tf_op | source)
XLA Modules:
  0.0 271.1 jit_solution(11331929486204957763)
XLA Ops:
  8.3 4.1 %collective-permute-start = (bf16[64,768]{1,0:T(8,128)(2,1)S(1)}, bf16[64,768]{1,0:T(8,128)(2,1)S(1)}, u32[]{:S(2)}, u32[]{:S(2)}) collective-permute-start(bf16[64,768]{1,0:T(8,128)(2,1)S(1)} %get-tuple-element.163), channel_id=1, source_target_pairs={{0,4},{1,5},{2,6},{3,7},{4,0},{5,1},{6,2},{7,3},{8,12},{9,13},{10,... | collective-permute-start | bytes 294920 | tf_op jit(solution)/shard_map/ppermute | solution.py:580
  17.5 1.3 collective-permute-done.2
  19.6 16.8 %all_to_all.40 = bf16[32,2,24,128]{3,2,1,0:T(8,128)(2,1)S(1)} all-to-all(bf16[32,2,24,128]{3,2,1,0:T(8,128)(2,1)S(1)} %head_slots.1), channel_id=1, replica_groups=mesh['head'=4,'blk'=8] {'head','blk'}, dimensions={0} | all-to-all | bytes 786432 | tf_op jit(solution)/shard_map/all_to_all | solution.py:497
  36.4 1.3 broadcast_in_dim.65
  37.8 3.6 %all-to-all-start = ((bf16[8,128,768]{2,1,0:T(8,128)(2,1)}), bf16[8,128,768]{2,1,0:T(8,128)(2,1)S(1)}, u32[]{:S(2)}, u32[]{:S(2)}) async-start(bf16[8,128,768]{2,1,0:T(8,128)(2,1)} %broadcast_in_dim.65), calls=%async_computation | async-start | bytes 3145728 | tf_op jit(solution)/shard_map/all_to_all | solution.py:497
  46.1 25.8 %all-to-all-done.a_ref = bf16[8,128,768]{2,1,0:T(8,128)(2,1)S(1)} async-done(((bf16[8,128,768]{2,1,0:T(8,128)(2,1)}), bf16[8,128,768]{2,1,0:T(8,128)(2,1)S(1)}, u32[]{:S(2)}, u32[]{:S(2)}) %all-to-all-start) | async-done | bytes 1572896 | tf_op jit(solution)/shard_map/all_to_all | solution.py:497
  74.8 1.5 broadcast_in_dim.66
  76.3 4.1 %all-to-all-start.2 = ((bf16[8,24,768]{2,1,0:T(8,128)(2,1)}), bf16[8,24,768]{2,1,0:T(8,128)(2,1)}, u32[]{:S(2)}, u32[]{:S(2)}) async-start(bf16[8,24,768]{2,1,0:T(8,128)(2,1)} %broadcast_in_dim.66), calls=%async_computation.2 | async-start | bytes 589824 | tf_op jit(solution)/shard_map/all_to_all | solution.py:497
  83.1 2.4 project.1
  87.1 10.4 %attend.1 = (bf16[32,32,128]{2,1,0:T(8,128)(2,1)}, f32[64,2048]{1,0:T(8,128)S(1)}, f32[1,2048]{1,0:T(1,128)S(1)}) custom-call(s32[4]{0:T(128)S(1)} %get-tuple-element.192.lo_ref, s32[4]{0:T(128)S(1)} %get-tuple-element.193.hi_ref, bf16[2048,64]{1,0:T(8,128)(2,1)S(1)} %get-tuple-element.81.q_ref, bf16[2048,64]{1,0:T(8,128)(2,1)S(1)} %get-tuple-element.82.k_ref, ...), custom_call_target="tpu_custom_call" | custom-call | flops 1000000 | bytes 1024 | tf_op jit(solution)/shard_map/attend/pallas_call | solution.py:192
  100.4 4.9 %all-to-all-start.3 = ((bf16[32,32,128]{2,1,0:T(8,128)(2,1)}), bf16[32,32,128]{2,1,0:T(8,128)(2,1)S(1)}, u32[]{:S(2)}, u32[]{:S(2)}) async-start(bf16[32,32,128]{2,1,0:T(8,128)(2,1)} %get-tuple-element.84), calls=%async_computation.3 | async-start | bytes 524288 | tf_op jit(solution)/shard_map/all_to_all | solution.py:497
  105.6 1.8 collective-permute-start.4
  107.5 1.8 fusion.21
  109.3 9.0 %collective-permute-done.4 = bf16[192,768]{1,0:T(8,128)(2,1)S(1)} collective-permute-done((bf16[192,768]{1,0:T(8,128)(2,1)}, bf16[192,768]{1,0:T(8,128)(2,1)S(1)}, u32[]{:S(2)}, u32[]{:S(2)}) %collective-permute-start.4) | collective-permute-done | bytes 294944 | tf_op jit(solution)/shard_map/ppermute | solution.py:493
  118.3 1.6 collective-permute-done.6
  124.3 6.0 %collective-permute-done.8.b_ref = bf16[128,768]{1,0:T(8,128)(2,1)S(1)} collective-permute-done((bf16[128,768]{1,0:T(8,128)(2,1)S(1)}, bf16[128,768]{1,0:T(8,128)(2,1)S(1)}, u32[]{:S(2)}, u32[]{:S(2)}) %collective-permute-start.8) | collective-permute-done | bytes 196640 | tf_op jit(solution)/shard_map/ppermute | solution.py:493
  130.3 1.4 collective-permute-done.10.d_ref
  131.7 2.5 inner.1
  134.5 1.6 collective-permute-done.11.got_ref
  137.1 6.0 %collective-permute-done.12.got_ref = bf16[128,768]{1,0:T(8,128)(2,1)S(1)} collective-permute-done((bf16[128,768]{1,0:T(8,128)(2,1)S(1)}, bf16[128,768]{1,0:T(8,128)(2,1)S(1)}, u32[]{:S(2)}, u32[]{:S(2)}) %collective-permute-start.12) | collective-permute-done | bytes 196640 | tf_op jit(solution)/shard_map/ppermute | solution.py:493
  145.8 6.7 %collective-permute-done.13.b_ref = bf16[128,768]{1,0:T(8,128)(2,1)S(1)} collective-permute-done((bf16[128,768]{1,0:T(8,128)(2,1)S(1)}, bf16[128,768]{1,0:T(8,128)(2,1)S(1)}, u32[]{:S(2)}, u32[]{:S(2)}) %collective-permute-start.13) | collective-permute-done | bytes 196640 | tf_op jit(solution)/shard_map/ppermute | solution.py:493
  152.5 1.4 collective-permute-done.15.d_ref
  154.0 2.9 %inner_back.1 = (bf16[512,768]{1,0:T(8,128)(2,1)S(1)}, bf16[512,768]{1,0:T(8,128)(2,1)S(1)}, f32[1,768]{1,0:T(1,128)S(1)}, f32[256,768]{1,0:T(8,128)S(1)}, bf16[256,768]{1,0:T(8,128)(2,1)S(1)}) custom-call(bf16[128,768]{1,0:T(8,128)(2,1)S(1)} %get-tuple-element.105.a_ref, bf16[128,768]{1,0:T(8,128)(2,1)S(1)} %collective-permute-done.13.b_ref, ...), custom_call_target="tpu_custom_call" | custom-call | flops 1000000 | bytes 1024 | tf_op jit(solution)/shard_map/inner_back/pallas_call | solution.py:291
  157.1 1.6 collective-permute-done.16.got_ref
  158.7 2.3 collective-permute-start.17
  161.1 2.8 %feed_grad.1 = bf16[8,8,24,768]{3,2,1,0:T(8,128)(2,1)} custom-call(bf16[512,768]{1,0:T(8,128)(2,1)S(1)} %get-tuple-element.111.low_ref, bf16[512,768]{1,0:T(8,128)(2,1)S(1)} %get-tuple-element.112.inner_ref, bf16[512,768]{1,0:T(8,128)(2,1)S(1)} %get-tuple-element.113.act_ref, bf16[512,768]{1,0:T(8,128)(2,1)S(1)} %get-tuple-element.114.ffn_ref), custom_call_target="tpu_custom_call" | custom-call | flops 1000000 | bytes 1024 | tf_op jit(solution)/shard_map/feed_grad/pallas_call | solution.py:291
  163.9 2.3 collective-permute-done.17.got_ref
  166.3 1.5 branch_back.1
  168.8 2.0 collective-permute-done.18
  171.9 1.7 collective-permute-start.19
  173.6 3.5 %all-to-all-start.4 = ((bf16[32,32,128]{2,1,0:T(8,128)(2,1)}), bf16[32,32,128]{2,1,0:T(8,128)(2,1)S(1)}, u32[]{:S(2)}, u32[]{:S(2)}) async-start(bf16[32,32,128]{2,1,0:T(8,128)(2,1)} %get-tuple-element.119), calls=%async_computation.4 | async-start | bytes 524288 | tf_op jit(solution)/shard_map/all_to_all | solution.py:497
  177.2 4.2 %collective-permute-done.19 = bf16[192,768]{1,0:T(8,128)(2,1)S(1)} collective-permute-done((bf16[192,768]{1,0:T(8,128)(2,1)S(1)}, bf16[192,768]{1,0:T(8,128)(2,1)S(1)}, u32[]{:S(2)}, u32[]{:S(2)}) %collective-permute-start.19) | collective-permute-done | bytes 294944 | tf_op jit(solution)/shard_map/ppermute | solution.py:493
  181.4 2.1 fusion.3
  183.5 9.8 %all-to-all-done.4.do_ref = bf16[32,32,128]{2,1,0:T(8,128)(2,1)S(1)} async-done(((bf16[32,32,128]{2,1,0:T(8,128)(2,1)}), bf16[32,32,128]{2,1,0:T(8,128)(2,1)S(1)}, u32[]{:S(2)}, u32[]{:S(2)}) %all-to-all-start.4) | async-done | bytes 262176 | tf_op jit(solution)/shard_map/all_to_all | solution.py:497
  193.3 3.4 %all-to-all-start.5 = ((bf16[8,24,768]{2,1,0:T(8,128)(2,1)}), bf16[8,24,768]{2,1,0:T(8,128)(2,1)S(1)}, u32[]{:S(2)}, u32[]{:S(2)}) async-start(bf16[8,24,768]{2,1,0:T(8,128)(2,1)} %bitcast.40), calls=%async_computation.5 | async-start | bytes 589824 | tf_op jit(solution)/shard_map/all_to_all | solution.py:497
  196.8 13.9 %attend_back.1 = (bf16[32,96,128]{2,1,0:T(8,128)(2,1)}, bf16[192,2048]{1,0:T(8,128)(2,1)S(1)}, f32[1,128]{1,0:T(1,128)S(1)}) custom-call(s32[4]{0:T(128)S(1)} %copy-done.46, s32[4]{0:T(128)S(1)} %copy-done.47, bf16[2048,64]{1,0:T(8,128)(2,1)S(1)} %copy-done.5, bf16[2048,64]{1,0:T(8,128)(2,1)S(1)} %copy-done.7, bf16[2048,64]{1,0:T(8,128)(2,1)S(1)} %copy-done.16, ...), custom_call_target="tpu_custom_call" | custom-call | flops 1000000 | bytes 1024 | tf_op jit(solution)/shard_map/attend_back/pallas_call | solution.py:270
  211.7 5.5 %all-to-all-start.6 = ((bf16[32,96,128]{2,1,0:T(8,128)(2,1)}), bf16[32,96,128]{2,1,0:T(8,128)(2,1)}, u32[]{:S(2)}, u32[]{:S(2)}) async-start(bf16[32,96,128]{2,1,0:T(8,128)(2,1)} %get-tuple-element.123), calls=%async_computation.6 | async-start | bytes 1572864 | tf_op jit(solution)/shard_map/all_to_all | solution.py:497
  219.1 2.2 copy.94
  222.7 1.3 stack_reshape_squeeze.8
  226.3 1.4 copy-done.1
  227.8 1.4 copy-done.3
  230.3 1.4 weight_grad.1
  233.5 5.4 %all-to-all-done.6.slots_ref = bf16[32,96,128]{2,1,0:T(8,128)(2,1)} async-done(((bf16[32,96,128]{2,1,0:T(8,128)(2,1)}), bf16[32,96,128]{2,1,0:T(8,128)(2,1)}, u32[]{:S(2)}, u32[]{:S(2)}) %all-to-all-start.6) | async-done | bytes 786464 | tf_op jit(solution)/shard_map/all_to_all | solution.py:497
  238.9 3.3 %all-to-all-start.7 = ((bf16[32,24,256]{2,1,0:T(8,128)(2,1)}), bf16[32,24,256]{2,1,0:T(8,128)(2,1)}, u32[]{:S(2)}, u32[]{:S(2)}) async-start(bf16[32,24,256]{2,1,0:T(8,128)(2,1)} %pad_maximum_fusion.2), calls=%async_computation.7 | async-start | bytes 786432 | tf_op jit(solution)/shard_map/all_to_all | solution.py:497
  243.2 3.2 %tokens.1 = bf16[128,768]{1,0:T(8,128)(2,1)} custom-call(bf16[32,96,128]{2,1,0:T(8,128)(2,1)} %all-to-all-done.6.slots_ref, bf16[3,768,768]{2,1,0:T(8,128)(2,1)S(1)} %bitcast.155, f32[128,768]{1,0:T(8,128)S(1)} %copy-done.21), custom_call_target="tpu_custom_call" | custom-call | flops 1000000 | bytes 1024 | tf_op jit(solution)/shard_map/tokens/pallas_call | solution.py:291
  246.4 9.6 %reduce-scatter.2.cloned.1.call-done = bf16[1,8,24,768]{3,2,1,0:T(8,128)(2,1)} async-done(((bf16[8,8,24,768]{3,2,1,0:T(8,128)(2,1)}), bf16[1,8,24,768]{3,2,1,0:T(8,128)(2,1)}) %reduce-scatter.2.cloned.1.call-update) | async-done | bytes 294928 | tf_op jit(solution)/shard_map/reduce_scatter | solution.py:727
  257.1 1.4 collective-permute-start.21
  262.0 1.8 collect.1
  (248 shorter events, 48.2 us)
Async XLA Ops:
  7.2 9.0 %copy-start.19 = (bf16[3,24,768]{2,1,0:T(8,128)(2,1)S(1)}, bf16[3,24,768]{2,1,0:T(8,128)(2,1)}, u32[]{:S(2)}) copy-start(bf16[3,24,768]{2,1,0:T(8,128)(2,1)} %w_ref.1) | copy-start | bytes 331780
  7.2 100.2 %all-gather.5.cloned.1.call-start = ((), (), s32[]{:S(2)}) async-start(), calls=%async_computation.10 | async-start | bytes 2654208 | tf_op jit(solution)/shard_map/all_gather | solution.py:613
  8.3 11.4 %collective-permute-start = (bf16[64,768]{1,0:T(8,128)(2,1)S(1)}, bf16[64,768]{1,0:T(8,128)(2,1)S(1)}, u32[]{:S(2)}, u32[]{:S(2)}) collective-permute-start(bf16[64,768]{1,0:T(8,128)(2,1)S(1)} %get-tuple-element.163), channel_id=1, source_target_pairs={{0,4},{1,5},{2,6},{3,7},{4,0},{5,1},{6,2},{7,3},{8,12},{9,13},{10,... | collective-permute-start | bytes 294920 | tf_op jit(solution)/shard_map/ppermute | solution.py:580
  13.7 3.8 %collective-permute-start.1 = (bf16[24,768]{1,0:T(8,128)(2,1)S(1)}, bf16[24,768]{1,0:T(8,128)(2,1)S(1)}, u32[]{:S(2)}, u32[]{:S(2)}) collective-permute-start(bf16[24,768]{1,0:T(8,128)(2,1)S(1)} %bitcast.181), channel_id=1, source_target_pairs={{0,24},{8,16},{16,8},{24,0},{1,25},{9,17},{17,9},{25,1},{2,26},{10... | collective-permute-start | bytes 110600 | tf_op jit(solution)/shard_map/ppermute | solution.py:540
  14.5 4.3 %collective-permute-start.2 = (bf16[24,768]{1,0:T(8,128)(2,1)S(1)}, bf16[24,768]{1,0:T(8,128)(2,1)S(1)}, u32[]{:S(2)}, u32[]{:S(2)}) collective-permute-start(bf16[24,768]{1,0:T(8,128)(2,1)S(1)} %bitcast.182), channel_id=1, source_target_pairs={{0,16},{16,0},{8,24},{24,8},{1,17},{17,1},{9,25},{25,9},{2,18},{18... | collective-permute-start | bytes 110600 | tf_op jit(solution)/shard_map/ppermute | solution.py:493
  15.4 3.4 %collective-permute-start.3 = (bf16[24,768]{1,0:T(8,128)(2,1)S(1)}, bf16[24,768]{1,0:T(8,128)(2,1)S(1)}, u32[]{:S(2)}, u32[]{:S(2)}) collective-permute-start(bf16[24,768]{1,0:T(8,128)(2,1)S(1)} %bitcast.183), channel_id=1, source_target_pairs={{0,8},{8,0},{16,24},{24,16},{1,9},{9,1},{17,25},{25,17},{2,10},{10... | collective-permute-start | bytes 110600 | tf_op jit(solution)/shard_map/ppermute | solution.py:489
  37.8 34.2 %all-to-all-start = ((bf16[8,128,768]{2,1,0:T(8,128)(2,1)}), bf16[8,128,768]{2,1,0:T(8,128)(2,1)S(1)}, u32[]{:S(2)}, u32[]{:S(2)}) async-start(bf16[8,128,768]{2,1,0:T(8,128)(2,1)} %broadcast_in_dim.65), calls=%async_computation | async-start | bytes 3145728 | tf_op jit(solution)/shard_map/all_to_all | solution.py:497
  41.3 177.7 %all-gather.7.cloned.1.call-start = ((), (), s32[]{:S(2)}) async-start(), calls=%async_computation.11 | async-start | bytes 3649536 | tf_op jit(solution)/shard_map/all_gather | solution.py:614
  71.9 13.6 %copy-start = (bf16[8,128,768]{2,1,0:T(8,128)(2,1)}, bf16[8,128,768]{2,1,0:T(8,128)(2,1)S(1)}, u32[]{:S(2)}) copy-start(bf16[8,128,768]{2,1,0:T(8,128)(2,1)S(1)} %all-to-all-done.a_ref) | copy-start | bytes 4718596
  71.9 10.5 %collective-permute-start.5 = (bf16[8,128,768]{2,1,0:T(8,128)(2,1)S(1)}, bf16[8,128,768]{2,1,0:T(8,128)(2,1)S(1)}, u32[]{:S(2)}, u32[]{:S(2)}) collective-permute-start(bf16[8,128,768]{2,1,0:T(8,128)(2,1)S(1)} %all-to-all-done.a_ref), channel_id=1, source_target_pairs={{0,8},{8,0},{16,24},{24,16},{1,9},{9,1},{17,25},{25,17},{2,10},{10... | collective-permute-start | bytes 4718600 | tf_op jit(solution)/shard_map/ppermute | solution.py:489
  76.3 24.1 %all-to-all-start.2 = ((bf16[8,24,768]{2,1,0:T(8,128)(2,1)}), bf16[8,24,768]{2,1,0:T(8,128)(2,1)}, u32[]{:S(2)}, u32[]{:S(2)}) async-start(bf16[8,24,768]{2,1,0:T(8,128)(2,1)} %broadcast_in_dim.66), calls=%async_computation.2 | async-start | bytes 589824 | tf_op jit(solution)/shard_map/all_to_all | solution.py:497
  100.4 17.9 %all-to-all-start.3 = ((bf16[32,32,128]{2,1,0:T(8,128)(2,1)}), bf16[32,32,128]{2,1,0:T(8,128)(2,1)S(1)}, u32[]{:S(2)}, u32[]{:S(2)}) async-start(bf16[32,32,128]{2,1,0:T(8,128)(2,1)} %get-tuple-element.84), calls=%async_computation.3 | async-start | bytes 524288 | tf_op jit(solution)/shard_map/all_to_all | solution.py:497
  105.4 150.6 %reduce-scatter.2.cloned.1.call-start = ((), (), s32[]{:S(2)}) async-start(), calls=%async_computation.9 | async-start | bytes 2654208 | tf_op jit(solution)/shard_map/reduce_scatter | solution.py:727
  105.6 12.7 %collective-permute-start.4 = (bf16[192,768]{1,0:T(8,128)(2,1)}, bf16[192,768]{1,0:T(8,128)(2,1)S(1)}, u32[]{:S(2)}, u32[]{:S(2)}) collective-permute-start(bf16[192,768]{1,0:T(8,128)(2,1)} %bitcast.16), channel_id=1, source_target_pairs={{0,16},{16,0},{8,24},{24,8},{1,17},{17,1},{9,25},{25,9},{2,18},{18... | collective-permute-start | bytes 884744 | tf_op jit(solution)/shard_map/ppermute | solution.py:493
  107.5 10.9 %collective-permute-start.7 = (bf16[192,768]{1,0:T(8,128)(2,1)}, bf16[192,768]{1,0:T(8,128)(2,1)S(1)}, u32[]{:S(2)}, u32[]{:S(2)}) collective-permute-start(bf16[192,768]{1,0:T(8,128)(2,1)} %bitcast.16), channel_id=1, source_target_pairs={{0,8},{8,0},{16,24},{24,16},{1,9},{9,1},{17,25},{25,17},{2,10},{10... | collective-permute-start | bytes 884744 | tf_op jit(solution)/shard_map/ppermute | solution.py:489
  118.3 1.6 collective-permute-start.6
  121.2 10.5 %copy-start.38 = (f32[1,768]{1,0:T(1,128)S(1)}, f32[1,768]{1,0:T(1,128)}, u32[]{:S(2)}) copy-start(f32[1,768]{1,0:T(1,128)} %constant_dynamic-slice_fusion.1.bias_ref) | copy-start | bytes 9220
  123.3 10.9 %copy-start.27 = (bf16[128,768]{1,0:T(8,128)(2,1)}, bf16[128,768]{1,0:T(8,128)(2,1)S(1)}, u32[]{:S(2)}) copy-start(bf16[128,768]{1,0:T(8,128)(2,1)S(1)} %get-tuple-element.121) | copy-start | bytes 589828
  123.3 19.8 %copy-start.8 = (f32[128,768]{1,0:T(8,128)}, f32[128,768]{1,0:T(8,128)S(1)}, u32[]{:S(2)}) copy-start(f32[128,768]{1,0:T(8,128)S(1)} %get-tuple-element.98.normed_ref) | copy-start | bytes 1179652
  123.3 6.9 %collective-permute-start.8 = (bf16[128,768]{1,0:T(8,128)(2,1)S(1)}, bf16[128,768]{1,0:T(8,128)(2,1)S(1)}, u32[]{:S(2)}, u32[]{:S(2)}) collective-permute-start(bf16[128,768]{1,0:T(8,128)(2,1)S(1)} %get-tuple-element.90.a_ref), channel_id=1, source_target_pairs={{0,16},{16,0},{8,24},{24,8},{1,17},{17,1},{9,25},{25,9},{2,18},{18... | collective-permute-start | bytes 589832 | tf_op jit(solution)/shard_map/ppermute | solution.py:493
  124.2 6.0 %collective-permute-start.9 = (bf16[128,768]{1,0:T(8,128)(2,1)S(1)}, bf16[128,768]{1,0:T(8,128)(2,1)S(1)}, u32[]{:S(2)}, u32[]{:S(2)}) collective-permute-start(bf16[128,768]{1,0:T(8,128)(2,1)S(1)} %get-tuple-element.90.a_ref), channel_id=1, source_target_pairs={{0,8},{8,0},{16,24},{24,16},{1,9},{9,1},{17,25},{25,17},{2,10},{10... | collective-permute-start | bytes 589832 | tf_op jit(solution)/shard_map/ppermute | solution.py:489
  130.3 1.4 collective-permute-start.10
  134.3 8.9 %copy-start.26 = (bf16[2,64,768]{2,1,0:T(8,128)(2,1)S(1)}, bf16[2,64,768]{2,1,0:T(8,128)(2,1)}, u32[]{:S(2)}) copy-start(bf16[2,64,768]{2,1,0:T(8,128)(2,1)} %param.13) | copy-start | bytes 589828
  134.3 1.8 collective-permute-start.11
  136.1 7.0 %collective-permute-start.12 = (bf16[128,768]{1,0:T(8,128)(2,1)S(1)}, bf16[128,768]{1,0:T(8,128)(2,1)S(1)}, u32[]{:S(2)}, u32[]{:S(2)}) collective-permute-start(bf16[128,768]{1,0:T(8,128)(2,1)S(1)} %get-tuple-element.97), channel_id=1, source_target_pairs={{0,16},{16,0},{8,24},{24,8},{1,17},{17,1},{9,25},{25,9},{2,18},{18... | collective-permute-start | bytes 589832 | tf_op jit(solution)/shard_map/ppermute | solution.py:493
  144.9 11.9 %copy-start.34 = (f32[8,768]{1,0:T(8,128)}, f32[8,768]{1,0:T(8,128)S(1)}, u32[]{:S(2)}) copy-start(f32[8,768]{1,0:T(8,128)S(1)} %get-tuple-element.129) | copy-start | bytes 73732
  144.9 7.6 %collective-permute-start.13 = (bf16[128,768]{1,0:T(8,128)(2,1)S(1)}, bf16[128,768]{1,0:T(8,128)(2,1)S(1)}, u32[]{:S(2)}, u32[]{:S(2)}) collective-permute-start(bf16[128,768]{1,0:T(8,128)(2,1)S(1)} %get-tuple-element.105.a_ref), channel_id=1, source_target_pairs={{0,16},{16,0},{8,24},{24,8},{1,17},{17,1},{9,25},{25,9},{2,18},{18... | collective-permute-start | bytes 589832 | tf_op jit(solution)/shard_map/ppermute | solution.py:493
  145.8 6.7 %collective-permute-start.14 = (bf16[128,768]{1,0:T(8,128)(2,1)S(1)}, bf16[128,768]{1,0:T(8,128)(2,1)S(1)}, u32[]{:S(2)}, u32[]{:S(2)}) collective-permute-start(bf16[128,768]{1,0:T(8,128)(2,1)S(1)} %get-tuple-element.105.a_ref), channel_id=1, source_target_pairs={{0,8},{8,0},{16,24},{24,16},{1,9},{9,1},{17,25},{25,17},{2,10},{10... | collective-permute-start | bytes 589832 | tf_op jit(solution)/shard_map/ppermute | solution.py:489
  152.5 1.4 collective-permute-start.15
  156.9 1.8 collective-permute-start.16
  158.7 7.5 %collective-permute-start.17 = (bf16[128,768]{1,0:T(8,128)(2,1)S(1)}, bf16[128,768]{1,0:T(8,128)(2,1)S(1)}, u32[]{:S(2)}, u32[]{:S(2)}) collective-permute-start(bf16[128,768]{1,0:T(8,128)(2,1)S(1)} %get-tuple-element.110), channel_id=1, source_target_pairs={{0,16},{16,0},{8,24},{24,8},{1,17},{17,1},{9,25},{25,9},{2,18},{18... | collective-permute-start | bytes 589832 | tf_op jit(solution)/shard_map/ppermute | solution.py:493
  168.7 2.1 collective-permute-start.18
  171.9 9.5 %collective-permute-start.19 = (bf16[192,768]{1,0:T(8,128)(2,1)S(1)}, bf16[192,768]{1,0:T(8,128)(2,1)S(1)}, u32[]{:S(2)}, u32[]{:S(2)}) collective-permute-start(bf16[192,768]{1,0:T(8,128)(2,1)S(1)} %fusion.6), channel_id=1, source_target_pairs={{0,16},{16,0},{8,24},{24,8},{1,17},{17,1},{9,25},{25,9},{2,18},{18... | collective-permute-start | bytes 884744 | tf_op jit(solution)/shard_map/ppermute | solution.py:493
  173.6 19.7 %all-to-all-start.4 = ((bf16[32,32,128]{2,1,0:T(8,128)(2,1)}), bf16[32,32,128]{2,1,0:T(8,128)(2,1)S(1)}, u32[]{:S(2)}, u32[]{:S(2)}) async-start(bf16[32,32,128]{2,1,0:T(8,128)(2,1)} %get-tuple-element.119), calls=%async_computation.4 | async-start | bytes 524288 | tf_op jit(solution)/shard_map/all_to_all | solution.py:497
  177.1 19.6 %copy-start.5 = (bf16[2048,64]{1,0:T(8,128)(2,1)S(1)}, bf16[2048,64]{1,0:T(8,128)(2,1)}, u32[]{:S(2)}) copy-start(bf16[2048,64]{1,0:T(8,128)(2,1)} %copy-done.4) | copy-start | bytes 786436
  177.1 19.6 %copy-start.7 = (bf16[2048,64]{1,0:T(8,128)(2,1)S(1)}, bf16[2048,64]{1,0:T(8,128)(2,1)}, u32[]{:S(2)}) copy-start(bf16[2048,64]{1,0:T(8,128)(2,1)} %copy-done.6) | copy-start | bytes 786436
  177.1 19.6 %copy-start.16 = (bf16[2048,64]{1,0:T(8,128)(2,1)S(1)}, bf16[2048,64]{1,0:T(8,128)(2,1)}, u32[]{:S(2)}) copy-start(bf16[2048,64]{1,0:T(8,128)(2,1)} %copy-done.15) | copy-start | bytes 786436
  177.1 19.6 %copy-start.18 = (f32[64,2048]{1,0:T(8,128)S(1)}, f32[64,2048]{1,0:T(8,128)}, u32[]{:S(2)}) copy-start(f32[64,2048]{1,0:T(8,128)} %copy-done.17) | copy-start | bytes 1572868
  177.1 19.6 %copy-start.25 = (bf16[64,2048]{1,0:T(8,128)(2,1)S(1)}, bf16[64,2048]{1,0:T(8,128)(2,1)}, u32[]{:S(2)}) copy-start(bf16[64,2048]{1,0:T(8,128)(2,1)} %copy-done.24) | copy-start | bytes 786436
  177.1 19.6 %copy-start.40 = (f32[1,2048]{1,0:T(1,128)S(1)}, f32[1,2048]{1,0:T(1,128)}, u32[]{:S(2)}) copy-start(f32[1,2048]{1,0:T(1,128)} %copy-done.39) | copy-start | bytes 24580
  177.1 19.6 %copy-start.46 = (s32[4]{0:T(128)S(1)}, s32[4]{0:T(128)}, u32[]{:S(2)}) copy-start(s32[4]{0:T(128)} %get-tuple-element.191.lo_ref) | copy-start | bytes 52
  177.2 19.6 %copy-start.47 = (s32[4]{0:T(128)S(1)}, s32[4]{0:T(128)}, u32[]{:S(2)}) copy-start(s32[4]{0:T(128)} %get-tuple-element.194.hi_ref) | copy-start | bytes 52
  193.3 18.4 %all-to-all-start.5 = ((bf16[8,24,768]{2,1,0:T(8,128)(2,1)}), bf16[8,24,768]{2,1,0:T(8,128)(2,1)S(1)}, u32[]{:S(2)}, u32[]{:S(2)}) async-start(bf16[8,24,768]{2,1,0:T(8,128)(2,1)} %bitcast.40), calls=%async_computation.5 | async-start | bytes 589824 | tf_op jit(solution)/shard_map/all_to_all | solution.py:497
  211.7 27.2 %all-to-all-start.6 = ((bf16[32,96,128]{2,1,0:T(8,128)(2,1)}), bf16[32,96,128]{2,1,0:T(8,128)(2,1)}, u32[]{:S(2)}, u32[]{:S(2)}) async-start(bf16[32,96,128]{2,1,0:T(8,128)(2,1)} %get-tuple-element.123), calls=%async_computation.6 | async-start | bytes 1572864 | tf_op jit(solution)/shard_map/all_to_all | solution.py:497
  238.9 23.1 %all-to-all-start.7 = ((bf16[32,24,256]{2,1,0:T(8,128)(2,1)}), bf16[32,24,256]{2,1,0:T(8,128)(2,1)}, u32[]{:S(2)}, u32[]{:S(2)}) async-start(bf16[32,24,256]{2,1,0:T(8,128)(2,1)} %pad_maximum_fusion.2), calls=%async_computation.7 | async-start | bytes 786432 | tf_op jit(solution)/shard_map/all_to_all | solution.py:497
  257.0 3.8 %collective-permute-start.20 = (bf16[24,768]{1,0:T(8,128)(2,1)S(1)}, bf16[24,768]{1,0:T(8,128)(2,1)S(1)}, u32[]{:S(2)}, u32[]{:S(2)}) collective-permute-start(bf16[24,768]{1,0:T(8,128)(2,1)S(1)} %get-tuple-element.168), channel_id=1, source_target_pairs={{0,24},{8,16},{16,8},{24,0},{1,25},{9,17},{17,9},{25,1},{2,26},{10... | collective-permute-start | bytes 110600 | tf_op jit(solution)/shard_map/ppermute | solution.py:540
  257.1 4.2 %collective-permute-start.21 = (bf16[24,768]{1,0:T(8,128)(2,1)S(1)}, bf16[24,768]{1,0:T(8,128)(2,1)S(1)}, u32[]{:S(2)}, u32[]{:S(2)}) collective-permute-start(bf16[24,768]{1,0:T(8,128)(2,1)S(1)} %get-tuple-element.167), channel_id=1, source_target_pairs={{0,16},{16,0},{8,24},{24,8},{1,17},{17,1},{9,25},{25,9},{2,18},{18... | collective-permute-start | bytes 110600 | tf_op jit(solution)/shard_map/ppermute | solution.py:493
  258.5 2.8 %collective-permute-start.22 = (bf16[24,768]{1,0:T(8,128)(2,1)S(1)}, bf16[24,768]{1,0:T(8,128)(2,1)S(1)}, u32[]{:S(2)}, u32[]{:S(2)}) collective-permute-start(bf16[24,768]{1,0:T(8,128)(2,1)S(1)} %get-tuple-element.166), channel_id=1, source_target_pairs={{0,8},{8,0},{16,24},{24,16},{1,9},{9,1},{17,25},{25,17},{2,10},{10... | collective-permute-start | bytes 110600 | tf_op jit(solution)/shard_map/ppermute | solution.py:489
  (48 other events, 148.9 us)
Sparse Core Ops, SparseCore 0:
  36.6 66.5 all-gather.4
  106.1 60.1 all-gather.6
  169.7 86.2 reduce-scatter.1

commit v6 on v5

--- a/solution.py
+++ b/solution.py
@@ -87,15 +87,18 @@
         out_shape=(rows, rows, rows, columns, columns),
         in_specs=[SMEM] + [VMEM] * 5,
         out_specs=(VMEM,) * 5,
-        compiler_params=SMALL if length <= 4096 else LARGE,
+        compiler_params=LARGE,
         cost_estimate=pl.CostEstimate(flops=1000000, bytes_accessed=1 << 10, transcendentals=0),
         name="project",
     )(place, a, b, qk, v, bias)
 
 
-def head_slots_kernel(w_ref, small_ref, out_ref, *, units):
-    hd = small_ref.shape[1]
-    small = small_ref[...]
+def head_slots_kernel(w_ref, bias_ref, gains_ref, shifts_ref, inner_ref, out_ref, *, units):
+    hd = w_ref.shape[2] // HEADS
+    rows = [ref[...].astype(F32) for ref in (bias_ref, gains_ref, shifts_ref)]
+    inner = inner_ref[...].astype(F32)
+    blank = jnp.zeros((inner.shape[0], hd - 8 - inner.shape[1]), F32)
+    small = jnp.concatenate([jnp.concatenate(rows, axis=0).T, inner, blank], axis=1).astype(BF)
     done = {}
     for d, j in enumerate(units):
         if j not in done:
@@ -199,7 +202,7 @@
         in_specs=[SMEM, SMEM] + [VMEM] * 4,
         out_specs=(VMEM,) * 3,
         scratch_shapes=[pltpu.VMEM((length, bq), F32)],
-        compiler_params=SMALL if length <= 4096 else LARGE,
+        compiler_params=LARGE,
         cost_estimate=pl.CostEstimate(flops=1000000, bytes_accessed=1 << 10, transcendentals=0),
         name="attend",
     )(lo, hi, q, k, vt, spans)
@@ -281,20 +284,20 @@
             pltpu.VMEM((length, hd), F32),
             pltpu.VMEM((length, hd), F32),
         ],
-        compiler_params=SMALL if length <= 4096 else LARGE,
+        compiler_params=LARGE,
         cost_estimate=pl.CostEstimate(flops=1000000, bytes_accessed=1 << 10, transcendentals=0),
         name="attend_back",
     )(lo, hi, q, k, v, kt, ot, lse, do, spans)
 
 
-def call(kernel, outs, ins, name, flops, scratch=()):
+def call(kernel, outs, ins, name, flops, scratch=(), params=SMALL):
     return pl.pallas_call(
         kernel,
         out_shape=tuple(jax.ShapeDtypeStruct(shape, kind) for shape, kind in outs),
         in_specs=[SMEM if v.dtype == jnp.int32 else VMEM for v in ins],
         out_specs=(VMEM,) * len(outs),
         scratch_shapes=list(scratch),
-        compiler_params=SMALL,
+        compiler_params=params,
         cost_estimate=pl.CostEstimate(
             flops=int(flops), bytes_accessed=1 << 10, transcendentals=0
         ),
@@ -584,22 +587,20 @@
         for c in range(2)
         for s in range(2)
     ]
-    inner_own = inner_weight.reshape(rows_dev, groups, ff_part)
+    inner_own = after(inner_weight, pair_x).reshape(rows_dev, groups, ff_part)
     inner_own = to_group(inner_own.transpose(1, 0, 2)).reshape(groups * rows_dev, ff_part)
-    ffn = jnp.concatenate([inner_own, outer_weight])
-
-    vectors = [bias_rows.T, norm_gains.T, norm_shifts.T, inner_bias.reshape(rows_dev, -1)]
-    small = jnp.concatenate(vectors, axis=1)
-    small = jnp.pad(small, ((0, 0), (0, hd - small.shape[1])))
+    ffn = jnp.concatenate([inner_own, outer_weight, out_weight])
+
     units = tuple(h * heads_dev + u for h in range(groups) for u in unit_of * 2)
     (slots,) = call(
         functools.partial(head_slots_kernel, units=units),
         (((devices, 2, rows_dev, 2 * hd), BF),),
-        (qkv_weight, small),
+        (qkv_weight, bias_rows, norm_gains, norm_shifts, inner_bias.reshape(rows_dev, -1)),
         "head_slots",
         1e6,
-    )
-    slots = swap(after(slots, pair_x, ffn), BOTH)
+        params=LARGE,
+    )
+    slots = swap(slots, BOTH)
     qk_weight = slots[:, 0].reshape(depth, 2 * hd)
     v_weight = slots[:, 1].reshape(depth, 2 * hd)
     small = slots[:, 1, :, hd : hd + 12].astype(F32).reshape(depth, 12).T
@@ -610,20 +611,8 @@
     unit_bias = lax.dynamic_slice(bias[0:2], (0, unit_head * hd), (2, hd))
     unit_bias = jnp.pad(unit_bias, ((0, 0), (0, hd)))
 
+    qkv_all = lax.all_gather(after(qkv_weight, ffn), BOTH, axis=0, tiled=False)
     ffn_all = lax.all_gather(after(ffn, slots), "blk", axis=0, tiled=False)
-    qkv_all = lax.all_gather(after(qkv_weight, ffn), BOTH, axis=0, tiled=False)
-    small_rows = (
-        stack_rows(bias[2], gains[0], shifts[0]),
-        stack_rows(gains[0], shifts[0], bias[3], gains[1], shifts[1]),
-        stack_rows(gains[0]),
-        inner_bias_part[None],
-    )
-    tokens_a, qk_weight, v_weight, unit_bias, small_rows = lax.optimization_barrier(
-        (spread_over(pair_x, BOTH, cycle, cube), qk_weight, v_weight, unit_bias, small_rows)
-    )
-    tokens_b = by_core(tokens_a)
-    out_part = spread_over(after(out_weight, tokens_a), "blk", cycle).reshape(depth // groups, depth)
-
     lengths = lax.dynamic_index_in_dim(doc_lengths, half, 0, keepdims=False)
     order = jnp.arange(lengths.shape[0], dtype=jnp.int32)
     bounds = jnp.sum(jnp.where(order[None, :] <= order[:, None], lengths[None, :], 0), axis=1)
@@ -638,12 +627,25 @@
     )
 
     place = jnp.stack([head_index % 2, half]).astype(jnp.int32)
+    block = 512 if length <= 4096 else 256
+    ranges = key_ranges(spans, block, 512), key_ranges(spans, 512, 256)
+    small_rows = (
+        stack_rows(bias[2], gains[0], shifts[0]),
+        stack_rows(gains[0], shifts[0], bias[3], gains[1], shifts[1]),
+        stack_rows(gains[0]),
+        inner_bias_part[None],
+    )
+    tokens_a = spread_over(pair_x, BOTH, cycle, cube)
+    prepared = (qk_weight, v_weight, unit_bias, small_rows, spans, place, ranges)
+    tokens_a, prepared = lax.optimization_barrier((tokens_a, prepared))
+    qk_weight, v_weight, unit_bias, small_rows, spans, place, ranges = prepared
+    tokens_b = by_core(tokens_a)
+
     per = max(1, 256 // tokens)
     q, k, v, kt, vt = project(
         place, tokens_a, tokens_b, qk_weight, v_weight, unit_bias, halves, per
     )
-    block = 512 if length <= 4096 else 256
-    lo, hi = key_ranges(spans, block, 512)
+    lo, hi = ranges[0]
     attn_out, attn_t, lse = attend(lo, hi, q, k, vt, spans, tokens, block, 512)
 
     ffn = after(ffn_all, attn_out)
@@ -653,7 +655,9 @@
         .transpose(1, 0, 2, 3)
         .reshape(depth, ff_part)
     )
-    outer_part = ffn[:, groups * rows_dev :].reshape(ff_part, depth)
+    last = groups * rows_dev + ff_dev
+    outer_part = ffn[:, groups * rows_dev : last].reshape(ff_part, depth)
+    out_part = ffn[:, last:].reshape(depth // groups, depth)
     attn_slots = swap(attn_out, BOTH)
     out_x, attn_slots, inner_part, outer_part = lax.optimization_barrier(
         (by_x(out_part), attn_slots, inner_part, outer_part)
@@ -724,9 +728,9 @@
     )
     d_heads = swap(d_heads, BOTH)
 
-    ffn_grad = lax.psum_scatter(ffn_grad, "blk", scatter_dimension=0, tiled=False).astype(F32)
-    outer_grad = ffn_grad[groups:].reshape(ff_dev, depth)
-    inner_grad = to_group(ffn_grad[:groups].astype(BF))
+    ffn_grad = lax.psum_scatter(ffn_grad, "blk", scatter_dimension=0, tiled=False)
+    outer_grad = ffn_grad[groups:].reshape(ff_dev, depth).astype(F32)
+    inner_grad = to_group(ffn_grad[:groups])
     inner_grad = inner_grad.transpose(1, 0, 2).reshape(rows_dev, groups * ff_part).astype(F32)
     out_grad = dot(attn, d_branch, TN).reshape(groups, depth // groups, depth)
 
@@ -741,7 +745,7 @@
         out_terms.astype(F32), axis=0
     )
 
-    lo, hi = key_ranges(spans, 512, 256)
+    lo, hi = ranges[1]
     qkv_out, qkv_t, qv_sums = attend_back(
         lo, hi, q, k, v, kt, attn_t, lse, d_heads, spans, tokens, 512, 256
     )
@@ -776,8 +780,7 @@
     ).astype(BF)
     extra = jnp.pad(extra, ((0, 0), (0, 0), (0, hd - extra.shape[2])))
     final = jnp.concatenate([unit_grad.reshape(devices, rows_dev, 3 * hd), extra], axis=2)
-    final = swap(after(final, qkv_home), BOTH)
-    final, inner_grad = lax.optimization_barrier((final, inner_grad))
+    final = after(swap(after(final, qkv_home), BOTH), grad_inputs)
     qkv_grad, bias_grad, gains_grad, shifts_grad, inner_bias_grad = call(
         functools.partial(collect_kernel, layout=layout),
         (

time: 272 us -> 272 us (level)
  waiting for transfers between devices: 99.3 us -> 124 us
  blocking collectives: 16.8 us -> 0 us
  local copies, waits for them, and re-layouts: 38.7 us -> 30.6 us
    all_to_all x7, waiting for transfers between devices: 41.1 us -> 58.4 us  [swap(): lax.all_to_all(value, axes, split_axis=0, concat_axis=0, tiled=True, axis...]
    all_to_all x1 -> x0, blocking collectives: 16.8 us -> none  [swap(): lax.all_to_all(value, axes, split_axis=0, concat_axis=0, tiled=True, axis...]
    all_gather x1, waiting for transfers between devices: 0.01 us -> 11.9 us  [local(): ffn_all = lax.all_gather(after(ffn, slots), 'blk', axis=0, tiled=False)]
    unnamed x132 -> x69, local copies, waits for them, and re-layouts: 14.9 us -> 5.36 us
    reduce_scatter x1, waiting for transfers between devices: 9.56 us -> 3.18 us  [local(): lax.psum_scatter(ffn_grad, 'blk', scatter_dimension=0, tiled=False)]
    ppermute x12, waiting for transfers between devices: 9.61 us -> 13 us  [by_core(): return lax.ppermute(value, 'head', [(0, 1), (1, 0), (2, 3), (3, 2)])]
  transfers between devices with their start and end apart: 33 -> 33, of which waited for: 20 -> 25; matrix products, arithmetic and copies ran while one was open for 12% -> 13% of each run, Pallas kernels for 16% -> 16%
where the time goes in v6:
time: 272 us
  waiting for transfers between devices  124 us (46%)
  starting transfers between devices  45.9 us (17%)
  Pallas kernels  44.5 us (16%)
  local copies, waits for them, and re-layouts  30.6 us (11%)
  between operations  14.5 us (5%)
  other arithmetic  11.4 us (4%)
    all_to_all x7, waiting for transfers between devices, swap(): lax.all_to_all(value, axes, split_axis=0, concat_axis=0, tiled=True, axis...  58.4 us
    ppermute x8, waiting for transfers between devices, by_x(): return lax.ppermute(value, 'head', [(0, 2), (2, 0), (1, 3), (3, 1)])  33.6 us
    all_to_all x7, starting transfers between devices, swap(): lax.all_to_all(value, axes, split_axis=0, concat_axis=0, tiled=True, axis...  28.9 us
    pallas_call x11, Pallas kernels, call(): pl.pallas_call(kernel, out_shape=tuple((jax.ShapeDtypeStruct(shape, kind)...  17.6 us
    ppermute x12, waiting for transfers between devices, by_core(): return lax.ppermute(value, 'head', [(0, 1), (1, 0), (2, 3), (3, 2)])  13 us
    pallas_call x1, Pallas kernels, attend_back(): pl.pallas_call(functools.partial(attend_back_kernel, bq=bq, bk=bk, pack=p...  12.1 us
    all_gather x1, waiting for transfers between devices, local(): ffn_all = lax.all_gather(after(ffn, slots), 'blk', axis=0, tiled=False)  11.9 us
    ppermute x8, starting transfers between devices, by_x(): return lax.ppermute(value, 'head', [(0, 2), (2, 0), (1, 3), (3, 1)])  9.08 us
  transfers between devices with their start and end apart: 33, of which 25 were waited for; matrix products, arithmetic and copies ran while one was open for 13% of the time, Pallas kernels for 16%

profile of v6, /device:TPU:0, one launch (start us, length us, event | category | flops | bytes accessed | tf_op | source)
XLA Modules:
  0.0 271.7 jit_solution(4669556559339884102)
XLA Ops:
  8.2 4.1 %collective-permute-start = (bf16[64,768]{1,0:T(8,128)(2,1)S(1)}, bf16[64,768]{1,0:T(8,128)(2,1)S(1)}, u32[]{:S(2)}, u32[]{:S(2)}) collective-permute-start(bf16[64,768]{1,0:T(8,128)(2,1)S(1)} %get-tuple-element.171), channel_id=1, source_target_pairs={{0,4},{1,5},{2,6},{3,7},{4,0},{5,1},{6,2},{7,3},{8,12},{9,13},{10,... | collective-permute-start | bytes 294920 | tf_op jit(solution)/shard_map/ppermute | solution.py:583
  13.7 1.9 head_slots.1
  15.5 3.8 %all-to-all-start = ((bf16[32,2,24,128]{3,2,1,0:T(8,128)(2,1)}), bf16[32,2,24,128]{3,2,1,0:T(8,128)(2,1)S(1)}, u32[]{:S(2)}, u32[]{:S(2)}) async-start(bf16[32,2,24,128]{3,2,1,0:T(8,128)(2,1)} %head_slots.1), calls=%async_computation | async-start | bytes 786432 | tf_op jit(solution)/shard_map/all_to_all | solution.py:500
  19.9 1.6 collective-permute-start.1
  22.0 2.6 collective-permute-done.1
  24.6 2.0 collective-permute-done.2
  27.4 5.5 %all-to-all-done = bf16[32,2,24,128]{3,2,1,0:T(8,128)(2,1)S(1)} async-done(((bf16[32,2,24,128]{3,2,1,0:T(8,128)(2,1)}), bf16[32,2,24,128]{3,2,1,0:T(8,128)(2,1)S(1)}, u32[]{:S(2)}, u32[]{:S(2)}) %all-to-all-start) | async-done | bytes 393248 | tf_op jit(solution)/shard_map/all_to_all | solution.py:500
  34.3 3.7 %all-to-all-start.1 = ((bf16[8,128,768]{2,1,0:T(8,128)(2,1)}), bf16[8,128,768]{2,1,0:T(8,128)(2,1)S(1)}, u32[]{:S(2)}, u32[]{:S(2)}) async-start(bf16[8,128,768]{2,1,0:T(8,128)(2,1)} %broadcast_in_dim.59), calls=%async_computation.1 | async-start | bytes 3145728 | tf_op jit(solution)/shard_map/all_to_all | solution.py:500
  45.2 24.6 %all-to-all-done.1.a_ref = bf16[8,128,768]{2,1,0:T(8,128)(2,1)S(1)} async-done(((bf16[8,128,768]{2,1,0:T(8,128)(2,1)}), bf16[8,128,768]{2,1,0:T(8,128)(2,1)S(1)}, u32[]{:S(2)}, u32[]{:S(2)}) %all-to-all-start.1) | async-done | bytes 1572896 | tf_op jit(solution)/shard_map/all_to_all | solution.py:500
  69.7 3.4 %collective-permute-done.4.b_ref = bf16[8,128,768]{2,1,0:T(8,128)(2,1)S(1)} collective-permute-done((bf16[8,128,768]{2,1,0:T(8,128)(2,1)S(1)}, bf16[8,128,768]{2,1,0:T(8,128)(2,1)S(1)}, u32[]{:S(2)}, u32[]{:S(2)}) %collective-permute-start.4) | collective-permute-done | bytes 1572896 | tf_op jit(solution)/shard_map/ppermute | solution.py:492
  74.3 5.0 %project.1 = (bf16[2048,64]{1,0:T(8,128)(2,1)}, bf16[2048,64]{1,0:T(8,128)(2,1)}, bf16[2048,64]{1,0:T(8,128)(2,1)}, bf16[64,2048]{1,0:T(8,128)(2,1)}, bf16[64,2048]{1,0:T(8,128)(2,1)}) custom-call(s32[2]{0:T(128)} %pad_add_fusion.1.place_ref, bf16[8,128,768]{2,1,0:T(8,128)(2,1)} %copy-done, bf16[8,128,768]{2,1,0:T(8,128)(2,1)} %copy-done.2, ...), custom_call_target="tpu_custom_call" | custom-call | flops 1000000 | bytes 1024 | tf_op jit(solution)/shard_map/project/pallas_call | solution.py:85
  79.3 8.4 %attend.1 = (bf16[32,32,128]{2,1,0:T(8,128)(2,1)}, f32[64,2048]{1,0:T(8,128)}, f32[1,2048]{1,0:T(1,128)}) custom-call(s32[4]{0:T(128)} %get-tuple-element.81.lo_ref, s32[4]{0:T(128)} %get-tuple-element.82.hi_ref, bf16[2048,64]{1,0:T(8,128)(2,1)} %get-tuple-element.88.q_ref, bf16[2048,64]{1,0:T(8,128)(2,1)} %get-tuple-element.89.k_ref, ...), custom_call_target="tpu_custom_call" | custom-call | flops 1000000 | bytes 1024 | tf_op jit(solution)/shard_map/attend/pallas_call | solution.py:195
  87.7 4.2 %all-to-all-start.2 = ((bf16[32,32,128]{2,1,0:T(8,128)(2,1)}), bf16[32,32,128]{2,1,0:T(8,128)(2,1)S(1)}, u32[]{:S(2)}, u32[]{:S(2)}) async-start(bf16[32,32,128]{2,1,0:T(8,128)(2,1)} %get-tuple-element.92), calls=%async_computation.2 | async-start | bytes 524288 | tf_op jit(solution)/shard_map/all_to_all | solution.py:500
  92.2 11.9 %all-gather.5.cloned.1.call-done = bf16[1728,768]{1,0:T(8,128)(2,1)} async-done(((bf16[216,768]{1,0:T(8,128)(2,1)}), bf16[1728,768]{1,0:T(8,128)(2,1)}) %all-gather.5.cloned.1.call-update) | async-done | bytes 2654224 | tf_op jit(solution)/shard_map/all_gather | solution.py:615
  105.0 1.5 collective-permute-start.5
  106.6 1.8 fusion.14
  108.5 3.4 %collective-permute-done.5 = bf16[192,768]{1,0:T(8,128)(2,1)S(1)} collective-permute-done((bf16[192,768]{1,0:T(8,128)(2,1)S(1)}, bf16[192,768]{1,0:T(8,128)(2,1)S(1)}, u32[]{:S(2)}, u32[]{:S(2)}) %collective-permute-start.5) | collective-permute-done | bytes 294944 | tf_op jit(solution)/shard_map/ppermute | solution.py:496
  111.8 1.6 collective-permute-done.6
  115.9 1.5 collective-permute-start.8
  117.3 5.5 %collective-permute-done.8.b_ref = bf16[128,768]{1,0:T(8,128)(2,1)S(1)} collective-permute-done((bf16[128,768]{1,0:T(8,128)(2,1)S(1)}, bf16[128,768]{1,0:T(8,128)(2,1)S(1)}, u32[]{:S(2)}, u32[]{:S(2)}) %collective-permute-start.8) | collective-permute-done | bytes 196640 | tf_op jit(solution)/shard_map/ppermute | solution.py:496
  124.3 2.5 inner.1
  127.0 1.6 collective-permute-done.11.got_ref
  128.7 1.5 collective-permute-start.12
  130.2 8.7 %collective-permute-done.12.got_ref = bf16[128,768]{1,0:T(8,128)(2,1)S(1)} collective-permute-done((bf16[128,768]{1,0:T(8,128)(2,1)S(1)}, bf16[128,768]{1,0:T(8,128)(2,1)S(1)}, u32[]{:S(2)}, u32[]{:S(2)}) %collective-permute-start.12) | collective-permute-done | bytes 196640 | tf_op jit(solution)/shard_map/ppermute | solution.py:496
  142.1 4.9 %collective-permute-done.13.b_ref = bf16[128,768]{1,0:T(8,128)(2,1)S(1)} collective-permute-done((bf16[128,768]{1,0:T(8,128)(2,1)S(1)}, bf16[128,768]{1,0:T(8,128)(2,1)S(1)}, u32[]{:S(2)}, u32[]{:S(2)}) %collective-permute-start.13) | collective-permute-done | bytes 196640 | tf_op jit(solution)/shard_map/ppermute | solution.py:496
  148.5 2.9 %inner_back.1 = (bf16[512,768]{1,0:T(8,128)(2,1)S(1)}, bf16[512,768]{1,0:T(8,128)(2,1)S(1)}, f32[1,768]{1,0:T(1,128)S(1)}, f32[256,768]{1,0:T(8,128)S(1)}, bf16[256,768]{1,0:T(8,128)(2,1)S(1)}) custom-call(bf16[128,768]{1,0:T(8,128)(2,1)S(1)} %get-tuple-element.114.a_ref, bf16[128,768]{1,0:T(8,128)(2,1)S(1)} %collective-permute-done.13.b_ref, ...), custom_call_target="tpu_custom_call" | custom-call | flops 1000000 | bytes 1024 | tf_op jit(solution)/shard_map/inner_back/pallas_call | solution.py:294
  151.6 1.6 collective-permute-done.16.got_ref
  153.2 1.8 collective-permute-start.17
  155.1 2.9 %feed_grad.1 = bf16[8,8,24,768]{3,2,1,0:T(8,128)(2,1)} custom-call(bf16[512,768]{1,0:T(8,128)(2,1)S(1)} %get-tuple-element.120.low_ref, bf16[512,768]{1,0:T(8,128)(2,1)S(1)} %get-tuple-element.121.inner_ref, bf16[512,768]{1,0:T(8,128)(2,1)S(1)} %get-tuple-element.122.act_ref, bf16[512,768]{1,0:T(8,128)(2,1)S(1)} %get-tuple-element.123.ffn_ref), custom_call_target="tpu_custom_call" | custom-call | flops 1000000 | bytes 1024 | tf_op jit(solution)/shard_map/feed_grad/pallas_call | solution.py:294
  157.9 4.8 %collective-permute-done.17.got_ref = bf16[128,768]{1,0:T(8,128)(2,1)S(1)} collective-permute-done((bf16[128,768]{1,0:T(8,128)(2,1)S(1)}, bf16[128,768]{1,0:T(8,128)(2,1)S(1)}, u32[]{:S(2)}, u32[]{:S(2)}) %collective-permute-start.17) | collective-permute-done | bytes 196640 | tf_op jit(solution)/shard_map/ppermute | solution.py:496
  162.8 1.5 branch_back.1
  165.0 2.0 collective-permute-done.18
  168.3 6.0 %all-to-all-start.3 = ((bf16[32,32,128]{2,1,0:T(8,128)(2,1)}), bf16[32,32,128]{2,1,0:T(8,128)(2,1)S(1)}, u32[]{:S(2)}, u32[]{:S(2)}) async-start(bf16[32,32,128]{2,1,0:T(8,128)(2,1)} %get-tuple-element.128), calls=%async_computation.3 | async-start | bytes 524288 | tf_op jit(solution)/shard_map/all_to_all | solution.py:500
  174.3 3.0 %collective-permute-done.19 = bf16[192,768]{1,0:T(8,128)(2,1)S(1)} collective-permute-done((bf16[192,768]{1,0:T(8,128)(2,1)}, bf16[192,768]{1,0:T(8,128)(2,1)S(1)}, u32[]{:S(2)}, u32[]{:S(2)}) %collective-permute-start.19) | collective-permute-done | bytes 294944 | tf_op jit(solution)/shard_map/ppermute | solution.py:496
  177.3 1.9 fusion.3
  179.1 5.8 %all-to-all-done.3.do_ref = bf16[32,32,128]{2,1,0:T(8,128)(2,1)S(1)} async-done(((bf16[32,32,128]{2,1,0:T(8,128)(2,1)}), bf16[32,32,128]{2,1,0:T(8,128)(2,1)S(1)}, u32[]{:S(2)}, u32[]{:S(2)}) %all-to-all-start.3) | async-done | bytes 262176 | tf_op jit(solution)/shard_map/all_to_all | solution.py:500
  185.0 4.5 %all-to-all-start.4 = ((bf16[8,24,768]{2,1,0:T(8,128)(2,1)}), bf16[8,24,768]{2,1,0:T(8,128)(2,1)S(1)}, u32[]{:S(2)}, u32[]{:S(2)}) async-start(bf16[8,24,768]{2,1,0:T(8,128)(2,1)} %bitcast.37), calls=%async_computation.4 | async-start | bytes 589824 | tf_op jit(solution)/shard_map/all_to_all | solution.py:500
  189.5 12.1 %attend_back.1 = (bf16[32,96,128]{2,1,0:T(8,128)(2,1)}, bf16[192,2048]{1,0:T(8,128)(2,1)}, f32[1,128]{1,0:T(1,128)}) custom-call(s32[4]{0:T(128)} %get-tuple-element.108.lo_ref, s32[4]{0:T(128)} %get-tuple-element.109.hi_ref, bf16[2048,64]{1,0:T(8,128)(2,1)} %get-tuple-element.88.q_ref, bf16[2048,64]{1,0:T(8,128)(2,1)} %get-tuple-element.89.k_ref, ...), custom_call_target="tpu_custom_call" | custom-call | flops 1000000 | bytes 1024 | tf_op jit(solution)/shard_map/attend_back/pallas_call | solution.py:273
  201.6 4.4 %all-to-all-done.4 = bf16[8,24,768]{2,1,0:T(8,128)(2,1)S(1)} async-done(((bf16[8,24,768]{2,1,0:T(8,128)(2,1)}), bf16[8,24,768]{2,1,0:T(8,128)(2,1)S(1)}, u32[]{:S(2)}, u32[]{:S(2)}) %all-to-all-start.4) | async-done | bytes 294944 | tf_op jit(solution)/shard_map/all_to_all | solution.py:500
  206.7 4.1 %all-to-all-start.5 = ((bf16[32,96,128]{2,1,0:T(8,128)(2,1)}), bf16[32,96,128]{2,1,0:T(8,128)(2,1)}, u32[]{:S(2)}, u32[]{:S(2)}) async-start(bf16[32,96,128]{2,1,0:T(8,128)(2,1)} %get-tuple-element.132), calls=%async_computation.5 | async-start | bytes 1572864 | tf_op jit(solution)/shard_map/all_to_all | solution.py:500
  214.5 1.7 copy.77
  221.4 1.5 copy.80
  226.6 6.2 %all-to-all-done.5.slots_ref = bf16[32,96,128]{2,1,0:T(8,128)(2,1)} async-done(((bf16[32,96,128]{2,1,0:T(8,128)(2,1)}), bf16[32,96,128]{2,1,0:T(8,128)(2,1)}, u32[]{:S(2)}, u32[]{:S(2)}) %all-to-all-start.5) | async-done | bytes 786464 | tf_op jit(solution)/shard_map/all_to_all | solution.py:500
  232.8 2.6 all-to-all-start.6
  235.4 2.3 copy.73
  238.4 3.3 %tokens.1 = bf16[128,768]{1,0:T(8,128)(2,1)} custom-call(bf16[32,96,128]{2,1,0:T(8,128)(2,1)} %all-to-all-done.5.slots_ref, bf16[3,768,768]{2,1,0:T(8,128)(2,1)S(1)} %bitcast.152, f32[128,768]{1,0:T(8,128)S(1)} %get-tuple-element.134.first_ref), custom_call_target="tpu_custom_call" | custom-call | flops 1000000 | bytes 1024 | tf_op jit(solution)/shard_map/tokens/pallas_call | solution.py:294
  241.7 11.9 %all-to-all-done.6.slots_ref = bf16[32,24,256]{2,1,0:T(8,128)(2,1)S(1)} async-done(((bf16[32,24,256]{2,1,0:T(8,128)(2,1)}), bf16[32,24,256]{2,1,0:T(8,128)(2,1)S(1)}, u32[]{:S(2)}, u32[]{:S(2)}) %all-to-all-start.6) | async-done | bytes 393248 | tf_op jit(solution)/shard_map/all_to_all | solution.py:500
  255.1 3.2 %reduce-scatter.2.cloned.1.call-done = bf16[1,8,24,768]{3,2,1,0:T(8,128)(2,1)} async-done(((bf16[8,8,24,768]{3,2,1,0:T(8,128)(2,1)}), bf16[1,8,24,768]{3,2,1,0:T(8,128)(2,1)}) %reduce-scatter.2.cloned.1.call-update) | async-done | bytes 294928 | tf_op jit(solution)/shard_map/reduce_scatter | solution.py:731
  (183 shorter events, 48.4 us)
Async XLA Ops:
  7.2 12.3 %copy-start.29 = (bf16[24,3072]{1,0:T(8,128)(2,1)S(1)}, bf16[24,3072]{1,0:T(8,128)(2,1)}, u32[]{:S(2)}) copy-start(bf16[24,3072]{1,0:T(8,128)(2,1)} %param.16) | copy-start | bytes 442372
  8.2 11.2 %collective-permute-start = (bf16[64,768]{1,0:T(8,128)(2,1)S(1)}, bf16[64,768]{1,0:T(8,128)(2,1)S(1)}, u32[]{:S(2)}, u32[]{:S(2)}) collective-permute-start(bf16[64,768]{1,0:T(8,128)(2,1)S(1)} %get-tuple-element.171), channel_id=1, source_target_pairs={{0,4},{1,5},{2,6},{3,7},{4,0},{5,1},{6,2},{7,3},{8,12},{9,13},{10,... | collective-permute-start | bytes 294920 | tf_op jit(solution)/shard_map/ppermute | solution.py:583
  15.5 17.4 %all-to-all-start = ((bf16[32,2,24,128]{3,2,1,0:T(8,128)(2,1)}), bf16[32,2,24,128]{3,2,1,0:T(8,128)(2,1)S(1)}, u32[]{:S(2)}, u32[]{:S(2)}) async-start(bf16[32,2,24,128]{3,2,1,0:T(8,128)(2,1)} %head_slots.1), calls=%async_computation | async-start | bytes 786432 | tf_op jit(solution)/shard_map/all_to_all | solution.py:500
  19.4 84.7 %all-gather.5.cloned.1.call-start = ((), (), s32[]{:S(2)}) async-start(), calls=%async_computation.9 | async-start | bytes 2985984 | tf_op jit(solution)/shard_map/all_gather | solution.py:615
  19.4 7.2 %copy-start.30 = (bf16[96,768]{1,0:T(8,128)(2,1)S(1)}, bf16[96,768]{1,0:T(8,128)(2,1)}, u32[]{:S(2)}) copy-start(bf16[96,768]{1,0:T(8,128)(2,1)} %param.17) | copy-start | bytes 442372
  19.5 7.2 %copy-start.31 = (bf16[24,768]{1,0:T(8,128)(2,1)S(1)}, bf16[24,768]{1,0:T(8,128)(2,1)}, u32[]{:S(2)}) copy-start(bf16[24,768]{1,0:T(8,128)(2,1)} %param.15) | copy-start | bytes 110596
  19.9 4.6 %collective-permute-start.1 = (bf16[24,768]{1,0:T(8,128)(2,1)S(1)}, bf16[24,768]{1,0:T(8,128)(2,1)S(1)}, u32[]{:S(2)}, u32[]{:S(2)}) collective-permute-start(bf16[24,768]{1,0:T(8,128)(2,1)S(1)} %bitcast.181), channel_id=1, source_target_pairs={{0,24},{8,16},{16,8},{24,0},{1,25},{9,17},{17,9},{25,1},{2,26},{10... | collective-permute-start | bytes 110600 | tf_op jit(solution)/shard_map/ppermute | solution.py:543
  21.5 5.1 %collective-permute-start.2 = (bf16[24,768]{1,0:T(8,128)(2,1)S(1)}, bf16[24,768]{1,0:T(8,128)(2,1)S(1)}, u32[]{:S(2)}, u32[]{:S(2)}) collective-permute-start(bf16[24,768]{1,0:T(8,128)(2,1)S(1)} %bitcast.182), channel_id=1, source_target_pairs={{0,16},{16,0},{8,24},{24,8},{1,17},{17,1},{9,25},{25,9},{2,18},{18... | collective-permute-start | bytes 110600 | tf_op jit(solution)/shard_map/ppermute | solution.py:496
  21.9 4.7 %collective-permute-start.3 = (bf16[24,768]{1,0:T(8,128)(2,1)S(1)}, bf16[24,768]{1,0:T(8,128)(2,1)S(1)}, u32[]{:S(2)}, u32[]{:S(2)}) collective-permute-start(bf16[24,768]{1,0:T(8,128)(2,1)S(1)} %bitcast.183), channel_id=1, source_target_pairs={{0,8},{8,0},{16,24},{24,16},{1,9},{9,1},{17,25},{25,17},{2,10},{10... | collective-permute-start | bytes 110600 | tf_op jit(solution)/shard_map/ppermute | solution.py:492
  34.3 35.4 %all-to-all-start.1 = ((bf16[8,128,768]{2,1,0:T(8,128)(2,1)}), bf16[8,128,768]{2,1,0:T(8,128)(2,1)S(1)}, u32[]{:S(2)}, u32[]{:S(2)}) async-start(bf16[8,128,768]{2,1,0:T(8,128)(2,1)} %broadcast_in_dim.59), calls=%async_computation.1 | async-start | bytes 3145728 | tf_op jit(solution)/shard_map/all_to_all | solution.py:500
  38.0 197.4 %all-gather.7.cloned.1.call-start = ((), (), s32[]{:S(2)}) async-start(), calls=%async_computation.10 | async-start | bytes 3649536 | tf_op jit(solution)/shard_map/all_gather | solution.py:614
  69.7 3.4 %collective-permute-start.4 = (bf16[8,128,768]{2,1,0:T(8,128)(2,1)S(1)}, bf16[8,128,768]{2,1,0:T(8,128)(2,1)S(1)}, u32[]{:S(2)}, u32[]{:S(2)}) collective-permute-start(bf16[8,128,768]{2,1,0:T(8,128)(2,1)S(1)} %all-to-all-done.1.a_ref), channel_id=1, source_target_pairs={{0,8},{8,0},{16,24},{24,16},{1,9},{9,1},{17,25},{25,17},{2,10},{10... | collective-permute-start | bytes 4718600 | tf_op jit(solution)/shard_map/ppermute | solution.py:492
  87.7 20.8 %all-to-all-start.2 = ((bf16[32,32,128]{2,1,0:T(8,128)(2,1)}), bf16[32,32,128]{2,1,0:T(8,128)(2,1)S(1)}, u32[]{:S(2)}, u32[]{:S(2)}) async-start(bf16[32,32,128]{2,1,0:T(8,128)(2,1)} %get-tuple-element.92), calls=%async_computation.2 | async-start | bytes 524288 | tf_op jit(solution)/shard_map/all_to_all | solution.py:500
  91.9 166.4 %reduce-scatter.2.cloned.1.call-start = ((), (), s32[]{:S(2)}) async-start(), calls=%async_computation.8 | async-start | bytes 2654208 | tf_op jit(solution)/shard_map/reduce_scatter | solution.py:731
  105.0 6.8 %collective-permute-start.5 = (bf16[192,768]{1,0:T(8,128)(2,1)S(1)}, bf16[192,768]{1,0:T(8,128)(2,1)S(1)}, u32[]{:S(2)}, u32[]{:S(2)}) collective-permute-start(bf16[192,768]{1,0:T(8,128)(2,1)S(1)} %bitcast.169), channel_id=1, source_target_pairs={{0,16},{16,0},{8,24},{24,8},{1,17},{17,1},{9,25},{25,9},{2,18},{18... | collective-permute-start | bytes 884744 | tf_op jit(solution)/shard_map/ppermute | solution.py:496
  106.6 5.3 %collective-permute-start.7 = (bf16[192,768]{1,0:T(8,128)(2,1)S(1)}, bf16[192,768]{1,0:T(8,128)(2,1)S(1)}, u32[]{:S(2)}, u32[]{:S(2)}) collective-permute-start(bf16[192,768]{1,0:T(8,128)(2,1)S(1)} %bitcast.170), channel_id=1, source_target_pairs={{0,8},{8,0},{16,24},{24,16},{1,9},{9,1},{17,25},{25,17},{2,10},{10... | collective-permute-start | bytes 884744 | tf_op jit(solution)/shard_map/ppermute | solution.py:492
  108.4 5.1 %copy-start.6 = (bf16[32,32,128]{2,1,0:T(8,128)(2,1)}, bf16[32,32,128]{2,1,0:T(8,128)(2,1)S(1)}, u32[]{:S(2)}) copy-start(bf16[32,32,128]{2,1,0:T(8,128)(2,1)S(1)} %all-to-all-done.2.slots_ref) | copy-start | bytes 786436
  111.8 1.6 collective-permute-start.6
  115.9 10.9 %copy-start.13 = (bf16[128,768]{1,0:T(8,128)(2,1)}, bf16[128,768]{1,0:T(8,128)(2,1)S(1)}, u32[]{:S(2)}) copy-start(bf16[128,768]{1,0:T(8,128)(2,1)S(1)} %get-tuple-element.130) | copy-start | bytes 589828
  115.9 23.0 %copy-start.4 = (f32[128,768]{1,0:T(8,128)}, f32[128,768]{1,0:T(8,128)S(1)}, u32[]{:S(2)}) copy-start(f32[128,768]{1,0:T(8,128)S(1)} %get-tuple-element.105.normed_ref) | copy-start | bytes 1179652
  115.9 6.9 %collective-permute-start.8 = (bf16[128,768]{1,0:T(8,128)(2,1)S(1)}, bf16[128,768]{1,0:T(8,128)(2,1)S(1)}, u32[]{:S(2)}, u32[]{:S(2)}) collective-permute-start(bf16[128,768]{1,0:T(8,128)(2,1)S(1)} %get-tuple-element.97.a_ref), channel_id=1, source_target_pairs={{0,16},{16,0},{8,24},{24,8},{1,17},{17,1},{9,25},{25,9},{2,18},{18... | collective-permute-start | bytes 589832 | tf_op jit(solution)/shard_map/ppermute | solution.py:496
  117.3 5.5 %collective-permute-start.9 = (bf16[128,768]{1,0:T(8,128)(2,1)S(1)}, bf16[128,768]{1,0:T(8,128)(2,1)S(1)}, u32[]{:S(2)}, u32[]{:S(2)}) collective-permute-start(bf16[128,768]{1,0:T(8,128)(2,1)S(1)} %get-tuple-element.97.a_ref), channel_id=1, source_target_pairs={{0,8},{8,0},{16,24},{24,16},{1,9},{9,1},{17,25},{25,17},{2,10},{10... | collective-permute-start | bytes 589832 | tf_op jit(solution)/shard_map/ppermute | solution.py:492
  122.8 1.4 collective-permute-start.10
  126.8 12.1 %copy-start.12 = (bf16[2,64,768]{2,1,0:T(8,128)(2,1)S(1)}, bf16[2,64,768]{2,1,0:T(8,128)(2,1)}, u32[]{:S(2)}) copy-start(bf16[2,64,768]{2,1,0:T(8,128)(2,1)} %param.13) | copy-start | bytes 589828
  126.8 12.1 %copy-start.16 = (f32[8,768]{1,0:T(8,128)S(1)}, f32[8,768]{1,0:T(8,128)}, u32[]{:S(2)}) copy-start(f32[8,768]{1,0:T(8,128)} %stack.88.vec_ref) | copy-start | bytes 73732
  126.8 1.8 collective-permute-start.11
  128.7 10.2 %collective-permute-start.12 = (bf16[128,768]{1,0:T(8,128)(2,1)S(1)}, bf16[128,768]{1,0:T(8,128)(2,1)S(1)}, u32[]{:S(2)}, u32[]{:S(2)}) collective-permute-start(bf16[128,768]{1,0:T(8,128)(2,1)S(1)} %get-tuple-element.104), channel_id=1, source_target_pairs={{0,16},{16,0},{8,24},{24,8},{1,17},{17,1},{9,25},{25,9},{2,18},{18... | collective-permute-start | bytes 589832 | tf_op jit(solution)/shard_map/ppermute | solution.py:496
  140.7 12.6 %copy-start.20 = (f32[8,768]{1,0:T(8,128)}, f32[8,768]{1,0:T(8,128)S(1)}, u32[]{:S(2)}) copy-start(f32[8,768]{1,0:T(8,128)S(1)} %get-tuple-element.138) | copy-start | bytes 73732
  140.7 6.4 %collective-permute-start.13 = (bf16[128,768]{1,0:T(8,128)(2,1)S(1)}, bf16[128,768]{1,0:T(8,128)(2,1)S(1)}, u32[]{:S(2)}, u32[]{:S(2)}) collective-permute-start(bf16[128,768]{1,0:T(8,128)(2,1)S(1)} %get-tuple-element.114.a_ref), channel_id=1, source_target_pairs={{0,16},{16,0},{8,24},{24,8},{1,17},{17,1},{9,25},{25,9},{2,18},{18... | collective-permute-start | bytes 589832 | tf_op jit(solution)/shard_map/ppermute | solution.py:496
  142.1 4.9 %collective-permute-start.14 = (bf16[128,768]{1,0:T(8,128)(2,1)S(1)}, bf16[128,768]{1,0:T(8,128)(2,1)S(1)}, u32[]{:S(2)}, u32[]{:S(2)}) collective-permute-start(bf16[128,768]{1,0:T(8,128)(2,1)S(1)} %get-tuple-element.114.a_ref), channel_id=1, source_target_pairs={{0,8},{8,0},{16,24},{24,16},{1,9},{9,1},{17,25},{25,17},{2,10},{10... | collective-permute-start | bytes 589832 | tf_op jit(solution)/shard_map/ppermute | solution.py:492
  147.1 1.4 collective-permute-start.15
  151.4 1.8 collective-permute-start.16
  153.2 9.5 %collective-permute-start.17 = (bf16[128,768]{1,0:T(8,128)(2,1)S(1)}, bf16[128,768]{1,0:T(8,128)(2,1)S(1)}, u32[]{:S(2)}, u32[]{:S(2)}) collective-permute-start(bf16[128,768]{1,0:T(8,128)(2,1)S(1)} %get-tuple-element.119), channel_id=1, source_target_pairs={{0,16},{16,0},{8,24},{24,8},{1,17},{17,1},{9,25},{25,9},{2,18},{18... | collective-permute-start | bytes 589832 | tf_op jit(solution)/shard_map/ppermute | solution.py:496
  157.9 4.9 %copy-start.11 = (f32[128,768]{1,0:T(8,128)S(1)}, f32[128,768]{1,0:T(8,128)}, u32[]{:S(2)}) copy-start(f32[128,768]{1,0:T(8,128)} %copy-done.10) | copy-start | bytes 1179652
  157.9 4.9 %copy-start.15 = (f32[8,768]{1,0:T(8,128)S(1)}, f32[8,768]{1,0:T(8,128)}, u32[]{:S(2)}) copy-start(f32[8,768]{1,0:T(8,128)} %pad_maximum_fusion.6.vec_ref) | copy-start | bytes 73732
  157.9 4.9 %copy-start.19 = (f32[128,1]{1,0:T(8,128)S(1)}, f32[128,1]{1,0:T(8,128)}, u32[]{:S(2)}) copy-start(f32[128,1]{1,0:T(8,128)} %copy-done.18) | copy-start | bytes 1540
  165.0 2.1 collective-permute-start.18
  168.0 9.3 %collective-permute-start.19 = (bf16[192,768]{1,0:T(8,128)(2,1)}, bf16[192,768]{1,0:T(8,128)(2,1)S(1)}, u32[]{:S(2)}, u32[]{:S(2)}) collective-permute-start(bf16[192,768]{1,0:T(8,128)(2,1)} %fusion.6), channel_id=1, source_target_pairs={{0,16},{16,0},{8,24},{24,8},{1,17},{17,1},{9,25},{25,9},{2,18},{18... | collective-permute-start | bytes 884744 | tf_op jit(solution)/shard_map/ppermute | solution.py:496
  168.3 16.7 %all-to-all-start.3 = ((bf16[32,32,128]{2,1,0:T(8,128)(2,1)}), bf16[32,32,128]{2,1,0:T(8,128)(2,1)S(1)}, u32[]{:S(2)}, u32[]{:S(2)}) async-start(bf16[32,32,128]{2,1,0:T(8,128)(2,1)} %get-tuple-element.128), calls=%async_computation.3 | async-start | bytes 524288 | tf_op jit(solution)/shard_map/all_to_all | solution.py:500
  185.0 21.1 %all-to-all-start.4 = ((bf16[8,24,768]{2,1,0:T(8,128)(2,1)}), bf16[8,24,768]{2,1,0:T(8,128)(2,1)S(1)}, u32[]{:S(2)}, u32[]{:S(2)}) async-start(bf16[8,24,768]{2,1,0:T(8,128)(2,1)} %bitcast.37), calls=%async_computation.4 | async-start | bytes 589824 | tf_op jit(solution)/shard_map/all_to_all | solution.py:500
  189.5 33.5 %copy-start.3 = (bf16[8,128,768]{2,1,0:T(8,128)(2,1)S(1)}, bf16[8,128,768]{2,1,0:T(8,128)(2,1)}, u32[]{:S(2)}) copy-start(bf16[8,128,768]{2,1,0:T(8,128)(2,1)} %copy-done.2) | copy-start | bytes 4718596
  206.7 16.2 %copy-start.1 = (bf16[8,128,768]{2,1,0:T(8,128)(2,1)S(1)}, bf16[8,128,768]{2,1,0:T(8,128)(2,1)}, u32[]{:S(2)}) copy-start(bf16[8,128,768]{2,1,0:T(8,128)(2,1)} %copy-done) | copy-start | bytes 4718596
  206.7 16.2 %copy-start.22 = (s32[2]{0:T(128)S(1)}, s32[2]{0:T(128)}, u32[]{:S(2)}) copy-start(s32[2]{0:T(128)} %pad_add_fusion.1.place_ref) | copy-start | bytes 28
  206.7 26.1 %all-to-all-start.5 = ((bf16[32,96,128]{2,1,0:T(8,128)(2,1)}), bf16[32,96,128]{2,1,0:T(8,128)(2,1)}, u32[]{:S(2)}, u32[]{:S(2)}) async-start(bf16[32,96,128]{2,1,0:T(8,128)(2,1)} %get-tuple-element.132), calls=%async_computation.5 | async-start | bytes 1572864 | tf_op jit(solution)/shard_map/all_to_all | solution.py:500
  232.8 20.8 %all-to-all-start.6 = ((bf16[32,24,256]{2,1,0:T(8,128)(2,1)}), bf16[32,24,256]{2,1,0:T(8,128)(2,1)S(1)}, u32[]{:S(2)}, u32[]{:S(2)}) async-start(bf16[32,24,256]{2,1,0:T(8,128)(2,1)} %pad_maximum_fusion.2), calls=%async_computation.6 | async-start | bytes 786432 | tf_op jit(solution)/shard_map/all_to_all | solution.py:500
  259.3 3.7 %collective-permute-start.20 = (bf16[24,768]{1,0:T(8,128)(2,1)S(1)}, bf16[24,768]{1,0:T(8,128)(2,1)S(1)}, u32[]{:S(2)}, u32[]{:S(2)}) collective-permute-start(bf16[24,768]{1,0:T(8,128)(2,1)S(1)} %get-tuple-element.176), channel_id=1, source_target_pairs={{0,24},{8,16},{16,8},{24,0},{1,25},{9,17},{17,9},{25,1},{2,26},{10... | collective-permute-start | bytes 110600 | tf_op jit(solution)/shard_map/ppermute | solution.py:543
  260.4 4.0 %collective-permute-start.21 = (bf16[24,768]{1,0:T(8,128)(2,1)S(1)}, bf16[24,768]{1,0:T(8,128)(2,1)S(1)}, u32[]{:S(2)}, u32[]{:S(2)}) collective-permute-start(bf16[24,768]{1,0:T(8,128)(2,1)S(1)} %get-tuple-element.175), channel_id=1, source_target_pairs={{0,16},{16,0},{8,24},{24,8},{1,17},{17,1},{9,25},{25,9},{2,18},{18... | collective-permute-start | bytes 110600 | tf_op jit(solution)/shard_map/ppermute | solution.py:496
  261.0 3.4 %collective-permute-start.22 = (bf16[24,768]{1,0:T(8,128)(2,1)S(1)}, bf16[24,768]{1,0:T(8,128)(2,1)S(1)}, u32[]{:S(2)}, u32[]{:S(2)}) collective-permute-start(bf16[24,768]{1,0:T(8,128)(2,1)S(1)} %get-tuple-element.174), channel_id=1, source_target_pairs={{0,8},{8,0},{16,24},{24,16},{1,9},{9,1},{17,25},{25,17},{2,10},{10... | collective-permute-start | bytes 110600 | tf_op jit(solution)/shard_map/ppermute | solution.py:492
  (18 other events, 35.5 us)
Sparse Core Ops, SparseCore 0:
  33.1 70.9 all-gather.4
  107.0 63.0 all-gather.6
  173.6 84.6 reduce-scatter.1

commit v7 on v6

--- a/solution.py
+++ b/solution.py
@@ -587,23 +587,30 @@
         for c in range(2)
         for s in range(2)
     ]
-    inner_own = after(inner_weight, pair_x).reshape(rows_dev, groups, ff_part)
+    inner_own = inner_weight.reshape(rows_dev, groups, ff_part)
     inner_own = to_group(inner_own.transpose(1, 0, 2)).reshape(groups * rows_dev, ff_part)
     ffn = jnp.concatenate([inner_own, outer_weight, out_weight])
 
-    units = tuple(h * heads_dev + u for h in range(groups) for u in unit_of * 2)
+    units = tuple(h * heads_dev + u for h in range(groups) for u in unit_of)
     (slots,) = call(
         functools.partial(head_slots_kernel, units=units),
-        (((devices, 2, rows_dev, 2 * hd), BF),),
+        (((groups * halves, 2, rows_dev, 2 * hd), BF),),
         (qkv_weight, bias_rows, norm_gains, norm_shifts, inner_bias.reshape(rows_dev, -1)),
         "head_slots",
         1e6,
         params=LARGE,
     )
-    slots = swap(slots, BOTH)
-    qk_weight = slots[:, 0].reshape(depth, 2 * hd)
-    v_weight = slots[:, 1].reshape(depth, 2 * hd)
-    small = slots[:, 1, :, hd : hd + 12].astype(F32).reshape(depth, 12).T
+    half_groups = [
+        [h * cycle + b for h in range(groups) for b in range(n * halves, (n + 1) * halves)]
+        for n in range(2)
+    ]
+    slots, pair_x = lax.optimization_barrier((swap(slots, BOTH, half_groups), pair_x))
+    far_slots = lax.ppermute(slots, "blk", [(i, (i + halves) % cycle) for i in range(cycle)])
+    near, far = [v.reshape(groups, halves, 2, rows_dev, 2 * hd) for v in (slots, far_slots)]
+    both = jnp.stack([jnp.where(half == 0, near, far), jnp.where(half == 0, far, near)], axis=1)
+    qk_weight = both[:, :, :, 0].reshape(depth, 2 * hd)
+    v_weight = both[:, :, :, 1].reshape(depth, 2 * hd)
+    small = both[:, :, :, 1, :, hd : hd + 12].astype(F32).reshape(depth, 12).T
 
     bias, gains, shifts = small[0:4], small[4:6], small[6:8]
     inner_bias_all = small[8:12].T.reshape(groups, ff_part)

time: 272 us -> 268 us (0.985)
  waiting for transfers between devices: 124 us -> 104 us
  starting transfers between devices: 45.9 us -> 56.4 us
  Pallas kernels: 44.5 us -> 50.2 us
    ppermute x0 -> x1, waiting for transfers between devices: none -> 26.1 us  [local(): lax.ppermute(slots, 'blk', [(i, (i + halves) % cycle) for i in range(cycl...]
    all_to_all x7, waiting for transfers between devices: 58.4 us -> 37.2 us  [swap(): lax.all_to_all(value, axes, split_axis=0, concat_axis=0, tiled=True, axis...]
    all_gather x1, waiting for transfers between devices: 11.9 us -> 0.02 us  [local(): ffn_all = lax.all_gather(after(ffn, slots), 'blk', axis=0, tiled=False)]
    ppermute x8, waiting for transfers between devices: 33.6 us -> 23.1 us  [by_x(): return lax.ppermute(value, 'head', [(0, 2), (2, 0), (1, 3), (3, 1)])]
    all_to_all x7, starting transfers between devices: 28.9 us -> 34.4 us  [swap(): lax.all_to_all(value, axes, split_axis=0, concat_axis=0, tiled=True, axis...]
    reduce_scatter x1, waiting for transfers between devices: 3.18 us -> 0.01 us  [local(): lax.psum_scatter(ffn_grad, 'blk', scatter_dimension=0, tiled=False)]
    pallas_call x1, Pallas kernels: 12.1 us -> 15.3 us  [attend_back(): pl.pallas_call(functools.partial(attend_back_kernel, bq=bq, bk=bk, pack=p...]
    ppermute x2, waiting for transfers between devices: 3.58 us -> 0.78 us  [to_group(): across = lax.ppermute(block(3), 'head', [(i, i ^ 3) for i in range(4)])]
  transfers between devices with their start and end apart: 33 -> 34, of which waited for: 25 -> 24; matrix products, arithmetic and copies ran while one was open for 13% -> 13% of each run, Pallas kernels for 16% -> 19%
where the time goes in v7:
time: 268 us; the launch traced here: 266 us
  waiting for transfers between devices  104 us (39%)
  starting transfers between devices  56.4 us (21%)
  Pallas kernels  50.2 us (19%)
  local copies, waits for them, and re-layouts  29 us (11%)
  between operations  14.5 us (5%)
  other arithmetic  12.4 us (5%)
    all_to_all x7, waiting for transfers between devices, swap(): lax.all_to_all(value, axes, split_axis=0, concat_axis=0, tiled=True, axis...  37.2 us
    all_to_all x7, starting transfers between devices, swap(): lax.all_to_all(value, axes, split_axis=0, concat_axis=0, tiled=True, axis...  34.4 us
    ppermute x1, waiting for transfers between devices, local(): lax.ppermute(slots, 'blk', [(i, (i + halves) % cycle) for i in range(cycl...  26.1 us
    ppermute x8, waiting for transfers between devices, by_x(): return lax.ppermute(value, 'head', [(0, 2), (2, 0), (1, 3), (3, 1)])  23.1 us
    pallas_call x11, Pallas kernels, call(): pl.pallas_call(kernel, out_shape=tuple((jax.ShapeDtypeStruct(shape, kind)...  17.4 us
    pallas_call x1, Pallas kernels, attend_back(): pl.pallas_call(functools.partial(attend_back_kernel, bq=bq, bk=bk, pack=p...  15.3 us
    ppermute x12, waiting for transfers between devices, by_core(): return lax.ppermute(value, 'head', [(0, 1), (1, 0), (2, 3), (3, 2)])  13 us
    ppermute x8, starting transfers between devices, by_x(): return lax.ppermute(value, 'head', [(0, 2), (2, 0), (1, 3), (3, 1)])  11.8 us
  transfers between devices with their start and end apart: 34, of which 24 were waited for; matrix products, arithmetic and copies ran while one was open for 13% of the time, Pallas kernels for 19%

profile of v7, /device:TPU:0, one launch (start us, length us, event | category | flops | bytes accessed | tf_op | source)
XLA Modules:
  0.0 266.4 jit_solution(3725097673257988438)
XLA Ops:
  8.6 2.4 collective-permute-start
  12.6 1.8 head_slots.1
  14.3 5.0 %all-to-all-start = ((bf16[16,2,24,128]{3,2,1,0:T(8,128)(2,1)}), bf16[16,2,24,128]{3,2,1,0:T(8,128)(2,1)S(1)}, u32[]{:S(2)}, u32[]{:S(2)}) async-start(bf16[16,2,24,128]{3,2,1,0:T(8,128)(2,1)} %head_slots.1), calls=%async_computation | async-start | bytes 393216 | tf_op jit(solution)/shard_map/all_to_all | solution.py:500
  19.5 2.7 collective-permute-start.3
  23.0 2.7 %collective-permute-done.3 = bf16[64,768]{1,0:T(8,128)(2,1)S(1)} collective-permute-done((bf16[64,768]{1,0:T(8,128)(2,1)S(1)}, bf16[64,768]{1,0:T(8,128)(2,1)S(1)}, u32[]{:S(2)}, u32[]{:S(2)}) %collective-permute-start.3) | collective-permute-done | bytes 98336 | tf_op jit(solution)/shard_map/ppermute | solution.py:583
  25.7 2.4 all-to-all-done
  29.5 4.4 %all-to-all-start.1 = ((bf16[8,128,768]{2,1,0:T(8,128)(2,1)}), bf16[8,128,768]{2,1,0:T(8,128)(2,1)S(1)}, u32[]{:S(2)}, u32[]{:S(2)}) async-start(bf16[8,128,768]{2,1,0:T(8,128)(2,1)} %broadcast_in_dim.59), calls=%async_computation.1 | async-start | bytes 3145728 | tf_op jit(solution)/shard_map/all_to_all | solution.py:500
  36.3 2.6 collective-permute-start.4
  39.5 26.1 %collective-permute-done.4 = bf16[16,2,24,128]{3,2,1,0:T(8,128)(2,1)S(1)} collective-permute-done((bf16[16,2,24,128]{3,2,1,0:T(8,128)(2,1)S(1)}, bf16[16,2,24,128]{3,2,1,0:T(8,128)(2,1)S(1)}, u32[]{:S(2)}, u32[]{:S(2)}) %collective-permute-start.4) | collective-permute-done | bytes 196640 | tf_op jit(solution)/shard_map/ppermute | solution.py:608
  70.1 3.4 %collective-permute-done.5.b_ref = bf16[8,128,768]{2,1,0:T(8,128)(2,1)S(1)} collective-permute-done((bf16[8,128,768]{2,1,0:T(8,128)(2,1)S(1)}, bf16[8,128,768]{2,1,0:T(8,128)(2,1)S(1)}, u32[]{:S(2)}, u32[]{:S(2)}) %collective-permute-start.5) | collective-permute-done | bytes 1572896 | tf_op jit(solution)/shard_map/ppermute | solution.py:492
  74.6 5.0 %project.1 = (bf16[2048,64]{1,0:T(8,128)(2,1)}, bf16[2048,64]{1,0:T(8,128)(2,1)}, bf16[2048,64]{1,0:T(8,128)(2,1)}, bf16[64,2048]{1,0:T(8,128)(2,1)}, bf16[64,2048]{1,0:T(8,128)(2,1)}) custom-call(s32[2]{0:T(128)} %pad_add_fusion.1.place_ref, bf16[8,128,768]{2,1,0:T(8,128)(2,1)} %copy-done, bf16[8,128,768]{2,1,0:T(8,128)(2,1)} %copy-done.2, ...), custom_call_target="tpu_custom_call" | custom-call | flops 1000000 | bytes 1024 | tf_op jit(solution)/shard_map/project/pallas_call | solution.py:85
  79.6 11.1 %attend.1 = (bf16[32,32,128]{2,1,0:T(8,128)(2,1)}, f32[64,2048]{1,0:T(8,128)}, f32[1,2048]{1,0:T(1,128)}) custom-call(s32[4]{0:T(128)} %get-tuple-element.83.lo_ref, s32[4]{0:T(128)} %get-tuple-element.84.hi_ref, bf16[2048,64]{1,0:T(8,128)(2,1)} %get-tuple-element.90.q_ref, bf16[2048,64]{1,0:T(8,128)(2,1)} %get-tuple-element.91.k_ref, ...), custom_call_target="tpu_custom_call" | custom-call | flops 1000000 | bytes 1024 | tf_op jit(solution)/shard_map/attend/pallas_call | solution.py:195
  90.7 7.5 %all-to-all-start.2 = ((bf16[32,32,128]{2,1,0:T(8,128)(2,1)}), bf16[32,32,128]{2,1,0:T(8,128)(2,1)S(1)}, u32[]{:S(2)}, u32[]{:S(2)}) async-start(bf16[32,32,128]{2,1,0:T(8,128)(2,1)} %get-tuple-element.94), calls=%async_computation.2 | async-start | bytes 524288 | tf_op jit(solution)/shard_map/all_to_all | solution.py:500
  99.5 1.8 collective-permute-start.6
  101.4 1.8 fusion.16
  103.3 5.7 %all-to-all-done.2.slots_ref = bf16[32,32,128]{2,1,0:T(8,128)(2,1)S(1)} async-done(((bf16[32,32,128]{2,1,0:T(8,128)(2,1)}), bf16[32,32,128]{2,1,0:T(8,128)(2,1)S(1)}, u32[]{:S(2)}, u32[]{:S(2)}) %all-to-all-start.2) | async-done | bytes 262176 | tf_op jit(solution)/shard_map/all_to_all | solution.py:500
  109.0 1.7 collective-permute-done.6
  110.7 1.6 collective-permute-done.7
  114.7 1.9 collective-permute-start.9
  116.6 5.2 %collective-permute-done.9.b_ref = bf16[128,768]{1,0:T(8,128)(2,1)S(1)} collective-permute-done((bf16[128,768]{1,0:T(8,128)(2,1)S(1)}, bf16[128,768]{1,0:T(8,128)(2,1)S(1)}, u32[]{:S(2)}, u32[]{:S(2)}) %collective-permute-start.9) | collective-permute-done | bytes 196640 | tf_op jit(solution)/shard_map/ppermute | solution.py:496
  123.2 2.5 inner.1
  126.0 1.6 collective-permute-done.12.got_ref
  127.7 1.8 collective-permute-start.13
  129.5 5.2 %collective-permute-done.13.got_ref = bf16[128,768]{1,0:T(8,128)(2,1)S(1)} collective-permute-done((bf16[128,768]{1,0:T(8,128)(2,1)S(1)}, bf16[128,768]{1,0:T(8,128)(2,1)S(1)}, u32[]{:S(2)}, u32[]{:S(2)}) %collective-permute-start.13) | collective-permute-done | bytes 196640 | tf_op jit(solution)/shard_map/ppermute | solution.py:496
  136.5 1.7 collective-permute-start.14
  138.2 4.4 %collective-permute-done.14.b_ref = bf16[128,768]{1,0:T(8,128)(2,1)S(1)} collective-permute-done((bf16[128,768]{1,0:T(8,128)(2,1)S(1)}, bf16[128,768]{1,0:T(8,128)(2,1)S(1)}, u32[]{:S(2)}, u32[]{:S(2)}) %collective-permute-start.14) | collective-permute-done | bytes 196640 | tf_op jit(solution)/shard_map/ppermute | solution.py:496
  142.6 1.5 collective-permute-done.16.d_ref
  144.1 2.9 %inner_back.1 = (bf16[512,768]{1,0:T(8,128)(2,1)S(1)}, bf16[512,768]{1,0:T(8,128)(2,1)S(1)}, f32[1,768]{1,0:T(1,128)S(1)}, f32[256,768]{1,0:T(8,128)S(1)}, bf16[256,768]{1,0:T(8,128)(2,1)S(1)}) custom-call(bf16[128,768]{1,0:T(8,128)(2,1)S(1)} %get-tuple-element.116.a_ref, bf16[128,768]{1,0:T(8,128)(2,1)S(1)} %collective-permute-done.14.b_ref, ...), custom_call_target="tpu_custom_call" | custom-call | flops 1000000 | bytes 1024 | tf_op jit(solution)/shard_map/inner_back/pallas_call | solution.py:294
  147.2 1.5 collective-permute-done.17.got_ref
  148.8 1.8 collective-permute-start.18
  150.6 2.9 %feed_grad.1 = bf16[8,8,24,768]{3,2,1,0:T(8,128)(2,1)} custom-call(bf16[512,768]{1,0:T(8,128)(2,1)S(1)} %get-tuple-element.122.low_ref, bf16[512,768]{1,0:T(8,128)(2,1)S(1)} %get-tuple-element.123.inner_ref, bf16[512,768]{1,0:T(8,128)(2,1)S(1)} %get-tuple-element.124.act_ref, bf16[512,768]{1,0:T(8,128)(2,1)S(1)} %get-tuple-element.125.ffn_ref), custom_call_target="tpu_custom_call" | custom-call | flops 1000000 | bytes 1024 | tf_op jit(solution)/shard_map/feed_grad/pallas_call | solution.py:294
  153.5 2.5 collective-permute-done.18.got_ref
  158.2 2.0 collective-permute-done.19
  161.1 1.7 collective-permute-start.20
  162.9 4.5 %all-to-all-start.3 = ((bf16[32,32,128]{2,1,0:T(8,128)(2,1)}), bf16[32,32,128]{2,1,0:T(8,128)(2,1)S(1)}, u32[]{:S(2)}, u32[]{:S(2)}) async-start(bf16[32,32,128]{2,1,0:T(8,128)(2,1)} %get-tuple-element.130), calls=%async_computation.3 | async-start | bytes 524288 | tf_op jit(solution)/shard_map/all_to_all | solution.py:500
  167.4 3.3 %collective-permute-done.20 = bf16[192,768]{1,0:T(8,128)(2,1)S(1)} collective-permute-done((bf16[192,768]{1,0:T(8,128)(2,1)}, bf16[192,768]{1,0:T(8,128)(2,1)S(1)}, u32[]{:S(2)}, u32[]{:S(2)}) %collective-permute-start.20) | collective-permute-done | bytes 294944 | tf_op jit(solution)/shard_map/ppermute | solution.py:496
  170.7 1.9 fusion.3
  172.5 7.5 %all-to-all-done.3.do_ref = bf16[32,32,128]{2,1,0:T(8,128)(2,1)S(1)} async-done(((bf16[32,32,128]{2,1,0:T(8,128)(2,1)}), bf16[32,32,128]{2,1,0:T(8,128)(2,1)S(1)}, u32[]{:S(2)}, u32[]{:S(2)}) %all-to-all-start.3) | async-done | bytes 262176 | tf_op jit(solution)/shard_map/all_to_all | solution.py:500
  180.0 5.6 %all-to-all-start.4 = ((bf16[8,24,768]{2,1,0:T(8,128)(2,1)}), bf16[8,24,768]{2,1,0:T(8,128)(2,1)S(1)}, u32[]{:S(2)}, u32[]{:S(2)}) async-start(bf16[8,24,768]{2,1,0:T(8,128)(2,1)} %bitcast.41), calls=%async_computation.4 | async-start | bytes 589824 | tf_op jit(solution)/shard_map/all_to_all | solution.py:500
  185.7 15.3 %attend_back.1 = (bf16[32,96,128]{2,1,0:T(8,128)(2,1)}, bf16[192,2048]{1,0:T(8,128)(2,1)}, f32[1,128]{1,0:T(1,128)}) custom-call(s32[4]{0:T(128)} %get-tuple-element.110.lo_ref, s32[4]{0:T(128)} %get-tuple-element.111.hi_ref, bf16[2048,64]{1,0:T(8,128)(2,1)} %get-tuple-element.90.q_ref, bf16[2048,64]{1,0:T(8,128)(2,1)} %get-tuple-element.91.k_ref, ...), custom_call_target="tpu_custom_call" | custom-call | flops 1000000 | bytes 1024 | tf_op jit(solution)/shard_map/attend_back/pallas_call | solution.py:273
  202.3 4.7 %all-to-all-start.5 = ((bf16[32,96,128]{2,1,0:T(8,128)(2,1)}), bf16[32,96,128]{2,1,0:T(8,128)(2,1)}, u32[]{:S(2)}, u32[]{:S(2)}) async-start(bf16[32,96,128]{2,1,0:T(8,128)(2,1)} %get-tuple-element.134), calls=%async_computation.5 | async-start | bytes 1572864 | tf_op jit(solution)/shard_map/all_to_all | solution.py:500
  210.6 1.7 copy.83
  217.5 1.5 copy.86
  222.7 6.2 %all-to-all-done.5.slots_ref = bf16[32,96,128]{2,1,0:T(8,128)(2,1)} async-done(((bf16[32,96,128]{2,1,0:T(8,128)(2,1)}), bf16[32,96,128]{2,1,0:T(8,128)(2,1)}, u32[]{:S(2)}, u32[]{:S(2)}) %all-to-all-start.5) | async-done | bytes 786464 | tf_op jit(solution)/shard_map/all_to_all | solution.py:500
  228.9 2.6 all-to-all-start.6
  231.6 2.3 copy.79
  234.5 3.2 %tokens.1 = bf16[128,768]{1,0:T(8,128)(2,1)} custom-call(bf16[32,96,128]{2,1,0:T(8,128)(2,1)} %all-to-all-done.5.slots_ref, bf16[3,768,768]{2,1,0:T(8,128)(2,1)S(1)} %bitcast.158, f32[128,768]{1,0:T(8,128)S(1)} %get-tuple-element.136.first_ref), custom_call_target="tpu_custom_call" | custom-call | flops 1000000 | bytes 1024 | tf_op jit(solution)/shard_map/tokens/pallas_call | solution.py:294
  237.7 14.5 %all-to-all-done.6.slots_ref = bf16[32,24,256]{2,1,0:T(8,128)(2,1)S(1)} async-done(((bf16[32,24,256]{2,1,0:T(8,128)(2,1)}), bf16[32,24,256]{2,1,0:T(8,128)(2,1)S(1)}, u32[]{:S(2)}, u32[]{:S(2)}) %all-to-all-start.6) | async-done | bytes 393248 | tf_op jit(solution)/shard_map/all_to_all | solution.py:500
  (188 shorter events, 46.4 us)
Async XLA Ops:
  7.2 4.7 %copy-start.32 = (bf16[96]{0:T(256)(128)(2,1)S(1)}, bf16[96]{0:T(256)(128)(2,1)}, u32[]{:S(2)}) copy-start(bf16[96]{0:T(256)(128)(2,1)} %param.19) | copy-start | bytes 580
  7.2 12.2 %copy-start.9 = (bf16[2,64,768]{2,1,0:T(8,128)(2,1)S(1)}, bf16[2,64,768]{2,1,0:T(8,128)(2,1)}, u32[]{:S(2)}) copy-start(bf16[2,64,768]{2,1,0:T(8,128)(2,1)} %param.11) | copy-start | bytes 589828
  8.6 13.6 %copy-start.30 = (bf16[96,768]{1,0:T(8,128)(2,1)S(1)}, bf16[96,768]{1,0:T(8,128)(2,1)}, u32[]{:S(2)}) copy-start(bf16[96,768]{1,0:T(8,128)(2,1)} %param.17) | copy-start | bytes 442372
  8.6 13.6 %copy-start.31 = (bf16[24,768]{1,0:T(8,128)(2,1)S(1)}, bf16[24,768]{1,0:T(8,128)(2,1)}, u32[]{:S(2)}) copy-start(bf16[24,768]{1,0:T(8,128)(2,1)} %param.15) | copy-start | bytes 110596
  8.6 13.5 %collective-permute-start = (bf16[24,768]{1,0:T(8,128)(2,1)S(1)}, bf16[24,768]{1,0:T(8,128)(2,1)S(1)}, u32[]{:S(2)}, u32[]{:S(2)}) collective-permute-start(bf16[24,768]{1,0:T(8,128)(2,1)S(1)} %bitcast.191), channel_id=1, source_target_pairs={{0,24},{8,16},{16,8},{24,0},{1,25},{9,17},{17,9},{25,1},{2,26},{10... | collective-permute-start | bytes 110600 | tf_op jit(solution)/shard_map/ppermute | solution.py:543
  11.1 11.0 %collective-permute-start.1 = (bf16[24,768]{1,0:T(8,128)(2,1)S(1)}, bf16[24,768]{1,0:T(8,128)(2,1)S(1)}, u32[]{:S(2)}, u32[]{:S(2)}) collective-permute-start(bf16[24,768]{1,0:T(8,128)(2,1)S(1)} %bitcast.192), channel_id=1, source_target_pairs={{0,16},{16,0},{8,24},{24,8},{1,17},{17,1},{9,25},{25,9},{2,18},{18... | collective-permute-start | bytes 110600 | tf_op jit(solution)/shard_map/ppermute | solution.py:496
  11.8 10.4 %collective-permute-start.2 = (bf16[24,768]{1,0:T(8,128)(2,1)S(1)}, bf16[24,768]{1,0:T(8,128)(2,1)S(1)}, u32[]{:S(2)}, u32[]{:S(2)}) collective-permute-start(bf16[24,768]{1,0:T(8,128)(2,1)S(1)} %bitcast.193), channel_id=1, source_target_pairs={{0,8},{8,0},{16,24},{24,16},{1,9},{9,1},{17,25},{25,17},{2,10},{10... | collective-permute-start | bytes 110600 | tf_op jit(solution)/shard_map/ppermute | solution.py:492
  14.3 13.8 %all-to-all-start = ((bf16[16,2,24,128]{3,2,1,0:T(8,128)(2,1)}), bf16[16,2,24,128]{3,2,1,0:T(8,128)(2,1)S(1)}, u32[]{:S(2)}, u32[]{:S(2)}) async-start(bf16[16,2,24,128]{3,2,1,0:T(8,128)(2,1)} %head_slots.1), calls=%async_computation | async-start | bytes 393216 | tf_op jit(solution)/shard_map/all_to_all | solution.py:500
  19.4 79.2 %all-gather.5.cloned.1.call-start = ((), (), s32[]{:S(2)}) async-start(), calls=%async_computation.9 | async-start | bytes 2985984 | tf_op jit(solution)/shard_map/all_gather | solution.py:622
  19.5 6.2 %collective-permute-start.3 = (bf16[64,768]{1,0:T(8,128)(2,1)S(1)}, bf16[64,768]{1,0:T(8,128)(2,1)S(1)}, u32[]{:S(2)}, u32[]{:S(2)}) collective-permute-start(bf16[64,768]{1,0:T(8,128)(2,1)S(1)} %get-tuple-element.175), channel_id=1, source_target_pairs={{0,4},{1,5},{2,6},{3,7},{4,0},{5,1},{6,2},{7,3},{8,12},{9,13},{10,... | collective-permute-start | bytes 294920 | tf_op jit(solution)/shard_map/ppermute | solution.py:583
  29.5 4.5 %copy-start.33 = (s32[2,32]{1,0:T(2,128)S(1)}, s32[2,32]{1,0:T(2,128)}, u32[]{:S(2)}) copy-start(s32[2,32]{1,0:T(2,128)} %param.12) | copy-start | bytes 772
  29.5 40.6 %all-to-all-start.1 = ((bf16[8,128,768]{2,1,0:T(8,128)(2,1)}), bf16[8,128,768]{2,1,0:T(8,128)(2,1)S(1)}, u32[]{:S(2)}, u32[]{:S(2)}) async-start(bf16[8,128,768]{2,1,0:T(8,128)(2,1)} %broadcast_in_dim.59), calls=%async_computation.1 | async-start | bytes 3145728 | tf_op jit(solution)/shard_map/all_to_all | solution.py:500
  33.9 197.6 %all-gather.7.cloned.1.call-start = ((), (), s32[]{:S(2)}) async-start(), calls=%async_computation.10 | async-start | bytes 3649536 | tf_op jit(solution)/shard_map/all_gather | solution.py:621
  36.3 29.4 %collective-permute-start.4 = (bf16[16,2,24,128]{3,2,1,0:T(8,128)(2,1)S(1)}, bf16[16,2,24,128]{3,2,1,0:T(8,128)(2,1)S(1)}, u32[]{:S(2)}, u32[]{:S(2)}) collective-permute-start(bf16[16,2,24,128]{3,2,1,0:T(8,128)(2,1)S(1)} %all-to-all-done), channel_id=1, source_target_pairs={{0,4},{1,5},{2,6},{3,7},{4,0},{5,1},{6,2},{7,3},{8,12},{9,13},{10,... | collective-permute-start | bytes 589832 | tf_op jit(solution)/shard_map/ppermute | solution.py:608
  70.1 3.4 %collective-permute-start.5 = (bf16[8,128,768]{2,1,0:T(8,128)(2,1)S(1)}, bf16[8,128,768]{2,1,0:T(8,128)(2,1)S(1)}, u32[]{:S(2)}, u32[]{:S(2)}) collective-permute-start(bf16[8,128,768]{2,1,0:T(8,128)(2,1)S(1)} %all-to-all-done.1.a_ref), channel_id=1, source_target_pairs={{0,8},{8,0},{16,24},{24,16},{1,9},{9,1},{17,25},{25,17},{2,10},{10... | collective-permute-start | bytes 4718600 | tf_op jit(solution)/shard_map/ppermute | solution.py:492
  90.7 18.2 %all-to-all-start.2 = ((bf16[32,32,128]{2,1,0:T(8,128)(2,1)}), bf16[32,32,128]{2,1,0:T(8,128)(2,1)S(1)}, u32[]{:S(2)}, u32[]{:S(2)}) async-start(bf16[32,32,128]{2,1,0:T(8,128)(2,1)} %get-tuple-element.94), calls=%async_computation.2 | async-start | bytes 524288 | tf_op jit(solution)/shard_map/all_to_all | solution.py:500
  98.3 155.5 %reduce-scatter.2.cloned.1.call-start = ((), (), s32[]{:S(2)}) async-start(), calls=%async_computation.8 | async-start | bytes 2654208 | tf_op jit(solution)/shard_map/reduce_scatter | solution.py:738
  99.5 11.1 %collective-permute-start.6 = (bf16[192,768]{1,0:T(8,128)(2,1)S(1)}, bf16[192,768]{1,0:T(8,128)(2,1)S(1)}, u32[]{:S(2)}, u32[]{:S(2)}) collective-permute-start(bf16[192,768]{1,0:T(8,128)(2,1)S(1)} %bitcast.179), channel_id=1, source_target_pairs={{0,16},{16,0},{8,24},{24,8},{1,17},{17,1},{9,25},{25,9},{2,18},{18... | collective-permute-start | bytes 884744 | tf_op jit(solution)/shard_map/ppermute | solution.py:496
  101.4 9.3 %collective-permute-start.8 = (bf16[192,768]{1,0:T(8,128)(2,1)S(1)}, bf16[192,768]{1,0:T(8,128)(2,1)S(1)}, u32[]{:S(2)}, u32[]{:S(2)}) collective-permute-start(bf16[192,768]{1,0:T(8,128)(2,1)S(1)} %bitcast.180), channel_id=1, source_target_pairs={{0,8},{8,0},{16,24},{24,16},{1,9},{9,1},{17,25},{25,17},{2,10},{10... | collective-permute-start | bytes 884744 | tf_op jit(solution)/shard_map/ppermute | solution.py:492
  110.7 1.6 collective-permute-start.7
  114.7 11.1 %copy-start.14 = (bf16[128,768]{1,0:T(8,128)(2,1)}, bf16[128,768]{1,0:T(8,128)(2,1)S(1)}, u32[]{:S(2)}) copy-start(bf16[128,768]{1,0:T(8,128)(2,1)S(1)} %get-tuple-element.132) | copy-start | bytes 589828
  114.7 20.0 %copy-start.4 = (f32[128,768]{1,0:T(8,128)}, f32[128,768]{1,0:T(8,128)S(1)}, u32[]{:S(2)}) copy-start(f32[128,768]{1,0:T(8,128)S(1)} %get-tuple-element.107.normed_ref) | copy-start | bytes 1179652
  114.7 7.1 %collective-permute-start.9 = (bf16[128,768]{1,0:T(8,128)(2,1)S(1)}, bf16[128,768]{1,0:T(8,128)(2,1)S(1)}, u32[]{:S(2)}, u32[]{:S(2)}) collective-permute-start(bf16[128,768]{1,0:T(8,128)(2,1)S(1)} %get-tuple-element.99.a_ref), channel_id=1, source_target_pairs={{0,16},{16,0},{8,24},{24,8},{1,17},{17,1},{9,25},{25,9},{2,18},{18... | collective-permute-start | bytes 589832 | tf_op jit(solution)/shard_map/ppermute | solution.py:496
  116.6 5.2 %collective-permute-start.10 = (bf16[128,768]{1,0:T(8,128)(2,1)S(1)}, bf16[128,768]{1,0:T(8,128)(2,1)S(1)}, u32[]{:S(2)}, u32[]{:S(2)}) collective-permute-start(bf16[128,768]{1,0:T(8,128)(2,1)S(1)} %get-tuple-element.99.a_ref), channel_id=1, source_target_pairs={{0,8},{8,0},{16,24},{24,16},{1,9},{9,1},{17,25},{25,17},{2,10},{10... | collective-permute-start | bytes 589832 | tf_op jit(solution)/shard_map/ppermute | solution.py:492
  121.8 1.4 collective-permute-start.11
  125.8 8.9 %copy-start.13 = (bf16[2,64,768]{2,1,0:T(8,128)(2,1)S(1)}, bf16[2,64,768]{2,1,0:T(8,128)(2,1)}, u32[]{:S(2)}) copy-start(bf16[2,64,768]{2,1,0:T(8,128)(2,1)} %param.13) | copy-start | bytes 589828
  125.8 8.9 %copy-start.17 = (f32[8,768]{1,0:T(8,128)S(1)}, f32[8,768]{1,0:T(8,128)}, u32[]{:S(2)}) copy-start(f32[8,768]{1,0:T(8,128)} %stack.94.vec_ref) | copy-start | bytes 73732
  125.8 1.8 collective-permute-start.12
  127.7 7.0 %collective-permute-start.13 = (bf16[128,768]{1,0:T(8,128)(2,1)S(1)}, bf16[128,768]{1,0:T(8,128)(2,1)S(1)}, u32[]{:S(2)}, u32[]{:S(2)}) collective-permute-start(bf16[128,768]{1,0:T(8,128)(2,1)S(1)} %get-tuple-element.106), channel_id=1, source_target_pairs={{0,16},{16,0},{8,24},{24,8},{1,17},{17,1},{9,25},{25,9},{2,18},{18... | collective-permute-start | bytes 589832 | tf_op jit(solution)/shard_map/ppermute | solution.py:496
  136.5 12.3 %copy-start.21 = (f32[8,768]{1,0:T(8,128)}, f32[8,768]{1,0:T(8,128)S(1)}, u32[]{:S(2)}) copy-start(f32[8,768]{1,0:T(8,128)S(1)} %get-tuple-element.140) | copy-start | bytes 73732
  136.5 6.1 %collective-permute-start.14 = (bf16[128,768]{1,0:T(8,128)(2,1)S(1)}, bf16[128,768]{1,0:T(8,128)(2,1)S(1)}, u32[]{:S(2)}, u32[]{:S(2)}) collective-permute-start(bf16[128,768]{1,0:T(8,128)(2,1)S(1)} %get-tuple-element.116.a_ref), channel_id=1, source_target_pairs={{0,16},{16,0},{8,24},{24,8},{1,17},{17,1},{9,25},{25,9},{2,18},{18... | collective-permute-start | bytes 589832 | tf_op jit(solution)/shard_map/ppermute | solution.py:496
  138.2 4.4 %collective-permute-start.15 = (bf16[128,768]{1,0:T(8,128)(2,1)S(1)}, bf16[128,768]{1,0:T(8,128)(2,1)S(1)}, u32[]{:S(2)}, u32[]{:S(2)}) collective-permute-start(bf16[128,768]{1,0:T(8,128)(2,1)S(1)} %get-tuple-element.116.a_ref), channel_id=1, source_target_pairs={{0,8},{8,0},{16,24},{24,16},{1,9},{9,1},{17,25},{25,17},{2,10},{10... | collective-permute-start | bytes 589832 | tf_op jit(solution)/shard_map/ppermute | solution.py:492
  142.6 1.5 collective-permute-start.16
  147.0 1.8 collective-permute-start.17
  148.8 7.1 %collective-permute-start.18 = (bf16[128,768]{1,0:T(8,128)(2,1)S(1)}, bf16[128,768]{1,0:T(8,128)(2,1)S(1)}, u32[]{:S(2)}, u32[]{:S(2)}) collective-permute-start(bf16[128,768]{1,0:T(8,128)(2,1)S(1)} %get-tuple-element.121), channel_id=1, source_target_pairs={{0,16},{16,0},{8,24},{24,8},{1,17},{17,1},{9,25},{25,9},{2,18},{18... | collective-permute-start | bytes 589832 | tf_op jit(solution)/shard_map/ppermute | solution.py:496
  158.1 2.1 collective-permute-start.19
  161.1 9.5 %collective-permute-start.20 = (bf16[192,768]{1,0:T(8,128)(2,1)}, bf16[192,768]{1,0:T(8,128)(2,1)S(1)}, u32[]{:S(2)}, u32[]{:S(2)}) collective-permute-start(bf16[192,768]{1,0:T(8,128)(2,1)} %fusion.6), channel_id=1, source_target_pairs={{0,16},{16,0},{8,24},{24,8},{1,17},{17,1},{9,25},{25,9},{2,18},{18... | collective-permute-start | bytes 884744 | tf_op jit(solution)/shard_map/ppermute | solution.py:496
  162.9 17.1 %all-to-all-start.3 = ((bf16[32,32,128]{2,1,0:T(8,128)(2,1)}), bf16[32,32,128]{2,1,0:T(8,128)(2,1)S(1)}, u32[]{:S(2)}, u32[]{:S(2)}) async-start(bf16[32,32,128]{2,1,0:T(8,128)(2,1)} %get-tuple-element.130), calls=%async_computation.3 | async-start | bytes 524288 | tf_op jit(solution)/shard_map/all_to_all | solution.py:500
  180.0 5.6 %copy-start.27 = (bf16[32,32,128]{2,1,0:T(8,128)(2,1)}, bf16[32,32,128]{2,1,0:T(8,128)(2,1)S(1)}, u32[]{:S(2)}) copy-start(bf16[32,32,128]{2,1,0:T(8,128)(2,1)S(1)} %all-to-all-done.3.do_ref) | copy-start | bytes 786436
  180.0 21.5 %all-to-all-start.4 = ((bf16[8,24,768]{2,1,0:T(8,128)(2,1)}), bf16[8,24,768]{2,1,0:T(8,128)(2,1)S(1)}, u32[]{:S(2)}, u32[]{:S(2)}) async-start(bf16[8,24,768]{2,1,0:T(8,128)(2,1)} %bitcast.41), calls=%async_computation.4 | async-start | bytes 589824 | tf_op jit(solution)/shard_map/all_to_all | solution.py:500
  185.7 33.4 %copy-start.3 = (bf16[8,128,768]{2,1,0:T(8,128)(2,1)S(1)}, bf16[8,128,768]{2,1,0:T(8,128)(2,1)}, u32[]{:S(2)}) copy-start(bf16[8,128,768]{2,1,0:T(8,128)(2,1)} %copy-done.2) | copy-start | bytes 4718596
  202.2 16.8 %copy-start.1 = (bf16[8,128,768]{2,1,0:T(8,128)(2,1)S(1)}, bf16[8,128,768]{2,1,0:T(8,128)(2,1)}, u32[]{:S(2)}) copy-start(bf16[8,128,768]{2,1,0:T(8,128)(2,1)} %copy-done) | copy-start | bytes 4718596
  202.3 16.8 %copy-start.23 = (s32[2]{0:T(128)S(1)}, s32[2]{0:T(128)}, u32[]{:S(2)}) copy-start(s32[2]{0:T(128)} %pad_add_fusion.1.place_ref) | copy-start | bytes 28
  202.3 26.7 %all-to-all-start.5 = ((bf16[32,96,128]{2,1,0:T(8,128)(2,1)}), bf16[32,96,128]{2,1,0:T(8,128)(2,1)}, u32[]{:S(2)}, u32[]{:S(2)}) async-start(bf16[32,96,128]{2,1,0:T(8,128)(2,1)} %get-tuple-element.134), calls=%async_computation.5 | async-start | bytes 1572864 | tf_op jit(solution)/shard_map/all_to_all | solution.py:500
  228.9 23.3 %all-to-all-start.6 = ((bf16[32,24,256]{2,1,0:T(8,128)(2,1)}), bf16[32,24,256]{2,1,0:T(8,128)(2,1)S(1)}, u32[]{:S(2)}, u32[]{:S(2)}) async-start(bf16[32,24,256]{2,1,0:T(8,128)(2,1)} %pad_maximum_fusion.2), calls=%async_computation.6 | async-start | bytes 786432 | tf_op jit(solution)/shard_map/all_to_all | solution.py:500
  254.8 3.4 %collective-permute-start.21 = (bf16[24,768]{1,0:T(8,128)(2,1)S(1)}, bf16[24,768]{1,0:T(8,128)(2,1)S(1)}, u32[]{:S(2)}, u32[]{:S(2)}) collective-permute-start(bf16[24,768]{1,0:T(8,128)(2,1)S(1)} %get-tuple-element.180), channel_id=1, source_target_pairs={{0,24},{8,16},{16,8},{24,0},{1,25},{9,17},{17,9},{25,1},{2,26},{10... | collective-permute-start | bytes 110600 | tf_op jit(solution)/shard_map/ppermute | solution.py:543
  255.2 4.0 %collective-permute-start.22 = (bf16[24,768]{1,0:T(8,128)(2,1)S(1)}, bf16[24,768]{1,0:T(8,128)(2,1)S(1)}, u32[]{:S(2)}, u32[]{:S(2)}) collective-permute-start(bf16[24,768]{1,0:T(8,128)(2,1)S(1)} %get-tuple-element.179), channel_id=1, source_target_pairs={{0,16},{16,0},{8,24},{24,8},{1,17},{17,1},{9,25},{25,9},{2,18},{18... | collective-permute-start | bytes 110600 | tf_op jit(solution)/shard_map/ppermute | solution.py:496
  255.6 3.5 %collective-permute-start.23 = (bf16[24,768]{1,0:T(8,128)(2,1)S(1)}, bf16[24,768]{1,0:T(8,128)(2,1)S(1)}, u32[]{:S(2)}, u32[]{:S(2)}) collective-permute-start(bf16[24,768]{1,0:T(8,128)(2,1)S(1)} %get-tuple-element.178), channel_id=1, source_target_pairs={{0,8},{8,0},{16,24},{24,16},{1,9},{9,1},{17,25},{25,17},{2,10},{10... | collective-permute-start | bytes 110600 | tf_op jit(solution)/shard_map/ppermute | solution.py:492
  (20 other events, 37.1 us)
Sparse Core Ops, SparseCore 0:
  28.3 69.9 all-gather.4
  101.1 59.2 all-gather.6
  163.9 87.0 reduce-scatter.1

commit v8 on v7

--- a/solution.py
+++ b/solution.py
@@ -334,13 +334,8 @@
 
 
 def normal_cdf(v):
-    bell = jnp.exp(-0.5 * v * v)
-    t = 1.0 / (1.0 + (0.3275911 * math.sqrt(0.5)) * jnp.abs(v))
-    tail = 0.5 * 1.061405429
-    for c in (-1.453152027, 1.421413741, -0.284496736, 0.254829592):
-        tail = tail * t + 0.5 * c
-    tail = tail * t * bell
-    return jnp.where(v < 0.0, tail, 1.0 - tail), bell * (1.0 / math.sqrt(2.0 * math.pi))
+    bell = jnp.exp(-0.5 * v * v) * (1.0 / math.sqrt(2.0 * math.pi))
+    return 0.5 * (1.0 + lax.erf(v * (1.0 / math.sqrt(2.0)))), bell
 
 
 def inner_kernel(a_ref, b_ref, c_ref, d_ref, wi_ref, wo_ref, bias_ref, act_ref, slope_ref, low_ref, keep_ref, send_ref):

time: 268 us -> 267 us (level)
  no operation moved by 1% of the time
where the time goes in v8:
time: 267 us
  waiting for transfers between devices  105 us (39%)
  starting transfers between devices  56.1 us (21%)
  Pallas kernels  49.7 us (19%)
  local copies, waits for them, and re-layouts  29 us (11%)
  between operations  14.5 us (5%)
  other arithmetic  12.4 us (5%)
    all_to_all x7, waiting for transfers between devices, swap(): lax.all_to_all(value, axes, split_axis=0, concat_axis=0, tiled=True, axis...  37.5 us
    all_to_all x7, starting transfers between devices, swap(): lax.all_to_all(value, axes, split_axis=0, concat_axis=0, tiled=True, axis...  35 us
    ppermute x1, waiting for transfers between devices, local(): lax.ppermute(slots, 'blk', [(i, (i + halves) % cycle) for i in range(cycl...  26.1 us
    ppermute x8, waiting for transfers between devices, by_x(): return lax.ppermute(value, 'head', [(0, 2), (2, 0), (1, 3), (3, 1)])  23.8 us
    pallas_call x11, Pallas kernels, call(): pl.pallas_call(kernel, out_shape=tuple((jax.ShapeDtypeStruct(shape, kind)...  16.8 us
    pallas_call x1, Pallas kernels, attend_back(): pl.pallas_call(functools.partial(attend_back_kernel, bq=bq, bk=bk, pack=p...  15.3 us
    ppermute x12, waiting for transfers between devices, by_core(): return lax.ppermute(value, 'head', [(0, 1), (1, 0), (2, 3), (3, 2)])  13.1 us
    pallas_call x1, Pallas kernels, attend(): pl.pallas_call(functools.partial(attend_kernel, bq=bq, bk=bk, pack=pack),...  11.1 us
  transfers between devices with their start and end apart: 34, of which 24 were waited for; matrix products, arithmetic and copies ran while one was open for 13% of the time, Pallas kernels for 19%

profile of v8, /device:TPU:0, one launch (start us, length us, event | category | flops | bytes accessed | tf_op | source)
XLA Modules:
  0.0 266.7 jit_solution(9201825257961677323)
XLA Ops:
  8.6 2.4 collective-permute-start
  12.6 1.8 head_slots.1
  14.3 5.0 %all-to-all-start = ((bf16[16,2,24,128]{3,2,1,0:T(8,128)(2,1)}), bf16[16,2,24,128]{3,2,1,0:T(8,128)(2,1)S(1)}, u32[]{:S(2)}, u32[]{:S(2)}) async-start(bf16[16,2,24,128]{3,2,1,0:T(8,128)(2,1)} %head_slots.1), calls=%async_computation | async-start | bytes 393216 | tf_op jit(solution)/shard_map/all_to_all | solution.py:495
  19.5 2.7 collective-permute-start.3
  23.0 2.7 %collective-permute-done.3 = bf16[64,768]{1,0:T(8,128)(2,1)S(1)} collective-permute-done((bf16[64,768]{1,0:T(8,128)(2,1)S(1)}, bf16[64,768]{1,0:T(8,128)(2,1)S(1)}, u32[]{:S(2)}, u32[]{:S(2)}) %collective-permute-start.3) | collective-permute-done | bytes 98336 | tf_op jit(solution)/shard_map/ppermute | solution.py:578
  25.7 2.4 all-to-all-done
  29.5 4.4 %all-to-all-start.1 = ((bf16[8,128,768]{2,1,0:T(8,128)(2,1)}), bf16[8,128,768]{2,1,0:T(8,128)(2,1)S(1)}, u32[]{:S(2)}, u32[]{:S(2)}) async-start(bf16[8,128,768]{2,1,0:T(8,128)(2,1)} %broadcast_in_dim.59), calls=%async_computation.1 | async-start | bytes 3145728 | tf_op jit(solution)/shard_map/all_to_all | solution.py:495
  36.3 2.6 collective-permute-start.4
  39.5 26.1 %collective-permute-done.4 = bf16[16,2,24,128]{3,2,1,0:T(8,128)(2,1)S(1)} collective-permute-done((bf16[16,2,24,128]{3,2,1,0:T(8,128)(2,1)S(1)}, bf16[16,2,24,128]{3,2,1,0:T(8,128)(2,1)S(1)}, u32[]{:S(2)}, u32[]{:S(2)}) %collective-permute-start.4) | collective-permute-done | bytes 196640 | tf_op jit(solution)/shard_map/ppermute | solution.py:603
  70.1 3.4 %collective-permute-done.5.b_ref = bf16[8,128,768]{2,1,0:T(8,128)(2,1)S(1)} collective-permute-done((bf16[8,128,768]{2,1,0:T(8,128)(2,1)S(1)}, bf16[8,128,768]{2,1,0:T(8,128)(2,1)S(1)}, u32[]{:S(2)}, u32[]{:S(2)}) %collective-permute-start.5) | collective-permute-done | bytes 1572896 | tf_op jit(solution)/shard_map/ppermute | solution.py:487
  74.6 5.0 %project.1 = (bf16[2048,64]{1,0:T(8,128)(2,1)}, bf16[2048,64]{1,0:T(8,128)(2,1)}, bf16[2048,64]{1,0:T(8,128)(2,1)}, bf16[64,2048]{1,0:T(8,128)(2,1)}, bf16[64,2048]{1,0:T(8,128)(2,1)}) custom-call(s32[2]{0:T(128)} %pad_add_fusion.1.place_ref, bf16[8,128,768]{2,1,0:T(8,128)(2,1)} %copy-done, bf16[8,128,768]{2,1,0:T(8,128)(2,1)} %copy-done.2, ...), custom_call_target="tpu_custom_call" | custom-call | flops 1000000 | bytes 1024 | tf_op jit(solution)/shard_map/project/pallas_call | solution.py:85
  79.6 11.1 %attend.1 = (bf16[32,32,128]{2,1,0:T(8,128)(2,1)}, f32[64,2048]{1,0:T(8,128)}, f32[1,2048]{1,0:T(1,128)}) custom-call(s32[4]{0:T(128)} %get-tuple-element.83.lo_ref, s32[4]{0:T(128)} %get-tuple-element.84.hi_ref, bf16[2048,64]{1,0:T(8,128)(2,1)} %get-tuple-element.90.q_ref, bf16[2048,64]{1,0:T(8,128)(2,1)} %get-tuple-element.91.k_ref, ...), custom_call_target="tpu_custom_call" | custom-call | flops 1000000 | bytes 1024 | tf_op jit(solution)/shard_map/attend/pallas_call | solution.py:195
  90.7 7.5 %all-to-all-start.2 = ((bf16[32,32,128]{2,1,0:T(8,128)(2,1)}), bf16[32,32,128]{2,1,0:T(8,128)(2,1)S(1)}, u32[]{:S(2)}, u32[]{:S(2)}) async-start(bf16[32,32,128]{2,1,0:T(8,128)(2,1)} %get-tuple-element.94), calls=%async_computation.2 | async-start | bytes 524288 | tf_op jit(solution)/shard_map/all_to_all | solution.py:495
  99.5 1.8 collective-permute-start.6
  101.4 1.8 fusion.16
  103.3 5.7 %all-to-all-done.2.slots_ref = bf16[32,32,128]{2,1,0:T(8,128)(2,1)S(1)} async-done(((bf16[32,32,128]{2,1,0:T(8,128)(2,1)}), bf16[32,32,128]{2,1,0:T(8,128)(2,1)S(1)}, u32[]{:S(2)}, u32[]{:S(2)}) %all-to-all-start.2) | async-done | bytes 262176 | tf_op jit(solution)/shard_map/all_to_all | solution.py:495
  109.0 1.7 collective-permute-done.6
  110.7 1.6 collective-permute-done.7
  114.7 1.9 collective-permute-start.9
  116.6 5.2 %collective-permute-done.9.b_ref = bf16[128,768]{1,0:T(8,128)(2,1)S(1)} collective-permute-done((bf16[128,768]{1,0:T(8,128)(2,1)S(1)}, bf16[128,768]{1,0:T(8,128)(2,1)S(1)}, u32[]{:S(2)}, u32[]{:S(2)}) %collective-permute-start.9) | collective-permute-done | bytes 196640 | tf_op jit(solution)/shard_map/ppermute | solution.py:491
  123.3 2.0 inner.1
  125.5 1.6 collective-permute-done.12.got_ref
  127.2 1.8 collective-permute-start.13
  129.0 5.5 %collective-permute-done.13.got_ref = bf16[128,768]{1,0:T(8,128)(2,1)S(1)} collective-permute-done((bf16[128,768]{1,0:T(8,128)(2,1)S(1)}, bf16[128,768]{1,0:T(8,128)(2,1)S(1)}, u32[]{:S(2)}, u32[]{:S(2)}) %collective-permute-start.13) | collective-permute-done | bytes 196640 | tf_op jit(solution)/shard_map/ppermute | solution.py:491
  136.2 1.5 collective-permute-start.14
  137.7 4.9 %collective-permute-done.14.b_ref = bf16[128,768]{1,0:T(8,128)(2,1)S(1)} collective-permute-done((bf16[128,768]{1,0:T(8,128)(2,1)S(1)}, bf16[128,768]{1,0:T(8,128)(2,1)S(1)}, u32[]{:S(2)}, u32[]{:S(2)}) %collective-permute-start.14) | collective-permute-done | bytes 196640 | tf_op jit(solution)/shard_map/ppermute | solution.py:491
  142.6 1.5 collective-permute-done.16.d_ref
  144.1 2.9 %inner_back.1 = (bf16[512,768]{1,0:T(8,128)(2,1)S(1)}, bf16[512,768]{1,0:T(8,128)(2,1)S(1)}, f32[1,768]{1,0:T(1,128)S(1)}, f32[256,768]{1,0:T(8,128)S(1)}, bf16[256,768]{1,0:T(8,128)(2,1)S(1)}) custom-call(bf16[128,768]{1,0:T(8,128)(2,1)S(1)} %get-tuple-element.116.a_ref, bf16[128,768]{1,0:T(8,128)(2,1)S(1)} %collective-permute-done.14.b_ref, ...), custom_call_target="tpu_custom_call" | custom-call | flops 1000000 | bytes 1024 | tf_op jit(solution)/shard_map/inner_back/pallas_call | solution.py:294
  147.2 1.5 collective-permute-done.17.got_ref
  148.9 1.5 collective-permute-start.18
  150.4 2.9 %feed_grad.1 = bf16[8,8,24,768]{3,2,1,0:T(8,128)(2,1)} custom-call(bf16[512,768]{1,0:T(8,128)(2,1)S(1)} %get-tuple-element.122.low_ref, bf16[512,768]{1,0:T(8,128)(2,1)S(1)} %get-tuple-element.123.inner_ref, bf16[512,768]{1,0:T(8,128)(2,1)S(1)} %get-tuple-element.124.act_ref, bf16[512,768]{1,0:T(8,128)(2,1)S(1)} %get-tuple-element.125.ffn_ref), custom_call_target="tpu_custom_call" | custom-call | flops 1000000 | bytes 1024 | tf_op jit(solution)/shard_map/feed_grad/pallas_call | solution.py:294
  153.2 2.7 %collective-permute-done.18.got_ref = bf16[128,768]{1,0:T(8,128)(2,1)S(1)} collective-permute-done((bf16[128,768]{1,0:T(8,128)(2,1)S(1)}, bf16[128,768]{1,0:T(8,128)(2,1)S(1)}, u32[]{:S(2)}, u32[]{:S(2)}) %collective-permute-start.18) | collective-permute-done | bytes 196640 | tf_op jit(solution)/shard_map/ppermute | solution.py:491
  156.0 1.5 branch_back.1
  158.2 2.0 collective-permute-done.19
  162.5 4.9 %all-to-all-start.3 = ((bf16[32,32,128]{2,1,0:T(8,128)(2,1)}), bf16[32,32,128]{2,1,0:T(8,128)(2,1)S(1)}, u32[]{:S(2)}, u32[]{:S(2)}) async-start(bf16[32,32,128]{2,1,0:T(8,128)(2,1)} %get-tuple-element.130), calls=%async_computation.3 | async-start | bytes 524288 | tf_op jit(solution)/shard_map/all_to_all | solution.py:495
  167.5 3.0 %collective-permute-done.20 = bf16[192,768]{1,0:T(8,128)(2,1)S(1)} collective-permute-done((bf16[192,768]{1,0:T(8,128)(2,1)}, bf16[192,768]{1,0:T(8,128)(2,1)S(1)}, u32[]{:S(2)}, u32[]{:S(2)}) %collective-permute-start.20) | collective-permute-done | bytes 294944 | tf_op jit(solution)/shard_map/ppermute | solution.py:491
  170.4 1.9 fusion.3
  172.3 7.9 %all-to-all-done.3.do_ref = bf16[32,32,128]{2,1,0:T(8,128)(2,1)S(1)} async-done(((bf16[32,32,128]{2,1,0:T(8,128)(2,1)}), bf16[32,32,128]{2,1,0:T(8,128)(2,1)S(1)}, u32[]{:S(2)}, u32[]{:S(2)}) %all-to-all-start.3) | async-done | bytes 262176 | tf_op jit(solution)/shard_map/all_to_all | solution.py:495
  180.2 5.8 %all-to-all-start.4 = ((bf16[8,24,768]{2,1,0:T(8,128)(2,1)}), bf16[8,24,768]{2,1,0:T(8,128)(2,1)S(1)}, u32[]{:S(2)}, u32[]{:S(2)}) async-start(bf16[8,24,768]{2,1,0:T(8,128)(2,1)} %bitcast.41), calls=%async_computation.4 | async-start | bytes 589824 | tf_op jit(solution)/shard_map/all_to_all | solution.py:495
  186.1 15.3 %attend_back.1 = (bf16[32,96,128]{2,1,0:T(8,128)(2,1)}, bf16[192,2048]{1,0:T(8,128)(2,1)}, f32[1,128]{1,0:T(1,128)}) custom-call(s32[4]{0:T(128)} %get-tuple-element.110.lo_ref, s32[4]{0:T(128)} %get-tuple-element.111.hi_ref, bf16[2048,64]{1,0:T(8,128)(2,1)} %get-tuple-element.90.q_ref, bf16[2048,64]{1,0:T(8,128)(2,1)} %get-tuple-element.91.k_ref, ...), custom_call_target="tpu_custom_call" | custom-call | flops 1000000 | bytes 1024 | tf_op jit(solution)/shard_map/attend_back/pallas_call | solution.py:273
  202.7 4.6 %all-to-all-start.5 = ((bf16[32,96,128]{2,1,0:T(8,128)(2,1)}), bf16[32,96,128]{2,1,0:T(8,128)(2,1)}, u32[]{:S(2)}, u32[]{:S(2)}) async-start(bf16[32,96,128]{2,1,0:T(8,128)(2,1)} %get-tuple-element.134), calls=%async_computation.5 | async-start | bytes 1572864 | tf_op jit(solution)/shard_map/all_to_all | solution.py:495
  211.0 1.7 copy.83
  217.9 1.5 copy.86
  223.1 6.2 %all-to-all-done.5.slots_ref = bf16[32,96,128]{2,1,0:T(8,128)(2,1)} async-done(((bf16[32,96,128]{2,1,0:T(8,128)(2,1)}), bf16[32,96,128]{2,1,0:T(8,128)(2,1)}, u32[]{:S(2)}, u32[]{:S(2)}) %all-to-all-start.5) | async-done | bytes 786464 | tf_op jit(solution)/shard_map/all_to_all | solution.py:495
  229.3 2.6 all-to-all-start.6
  231.9 2.3 copy.79
  234.9 3.2 %tokens.1 = bf16[128,768]{1,0:T(8,128)(2,1)} custom-call(bf16[32,96,128]{2,1,0:T(8,128)(2,1)} %all-to-all-done.5.slots_ref, bf16[3,768,768]{2,1,0:T(8,128)(2,1)S(1)} %bitcast.158, f32[128,768]{1,0:T(8,128)S(1)} %get-tuple-element.136.first_ref), custom_call_target="tpu_custom_call" | custom-call | flops 1000000 | bytes 1024 | tf_op jit(solution)/shard_map/tokens/pallas_call | solution.py:294
  238.1 14.5 %all-to-all-done.6.slots_ref = bf16[32,24,256]{2,1,0:T(8,128)(2,1)S(1)} async-done(((bf16[32,24,256]{2,1,0:T(8,128)(2,1)}), bf16[32,24,256]{2,1,0:T(8,128)(2,1)S(1)}, u32[]{:S(2)}, u32[]{:S(2)}) %all-to-all-start.6) | async-done | bytes 393248 | tf_op jit(solution)/shard_map/all_to_all | solution.py:495
  (188 shorter events, 46.3 us)
Async XLA Ops:
  7.2 4.7 %copy-start.32 = (bf16[96]{0:T(256)(128)(2,1)S(1)}, bf16[96]{0:T(256)(128)(2,1)}, u32[]{:S(2)}) copy-start(bf16[96]{0:T(256)(128)(2,1)} %param.19) | copy-start | bytes 580
  7.2 12.2 %copy-start.9 = (bf16[2,64,768]{2,1,0:T(8,128)(2,1)S(1)}, bf16[2,64,768]{2,1,0:T(8,128)(2,1)}, u32[]{:S(2)}) copy-start(bf16[2,64,768]{2,1,0:T(8,128)(2,1)} %param.11) | copy-start | bytes 589828
  8.6 13.6 %copy-start.30 = (bf16[96,768]{1,0:T(8,128)(2,1)S(1)}, bf16[96,768]{1,0:T(8,128)(2,1)}, u32[]{:S(2)}) copy-start(bf16[96,768]{1,0:T(8,128)(2,1)} %param.17) | copy-start | bytes 442372
  8.6 13.6 %copy-start.31 = (bf16[24,768]{1,0:T(8,128)(2,1)S(1)}, bf16[24,768]{1,0:T(8,128)(2,1)}, u32[]{:S(2)}) copy-start(bf16[24,768]{1,0:T(8,128)(2,1)} %param.15) | copy-start | bytes 110596
  8.6 13.5 %collective-permute-start = (bf16[24,768]{1,0:T(8,128)(2,1)S(1)}, bf16[24,768]{1,0:T(8,128)(2,1)S(1)}, u32[]{:S(2)}, u32[]{:S(2)}) collective-permute-start(bf16[24,768]{1,0:T(8,128)(2,1)S(1)} %bitcast.191), channel_id=1, source_target_pairs={{0,24},{8,16},{16,8},{24,0},{1,25},{9,17},{17,9},{25,1},{2,26},{10... | collective-permute-start | bytes 110600 | tf_op jit(solution)/shard_map/ppermute | solution.py:538
  11.1 11.0 %collective-permute-start.1 = (bf16[24,768]{1,0:T(8,128)(2,1)S(1)}, bf16[24,768]{1,0:T(8,128)(2,1)S(1)}, u32[]{:S(2)}, u32[]{:S(2)}) collective-permute-start(bf16[24,768]{1,0:T(8,128)(2,1)S(1)} %bitcast.192), channel_id=1, source_target_pairs={{0,16},{16,0},{8,24},{24,8},{1,17},{17,1},{9,25},{25,9},{2,18},{18... | collective-permute-start | bytes 110600 | tf_op jit(solution)/shard_map/ppermute | solution.py:491
  11.8 10.4 %collective-permute-start.2 = (bf16[24,768]{1,0:T(8,128)(2,1)S(1)}, bf16[24,768]{1,0:T(8,128)(2,1)S(1)}, u32[]{:S(2)}, u32[]{:S(2)}) collective-permute-start(bf16[24,768]{1,0:T(8,128)(2,1)S(1)} %bitcast.193), channel_id=1, source_target_pairs={{0,8},{8,0},{16,24},{24,16},{1,9},{9,1},{17,25},{25,17},{2,10},{10... | collective-permute-start | bytes 110600 | tf_op jit(solution)/shard_map/ppermute | solution.py:487
  14.3 13.8 %all-to-all-start = ((bf16[16,2,24,128]{3,2,1,0:T(8,128)(2,1)}), bf16[16,2,24,128]{3,2,1,0:T(8,128)(2,1)S(1)}, u32[]{:S(2)}, u32[]{:S(2)}) async-start(bf16[16,2,24,128]{3,2,1,0:T(8,128)(2,1)} %head_slots.1), calls=%async_computation | async-start | bytes 393216 | tf_op jit(solution)/shard_map/all_to_all | solution.py:495
  19.4 79.2 %all-gather.5.cloned.1.call-start = ((), (), s32[]{:S(2)}) async-start(), calls=%async_computation.9 | async-start | bytes 2985984 | tf_op jit(solution)/shard_map/all_gather | solution.py:617
  19.5 6.2 %collective-permute-start.3 = (bf16[64,768]{1,0:T(8,128)(2,1)S(1)}, bf16[64,768]{1,0:T(8,128)(2,1)S(1)}, u32[]{:S(2)}, u32[]{:S(2)}) collective-permute-start(bf16[64,768]{1,0:T(8,128)(2,1)S(1)} %get-tuple-element.175), channel_id=1, source_target_pairs={{0,4},{1,5},{2,6},{3,7},{4,0},{5,1},{6,2},{7,3},{8,12},{9,13},{10,... | collective-permute-start | bytes 294920 | tf_op jit(solution)/shard_map/ppermute | solution.py:578
  29.5 4.5 %copy-start.33 = (s32[2,32]{1,0:T(2,128)S(1)}, s32[2,32]{1,0:T(2,128)}, u32[]{:S(2)}) copy-start(s32[2,32]{1,0:T(2,128)} %param.12) | copy-start | bytes 772
  29.5 40.6 %all-to-all-start.1 = ((bf16[8,128,768]{2,1,0:T(8,128)(2,1)}), bf16[8,128,768]{2,1,0:T(8,128)(2,1)S(1)}, u32[]{:S(2)}, u32[]{:S(2)}) async-start(bf16[8,128,768]{2,1,0:T(8,128)(2,1)} %broadcast_in_dim.59), calls=%async_computation.1 | async-start | bytes 3145728 | tf_op jit(solution)/shard_map/all_to_all | solution.py:495
  33.9 198.0 %all-gather.7.cloned.1.call-start = ((), (), s32[]{:S(2)}) async-start(), calls=%async_computation.10 | async-start | bytes 3649536 | tf_op jit(solution)/shard_map/all_gather | solution.py:616
  36.3 29.4 %collective-permute-start.4 = (bf16[16,2,24,128]{3,2,1,0:T(8,128)(2,1)S(1)}, bf16[16,2,24,128]{3,2,1,0:T(8,128)(2,1)S(1)}, u32[]{:S(2)}, u32[]{:S(2)}) collective-permute-start(bf16[16,2,24,128]{3,2,1,0:T(8,128)(2,1)S(1)} %all-to-all-done), channel_id=1, source_target_pairs={{0,4},{1,5},{2,6},{3,7},{4,0},{5,1},{6,2},{7,3},{8,12},{9,13},{10,... | collective-permute-start | bytes 589832 | tf_op jit(solution)/shard_map/ppermute | solution.py:603
  70.1 3.4 %collective-permute-start.5 = (bf16[8,128,768]{2,1,0:T(8,128)(2,1)S(1)}, bf16[8,128,768]{2,1,0:T(8,128)(2,1)S(1)}, u32[]{:S(2)}, u32[]{:S(2)}) collective-permute-start(bf16[8,128,768]{2,1,0:T(8,128)(2,1)S(1)} %all-to-all-done.1.a_ref), channel_id=1, source_target_pairs={{0,8},{8,0},{16,24},{24,16},{1,9},{9,1},{17,25},{25,17},{2,10},{10... | collective-permute-start | bytes 4718600 | tf_op jit(solution)/shard_map/ppermute | solution.py:487
  90.7 18.2 %all-to-all-start.2 = ((bf16[32,32,128]{2,1,0:T(8,128)(2,1)}), bf16[32,32,128]{2,1,0:T(8,128)(2,1)S(1)}, u32[]{:S(2)}, u32[]{:S(2)}) async-start(bf16[32,32,128]{2,1,0:T(8,128)(2,1)} %get-tuple-element.94), calls=%async_computation.2 | async-start | bytes 524288 | tf_op jit(solution)/shard_map/all_to_all | solution.py:495
  98.3 155.8 %reduce-scatter.2.cloned.1.call-start = ((), (), s32[]{:S(2)}) async-start(), calls=%async_computation.8 | async-start | bytes 2654208 | tf_op jit(solution)/shard_map/reduce_scatter | solution.py:733
  99.5 11.1 %collective-permute-start.6 = (bf16[192,768]{1,0:T(8,128)(2,1)S(1)}, bf16[192,768]{1,0:T(8,128)(2,1)S(1)}, u32[]{:S(2)}, u32[]{:S(2)}) collective-permute-start(bf16[192,768]{1,0:T(8,128)(2,1)S(1)} %bitcast.179), channel_id=1, source_target_pairs={{0,16},{16,0},{8,24},{24,8},{1,17},{17,1},{9,25},{25,9},{2,18},{18... | collective-permute-start | bytes 884744 | tf_op jit(solution)/shard_map/ppermute | solution.py:491
  101.4 9.3 %collective-permute-start.8 = (bf16[192,768]{1,0:T(8,128)(2,1)S(1)}, bf16[192,768]{1,0:T(8,128)(2,1)S(1)}, u32[]{:S(2)}, u32[]{:S(2)}) collective-permute-start(bf16[192,768]{1,0:T(8,128)(2,1)S(1)} %bitcast.180), channel_id=1, source_target_pairs={{0,8},{8,0},{16,24},{24,16},{1,9},{9,1},{17,25},{25,17},{2,10},{10... | collective-permute-start | bytes 884744 | tf_op jit(solution)/shard_map/ppermute | solution.py:487
  110.7 1.6 collective-permute-start.7
  114.7 10.6 %copy-start.14 = (bf16[128,768]{1,0:T(8,128)(2,1)}, bf16[128,768]{1,0:T(8,128)(2,1)S(1)}, u32[]{:S(2)}) copy-start(bf16[128,768]{1,0:T(8,128)(2,1)S(1)} %get-tuple-element.132) | copy-start | bytes 589828
  114.7 19.8 %copy-start.4 = (f32[128,768]{1,0:T(8,128)}, f32[128,768]{1,0:T(8,128)S(1)}, u32[]{:S(2)}) copy-start(f32[128,768]{1,0:T(8,128)S(1)} %get-tuple-element.107.normed_ref) | copy-start | bytes 1179652
  114.7 7.1 %collective-permute-start.9 = (bf16[128,768]{1,0:T(8,128)(2,1)S(1)}, bf16[128,768]{1,0:T(8,128)(2,1)S(1)}, u32[]{:S(2)}, u32[]{:S(2)}) collective-permute-start(bf16[128,768]{1,0:T(8,128)(2,1)S(1)} %get-tuple-element.99.a_ref), channel_id=1, source_target_pairs={{0,16},{16,0},{8,24},{24,8},{1,17},{17,1},{9,25},{25,9},{2,18},{18... | collective-permute-start | bytes 589832 | tf_op jit(solution)/shard_map/ppermute | solution.py:491
  116.6 5.2 %collective-permute-start.10 = (bf16[128,768]{1,0:T(8,128)(2,1)S(1)}, bf16[128,768]{1,0:T(8,128)(2,1)S(1)}, u32[]{:S(2)}, u32[]{:S(2)}) collective-permute-start(bf16[128,768]{1,0:T(8,128)(2,1)S(1)} %get-tuple-element.99.a_ref), channel_id=1, source_target_pairs={{0,8},{8,0},{16,24},{24,16},{1,9},{9,1},{17,25},{25,17},{2,10},{10... | collective-permute-start | bytes 589832 | tf_op jit(solution)/shard_map/ppermute | solution.py:487
  121.8 1.4 collective-permute-start.11
  125.3 9.2 %copy-start.13 = (bf16[2,64,768]{2,1,0:T(8,128)(2,1)S(1)}, bf16[2,64,768]{2,1,0:T(8,128)(2,1)}, u32[]{:S(2)}) copy-start(bf16[2,64,768]{2,1,0:T(8,128)(2,1)} %param.13) | copy-start | bytes 589828
  125.3 9.2 %copy-start.17 = (f32[8,768]{1,0:T(8,128)S(1)}, f32[8,768]{1,0:T(8,128)}, u32[]{:S(2)}) copy-start(f32[8,768]{1,0:T(8,128)} %stack.94.vec_ref) | copy-start | bytes 73732
  125.3 1.8 collective-permute-start.12
  127.2 7.3 %collective-permute-start.13 = (bf16[128,768]{1,0:T(8,128)(2,1)S(1)}, bf16[128,768]{1,0:T(8,128)(2,1)S(1)}, u32[]{:S(2)}, u32[]{:S(2)}) collective-permute-start(bf16[128,768]{1,0:T(8,128)(2,1)S(1)} %get-tuple-element.106), channel_id=1, source_target_pairs={{0,16},{16,0},{8,24},{24,8},{1,17},{17,1},{9,25},{25,9},{2,18},{18... | collective-permute-start | bytes 589832 | tf_op jit(solution)/shard_map/ppermute | solution.py:491
  136.2 12.6 %copy-start.21 = (f32[8,768]{1,0:T(8,128)}, f32[8,768]{1,0:T(8,128)S(1)}, u32[]{:S(2)}) copy-start(f32[8,768]{1,0:T(8,128)S(1)} %get-tuple-element.140) | copy-start | bytes 73732
  136.2 6.4 %collective-permute-start.14 = (bf16[128,768]{1,0:T(8,128)(2,1)S(1)}, bf16[128,768]{1,0:T(8,128)(2,1)S(1)}, u32[]{:S(2)}, u32[]{:S(2)}) collective-permute-start(bf16[128,768]{1,0:T(8,128)(2,1)S(1)} %get-tuple-element.116.a_ref), channel_id=1, source_target_pairs={{0,16},{16,0},{8,24},{24,8},{1,17},{17,1},{9,25},{25,9},{2,18},{18... | collective-permute-start | bytes 589832 | tf_op jit(solution)/shard_map/ppermute | solution.py:491
  137.7 4.9 %collective-permute-start.15 = (bf16[128,768]{1,0:T(8,128)(2,1)S(1)}, bf16[128,768]{1,0:T(8,128)(2,1)S(1)}, u32[]{:S(2)}, u32[]{:S(2)}) collective-permute-start(bf16[128,768]{1,0:T(8,128)(2,1)S(1)} %get-tuple-element.116.a_ref), channel_id=1, source_target_pairs={{0,8},{8,0},{16,24},{24,16},{1,9},{9,1},{17,25},{25,17},{2,10},{10... | collective-permute-start | bytes 589832 | tf_op jit(solution)/shard_map/ppermute | solution.py:487
  142.6 1.5 collective-permute-start.16
  147.0 1.8 collective-permute-start.17
  148.9 7.1 %collective-permute-start.18 = (bf16[128,768]{1,0:T(8,128)(2,1)S(1)}, bf16[128,768]{1,0:T(8,128)(2,1)S(1)}, u32[]{:S(2)}, u32[]{:S(2)}) collective-permute-start(bf16[128,768]{1,0:T(8,128)(2,1)S(1)} %get-tuple-element.121), channel_id=1, source_target_pairs={{0,16},{16,0},{8,24},{24,8},{1,17},{17,1},{9,25},{25,9},{2,18},{18... | collective-permute-start | bytes 589832 | tf_op jit(solution)/shard_map/ppermute | solution.py:491
  158.1 2.1 collective-permute-start.19
  161.2 9.3 %collective-permute-start.20 = (bf16[192,768]{1,0:T(8,128)(2,1)}, bf16[192,768]{1,0:T(8,128)(2,1)S(1)}, u32[]{:S(2)}, u32[]{:S(2)}) collective-permute-start(bf16[192,768]{1,0:T(8,128)(2,1)} %fusion.6), channel_id=1, source_target_pairs={{0,16},{16,0},{8,24},{24,8},{1,17},{17,1},{9,25},{25,9},{2,18},{18... | collective-permute-start | bytes 884744 | tf_op jit(solution)/shard_map/ppermute | solution.py:491
  162.5 17.7 %all-to-all-start.3 = ((bf16[32,32,128]{2,1,0:T(8,128)(2,1)}), bf16[32,32,128]{2,1,0:T(8,128)(2,1)S(1)}, u32[]{:S(2)}, u32[]{:S(2)}) async-start(bf16[32,32,128]{2,1,0:T(8,128)(2,1)} %get-tuple-element.130), calls=%async_computation.3 | async-start | bytes 524288 | tf_op jit(solution)/shard_map/all_to_all | solution.py:495
  180.2 5.8 %copy-start.27 = (bf16[32,32,128]{2,1,0:T(8,128)(2,1)}, bf16[32,32,128]{2,1,0:T(8,128)(2,1)S(1)}, u32[]{:S(2)}) copy-start(bf16[32,32,128]{2,1,0:T(8,128)(2,1)S(1)} %all-to-all-done.3.do_ref) | copy-start | bytes 786436
  180.2 21.8 %all-to-all-start.4 = ((bf16[8,24,768]{2,1,0:T(8,128)(2,1)}), bf16[8,24,768]{2,1,0:T(8,128)(2,1)S(1)}, u32[]{:S(2)}, u32[]{:S(2)}) async-start(bf16[8,24,768]{2,1,0:T(8,128)(2,1)} %bitcast.41), calls=%async_computation.4 | async-start | bytes 589824 | tf_op jit(solution)/shard_map/all_to_all | solution.py:495
  186.1 33.3 %copy-start.3 = (bf16[8,128,768]{2,1,0:T(8,128)(2,1)S(1)}, bf16[8,128,768]{2,1,0:T(8,128)(2,1)}, u32[]{:S(2)}) copy-start(bf16[8,128,768]{2,1,0:T(8,128)(2,1)} %copy-done.2) | copy-start | bytes 4718596
  202.7 16.7 %copy-start.1 = (bf16[8,128,768]{2,1,0:T(8,128)(2,1)S(1)}, bf16[8,128,768]{2,1,0:T(8,128)(2,1)}, u32[]{:S(2)}) copy-start(bf16[8,128,768]{2,1,0:T(8,128)(2,1)} %copy-done) | copy-start | bytes 4718596
  202.7 16.7 %copy-start.23 = (s32[2]{0:T(128)S(1)}, s32[2]{0:T(128)}, u32[]{:S(2)}) copy-start(s32[2]{0:T(128)} %pad_add_fusion.1.place_ref) | copy-start | bytes 28
  202.7 26.6 %all-to-all-start.5 = ((bf16[32,96,128]{2,1,0:T(8,128)(2,1)}), bf16[32,96,128]{2,1,0:T(8,128)(2,1)}, u32[]{:S(2)}, u32[]{:S(2)}) async-start(bf16[32,96,128]{2,1,0:T(8,128)(2,1)} %get-tuple-element.134), calls=%async_computation.5 | async-start | bytes 1572864 | tf_op jit(solution)/shard_map/all_to_all | solution.py:495
  229.3 23.3 %all-to-all-start.6 = ((bf16[32,24,256]{2,1,0:T(8,128)(2,1)}), bf16[32,24,256]{2,1,0:T(8,128)(2,1)S(1)}, u32[]{:S(2)}, u32[]{:S(2)}) async-start(bf16[32,24,256]{2,1,0:T(8,128)(2,1)} %pad_maximum_fusion.2), calls=%async_computation.6 | async-start | bytes 786432 | tf_op jit(solution)/shard_map/all_to_all | solution.py:495
  255.1 3.4 %collective-permute-start.21 = (bf16[24,768]{1,0:T(8,128)(2,1)S(1)}, bf16[24,768]{1,0:T(8,128)(2,1)S(1)}, u32[]{:S(2)}, u32[]{:S(2)}) collective-permute-start(bf16[24,768]{1,0:T(8,128)(2,1)S(1)} %get-tuple-element.180), channel_id=1, source_target_pairs={{0,24},{8,16},{16,8},{24,0},{1,25},{9,17},{17,9},{25,1},{2,26},{10... | collective-permute-start | bytes 110600 | tf_op jit(solution)/shard_map/ppermute | solution.py:538
  255.5 4.0 %collective-permute-start.22 = (bf16[24,768]{1,0:T(8,128)(2,1)S(1)}, bf16[24,768]{1,0:T(8,128)(2,1)S(1)}, u32[]{:S(2)}, u32[]{:S(2)}) collective-permute-start(bf16[24,768]{1,0:T(8,128)(2,1)S(1)} %get-tuple-element.179), channel_id=1, source_target_pairs={{0,16},{16,0},{8,24},{24,8},{1,17},{17,1},{9,25},{25,9},{2,18},{18... | collective-permute-start | bytes 110600 | tf_op jit(solution)/shard_map/ppermute | solution.py:491
  255.8 3.6 %collective-permute-start.23 = (bf16[24,768]{1,0:T(8,128)(2,1)S(1)}, bf16[24,768]{1,0:T(8,128)(2,1)S(1)}, u32[]{:S(2)}, u32[]{:S(2)}) collective-permute-start(bf16[24,768]{1,0:T(8,128)(2,1)S(1)} %get-tuple-element.178), channel_id=1, source_target_pairs={{0,8},{8,0},{16,24},{24,16},{1,9},{9,1},{17,25},{25,17},{2,10},{10... | collective-permute-start | bytes 110600 | tf_op jit(solution)/shard_map/ppermute | solution.py:487
  (20 other events, 37.8 us)
Sparse Core Ops, SparseCore 0:
  28.3 69.8 all-gather.4
  101.0 59.3 all-gather.6
  163.9 87.1 reduce-scatter.1

commit v9 on v8

--- a/solution.py
+++ b/solution.py
@@ -20,7 +20,7 @@
 masked_score = -1e30
 VMEM = pl.BlockSpec(memory_space=pltpu.VMEM)
 SMEM = pl.BlockSpec(memory_space=pltpu.SMEM)
-SMALL = pltpu.CompilerParams(vmem_limit_bytes=20 << 20)
+SMALL = pltpu.CompilerParams(vmem_limit_bytes=14 << 20)
 LARGE = pltpu.CompilerParams(vmem_limit_bytes=56 << 20)
 
 
@@ -638,9 +638,9 @@
         inner_bias_part[None],
     )
     tokens_a = spread_over(pair_x, BOTH, cycle, cube)
-    prepared = (qk_weight, v_weight, unit_bias, small_rows, spans, place, ranges)
+    prepared = (qk_weight, v_weight, unit_bias, spans, place, ranges)
     tokens_a, prepared = lax.optimization_barrier((tokens_a, prepared))
-    qk_weight, v_weight, unit_bias, small_rows, spans, place, ranges = prepared
+    qk_weight, v_weight, unit_bias, spans, place, ranges = prepared
     tokens_b = by_core(tokens_a)
 
     per = max(1, 256 // tokens)
@@ -661,8 +661,8 @@
     outer_part = ffn[:, groups * rows_dev : last].reshape(ff_part, depth)
     out_part = ffn[:, last:].reshape(depth // groups, depth)
     attn_slots = swap(attn_out, BOTH)
-    out_x, attn_slots, inner_part, outer_part = lax.optimization_barrier(
-        (by_x(out_part), attn_slots, inner_part, outer_part)
+    out_x, attn_slots, inner_part, outer_part, small_rows = lax.optimization_barrier(
+        (by_x(out_part), attn_slots, inner_part, outer_part, small_rows)
     )
     out_all = in_order((out_part, out_x, by_core(out_part), by_core(out_x))).reshape(depth, depth)
 

time: 267 us -> 269 us (level)
  starting transfers between devices: 56.1 us -> 49.1 us
  waiting for transfers between devices: 105 us -> 112 us
    ppermute x8, waiting for transfers between devices: 23.8 us -> 33.3 us  [by_x(): return lax.ppermute(value, 'head', [(0, 2), (2, 0), (1, 3), (3, 1)])]
    ppermute x8, starting transfers between devices: 10.9 us -> 5.84 us  [by_x(): return lax.ppermute(value, 'head', [(0, 2), (2, 0), (1, 3), (3, 1)])]
  transfers between devices with their start and end apart: 34 -> 34, of which waited for: 24 -> 25; matrix products, arithmetic and copies ran while one was open for 13% -> 13% of each run, Pallas kernels for 19% -> 19%
where the time goes in v9:
time: 269 us; the launch traced here: 267 us
  waiting for transfers between devices  112 us (42%)
  Pallas kernels  49.6 us (18%)
  starting transfers between devices  49.1 us (18%)
  local copies, waits for them, and re-layouts  29.8 us (11%)
  between operations  14.5 us (5%)
  other arithmetic  12.3 us (5%)
    all_to_all x7, waiting for transfers between devices, swap(): lax.all_to_all(value, axes, split_axis=0, concat_axis=0, tiled=True, axis...  36.1 us
    ppermute x8, waiting for transfers between devices, by_x(): return lax.ppermute(value, 'head', [(0, 2), (2, 0), (1, 3), (3, 1)])  33.3 us
    all_to_all x7, starting transfers between devices, swap(): lax.all_to_all(value, axes, split_axis=0, concat_axis=0, tiled=True, axis...  33.1 us
    ppermute x1, waiting for transfers between devices, local(): lax.ppermute(slots, 'blk', [(i, (i + halves) % cycle) for i in range(cycl...  26.1 us
    pallas_call x11, Pallas kernels, call(): pl.pallas_call(kernel, out_shape=tuple((jax.ShapeDtypeStruct(shape, kind)...  16.8 us
    pallas_call x1, Pallas kernels, attend_back(): pl.pallas_call(functools.partial(attend_back_kernel, bq=bq, bk=bk, pack=p...  15.3 us
    pallas_call x1, Pallas kernels, attend(): pl.pallas_call(functools.partial(attend_kernel, bq=bq, bk=bk, pack=pack),...  11.1 us
    ppermute x12, waiting for transfers between devices, by_core(): return lax.ppermute(value, 'head', [(0, 1), (1, 0), (2, 3), (3, 2)])  10.6 us
  transfers between devices with their start and end apart: 34, of which 25 were waited for; matrix products, arithmetic and copies ran while one was open for 13% of the time, Pallas kernels for 19%

profile of v9, /device:TPU:0, one launch (start us, length us, event | category | flops | bytes accessed | tf_op | source)
XLA Modules:
  0.0 267.4 jit_solution(14928886053873885346)
XLA Ops:
  8.6 2.4 collective-permute-start
  12.6 1.8 head_slots.1
  14.3 5.0 %all-to-all-start = ((bf16[16,2,24,128]{3,2,1,0:T(8,128)(2,1)}), bf16[16,2,24,128]{3,2,1,0:T(8,128)(2,1)S(1)}, u32[]{:S(2)}, u32[]{:S(2)}) async-start(bf16[16,2,24,128]{3,2,1,0:T(8,128)(2,1)} %head_slots.1), calls=%async_computation | async-start | bytes 393216 | tf_op jit(solution)/shard_map/all_to_all | solution.py:495
  19.5 2.7 collective-permute-start.3
  23.0 2.7 collective-permute-done.3
  25.7 2.4 all-to-all-done
  28.1 1.3 broadcast_in_dim.59
  29.5 4.4 %all-to-all-start.1 = ((bf16[8,128,768]{2,1,0:T(8,128)(2,1)}), bf16[8,128,768]{2,1,0:T(8,128)(2,1)S(1)}, u32[]{:S(2)}, u32[]{:S(2)}) async-start(bf16[8,128,768]{2,1,0:T(8,128)(2,1)} %broadcast_in_dim.59), calls=%async_computation.1 | async-start | bytes 3145728 | tf_op jit(solution)/shard_map/all_to_all | solution.py:495
  36.5 2.6 collective-permute-start.4
  39.6 26.1 %collective-permute-done.4 = bf16[16,2,24,128]{3,2,1,0:T(8,128)(2,1)S(1)} collective-permute-done((bf16[16,2,24,128]{3,2,1,0:T(8,128)(2,1)S(1)}, bf16[16,2,24,128]{3,2,1,0:T(8,128)(2,1)S(1)}, u32[]{:S(2)}, u32[]{:S(2)}) %collective-permute-start.4) | collective-permute-done | bytes 196640 | tf_op jit(solution)/shard_map/ppermute | solution.py:603
  67.5 2.7 %all-to-all-done.1.a_ref = bf16[8,128,768]{2,1,0:T(8,128)(2,1)S(1)} async-done(((bf16[8,128,768]{2,1,0:T(8,128)(2,1)}), bf16[8,128,768]{2,1,0:T(8,128)(2,1)S(1)}, u32[]{:S(2)}, u32[]{:S(2)}) %all-to-all-start.1) | async-done | bytes 1572896 | tf_op jit(solution)/shard_map/all_to_all | solution.py:495
  74.8 5.0 %project.1 = (bf16[2048,64]{1,0:T(8,128)(2,1)}, bf16[2048,64]{1,0:T(8,128)(2,1)}, bf16[2048,64]{1,0:T(8,128)(2,1)}, bf16[64,2048]{1,0:T(8,128)(2,1)}, bf16[64,2048]{1,0:T(8,128)(2,1)}) custom-call(s32[2]{0:T(128)} %pad_add_fusion.1.place_ref, bf16[8,128,768]{2,1,0:T(8,128)(2,1)} %copy-done, bf16[8,128,768]{2,1,0:T(8,128)(2,1)} %copy-done.2, ...), custom_call_target="tpu_custom_call" | custom-call | flops 1000000 | bytes 1024 | tf_op jit(solution)/shard_map/project/pallas_call | solution.py:85
  79.7 11.1 %attend.1 = (bf16[32,32,128]{2,1,0:T(8,128)(2,1)}, f32[64,2048]{1,0:T(8,128)}, f32[1,2048]{1,0:T(1,128)}) custom-call(s32[4]{0:T(128)} %get-tuple-element.83.lo_ref, s32[4]{0:T(128)} %get-tuple-element.84.hi_ref, bf16[2048,64]{1,0:T(8,128)(2,1)} %get-tuple-element.90.q_ref, bf16[2048,64]{1,0:T(8,128)(2,1)} %get-tuple-element.91.k_ref, ...), custom_call_target="tpu_custom_call" | custom-call | flops 1000000 | bytes 1024 | tf_op jit(solution)/shard_map/attend/pallas_call | solution.py:195
  90.8 5.1 %all-to-all-start.2 = ((bf16[32,32,128]{2,1,0:T(8,128)(2,1)}), bf16[32,32,128]{2,1,0:T(8,128)(2,1)S(1)}, u32[]{:S(2)}, u32[]{:S(2)}) async-start(bf16[32,32,128]{2,1,0:T(8,128)(2,1)} %get-tuple-element.94), calls=%async_computation.2 | async-start | bytes 524288 | tf_op jit(solution)/shard_map/all_to_all | solution.py:495
  99.1 1.5 collective-permute-start.6
  100.7 1.8 fusion.16
  102.5 4.1 %all-to-all-done.2.slots_ref = bf16[32,32,128]{2,1,0:T(8,128)(2,1)S(1)} async-done(((bf16[32,32,128]{2,1,0:T(8,128)(2,1)}), bf16[32,32,128]{2,1,0:T(8,128)(2,1)S(1)}, u32[]{:S(2)}, u32[]{:S(2)}) %all-to-all-start.2) | async-done | bytes 262176 | tf_op jit(solution)/shard_map/all_to_all | solution.py:495
  106.6 2.0 collective-permute-done.6
  108.7 1.6 collective-permute-done.7
  113.4 5.7 %collective-permute-done.9.b_ref = bf16[128,768]{1,0:T(8,128)(2,1)S(1)} collective-permute-done((bf16[128,768]{1,0:T(8,128)(2,1)S(1)}, bf16[128,768]{1,0:T(8,128)(2,1)S(1)}, u32[]{:S(2)}, u32[]{:S(2)}) %collective-permute-start.9) | collective-permute-done | bytes 196640 | tf_op jit(solution)/shard_map/ppermute | solution.py:491
  119.1 1.4 collective-permute-done.11.d_ref
  120.5 2.0 inner.1
  122.8 1.6 collective-permute-done.12.got_ref
  125.8 8.7 %collective-permute-done.13.got_ref = bf16[128,768]{1,0:T(8,128)(2,1)S(1)} collective-permute-done((bf16[128,768]{1,0:T(8,128)(2,1)S(1)}, bf16[128,768]{1,0:T(8,128)(2,1)S(1)}, u32[]{:S(2)}, u32[]{:S(2)}) %collective-permute-start.13) | collective-permute-done | bytes 196640 | tf_op jit(solution)/shard_map/ppermute | solution.py:491
  136.5 6.5 %collective-permute-done.14.b_ref = bf16[128,768]{1,0:T(8,128)(2,1)S(1)} collective-permute-done((bf16[128,768]{1,0:T(8,128)(2,1)S(1)}, bf16[128,768]{1,0:T(8,128)(2,1)S(1)}, u32[]{:S(2)}, u32[]{:S(2)}) %collective-permute-start.14) | collective-permute-done | bytes 196640 | tf_op jit(solution)/shard_map/ppermute | solution.py:491
  143.1 1.4 collective-permute-done.16.d_ref
  144.5 2.9 %inner_back.1 = (bf16[512,768]{1,0:T(8,128)(2,1)S(1)}, bf16[512,768]{1,0:T(8,128)(2,1)S(1)}, f32[1,768]{1,0:T(1,128)S(1)}, f32[256,768]{1,0:T(8,128)S(1)}, bf16[256,768]{1,0:T(8,128)(2,1)S(1)}) custom-call(bf16[128,768]{1,0:T(8,128)(2,1)S(1)} %get-tuple-element.116.a_ref, bf16[128,768]{1,0:T(8,128)(2,1)S(1)} %collective-permute-done.14.b_ref, ...), custom_call_target="tpu_custom_call" | custom-call | flops 1000000 | bytes 1024 | tf_op jit(solution)/shard_map/inner_back/pallas_call | solution.py:294
  147.6 1.6 collective-permute-done.17.got_ref
  149.6 2.9 %feed_grad.1 = bf16[8,8,24,768]{3,2,1,0:T(8,128)(2,1)} custom-call(bf16[512,768]{1,0:T(8,128)(2,1)S(1)} %get-tuple-element.122.low_ref, bf16[512,768]{1,0:T(8,128)(2,1)S(1)} %get-tuple-element.123.inner_ref, bf16[512,768]{1,0:T(8,128)(2,1)S(1)} %get-tuple-element.124.act_ref, bf16[512,768]{1,0:T(8,128)(2,1)S(1)} %get-tuple-element.125.ffn_ref), custom_call_target="tpu_custom_call" | custom-call | flops 1000000 | bytes 1024 | tf_op jit(solution)/shard_map/feed_grad/pallas_call | solution.py:294
  152.5 4.8 %collective-permute-done.18.got_ref = bf16[128,768]{1,0:T(8,128)(2,1)S(1)} collective-permute-done((bf16[128,768]{1,0:T(8,128)(2,1)S(1)}, bf16[128,768]{1,0:T(8,128)(2,1)S(1)}, u32[]{:S(2)}, u32[]{:S(2)}) %collective-permute-start.18) | collective-permute-done | bytes 196640 | tf_op jit(solution)/shard_map/ppermute | solution.py:491
  157.4 1.5 branch_back.1
  159.5 2.4 collective-permute-done.19
  163.2 5.3 %all-to-all-start.3 = ((bf16[32,32,128]{2,1,0:T(8,128)(2,1)}), bf16[32,32,128]{2,1,0:T(8,128)(2,1)S(1)}, u32[]{:S(2)}, u32[]{:S(2)}) async-start(bf16[32,32,128]{2,1,0:T(8,128)(2,1)} %get-tuple-element.130), calls=%async_computation.3 | async-start | bytes 524288 | tf_op jit(solution)/shard_map/all_to_all | solution.py:495
  168.6 4.7 %collective-permute-done.20 = bf16[192,768]{1,0:T(8,128)(2,1)S(1)} collective-permute-done((bf16[192,768]{1,0:T(8,128)(2,1)}, bf16[192,768]{1,0:T(8,128)(2,1)S(1)}, u32[]{:S(2)}, u32[]{:S(2)}) %collective-permute-start.20) | collective-permute-done | bytes 294944 | tf_op jit(solution)/shard_map/ppermute | solution.py:491
  173.3 1.9 fusion.3
  175.1 5.6 %all-to-all-done.3.do_ref = bf16[32,32,128]{2,1,0:T(8,128)(2,1)S(1)} async-done(((bf16[32,32,128]{2,1,0:T(8,128)(2,1)}), bf16[32,32,128]{2,1,0:T(8,128)(2,1)S(1)}, u32[]{:S(2)}, u32[]{:S(2)}) %all-to-all-start.3) | async-done | bytes 262176 | tf_op jit(solution)/shard_map/all_to_all | solution.py:495
  180.7 5.9 %all-to-all-start.4 = ((bf16[8,24,768]{2,1,0:T(8,128)(2,1)}), bf16[8,24,768]{2,1,0:T(8,128)(2,1)S(1)}, u32[]{:S(2)}, u32[]{:S(2)}) async-start(bf16[8,24,768]{2,1,0:T(8,128)(2,1)} %bitcast.41), calls=%async_computation.4 | async-start | bytes 589824 | tf_op jit(solution)/shard_map/all_to_all | solution.py:495
  186.6 15.3 %attend_back.1 = (bf16[32,96,128]{2,1,0:T(8,128)(2,1)}, bf16[192,2048]{1,0:T(8,128)(2,1)}, f32[1,128]{1,0:T(1,128)}) custom-call(s32[4]{0:T(128)} %get-tuple-element.110.lo_ref, s32[4]{0:T(128)} %get-tuple-element.111.hi_ref, bf16[2048,64]{1,0:T(8,128)(2,1)} %get-tuple-element.90.q_ref, bf16[2048,64]{1,0:T(8,128)(2,1)} %get-tuple-element.91.k_ref, ...), custom_call_target="tpu_custom_call" | custom-call | flops 1000000 | bytes 1024 | tf_op jit(solution)/shard_map/attend_back/pallas_call | solution.py:273
  203.2 4.7 %all-to-all-start.5 = ((bf16[32,96,128]{2,1,0:T(8,128)(2,1)}), bf16[32,96,128]{2,1,0:T(8,128)(2,1)}, u32[]{:S(2)}, u32[]{:S(2)}) async-start(bf16[32,96,128]{2,1,0:T(8,128)(2,1)} %get-tuple-element.134), calls=%async_computation.5 | async-start | bytes 1572864 | tf_op jit(solution)/shard_map/all_to_all | solution.py:495
  211.6 1.7 copy.83
  217.1 1.4 stack.108
  218.5 1.5 copy.86
  221.1 1.4 weight_grad.1
  223.7 6.2 %all-to-all-done.5.slots_ref = bf16[32,96,128]{2,1,0:T(8,128)(2,1)} async-done(((bf16[32,96,128]{2,1,0:T(8,128)(2,1)}), bf16[32,96,128]{2,1,0:T(8,128)(2,1)}, u32[]{:S(2)}, u32[]{:S(2)}) %all-to-all-start.5) | async-done | bytes 786464 | tf_op jit(solution)/shard_map/all_to_all | solution.py:495
  229.9 2.6 all-to-all-start.6
  232.5 2.3 copy.79
  235.5 3.2 %tokens.1 = bf16[128,768]{1,0:T(8,128)(2,1)} custom-call(bf16[32,96,128]{2,1,0:T(8,128)(2,1)} %all-to-all-done.5.slots_ref, bf16[3,768,768]{2,1,0:T(8,128)(2,1)S(1)} %bitcast.158, f32[128,768]{1,0:T(8,128)S(1)} %get-tuple-element.136.first_ref), custom_call_target="tpu_custom_call" | custom-call | flops 1000000 | bytes 1024 | tf_op jit(solution)/shard_map/tokens/pallas_call | solution.py:294
  238.7 14.5 %all-to-all-done.6.slots_ref = bf16[32,24,256]{2,1,0:T(8,128)(2,1)S(1)} async-done(((bf16[32,24,256]{2,1,0:T(8,128)(2,1)}), bf16[32,24,256]{2,1,0:T(8,128)(2,1)S(1)}, u32[]{:S(2)}, u32[]{:S(2)}) %all-to-all-start.6) | async-done | bytes 393248 | tf_op jit(solution)/shard_map/all_to_all | solution.py:495
  (190 shorter events, 45.0 us)
Async XLA Ops:
  7.2 12.2 %copy-start.9 = (bf16[2,64,768]{2,1,0:T(8,128)(2,1)S(1)}, bf16[2,64,768]{2,1,0:T(8,128)(2,1)}, u32[]{:S(2)}) copy-start(bf16[2,64,768]{2,1,0:T(8,128)(2,1)} %param.11) | copy-start | bytes 589828
  8.6 13.6 %copy-start.31 = (bf16[96,768]{1,0:T(8,128)(2,1)S(1)}, bf16[96,768]{1,0:T(8,128)(2,1)}, u32[]{:S(2)}) copy-start(bf16[96,768]{1,0:T(8,128)(2,1)} %param.17) | copy-start | bytes 442372
  8.6 13.6 %copy-start.32 = (bf16[24,768]{1,0:T(8,128)(2,1)S(1)}, bf16[24,768]{1,0:T(8,128)(2,1)}, u32[]{:S(2)}) copy-start(bf16[24,768]{1,0:T(8,128)(2,1)} %param.15) | copy-start | bytes 110596
  8.6 13.5 %collective-permute-start = (bf16[24,768]{1,0:T(8,128)(2,1)S(1)}, bf16[24,768]{1,0:T(8,128)(2,1)S(1)}, u32[]{:S(2)}, u32[]{:S(2)}) collective-permute-start(bf16[24,768]{1,0:T(8,128)(2,1)S(1)} %bitcast.191), channel_id=1, source_target_pairs={{0,24},{8,16},{16,8},{24,0},{1,25},{9,17},{17,9},{25,1},{2,26},{10... | collective-permute-start | bytes 110600 | tf_op jit(solution)/shard_map/ppermute | solution.py:538
  11.1 11.0 %collective-permute-start.1 = (bf16[24,768]{1,0:T(8,128)(2,1)S(1)}, bf16[24,768]{1,0:T(8,128)(2,1)S(1)}, u32[]{:S(2)}, u32[]{:S(2)}) collective-permute-start(bf16[24,768]{1,0:T(8,128)(2,1)S(1)} %bitcast.192), channel_id=1, source_target_pairs={{0,16},{16,0},{8,24},{24,8},{1,17},{17,1},{9,25},{25,9},{2,18},{18... | collective-permute-start | bytes 110600 | tf_op jit(solution)/shard_map/ppermute | solution.py:491
  11.8 10.4 %collective-permute-start.2 = (bf16[24,768]{1,0:T(8,128)(2,1)S(1)}, bf16[24,768]{1,0:T(8,128)(2,1)S(1)}, u32[]{:S(2)}, u32[]{:S(2)}) collective-permute-start(bf16[24,768]{1,0:T(8,128)(2,1)S(1)} %bitcast.193), channel_id=1, source_target_pairs={{0,8},{8,0},{16,24},{24,16},{1,9},{9,1},{17,25},{25,17},{2,10},{10... | collective-permute-start | bytes 110600 | tf_op jit(solution)/shard_map/ppermute | solution.py:487
  14.3 13.8 %all-to-all-start = ((bf16[16,2,24,128]{3,2,1,0:T(8,128)(2,1)}), bf16[16,2,24,128]{3,2,1,0:T(8,128)(2,1)S(1)}, u32[]{:S(2)}, u32[]{:S(2)}) async-start(bf16[16,2,24,128]{3,2,1,0:T(8,128)(2,1)} %head_slots.1), calls=%async_computation | async-start | bytes 393216 | tf_op jit(solution)/shard_map/all_to_all | solution.py:495
  19.4 78.8 %all-gather.5.cloned.1.call-start = ((), (), s32[]{:S(2)}) async-start(), calls=%async_computation.9 | async-start | bytes 2985984 | tf_op jit(solution)/shard_map/all_gather | solution.py:617
  19.5 6.2 %collective-permute-start.3 = (bf16[64,768]{1,0:T(8,128)(2,1)S(1)}, bf16[64,768]{1,0:T(8,128)(2,1)S(1)}, u32[]{:S(2)}, u32[]{:S(2)}) collective-permute-start(bf16[64,768]{1,0:T(8,128)(2,1)S(1)} %get-tuple-element.175), channel_id=1, source_target_pairs={{0,4},{1,5},{2,6},{3,7},{4,0},{5,1},{6,2},{7,3},{8,12},{9,13},{10,... | collective-permute-start | bytes 294920 | tf_op jit(solution)/shard_map/ppermute | solution.py:578
  29.5 5.2 %copy-start.34 = (s32[2,32]{1,0:T(2,128)S(1)}, s32[2,32]{1,0:T(2,128)}, u32[]{:S(2)}) copy-start(s32[2,32]{1,0:T(2,128)} %param.12) | copy-start | bytes 772
  29.5 40.7 %all-to-all-start.1 = ((bf16[8,128,768]{2,1,0:T(8,128)(2,1)}), bf16[8,128,768]{2,1,0:T(8,128)(2,1)S(1)}, u32[]{:S(2)}, u32[]{:S(2)}) async-start(bf16[8,128,768]{2,1,0:T(8,128)(2,1)} %broadcast_in_dim.59), calls=%async_computation.1 | async-start | bytes 3145728 | tf_op jit(solution)/shard_map/all_to_all | solution.py:495
  33.9 198.6 %all-gather.7.cloned.1.call-start = ((), (), s32[]{:S(2)}) async-start(), calls=%async_computation.10 | async-start | bytes 3649536 | tf_op jit(solution)/shard_map/all_gather | solution.py:616
  36.5 29.2 %collective-permute-start.4 = (bf16[16,2,24,128]{3,2,1,0:T(8,128)(2,1)S(1)}, bf16[16,2,24,128]{3,2,1,0:T(8,128)(2,1)S(1)}, u32[]{:S(2)}, u32[]{:S(2)}) collective-permute-start(bf16[16,2,24,128]{3,2,1,0:T(8,128)(2,1)S(1)} %all-to-all-done), channel_id=1, source_target_pairs={{0,4},{1,5},{2,6},{3,7},{4,0},{5,1},{6,2},{7,3},{8,12},{9,13},{10,... | collective-permute-start | bytes 589832 | tf_op jit(solution)/shard_map/ppermute | solution.py:603
  70.2 3.4 %collective-permute-start.5 = (bf16[8,128,768]{2,1,0:T(8,128)(2,1)S(1)}, bf16[8,128,768]{2,1,0:T(8,128)(2,1)S(1)}, u32[]{:S(2)}, u32[]{:S(2)}) collective-permute-start(bf16[8,128,768]{2,1,0:T(8,128)(2,1)S(1)} %all-to-all-done.1.a_ref), channel_id=1, source_target_pairs={{0,8},{8,0},{16,24},{24,16},{1,9},{9,1},{17,25},{25,17},{2,10},{10... | collective-permute-start | bytes 4718600 | tf_op jit(solution)/shard_map/ppermute | solution.py:487
  90.8 15.8 %all-to-all-start.2 = ((bf16[32,32,128]{2,1,0:T(8,128)(2,1)}), bf16[32,32,128]{2,1,0:T(8,128)(2,1)S(1)}, u32[]{:S(2)}, u32[]{:S(2)}) async-start(bf16[32,32,128]{2,1,0:T(8,128)(2,1)} %get-tuple-element.94), calls=%async_computation.2 | async-start | bytes 524288 | tf_op jit(solution)/shard_map/all_to_all | solution.py:495
  96.0 158.8 %reduce-scatter.2.cloned.1.call-start = ((), (), s32[]{:S(2)}) async-start(), calls=%async_computation.8 | async-start | bytes 2654208 | tf_op jit(solution)/shard_map/reduce_scatter | solution.py:733
  99.1 9.5 %collective-permute-start.6 = (bf16[192,768]{1,0:T(8,128)(2,1)S(1)}, bf16[192,768]{1,0:T(8,128)(2,1)S(1)}, u32[]{:S(2)}, u32[]{:S(2)}) collective-permute-start(bf16[192,768]{1,0:T(8,128)(2,1)S(1)} %bitcast.179), channel_id=1, source_target_pairs={{0,16},{16,0},{8,24},{24,8},{1,17},{17,1},{9,25},{25,9},{2,18},{18... | collective-permute-start | bytes 884744 | tf_op jit(solution)/shard_map/ppermute | solution.py:491
  100.7 8.0 %collective-permute-start.8 = (bf16[192,768]{1,0:T(8,128)(2,1)S(1)}, bf16[192,768]{1,0:T(8,128)(2,1)S(1)}, u32[]{:S(2)}, u32[]{:S(2)}) collective-permute-start(bf16[192,768]{1,0:T(8,128)(2,1)S(1)} %bitcast.180), channel_id=1, source_target_pairs={{0,8},{8,0},{16,24},{24,16},{1,9},{9,1},{17,25},{25,17},{2,10},{10... | collective-permute-start | bytes 884744 | tf_op jit(solution)/shard_map/ppermute | solution.py:487
  108.6 1.6 collective-permute-start.7
  112.1 10.5 %copy-start.14 = (bf16[128,768]{1,0:T(8,128)(2,1)}, bf16[128,768]{1,0:T(8,128)(2,1)S(1)}, u32[]{:S(2)}) copy-start(bf16[128,768]{1,0:T(8,128)(2,1)S(1)} %get-tuple-element.132) | copy-start | bytes 589828
  112.1 10.5 %copy-start.19 = (f32[128,1]{1,0:T(8,128)}, f32[128,1]{1,0:T(8,128)S(1)}, u32[]{:S(2)}) copy-start(f32[128,1]{1,0:T(8,128)S(1)} %get-tuple-element.128.inv_ref) | copy-start | bytes 1540
  112.1 22.4 %copy-start.4 = (f32[128,768]{1,0:T(8,128)}, f32[128,768]{1,0:T(8,128)S(1)}, u32[]{:S(2)}) copy-start(f32[128,768]{1,0:T(8,128)S(1)} %get-tuple-element.107.normed_ref) | copy-start | bytes 1179652
  112.1 7.0 %collective-permute-start.9 = (bf16[128,768]{1,0:T(8,128)(2,1)S(1)}, bf16[128,768]{1,0:T(8,128)(2,1)S(1)}, u32[]{:S(2)}, u32[]{:S(2)}) collective-permute-start(bf16[128,768]{1,0:T(8,128)(2,1)S(1)} %get-tuple-element.99.a_ref), channel_id=1, source_target_pairs={{0,16},{16,0},{8,24},{24,8},{1,17},{17,1},{9,25},{25,9},{2,18},{18... | collective-permute-start | bytes 589832 | tf_op jit(solution)/shard_map/ppermute | solution.py:491
  113.4 5.7 %collective-permute-start.10 = (bf16[128,768]{1,0:T(8,128)(2,1)S(1)}, bf16[128,768]{1,0:T(8,128)(2,1)S(1)}, u32[]{:S(2)}, u32[]{:S(2)}) collective-permute-start(bf16[128,768]{1,0:T(8,128)(2,1)S(1)} %get-tuple-element.99.a_ref), channel_id=1, source_target_pairs={{0,8},{8,0},{16,24},{24,16},{1,9},{9,1},{17,25},{25,17},{2,10},{10... | collective-permute-start | bytes 589832 | tf_op jit(solution)/shard_map/ppermute | solution.py:487
  119.1 1.4 collective-permute-start.11
  122.6 11.9 %copy-start.13 = (bf16[2,64,768]{2,1,0:T(8,128)(2,1)S(1)}, bf16[2,64,768]{2,1,0:T(8,128)(2,1)}, u32[]{:S(2)}) copy-start(bf16[2,64,768]{2,1,0:T(8,128)(2,1)} %param.13) | copy-start | bytes 589828
  122.6 11.9 %copy-start.17 = (f32[8,768]{1,0:T(8,128)S(1)}, f32[8,768]{1,0:T(8,128)}, u32[]{:S(2)}) copy-start(f32[8,768]{1,0:T(8,128)} %stack.100.vec_ref) | copy-start | bytes 73732
  122.6 1.8 collective-permute-start.12
  124.5 10.0 %collective-permute-start.13 = (bf16[128,768]{1,0:T(8,128)(2,1)S(1)}, bf16[128,768]{1,0:T(8,128)(2,1)S(1)}, u32[]{:S(2)}, u32[]{:S(2)}) collective-permute-start(bf16[128,768]{1,0:T(8,128)(2,1)S(1)} %get-tuple-element.106), channel_id=1, source_target_pairs={{0,16},{16,0},{8,24},{24,8},{1,17},{17,1},{9,25},{25,9},{2,18},{18... | collective-permute-start | bytes 589832 | tf_op jit(solution)/shard_map/ppermute | solution.py:491
  136.2 13.0 %copy-start.21 = (f32[8,768]{1,0:T(8,128)}, f32[8,768]{1,0:T(8,128)S(1)}, u32[]{:S(2)}) copy-start(f32[8,768]{1,0:T(8,128)S(1)} %get-tuple-element.140) | copy-start | bytes 73732
  136.2 6.8 %collective-permute-start.14 = (bf16[128,768]{1,0:T(8,128)(2,1)S(1)}, bf16[128,768]{1,0:T(8,128)(2,1)S(1)}, u32[]{:S(2)}, u32[]{:S(2)}) collective-permute-start(bf16[128,768]{1,0:T(8,128)(2,1)S(1)} %get-tuple-element.116.a_ref), channel_id=1, source_target_pairs={{0,16},{16,0},{8,24},{24,8},{1,17},{17,1},{9,25},{25,9},{2,18},{18... | collective-permute-start | bytes 589832 | tf_op jit(solution)/shard_map/ppermute | solution.py:491
  136.5 6.5 %collective-permute-start.15 = (bf16[128,768]{1,0:T(8,128)(2,1)S(1)}, bf16[128,768]{1,0:T(8,128)(2,1)S(1)}, u32[]{:S(2)}, u32[]{:S(2)}) collective-permute-start(bf16[128,768]{1,0:T(8,128)(2,1)S(1)} %get-tuple-element.116.a_ref), channel_id=1, source_target_pairs={{0,8},{8,0},{16,24},{24,16},{1,9},{9,1},{17,25},{25,17},{2,10},{10... | collective-permute-start | bytes 589832 | tf_op jit(solution)/shard_map/ppermute | solution.py:487
  143.1 1.4 collective-permute-start.16
  147.4 1.8 collective-permute-start.17
  149.2 8.0 %collective-permute-start.18 = (bf16[128,768]{1,0:T(8,128)(2,1)S(1)}, bf16[128,768]{1,0:T(8,128)(2,1)S(1)}, u32[]{:S(2)}, u32[]{:S(2)}) collective-permute-start(bf16[128,768]{1,0:T(8,128)(2,1)S(1)} %get-tuple-element.121), channel_id=1, source_target_pairs={{0,16},{16,0},{8,24},{24,8},{1,17},{17,1},{9,25},{25,9},{2,18},{18... | collective-permute-start | bytes 589832 | tf_op jit(solution)/shard_map/ppermute | solution.py:491
  159.5 2.5 collective-permute-start.19
  162.9 10.3 %collective-permute-start.20 = (bf16[192,768]{1,0:T(8,128)(2,1)}, bf16[192,768]{1,0:T(8,128)(2,1)S(1)}, u32[]{:S(2)}, u32[]{:S(2)}) collective-permute-start(bf16[192,768]{1,0:T(8,128)(2,1)} %fusion.6), channel_id=1, source_target_pairs={{0,16},{16,0},{8,24},{24,8},{1,17},{17,1},{9,25},{25,9},{2,18},{18... | collective-permute-start | bytes 884744 | tf_op jit(solution)/shard_map/ppermute | solution.py:491
  163.2 17.5 %all-to-all-start.3 = ((bf16[32,32,128]{2,1,0:T(8,128)(2,1)}), bf16[32,32,128]{2,1,0:T(8,128)(2,1)S(1)}, u32[]{:S(2)}, u32[]{:S(2)}) async-start(bf16[32,32,128]{2,1,0:T(8,128)(2,1)} %get-tuple-element.130), calls=%async_computation.3 | async-start | bytes 524288 | tf_op jit(solution)/shard_map/all_to_all | solution.py:495
  180.7 5.9 %copy-start.27 = (bf16[32,32,128]{2,1,0:T(8,128)(2,1)}, bf16[32,32,128]{2,1,0:T(8,128)(2,1)S(1)}, u32[]{:S(2)}) copy-start(bf16[32,32,128]{2,1,0:T(8,128)(2,1)S(1)} %all-to-all-done.3.do_ref) | copy-start | bytes 786436
  180.7 21.7 %all-to-all-start.4 = ((bf16[8,24,768]{2,1,0:T(8,128)(2,1)}), bf16[8,24,768]{2,1,0:T(8,128)(2,1)S(1)}, u32[]{:S(2)}, u32[]{:S(2)}) async-start(bf16[8,24,768]{2,1,0:T(8,128)(2,1)} %bitcast.41), calls=%async_computation.4 | async-start | bytes 589824 | tf_op jit(solution)/shard_map/all_to_all | solution.py:495
  186.6 33.4 %copy-start.3 = (bf16[8,128,768]{2,1,0:T(8,128)(2,1)S(1)}, bf16[8,128,768]{2,1,0:T(8,128)(2,1)}, u32[]{:S(2)}) copy-start(bf16[8,128,768]{2,1,0:T(8,128)(2,1)} %copy-done.2) | copy-start | bytes 4718596
  203.2 16.8 %copy-start.1 = (bf16[8,128,768]{2,1,0:T(8,128)(2,1)S(1)}, bf16[8,128,768]{2,1,0:T(8,128)(2,1)}, u32[]{:S(2)}) copy-start(bf16[8,128,768]{2,1,0:T(8,128)(2,1)} %copy-done) | copy-start | bytes 4718596
  203.2 16.8 %copy-start.23 = (s32[2]{0:T(128)S(1)}, s32[2]{0:T(128)}, u32[]{:S(2)}) copy-start(s32[2]{0:T(128)} %pad_add_fusion.1.place_ref) | copy-start | bytes 28
  203.2 26.7 %all-to-all-start.5 = ((bf16[32,96,128]{2,1,0:T(8,128)(2,1)}), bf16[32,96,128]{2,1,0:T(8,128)(2,1)}, u32[]{:S(2)}, u32[]{:S(2)}) async-start(bf16[32,96,128]{2,1,0:T(8,128)(2,1)} %get-tuple-element.134), calls=%async_computation.5 | async-start | bytes 1572864 | tf_op jit(solution)/shard_map/all_to_all | solution.py:495
  229.9 23.3 %all-to-all-start.6 = ((bf16[32,24,256]{2,1,0:T(8,128)(2,1)}), bf16[32,24,256]{2,1,0:T(8,128)(2,1)S(1)}, u32[]{:S(2)}, u32[]{:S(2)}) async-start(bf16[32,24,256]{2,1,0:T(8,128)(2,1)} %pad_maximum_fusion.2), calls=%async_computation.6 | async-start | bytes 786432 | tf_op jit(solution)/shard_map/all_to_all | solution.py:495
  255.8 3.4 %collective-permute-start.21 = (bf16[24,768]{1,0:T(8,128)(2,1)S(1)}, bf16[24,768]{1,0:T(8,128)(2,1)S(1)}, u32[]{:S(2)}, u32[]{:S(2)}) collective-permute-start(bf16[24,768]{1,0:T(8,128)(2,1)S(1)} %get-tuple-element.180), channel_id=1, source_target_pairs={{0,24},{8,16},{16,8},{24,0},{1,25},{9,17},{17,9},{25,1},{2,26},{10... | collective-permute-start | bytes 110600 | tf_op jit(solution)/shard_map/ppermute | solution.py:538
  256.1 4.0 %collective-permute-start.22 = (bf16[24,768]{1,0:T(8,128)(2,1)S(1)}, bf16[24,768]{1,0:T(8,128)(2,1)S(1)}, u32[]{:S(2)}, u32[]{:S(2)}) collective-permute-start(bf16[24,768]{1,0:T(8,128)(2,1)S(1)} %get-tuple-element.179), channel_id=1, source_target_pairs={{0,16},{16,0},{8,24},{24,8},{1,17},{17,1},{9,25},{25,9},{2,18},{18... | collective-permute-start | bytes 110600 | tf_op jit(solution)/shard_map/ppermute | solution.py:491
  256.5 3.5 %collective-permute-start.23 = (bf16[24,768]{1,0:T(8,128)(2,1)S(1)}, bf16[24,768]{1,0:T(8,128)(2,1)S(1)}, u32[]{:S(2)}, u32[]{:S(2)}) collective-permute-start(bf16[24,768]{1,0:T(8,128)(2,1)S(1)} %get-tuple-element.178), channel_id=1, source_target_pairs={{0,8},{8,0},{16,24},{24,16},{1,9},{9,1},{17,25},{25,17},{2,10},{10... | collective-permute-start | bytes 110600 | tf_op jit(solution)/shard_map/ppermute | solution.py:487
  (21 other events, 54.2 us)
Sparse Core Ops, SparseCore 0:
  28.3 69.8 all-gather.4
  101.1 61.3 all-gather.6
  166.0 85.9 reduce-scatter.1
